TPU v7x, 128 devices: a whole 4x4x4 slice. The times are simulated.
128 devices in a mesh: gx: 8 (over x, z_lo), gy: 16 (over y, z_hi, core).
Axes of the slice: x: 4, y: 4, z: 4 (z_hi: 2, z_lo: 2; z = z_hi * 2 + z_lo), core: 2. Of those that a mesh axis runs over, the one named last changes fastest.
Arguments:
- initial_fields: float32 [5, 32, 64, 2048], P(None, 'gx', 'gy'), may hold values from -6 to 6
- velocity: float32 [3, 32, 64, 2048], P(None, 'gx', 'gy'), may hold values from -0.16 to 0.16
- diffusivity: float32 [32, 64, 2048], P('gx', 'gy'), may hold values from 0.08 to 0.16
- patch_anchor: int32 [8, 16, 2], P('gx', 'gy'), may hold values from 0 to 56
- patch_count: int32 [8, 16], P('gx', 'gy'), may hold values from 1 to 2, as said below
- weight_one: float32 [32, 5, 3, 3, 3], replicated, may hold values from -0.5 to 0.5
- bias_one: float32 [32], replicated, may hold values from -3 to 3
- weight_two: float32 [32, 32, 3, 3, 3], replicated, may hold values from -0.21875 to 0.21875
- bias_two: float32 [32], replicated, may hold values from -3 to 3
- weight_three: float32 [5, 32, 3, 3, 3], replicated, may hold values from -0.21875 to 0.21875
- bias_three: float32 [5], replicated, may hold values from -3 to 3
Outputs:
- final_fields: float32 [5, 32, 64, 2048], P(None, 'gx', 'gy')
- grad_weight_one: float32 [32, 5, 3, 3, 3], replicated
- grad_bias_one: float32 [32], replicated
- grad_weight_two: float32 [32, 32, 3, 3, 3], replicated
- grad_bias_two: float32 [32], replicated
- grad_weight_three: float32 [5, 32, 3, 3, 3], replicated
- grad_bias_three: float32 [5], replicated
- loss: float32 [], replicated
Inputs may be any that keep to these rules, and one draw needn't show every extreme that they name: `patch_count`: slots 0 to count - 1 of a shard are live; at least one shard has all 2 slots live in every draw.
All inputs are finite; a program needn't handle non-finite values.
Results may differ from a plain program's by a relative error of at most 0.005.
Values sent between devices are 32-bit elements; how exact they have to be, the bound alone decides.
No kernel may reach another device: no remote copies, remote signals or barrier semaphores. Data moves between devices by JAX's collectives and lax.ppermute only.
A program may use at most 128 MiB of HBM per device.

v0:
```python
import jax
import jax.numpy as jnp
from jax import lax
from jax.sharding import PartitionSpec as P

STEPS = 3
PY = 8


def padded_2(cells, sides, width):
    for axis, dim in sides:
        count = lax.axis_size(axis)
        ends = count - 1
        head = lax.slice_in_dim(cells, 0, width, axis=dim)
        tail = lax.slice_in_dim(cells, cells.shape[dim] - width, cells.shape[dim], axis=dim)
        cells = jnp.concatenate(
            [
                lax.ppermute(tail, axis, [(i, (i + 1) % count) for i in range(ends)]),
                cells,
                lax.ppermute(head, axis, [((i + 1) % count, i) for i in range(ends)]),
            ],
            axis=dim,
        )
    return cells


def transport(extended, velocity, diffusivity):
    padded = jnp.pad(extended, ((0, 0), (0, 0), (0, 0), (1, 1)))
    middle = padded[:, 1:-1, 1:-1, 1:-1]
    x_plus = padded[:, 2:, 1:-1, 1:-1]
    x_minus = padded[:, :-2, 1:-1, 1:-1]
    y_plus = padded[:, 1:-1, 2:, 1:-1]
    y_minus = padded[:, 1:-1, :-2, 1:-1]
    z_plus = padded[:, 1:-1, 1:-1, 2:]
    z_minus = padded[:, 1:-1, 1:-1, :-2]
    carried = (
        velocity[0] * (x_plus - x_minus)
        + velocity[1] * (y_plus - y_minus)
        + velocity[2] * (z_plus - z_minus)
    )
    spread = x_plus + x_minus + y_plus + y_minus + z_plus + z_minus - 6.0 * middle
    return middle - 0.5 * carried + diffusivity * spread


def convolve(inputs, kernel):
    return lax.conv_general_dilated(
        inputs,
        kernel.astype(jnp.bfloat16),
        (1, 1, 1),
        "SAME",
        dimension_numbers=("NCDHW", "OIDHW", "NCDHW"),
        preferred_element_type=jnp.float32,
    )


def patch_loss(params, inputs, delta, live):
    weight_one, bias_one, weight_two, bias_two, weight_three, bias_three = params
    hidden_one = jax.nn.silu(
        convolve(inputs, weight_one) + bias_one[None, :, None, None, None]
    ).astype(jnp.bfloat16)
    hidden_two = jax.nn.silu(
        convolve(hidden_one, weight_two) + bias_two[None, :, None, None, None]
    ).astype(jnp.bfloat16)
    predicted = convolve(hidden_two, weight_three) + bias_three[None, :, None, None, None]
    error = predicted - delta
    cells = delta.shape[1] * delta.shape[2] * delta.shape[3] * delta.shape[4]
    return jnp.sum(live[:, None, None, None, None] * error * error) / cells


def on_device(
    initial_fields,
    velocity,
    diffusivity,
    patch_anchor,
    patch_count,
    weight_one,
    bias_one,
    weight_two,
    bias_two,
    weight_three,
    bias_three,
):
    fields = initial_fields
    for step in range(STEPS):
        extended = padded_2(fields, (("gx", 1), ("gy", 2)), 1)
        fields = transport(extended, velocity, diffusivity)
    first, last = (
        lax.all_to_all(initial_fields, "gy", split_axis=3, concat_axis=2, tiled=True),
        lax.all_to_all(fields, "gy", split_axis=3, concat_axis=2, tiled=True),
    )
    anchors = patch_anchor.reshape(-1)
    count = patch_count.reshape(())
    slots = anchors.shape[0]
    first_patches = jax.vmap(lambda o: lax.dynamic_slice_in_dim(first, o, PY, 2))(anchors)
    last_patches = jax.vmap(lambda o: lax.dynamic_slice_in_dim(last, o, PY, 2))(anchors)
    delta = last_patches - first_patches
    live = (jnp.arange(slots, dtype=jnp.int32) < count).astype(jnp.float32)
    params = (weight_one, bias_one, weight_two, bias_two, weight_three, bias_three)
    value, pullback = jax.vjp(
        lambda p: patch_loss(p, first_patches.astype(jnp.bfloat16), delta, live), params
    )
    grads = pullback(jnp.ones((), jnp.float32))[0]
    summed = lax.psum(
        (
            grads[0],
            grads[1],
            grads[2],
            grads[3],
            grads[4],
            grads[5],
            value,
            count.astype(jnp.float32),
        ),
        ("gx", "gy"),
    )
    total = summed[7]
    return (
        fields,
        summed[0] / total,
        summed[1] / total,
        summed[2] / total,
        summed[3] / total,
        summed[4] / total,
        summed[5] / total,
        summed[6] / total,
    )


def solution(mesh):
    return jax.shard_map(
        on_device,
        mesh=mesh,
        in_specs=(
            P(None, "gx", "gy", None),
            P(None, "gx", "gy", None),
            P("gx", "gy", None),
            P("gx", "gy", None),
            P("gx", "gy"),
            P(),
            P(),
            P(),
            P(),
            P(),
            P(),
        ),
        out_specs=(P(None, "gx", "gy", None), P(), P(), P(), P(), P(), P(), P()),
        check_vma=False,
    )
```

profile of v0, /device:TPU:1, one launch (start us, length us, event | category | flops | bytes accessed | tf_op | source)
XLA Modules:
  0.0 687.6 jit_solution(10052513022806547473)
XLA Ops:
  9.5 5.0 collective-permute-start.1
  14.5 13.4 %copy.137 = f32[5,4,4,2048]{0,2,1,3:T(4,128)} copy(f32[5,4,4,2048]{3,2,1,0:T(4,128)} %param.11) | data formatting | bytes 1310720 | tf_op args[0]
  27.9 19.9 %reshape.169 = f32[16,1,10240]{2,1,0:T(1,128)} reshape(f32[2048,4,4,5]{3,2,1,0:T(4,128)} %bitcast.127) | data formatting | bytes 1310720
  47.8 9.0 %all-to-all-start = ((f32[16,1,10240]{2,1,0:T(1,128)}), f32[16,1,10240]{2,1,0:T(1,128)S(1)}, u32[]{:S(2)}, u32[]{:S(2)}) async-start(f32[16,1,10240]{2,1,0:T(1,128)} %reshape.169), calls=%async_computation | async-start | bytes 1310720 | tf_op jit(solution)/shard_map/all_to_all | solution.py:88
  59.8 5.1 collective-permute-start.3
  66.0 5.9 collective-permute-done.2
  72.0 3.9 collective-permute-done.3
  77.3 2.3 multiply_add_fusion.2
  81.4 4.0 collective-permute-start.5
  91.2 7.5 %collective-permute-start.7 = (f32[5,6,1,2048]{3,1,2,0:T(8,128)}, f32[5,6,1,2048]{3,1,2,0:T(8,128)}, u32[]{:S(2)}, u32[]{:S(2)}) collective-permute-start(f32[5,6,1,2048]{3,1,2,0:T(8,128)} %get-tuple-element.64), channel_id=1, source_target_pairs={{0,1},{1,2},{2,3},{3,4},{4,5},{5,6},{6,7},{7,8},{8,9},{9,10},{10,1... | collective-permute-start | bytes 737288 | tf_op jit(solution)/shard_map/ppermute | solution.py:18
  101.5 28.6 %reshape.170 = f32[2048,4,4,5]{3,2,1,0:T(4,128)} reshape(f32[16,10240]{1,0:T(8,128)S(1)} %reduce) | data formatting | bytes 1310720
  130.0 14.0 %copy.138 = f32[5,4,4,16,128]{4,0,1,2,3:T(8,128)S(1)} copy(f32[5,4,4,16,128]{0,2,1,4,3:T(4,128)} %bitcast.125) | data formatting | bytes 1310720 | tf_op jit(solution)/shard_map/all_to_all | solution.py:88
  146.6 2.9 copy.148
  149.5 10.3 %fusion.36 = (bf16[4,8,16,17,32]{4,2,3,1,0:T(8,128)(2,1)S(1)}, f32[4,8,16,17,32]{4,2,3,1,0:T(8,128)}) fusion(f32[32]{0:T(128)} %param.17, pred[16,17]{0,1:T(8,128)(4,1)S(1)} %copy-done.44, bf16[5,4,8,16,19]{3,0,4,2,1:T(8,128)(2,1)} %copy.148, bf16[32,5,3,3,3]{0,4,3,2,1:T(4,128)(2,1)} %convert_element_type.69), kind=kOutput, calls=%fused_computation.67 | convolution fusion | flops 59674624 | bytes 1777488 | tf_op jit(solution)/shard_map/jvp()/conv_general_dilated | solution.py:46
  160.0 9.8 %fusion.37 = (bf16[4,8,16,17,32]{4,2,3,1,0:T(8,128)(2,1)S(1)}, f32[4,8,16,17,32]{4,2,3,1,0:T(8,128)}) fusion(f32[32]{0:T(128)S(1)} %copy-done.48, pred[16,17]{0,1:T(8,128)(4,1)S(1)} %copy-done.44, f32[32,32,3,3,3]{1,0,4,3,2:T(8,128)S(1)} %copy-done.45, bf16[4,8,2,8,1,32]{5,3,2,4,1,0:T(8,128)(2,1)S(1)} %pad.16, ...), kind=kOutput, calls=%fused_computation.68 | convolution fusion | flops 371502080 | bytes 2404752 | tf_op jit(solution)/shard_map/jvp()/conv_general_dilated | solution.py:46
  170.0 2.7 fusion.113
  176.4 65.1 %fusion.42 = f32[4,8,16,17,5]{2,4,3,1,0:T(8,128)} fusion(bf16[4,8,2,8,1,32]{5,3,2,4,1,0:T(8,128)(2,1)} %pad.21, bf16[4,8,2,8,17,32]{5,3,2,4,1,0:T(8,128)(2,1)} %bitcast.135, bf16[4,8,2,8,1,32]{5,3,2,4,1,0:T(8,128)(2,1)} %pad.20, f32[5]{0:T(128)} %param.21, bf16[5,32,3,3,3]{1,4,3,2,0:T(4,128)(2,1)} %convert_element_type.73), kind=kOutput, calls=%fused_computation.83 | convolution fusion | flops 59357696 | bytes 805332 | tf_op jit(solution)/shard_map/jvp()/conv_general_dilated | solution.py:46
  241.5 2.6 select_maximum_fusion.7
  244.2 3.3 multiply_add_fusion.1
  249.2 4.1 collective-permute-start.9
  254.9 2.4 collective-permute-done.9
  259.7 6.5 collective-permute-start.11
  267.5 3.0 maximum_bitcast_fusion.6
  270.5 2.5 collective-permute-done.11
  274.5 2.4 multiply_add_fusion
  276.8 12.0 %copy.153 = f32[5,4,4,2048]{0,2,1,3:T(4,128)} copy(f32[5,4,4,2048]{3,1,2,0:T(4,128)S(1)} %multiply_add_fusion) | data formatting | bytes 1310720 | tf_op jit(solution)/shard_map/add | solution.py:42
  288.9 19.9 %reshape.171 = f32[16,1,10240]{2,1,0:T(1,128)} reshape(f32[2048,4,4,5]{3,2,1,0:T(4,128)} %bitcast.128) | data formatting | bytes 1310720
  308.7 8.1 %all-to-all-start.1 = ((f32[16,1,10240]{2,1,0:T(1,128)}), f32[16,1,10240]{2,1,0:T(1,128)}, u32[]{:S(2)}, u32[]{:S(2)}) async-start(f32[16,1,10240]{2,1,0:T(1,128)} %reshape.171), calls=%async_computation.1 | async-start | bytes 1310720 | tf_op jit(solution)/shard_map/all_to_all | solution.py:89
  317.1 3.6 fusion.86
  321.6 3.2 copy.151
  328.7 2.6 copy.143
  332.5 2.6 copy.145
  336.5 2.6 copy.144
  340.1 3.0 maximum_bitcast_fusion.4
  344.3 3.3 reduce.1
  347.6 29.0 %reshape.172 = f32[2048,4,4,5]{3,2,1,0:T(4,128)} reshape(f32[16,10240]{1,0:T(8,128)S(1)} %reduce.1) | data formatting | bytes 1310720
  376.6 14.0 %copy.154 = f32[5,4,4,16,128]{4,0,1,2,3:T(8,128)S(1)} copy(f32[5,4,4,16,128]{0,2,1,4,3:T(4,128)} %bitcast.126) | data formatting | bytes 1310720 | tf_op jit(solution)/shard_map/all_to_all | solution.py:89
  396.7 2.7 copy.157
  399.4 9.2 %fusion.10 = f32[4,8,16,17,32]{4,2,3,1,0:T(8,128)S(1)} fusion(f32[4,8,16,17,32]{4,2,3,1,0:T(8,128)} %get-tuple-element.84, f32[32]{0:T(128)S(1)} %copy-done.49, pred[16,17]{0,1:T(8,128)(4,1)S(1)} %copy-done.44, bf16[5,4,8,16,19]{3,0,4,2,1:T(8,128)(2,1)S(1)} %copy.157, bf16[5,32,3,3,3]{1,4,3,2,0:T(4,128)(2,1)} %convert_element_type.73), kind=kOutput, calls=%fused_computation.23 | convolution fusion | flops 60788736 | bytes 2334544 | tf_op jit(solution)/shard_map/transpose(jvp())/conv_general_dilated | solution.py:46
  408.7 2.2 select_bitcast_fusion
  411.6 2.8 copy.160
  415.1 2.6 copy.165
  419.4 12.7 %select_reduce_fusion.1 = (f32[32]{0:T(128)S(1)}, f32[32]{0:T(128)S(1)}, bf16[4,8,16,17,32]{4,2,3,1,0:T(8,128)(2,1)S(1)}) fusion(f32[4,8,16,17,32]{4,2,3,1,0:T(8,128)} %copy-done, pred[16,17]{0,1:T(8,128)(4,1)S(1)} %copy-done.44, f32[32]{0:T(128)S(1)} %copy-done.50, f32[4,8,16,17,32]{4,2,3,1,0:T(8,128)} %get-tuple-element.82, ...), kind=kOutput, calls=%fused_computation.39 | convolution fusion | flops 375532480 | bytes 3510928 | tf_op jit(solution)/shard_map/transpose(jvp())/conv_general_dilated | solution.py:46
  432.2 6.6 fusion.82
  438.8 8.0 %fusion.74 = f32[32,5,3,3,3]{0,1,4,3,2:T(8,128)S(1)} fusion(bf16[4,8,16,17,32]{4,2,3,1,0:T(8,128)(2,1)S(1)} %get-tuple-element.85, pred[16,17]{0,1:T(8,128)(4,1)S(1)} %copy-done.44, bf16[5,4,8,16,17,1]{3,0,5,4,2,1:T(8,128)(2,1)S(1)} %copy-done.30, bf16[5,4,8,16,17,1]{3,0,5,4,2,1:T(8,128)(2,1)S(1)} %copy-done.31, ...), kind=kOutput, calls=%fused_computation.98 | convolution fusion | flops 58512608 | bytes 835728 | tf_op jit(solution)/shard_map/transpose(jvp())/conv_general_dilated | solution.py:46
  446.7 69.4 %all-reduce.3 = (f32[32,5,3,3,3]{0,1,4,3,2:T(8,128)S(1)}, f32[]{:T(128)}, f32[32]{0:T(128)S(1)}, f32[32]{0:T(128)S(1)}, f32[5,32,3,3,3]{1,0,4,3,2:T(8,128)S(1)}, /*index=5*/f32[5]{0:T(128)S(1)}, f32[]{:T(128)}) all-reduce(f32[32,5,3,3,3]{0,1,4,3,2:T(8,128)S(1)} %fusion.74, ...), channel_id=1, replica_groups=mesh['gx'=8,'gy'=16] {'gx','gy'}, use_global_device_ids=true, to_apply=%region_0.1 | all-reduce | flops 8711 | bytes 69688 | tf_op jit(solution)/shard_map/psum | solution.py:103
  522.8 13.0 %fusion.56 = f32[32,32,3,3,3]{0,1,4,3,2:T(8,128)} fusion(bf16[32,4,8,16,17,1]{0,2,4,3,1,5:T(8,128)(2,1)S(1)} %bitcast.140, bf16[4,8,16,17,32,1]{4,2,3,1,0,5:T(8,128)(2,1)S(1)} %copy-done.16, bf16[4,8,16,17,32,1]{4,2,3,1,0,5:T(8,128)(2,1)S(1)} %bitcast.132, bf16[4,8,16,17,32,1]{4,2,3,1,0,5:T(8,128)(2,1)S(1)} %copy-done.15), kind=kOutput, calls=%fused_computation.94 | convolution fusion | flops 369355776 | bytes 2338816 | tf_op jit(solution)/shard_map/transpose(jvp())/conv_general_dilated | solution.py:46
  540.5 136.0 %all-reduce.6.cloned.1.call-done = f32[32,32,3,3,3]{0,1,4,3,2:T(8,128)} async-done(((f32[32,32,3,3,3]{0,1,4,3,2:T(8,128)}), f32[32,32,3,3,3]{0,1,4,3,2:T(8,128)}) %all-reduce.6.cloned.1.call-update) | async-done | bytes 110608 | tf_op jit(solution)/shard_map/psum | solution.py:103
  (200 shorter events, 63.0 us)
Async XLA Ops:
  8.2 49.0 %collective-permute-start = (f32[5,1,4,2048]{3,2,1,0:T(4,128)S(1)}, f32[5,1,4,2048]{3,2,1,0:T(4,128)S(1)}, u32[]{:S(2)}, u32[]{:S(2)}) collective-permute-start(f32[5,1,4,2048]{3,2,1,0:T(4,128)S(1)} %get-tuple-element.77), channel_id=1, source_target_pairs={{16,0},{32,16},{48,32},{64,48},{80,64},{96,80},{112,96},{17,1},{33... | collective-permute-start | bytes 491528 | tf_op jit(solution)/shard_map/ppermute | solution.py:20
  9.5 47.9 %collective-permute-start.1 = (f32[5,1,4,2048]{3,2,1,0:T(4,128)S(1)}, f32[5,1,4,2048]{3,2,1,0:T(4,128)S(1)}, u32[]{:S(2)}, u32[]{:S(2)}) collective-permute-start(f32[5,1,4,2048]{3,2,1,0:T(4,128)S(1)} %get-tuple-element.76), channel_id=1, source_target_pairs={{0,16},{16,32},{32,48},{48,64},{64,80},{80,96},{96,112},{1,17},{17... | collective-permute-start | bytes 491528 | tf_op jit(solution)/shard_map/ppermute | solution.py:18
  27.9 28.9 %copy-start.5 = (f32[5,4,4,2048]{3,2,1,0:T(4,128)S(1)}, f32[5,4,4,2048]{3,2,1,0:T(4,128)}, u32[]{:S(2)}) copy-start(f32[5,4,4,2048]{3,2,1,0:T(4,128)} %param.11) | copy-start | bytes 1966084
  47.8 17.1 %copy-start.39 = (f32[3,4,4,2048]{3,2,1,0:T(4,128)S(1)}, f32[3,4,4,2048]{3,2,1,0:T(4,128)}, u32[]{:S(2)}) copy-start(f32[3,4,4,2048]{3,2,1,0:T(4,128)} %param.12) | copy-start | bytes 1179652
  47.8 51.0 %all-to-all-start = ((f32[16,1,10240]{2,1,0:T(1,128)}), f32[16,1,10240]{2,1,0:T(1,128)S(1)}, u32[]{:S(2)}, u32[]{:S(2)}) async-start(f32[16,1,10240]{2,1,0:T(1,128)} %reshape.169), calls=%async_computation | async-start | bytes 1310720 | tf_op jit(solution)/shard_map/all_to_all | solution.py:88
  57.2 8.1 %copy-start.41 = (f32[4,4,2048]{2,1,0:T(4,128)S(1)}, f32[4,4,2048]{2,1,0:T(4,128)}, u32[]{:S(2)}) copy-start(f32[4,4,2048]{2,1,0:T(4,128)} %param.13) | copy-start | bytes 393220
  57.2 8.8 %copy-start.47 = (s32[1,1,2]{2,1,0:T(1,128)S(1)}, s32[1,1,2]{2,1,0:T(1,128)}, u32[]{:S(2)}) copy-start(s32[1,1,2]{2,1,0:T(1,128)} %param.14) | copy-start | bytes 28
  57.8 14.1 %collective-permute-start.2 = (f32[5,6,1,2048]{3,1,2,0:T(8,128)S(1)}, f32[5,6,1,2048]{3,1,2,0:T(8,128)S(1)}, u32[]{:S(2)}, u32[]{:S(2)}) collective-permute-start(f32[5,6,1,2048]{3,1,2,0:T(8,128)S(1)} %get-tuple-element.67), channel_id=1, source_target_pairs={{1,0},{2,1},{3,2},{4,3},{5,4},{6,5},{7,6},{8,7},{9,8},{10,9},{11,1... | collective-permute-start | bytes 737288 | tf_op jit(solution)/shard_map/ppermute | solution.py:20
  59.8 16.0 %collective-permute-start.3 = (f32[5,6,1,2048]{3,1,2,0:T(8,128)S(1)}, f32[5,6,1,2048]{3,1,2,0:T(8,128)S(1)}, u32[]{:S(2)}, u32[]{:S(2)}) collective-permute-start(f32[5,6,1,2048]{3,1,2,0:T(8,128)S(1)} %get-tuple-element.66), channel_id=1, source_target_pairs={{0,1},{1,2},{2,3},{3,4},{4,5},{5,6},{6,7},{7,8},{8,9},{9,10},{10,1... | collective-permute-start | bytes 737288 | tf_op jit(solution)/shard_map/ppermute | solution.py:18
  65.0 12.2 %copy-start.17 = (f32[4,4,2048]{2,0,1:T(4,128)}, f32[4,4,2048]{2,0,1:T(4,128)S(1)}, u32[]{:S(2)}) copy-start(f32[4,4,2048]{2,0,1:T(4,128)S(1)} %copy.112) | copy-start | bytes 393220
  65.1 14.5 %copy-start.19 = (f32[4,4,2048]{2,0,1:T(4,128)}, f32[4,4,2048]{2,0,1:T(4,128)S(1)}, u32[]{:S(2)}) copy-start(f32[4,4,2048]{2,0,1:T(4,128)S(1)} %copy.117) | copy-start | bytes 393220
  65.2 14.4 %copy-start.21 = (f32[4,4,2048]{2,0,1:T(4,128)}, f32[4,4,2048]{2,0,1:T(4,128)S(1)}, u32[]{:S(2)}) copy-start(f32[4,4,2048]{2,0,1:T(4,128)S(1)} %copy.121) | copy-start | bytes 393220
  65.4 14.3 %copy-start.23 = (f32[4,4,2048]{2,0,1:T(4,128)}, f32[4,4,2048]{2,0,1:T(4,128)S(1)}, u32[]{:S(2)}) copy-start(f32[4,4,2048]{2,0,1:T(4,128)S(1)} %copy.123) | copy-start | bytes 393220
  77.3 8.1 %copy-start.42 = (f32[32,5,3,3,3]{0,4,3,2,1:T(4,128)S(1)}, f32[32,5,3,3,3]{0,4,3,2,1:T(4,128)}, u32[]{:S(2)}) copy-start(f32[32,5,3,3,3]{0,4,3,2,1:T(4,128)} %param.16) | copy-start | bytes 51844
  77.3 8.8 %copy-start.43 = (f32[5,32,3,3,3]{1,4,3,2,0:T(4,128)S(1)}, f32[5,32,3,3,3]{1,4,3,2,0:T(4,128)}, u32[]{:S(2)}) copy-start(f32[5,32,3,3,3]{1,4,3,2,0:T(4,128)} %param.20) | copy-start | bytes 51844
  80.0 6.7 collective-permute-start.4
  81.4 6.6 collective-permute-start.5
  89.3 152.2 %collective-permute-start.6 = (f32[5,6,1,2048]{3,1,2,0:T(8,128)}, f32[5,6,1,2048]{3,1,2,0:T(8,128)}, u32[]{:S(2)}, u32[]{:S(2)}) collective-permute-start(f32[5,6,1,2048]{3,1,2,0:T(8,128)} %get-tuple-element.65), channel_id=1, source_target_pairs={{1,0},{2,1},{3,2},{4,3},{5,4},{6,5},{7,6},{8,7},{9,8},{10,9},{11,1... | collective-permute-start | bytes 737288 | tf_op jit(solution)/shard_map/ppermute | solution.py:20
  91.2 150.3 %collective-permute-start.7 = (f32[5,6,1,2048]{3,1,2,0:T(8,128)}, f32[5,6,1,2048]{3,1,2,0:T(8,128)}, u32[]{:S(2)}, u32[]{:S(2)}) collective-permute-start(f32[5,6,1,2048]{3,1,2,0:T(8,128)} %get-tuple-element.64), channel_id=1, source_target_pairs={{0,1},{1,2},{2,3},{3,4},{4,5},{5,6},{6,7},{7,8},{8,9},{9,10},{10,1... | collective-permute-start | bytes 737288 | tf_op jit(solution)/shard_map/ppermute | solution.py:18
  149.5 10.5 %copy-start.45 = (f32[32,32,3,3,3]{1,0,4,3,2:T(8,128)S(1)}, f32[32,32,3,3,3]{1,0,4,3,2:T(8,128)}, u32[]{:S(2)}) copy-start(f32[32,32,3,3,3]{1,0,4,3,2:T(8,128)} %param.18) | copy-start | bytes 331780
  149.5 10.5 %copy-start.48 = (f32[32]{0:T(128)S(1)}, f32[32]{0:T(128)}, u32[]{:S(2)}) copy-start(f32[32]{0:T(128)} %param.19) | copy-start | bytes 388
  159.9 9.9 %copy-start.33 = (bf16[4,8,2,8,1,32]{5,3,2,4,1,0:T(8,128)(2,1)}, bf16[4,8,2,8,1,32]{5,3,2,4,1,0:T(8,128)(2,1)S(1)}, u32[]{:S(2)}) copy-start(bf16[4,8,2,8,1,32]{5,3,2,4,1,0:T(8,128)(2,1)S(1)} %pad.15) | copy-start | bytes 98308
  160.0 9.9 %copy-start.35 = (bf16[4,8,2,8,1,32]{5,3,2,4,1,0:T(8,128)(2,1)}, bf16[4,8,2,8,1,32]{5,3,2,4,1,0:T(8,128)(2,1)S(1)}, u32[]{:S(2)}) copy-start(bf16[4,8,2,8,1,32]{5,3,2,4,1,0:T(8,128)(2,1)S(1)} %pad.16) | copy-start | bytes 98308
  176.4 65.1 %copy-start.7 = (f32[5,1,4,2048]{3,1,2,0:T(1,128)S(1)}, f32[5,1,4,2048]{3,1,2,0:T(1,128)}, u32[]{:S(2)}) copy-start(f32[5,1,4,2048]{3,1,2,0:T(1,128)} %copy-done.6) | copy-start | bytes 491524
  176.4 65.1 %copy-start.9 = (f32[5,1,4,2048]{3,1,2,0:T(1,128)S(1)}, f32[5,1,4,2048]{3,1,2,0:T(1,128)}, u32[]{:S(2)}) copy-start(f32[5,1,4,2048]{3,1,2,0:T(1,128)} %copy-done.8) | copy-start | bytes 491524
  247.8 6.9 collective-permute-start.8
  249.2 8.1 %collective-permute-start.9 = (f32[5,1,4,2048]{3,2,1,0:T(4,128)S(1)}, f32[5,1,4,2048]{3,2,1,0:T(4,128)S(1)}, u32[]{:S(2)}, u32[]{:S(2)}) collective-permute-start(f32[5,1,4,2048]{3,2,1,0:T(4,128)S(1)} %copy.133), channel_id=1, source_target_pairs={{0,16},{16,32},{32,48},{48,64},{64,80},{80,96},{96,112},{1,17},{17... | collective-permute-start | bytes 491528 | tf_op jit(solution)/shard_map/ppermute | solution.py:18
  254.9 12.6 %copy-start.3 = (bf16[4,8,2,8,16,32]{5,3,2,4,1,0:T(8,128)(2,1)S(1)}, bf16[4,8,2,8,16,32]{5,3,2,4,1,0:T(8,128)(2,1)}, u32[]{:S(2)}) copy-start(bf16[4,8,2,8,16,32]{5,3,2,4,1,0:T(8,128)(2,1)} %get-tuple-element.54) | copy-start | bytes 1572868
  254.9 12.6 %copy-start.4 = (bf16[4,8,2,8,16,32]{5,3,2,4,1,0:T(8,128)(2,1)S(1)}, bf16[4,8,2,8,16,32]{5,3,2,4,1,0:T(8,128)(2,1)}, u32[]{:S(2)}) copy-start(bf16[4,8,2,8,16,32]{5,3,2,4,1,0:T(8,128)(2,1)} %get-tuple-element.55) | copy-start | bytes 1572868
  254.9 12.6 %copy-start.37 = (bf16[4,8,2,8,1,32]{5,3,2,4,1,0:T(8,128)(2,1)S(1)}, bf16[4,8,2,8,1,32]{5,3,2,4,1,0:T(8,128)(2,1)}, u32[]{:S(2)}) copy-start(bf16[4,8,2,8,1,32]{5,3,2,4,1,0:T(8,128)(2,1)} %pad.20) | copy-start | bytes 98308
  254.9 12.6 %copy-start.38 = (bf16[4,8,2,8,1,32]{5,3,2,4,1,0:T(8,128)(2,1)S(1)}, bf16[4,8,2,8,1,32]{5,3,2,4,1,0:T(8,128)(2,1)}, u32[]{:S(2)}) copy-start(bf16[4,8,2,8,1,32]{5,3,2,4,1,0:T(8,128)(2,1)} %pad.21) | copy-start | bytes 98308
  257.7 12.8 %collective-permute-start.10 = (f32[5,6,1,2048]{3,1,2,0:T(8,128)S(1)}, f32[5,6,1,2048]{3,1,2,0:T(8,128)S(1)}, u32[]{:S(2)}, u32[]{:S(2)}) collective-permute-start(f32[5,6,1,2048]{3,1,2,0:T(8,128)S(1)} %get-tuple-element.63), channel_id=1, source_target_pairs={{1,0},{2,1},{3,2},{4,3},{5,4},{6,5},{7,6},{8,7},{9,8},{10,9},{11,1... | collective-permute-start | bytes 737288 | tf_op jit(solution)/shard_map/ppermute | solution.py:20
  259.7 13.4 %collective-permute-start.11 = (f32[5,6,1,2048]{3,1,2,0:T(8,128)S(1)}, f32[5,6,1,2048]{3,1,2,0:T(8,128)S(1)}, u32[]{:S(2)}, u32[]{:S(2)}) collective-permute-start(f32[5,6,1,2048]{3,1,2,0:T(8,128)S(1)} %get-tuple-element.62), channel_id=1, source_target_pairs={{0,1},{1,2},{2,3},{3,4},{4,5},{5,6},{6,7},{7,8},{8,9},{9,10},{10,1... | collective-permute-start | bytes 737288 | tf_op jit(solution)/shard_map/ppermute | solution.py:18
  288.9 28.3 %copy-start.10 = (bf16[5,4,8,2,8,16]{5,4,2,3,1,0:T(8,128)(2,1)S(1)}, bf16[5,4,8,2,8,16]{5,4,2,3,1,0:T(8,128)(2,1)}, u32[]{:S(2)}) copy-start(bf16[5,4,8,2,8,16]{5,4,2,3,1,0:T(8,128)(2,1)} %get-tuple-element.68) | copy-start | bytes 245764
  308.7 35.6 %all-to-all-start.1 = ((f32[16,1,10240]{2,1,0:T(1,128)}), f32[16,1,10240]{2,1,0:T(1,128)}, u32[]{:S(2)}, u32[]{:S(2)}) async-start(f32[16,1,10240]{2,1,0:T(1,128)} %reshape.171), calls=%async_computation.1 | async-start | bytes 1310720 | tf_op jit(solution)/shard_map/all_to_all | solution.py:89
  316.9 359.6 %all-reduce.6.cloned.1.call-start = ((), (), s32[]{:S(2)}) async-start(), calls=%async_computation.2 | async-start | bytes 884736 | tf_op jit(solution)/shard_map/psum | solution.py:103
  317.1 3.6 copy-start.12
  376.6 15.3 %copy-start.26 = (f32[2,5,4,8,128]{4,1,2,3,0:T(8,128)S(1)}, f32[2,5,4,8,128]{4,1,2,3,0:T(8,128)}, u32[]{:S(2)}) copy-start(f32[2,5,4,8,128]{4,1,2,3,0:T(8,128)} %copy-done.25) | copy-start | bytes 491524
  395.4 4.1 copy-start.49
  414.4 4.9 copy-start.50
  414.6 4.8 copy-start.46
  419.4 12.7 %copy-start.2 = (bf16[4,8,16,17,32]{4,2,3,1,0:T(8,128)(2,1)S(1)}, bf16[4,8,16,17,32]{4,2,3,1,0:T(8,128)(2,1)}, u32[]{:S(2)}) copy-start(bf16[4,8,16,17,32]{4,2,3,1,0:T(8,128)(2,1)} %copy-done.1) | copy-start | bytes 1671172
  419.4 12.7 %copy-start.13 = (bf16[4,8,16,17,32,1]{4,2,3,1,0,5:T(8,128)(2,1)S(1)}, bf16[4,8,16,17,32,1]{4,2,3,1,0,5:T(8,128)(2,1)}, u32[]{:S(2)}) copy-start(bf16[4,8,16,17,32,1]{4,2,3,1,0,5:T(8,128)(2,1)} %get-tuple-element.88) | copy-start | bytes 1671172
  419.4 12.7 %copy-start.14 = (bf16[4,8,16,17,32,1]{4,2,3,1,0,5:T(8,128)(2,1)S(1)}, bf16[4,8,16,17,32,1]{4,2,3,1,0,5:T(8,128)(2,1)}, u32[]{:S(2)}) copy-start(bf16[4,8,16,17,32,1]{4,2,3,1,0,5:T(8,128)(2,1)} %get-tuple-element.89) | copy-start | bytes 1671172
  419.4 12.7 %copy-start.32 = (bf16[5,4,8,16,17,1]{3,0,5,4,2,1:T(8,128)(2,1)S(1)}, bf16[5,4,8,16,17,1]{3,0,5,4,2,1:T(8,128)(2,1)}, u32[]{:S(2)}) copy-start(bf16[5,4,8,16,17,1]{3,0,5,4,2,1:T(8,128)(2,1)} %copy.165) | copy-start | bytes 261124
  432.1 6.6 copy-start.29
  432.1 6.6 copy-start.30
  432.2 6.6 copy-start.31
  (18 other events, 36.5 us)
Sparse Core Ops, SparseCore 0:
  536.0 140.4 all-reduce.5
where the time goes:
time: 697 us; the launch traced here: 688 us
  local copies, waits for them, and re-layouts  209 us (30%)
  waiting for transfers between devices  152 us (22%)
  matrix products  135 us (19%)
  blocking collectives  69.4 us (10%)
  starting transfers between devices  59.3 us (9%)
  other arithmetic  43.9 us (6%)
  between operations  19.5 us (3%)
    psum x1, waiting for transfers between devices, on_device(): lax.psum((grads[0], grads[1], grads[2], grads[3], grads[4], grads[5], val...  136 us
    conv_general_dilated x8, matrix products, convolve(): lax.conv_general_dilated(inputs, kernel.astype(jnp.bfloat16), (1, 1, 1),...  135 us
    unnamed x116, local copies, waits for them, and re-layouts  118 us
    psum x1, blocking collectives, on_device(): lax.psum((grads[0], grads[1], grads[2], grads[3], grads[4], grads[5], val...  69.4 us
    ppermute x6, starting transfers between devices, padded_2(): lax.ppermute(tail, axis, [(i, (i + 1) % count) for i in range(ends)])  32.2 us
    convert_element_type x13, local copies, waits for them, and re-layouts, on_device(): first_patches.astype(jnp.bfloat16)  17.5 us
    all_to_all x2, local copies, waits for them, and re-layouts, on_device(): lax.all_to_all(initial_fields, 'gy', split_axis=3, concat_axis=2, tiled=T...  14.5 us
    all_to_all x1, local copies, waits for them, and re-layouts, on_device(): lax.all_to_all(fields, 'gy', split_axis=3, concat_axis=2, tiled=True)  14 us
  transfers between devices with their start and end apart: 15, of which 6 were waited for; matrix products, arithmetic and copies ran while one was open for 32% of the time, Pallas kernels for 0%

commit v1 on v0

v1 whole, which is shorter than its diff:
```python
import jax
import jax.numpy as jnp
from jax import lax
from jax.experimental import pallas as pl
from jax.experimental.pallas import tpu as pltpu
from jax.sharding import PartitionSpec as P

STEPS = 3
F = 5
C = 32
X = 4
PY = 8
Z = 128
ROWS = 24
TAPS = 9
CELLS = 20480.0
BF = jnp.bfloat16
F32 = jnp.float32
VMEM = pl.BlockSpec(memory_space=pltpu.VMEM)
SMEM = pl.BlockSpec(memory_space=pltpu.SMEM)
LIMIT = 48 * 1024 * 1024


def call(kernel, outs, scratch=(), flops=0, nbytes=0, ins=()):
    return pl.pallas_call(
        kernel,
        out_shape=[jax.ShapeDtypeStruct(s, d) for s, d in outs],
        in_specs=list(ins),
        out_specs=[VMEM] * len(outs),
        scratch_shapes=list(scratch),
        compiler_params=pltpu.CompilerParams(vmem_limit_bytes=LIMIT),
        cost_estimate=pl.CostEstimate(flops=flops, bytes_accessed=nbytes, transcendentals=0),
    )


def pack_slabs(get, out_ref):
    for row in range(F * X):
        cells = get(row)
        for y in range(4):
            for j in range(16):
                out_ref[j, y // 2, pl.ds((y % 2) * F * X + row, 1), :] = cells[y : y + 1, j * Z : (j + 1) * Z]


def write_edges(get, odd_x, odd_y, xa_ref, xb_ref, ya_ref, yb_ref):
    for f in range(F):
        head, tail = get(f * X), get(f * X + X - 1)
        xa_ref[f] = jnp.where(odd_x, head, tail)
        xb_ref[f] = jnp.where(odd_x, tail, head)
    for row in range(F * X):
        cells = get(row)
        head, tail = cells[0:1], cells[3:4]
        ya_ref[pl.ds(row, 1), :] = jnp.where(odd_y, head, tail)
        yb_ref[pl.ds(row, 1), :] = jnp.where(odd_y, tail, head)


def start_kernel(place, u_ref, slabs_ref, xa_ref, xb_ref, ya_ref, yb_ref):
    get = lambda row: u_ref[row]
    write_edges(get, place[0] % 2 == 1, place[1] % 2 == 1, xa_ref, xb_ref, ya_ref, yb_ref)
    pack_slabs(get, slabs_ref)


def step_kernel(last, place, u_ref, rxa, rxb, rya, ryb, vel_ref, dif_ref, new_ref, *outs):
    gx, gy = place[0], place[1]
    odd_x, odd_y = gx % 2 == 1, gy % 2 == 1
    lane = lax.broadcasted_iota(jnp.int32, (4, 2048), 1)
    not_first, not_last = lane > 0, lane < 2047
    for x in range(X):
        v0, v1, v2, dif = vel_ref[x], vel_ref[X + x], vel_ref[2 * X + x], dif_ref[x]
        for f in range(F):
            row = f * X + x
            middle = u_ref[row]
            if x < X - 1:
                x_plus = u_ref[row + 1]
            else:
                x_plus = jnp.where(odd_x, rxb[f], rxa[f])
                x_plus = jnp.where(gx == 7, 0.0, x_plus)
            if x > 0:
                x_minus = u_ref[row - 1]
            else:
                x_minus = jnp.where(odd_x, rxa[f], rxb[f])
                x_minus = jnp.where(gx == 0, 0.0, x_minus)
            a, b = rya[pl.ds(row, 1), :], ryb[pl.ds(row, 1), :]
            above = jnp.where(gy == 15, 0.0, jnp.where(odd_y, b, a))
            below = jnp.where(gy == 0, 0.0, jnp.where(odd_y, a, b))
            y_plus = jnp.concatenate([middle[1:4], above], axis=0)
            y_minus = jnp.concatenate([below, middle[0:3]], axis=0)
            z_plus = jnp.where(not_last, pltpu.roll(middle, 2047, 1), 0.0)
            z_minus = jnp.where(not_first, pltpu.roll(middle, 1, 1), 0.0)
            carried = v0 * (x_plus - x_minus) + v1 * (y_plus - y_minus) + v2 * (z_plus - z_minus)
            spread = x_plus + x_minus + y_plus + y_minus + z_plus + z_minus - 6.0 * middle
            new_ref[row] = middle - 0.5 * carried + dif * spread
    get = lambda row: new_ref[row]
    if last:
        pack_slabs(get, outs[0])
    else:
        write_edges(get, odd_x, odd_y, *outs)


EDGES = [((F, X, 2048), F32)] * 2 + [((F * X, 2048), F32)] * 2
SLABS = ((16, 2, 2 * F * X, Z), F32)


def exchange(edges):
    def pairs(n, second):
        partner = lambda i: (i ^ 1) if not second else ((i + 1) if i % 2 else (i - 1)) % n
        return [(i, partner(i)) for i in range(n)]

    xa, xb, ya, yb = edges
    return (
        lax.ppermute(xa, "gx", pairs(8, False)),
        lax.ppermute(xb, "gx", pairs(8, True)),
        lax.ppermute(ya, "gy", pairs(16, False)),
        lax.ppermute(yb, "gy", pairs(16, True)),
    )


def patch_rows(slabs_ref, anchor, out_ref):
    out_ref[...] = jnp.zeros_like(out_ref)
    for k in range(PY):
        y = anchor + k
        both = slabs_ref[y // 2]
        rows = jnp.where(y % 2 == 1, both[F * X :], both[: F * X])
        out_ref[0 : F * X, k * Z : (k + 1) * Z] = rows


def z_shifted(cells, dz, lane):
    if dz == 0:
        return cells
    moved = pltpu.roll(cells, (-dz) % Z, 1)
    return jnp.where(lane == (Z - 1 if dz > 0 else 0), 0.0, moved)


def fill_taps(cells_ref, out_ref, sign):
    rows = cells_ref.shape[0]
    lane = lax.broadcasted_iota(jnp.int32, (rows, Z), 1)
    zero = jnp.zeros((rows, Z), F32)
    shifted = [[z_shifted(cells_ref[:, k * Z : (k + 1) * Z], sign * (dz - 1), lane) for dz in range(3)] for k in range(PY)]
    for k in range(PY):
        parts = []
        for dy in range(3):
            at = k + sign * (dy - 1)
            for dz in range(3):
                parts.append(shifted[at][dz] if 0 <= at < PY else zero)
        out_ref[:, k * Z : (k + 1) * Z] = jnp.concatenate(parts, axis=0).astype(BF)


def fill_z(cells, k, out_ref, sign):
    lane = lax.broadcasted_iota(jnp.int32, cells.shape, 1)
    for dz in range(3):
        moved = z_shifted(cells, sign * (dz - 1), lane)
        out_ref[dz * 128 : (dz + 1) * 128, (k + 1) * Z : (k + 2) * Z] = moved.astype(BF)


def clear_ends(ref):
    ref[:, 0:Z] = jnp.zeros((ref.shape[0], Z), ref.dtype)
    ref[:, (PY + 1) * Z :] = jnp.zeros((ref.shape[0], Z), ref.dtype)


def dot(a, b):
    return jnp.dot(a, b, preferred_element_type=F32)


def dot_t(a, b):
    return lax.dot_general(a, b, (((1,), (1,)), ((), ())), preferred_element_type=F32)


def activate(y):
    sig = 1.0 / (1.0 + jnp.exp(-y))
    return y * sig, sig * (1.0 + y * (1.0 - sig))


def bands_kernel(w2_ref, fwd_ref, bwd_ref):
    zero = jnp.zeros((C, C), F32)
    for dy in range(3):
        for dz in range(3):
            rows = []
            for xo in range(X):
                parts = []
                for xi in range(X):
                    dx = xi - xo + 1
                    parts.append(w2_ref[dx * 9 + dy * 3 + dz] if 0 <= dx < 3 else zero)
                rows.append(jnp.concatenate(parts, axis=1))
            block = jnp.concatenate(rows, axis=0)
            fwd_ref[dy, :, dz * 128 : (dz + 1) * 128] = block.astype(BF)
            bwd_ref[dy, :, dz * 128 : (dz + 1) * 128] = block.T.astype(BF)


def forward_kernel(
    anchors, slabs_ref, w1_ref, w2_ref, w3_ref, b1_ref, b2_ref, b3_ref,
    first_ref, taps_ref, a1_ref, d1_ref, a2_ref, d2_ref, pred_ref,
):
    for p in range(2):
        patch_rows(slabs_ref, anchors[p], first_ref.at[p])
        fill_taps(first_ref.at[p], taps_ref.at[p], 1)
        y1 = dot(w1_ref[...], taps_ref[p])
        act, slope = activate(y1 + b1_ref[...])
        d1_ref[p] = slope
        clear_ends(a1_ref.at[p])
        for k in range(PY):
            fill_z(act[:, k * Z : (k + 1) * Z], k, a1_ref.at[p], 1)
        y2 = b2_ref[...] + dot(w2_ref[0], a1_ref[p, :, 0 : PY * Z])
        for dy in range(1, 3):
            y2 = y2 + dot(w2_ref[dy], a1_ref[p, :, dy * Z : (dy + PY) * Z])
        act, slope = activate(y2)
        d2_ref[p] = slope
        a2_ref[p] = act.astype(BF)
        terms = dot(w3_ref[...], a2_ref[p])
        lane = lax.broadcasted_iota(jnp.int32, (ROWS, Z), 1)
        for k in range(PY):
            out = b3_ref[...] + jnp.zeros((ROWS, Z), F32)
            for dz in range(3):
                part = None
                for dy in range(3):
                    at = k + dy - 1
                    if 0 <= at < PY:
                        t = (dy * 3 + dz) * ROWS
                        term = terms[t : t + ROWS, at * Z : (at + 1) * Z]
                        part = term if part is None else part + term
                out = out + z_shifted(part, dz - 1, lane)
            pred_ref[p, :, k * Z : (k + 1) * Z] = out


def band_sum(full):
    lane = lax.broadcasted_iota(jnp.int32, (C, 256), 1)
    total = None
    for x in range(X):
        block = full[x * C : (x + 1) * C]
        block = jnp.concatenate([block, jnp.zeros((C, 256 - TAPS * ROWS), F32)], axis=1)
        moved = pltpu.roll(block, (1 - x) % 256, 1)
        e = lane % 4
        ok = (e < 3) & (x + e - 1 >= 0) & (x + e - 1 < X) & (lane < TAPS * ROWS)
        moved = jnp.where(ok, moved, 0.0)
        total = moved if total is None else total + moved
    out = None
    for f in range(F):
        part = jnp.where((lane % ROWS) // 4 == f, total, 0.0)
        part = pltpu.roll(part, (256 - f) % 256, 1)
        out = part if out is None else out + part
    return out


def backward_kernel(
    place, anchors, count, slabs_ref, first_ref, taps_ref, a1_ref, d1_ref, a2_ref, d2_ref, pred_ref, w2_ref, w3_ref,
    keep_ref, send_ref,
    last_ref, err_ref, g_ref, b_ref, grads_ref,
):
    db1 = jnp.zeros((128, 1), F32)
    db2 = jnp.zeros((128, 1), F32)
    db3 = jnp.zeros((ROWS, 1), F32)
    loss = jnp.zeros((ROWS, 1), F32)
    dw1 = jnp.zeros((128, TAPS * ROWS), F32)
    dw3 = jnp.zeros((128, TAPS * ROWS), F32)
    dw2 = [jnp.zeros((128, 384), F32) for _ in range(3)]
    clear_ends(b_ref)
    for p in range(2):
        live = jnp.where(p < count[0], 1.0, 0.0).astype(F32)
        patch_rows(slabs_ref, anchors[p], last_ref)
        err = pred_ref[p] - (last_ref[...] - first_ref[p])
        loss = loss + live * jnp.sum(err * err, axis=1, keepdims=True)
        err = err * (live * (2.0 / CELLS))
        err_ref[...] = err
        db3 = db3 + jnp.sum(err, axis=1, keepdims=True)
        fill_taps(err_ref, g_ref, -1)
        da2 = dot(w3_ref[...], g_ref[...])
        dw3 = dw3 + dot_t(a2_ref[p], g_ref[...])
        dy2 = da2 * d2_ref[p]
        db2 = db2 + jnp.sum(dy2, axis=1, keepdims=True)
        for k in range(PY):
            fill_z(dy2[:, k * Z : (k + 1) * Z], k, b_ref, -1)
        middle = b_ref[128:256, Z : (PY + 1) * Z]
        da1 = None
        for dy in range(3):
            dw2[dy] = dw2[dy] + dot_t(middle, a1_ref[p, :, dy * Z : (dy + PY) * Z])
            term = dot(w2_ref[dy], b_ref[:, (2 - dy) * Z : (2 - dy + PY) * Z])
            da1 = term if da1 is None else da1 + term
        dy1 = da1 * d1_ref[p]
        db1 = db1 + jnp.sum(dy1, axis=1, keepdims=True)
        dw1 = dw1 + dot_t(dy1.astype(BF), taps_ref[p])

    lane = lax.broadcasted_iota(jnp.int32, (C, 128), 1)
    small1, small3 = band_sum(dw1), band_sum(dw3)
    fold = lambda v: v[0:C] + v[C : 2 * C] + v[2 * C : 3 * C] + v[3 * C : 4 * C]
    grow = lambda v: jnp.concatenate([v, jnp.zeros((C - ROWS, 1), F32)], axis=0)
    extras = {0: (fold(db1), fold(db2)), 1: (grow(db3), grow(loss)), 2: (jnp.full((C, 1), 1.0, F32) * count[0].astype(F32), None)}
    for t in range(TAPS):
        dy, dz = t // 3, t % 3
        total = jnp.zeros((C, 128), F32)
        for xo in range(X):
            block = dw2[dy][xo * C : (xo + 1) * C, dz * 128 : (dz + 1) * 128]
            moved = pltpu.roll(block, ((1 - xo) * C) % 128, 1)
            dx = lane // C
            ok = (dx < 3) & (xo + dx - 1 >= 0) & (xo + dx - 1 < X)
            total = total + jnp.where(ok, moved, 0.0)
        one = pltpu.roll(small1, (96 - ROWS * t) % 256, 1)[:, 0:128]
        three = pltpu.roll(small3, (111 - ROWS * t) % 256, 1)[:, 0:128]
        total = jnp.where((lane >= 96) & (lane < 111), one, total)
        total = jnp.where((lane >= 111) & (lane < 126), three, total)
        if t in extras:
            a, b = extras[t]
            total = jnp.where(lane == 126, a, total)
            if b is not None:
                total = jnp.where(lane == 127, b, total)
        grads_ref[t * C : (t + 1) * C] = total
    core = place[1] % 2
    low, high = grads_ref[0:144], grads_ref[144:288]
    keep_ref[...] = jnp.where(core == 0, low, high)
    send_ref[...] = jnp.where(core == 0, high, low)


def reduce_steps():
    def near(c):
        return c ^ 1

    def far(c):
        return 3 - c

    orders = (("x", "y", "z"), ("y", "z", "x"))
    steps = []
    for n in range(6):
        pairs = []
        for gx in range(8):
            for gy in range(16):
                at = {"x": gx // 2, "y": gy // 4, "z": (gy // 2 % 2) * 2 + gx % 2}
                core = gy % 2
                axis = orders[core][n // 2]
                at[axis] = (near, far)[n % 2](at[axis])
                to = (at["x"] * 2 + at["z"] % 2) * 16 + at["y"] * 4 + (at["z"] // 2) * 2 + core
                pairs.append((gx * 16 + gy, to))
        steps.append(pairs)
    return steps


def sum_all(keep, send):
    both = ("gx", "gy")
    cores = [(i, i ^ 1) for i in range(16)]
    mine = keep + lax.ppermute(send, "gy", cores)
    for pairs in reduce_steps():
        mine = mine + lax.ppermute(mine, both, pairs)
    return mine, lax.ppermute(mine, "gy", cores)


def banded(w, flip):
    bands = []
    for x in range(X):
        if flip:
            w_ = w[:, ::-1]
        else:
            w_ = w
        padded = jnp.pad(w_, ((0, 0), (x, X - 1 - x), (0, 0), (0, 0), (0, 0)))
        bands.append(padded[:, 1 : X + 1])
    all_x = jnp.stack(bands, axis=4)
    rows = jnp.transpose(all_x, (2, 3, 0, 1, 4, 5)).reshape(TAPS, F * X, X * C)
    return jnp.pad(rows, ((0, 0), (0, ROWS - F * X), (0, 0))).reshape(TAPS * ROWS, X * C).astype(BF)


def on_device(
    initial_fields, velocity, diffusivity, patch_anchor, patch_count,
    weight_one, bias_one, weight_two, bias_two, weight_three, bias_three,
):
    place = jnp.stack([lax.axis_index("gx"), lax.axis_index("gy")]).astype(jnp.int32)
    u = initial_fields.reshape(F * X, 4, 2048)
    vel = velocity.reshape(3 * X, 4, 2048)
    anchors = patch_anchor.reshape(2)
    count = patch_count.reshape(1)

    slabs, *edges = call(start_kernel, [SLABS] + EDGES, ins=[SMEM, VMEM], nbytes=1_500_000)(place, u)
    first_slabs = lax.all_to_all(slabs, "gy", 0, 0, tiled=True).reshape(32, 2 * F * X, Z)

    w2 = jnp.transpose(weight_two, (2, 3, 4, 0, 1)).reshape(27, C, C)
    w2_fwd, w2_bwd = call(bands_kernel, [((3, 128, 384), BF)] * 2, ins=[VMEM], nbytes=1_000_000)(w2)
    w1_band = banded(jnp.transpose(weight_one, (1, 2, 3, 4, 0)), False)
    w3_band = banded(jnp.transpose(weight_three, (0, 2, 3, 4, 1)), True)
    b1 = jnp.tile(bias_one, X).reshape(128, 1)
    b2 = jnp.tile(bias_two, X).reshape(128, 1)
    b3 = jnp.pad(jnp.repeat(bias_three, X), (0, ROWS - F * X)).reshape(ROWS, 1)

    for step in range(STEPS):
        last = step == STEPS - 1
        outs = [((F * X, 4, 2048), F32)] + ([SLABS] if last else EDGES)
        received = exchange(edges)
        kernel = lambda *refs, last=last: step_kernel(last, *refs)
        u, *edges = call(kernel, outs, ins=[SMEM] + [VMEM] * 7, nbytes=4_000_000)(
            place, u, *received, vel, diffusivity
        )

    learned = call(
        forward_kernel,
        [
            ((2, ROWS, PY * Z), F32),
            ((2, TAPS * ROWS, PY * Z), BF),
            ((2, 384, (PY + 2) * Z), BF),
            ((2, 128, PY * Z), F32),
            ((2, 128, PY * Z), BF),
            ((2, 128, PY * Z), F32),
            ((2, ROWS, PY * Z), F32),
        ],
        ins=[SMEM] + [VMEM] * 7,
        flops=2_000_000_000,
        nbytes=8_000_000,
    )(anchors, first_slabs, w1_band.T, w2_fwd, w3_band, b1, b2, b3)

    last_slabs = lax.all_to_all(edges[0], "gy", 0, 0, tiled=True).reshape(32, 2 * F * X, Z)
    keep, send = call(
        backward_kernel,
        [((144, 128), F32)] * 2,
        scratch=[
            pltpu.VMEM((ROWS, PY * Z), F32),
            pltpu.VMEM((ROWS, PY * Z), F32),
            pltpu.VMEM((TAPS * ROWS, PY * Z), BF),
            pltpu.VMEM((384, (PY + 2) * Z), BF),
            pltpu.VMEM((288, 128), F32),
        ],
        ins=[SMEM] * 3 + [VMEM] * 10,
        flops=4_000_000_000,
        nbytes=10_000_000,
    )(place, anchors, count, last_slabs, *learned, w2_bwd, w3_band.T)

    mine, other = sum_all(keep, send)
    core = place[1] % 2
    grads = jnp.where(core == 0, jnp.concatenate([mine, other]), jnp.concatenate([other, mine]))
    grads = grads.reshape(TAPS, C, 128)
    total = grads[2, 0, 126]
    grads = grads / total
    g2 = jnp.transpose(grads[:, :, 0:96].reshape(3, 3, C, 3, C), (2, 4, 3, 0, 1))
    g1 = jnp.transpose(grads[:, :, 96:111].reshape(3, 3, C, F, 3), (2, 3, 4, 0, 1))
    g3 = jnp.transpose(grads[:, :, 111:126].reshape(3, 3, C, F, 3), (3, 2, 4, 0, 1))[:, :, ::-1]
    gb1, gb2 = grads[0, :, 126], grads[0, :, 127]
    gb3 = grads[1, 0 : F * X, 126].reshape(F, X).sum(1)
    loss = grads[1, 0 : F * X, 127].sum() / CELLS
    return u.reshape(F, X, 4, 2048), g1, gb1, g2, gb2, g3, gb3, loss


def solution(mesh):
    return jax.shard_map(
        on_device,
        mesh=mesh,
        in_specs=(
            P(None, "gx", "gy", None),
            P(None, "gx", "gy", None),
            P("gx", "gy", None),
            P("gx", "gy", None),
            P("gx", "gy"),
            P(),
            P(),
            P(),
            P(),
            P(),
            P(),
        ),
        out_specs=(P(None, "gx", "gy", None), P(), P(), P(), P(), P(), P(), P()),
        check_vma=False,
    )
```

time: 697 us -> 135 us (0.19); the launches traced: 688 us -> 134 us
  local copies, waits for them, and re-layouts: 209 us -> 16 us
  matrix products: 135 us -> 0 us
  waiting for transfers between devices: 152 us -> 42.6 us
  blocking collectives: 69.4 us -> 0 us
  other arithmetic: 43.9 us -> 3.22 us
  Pallas kernels: 0 us -> 18.8 us
  between operations: 19.5 us -> 3.48 us
  starting transfers between devices: 59.3 us -> 50.2 us
    psum x1 -> x0, waiting for transfers between devices: 136 us -> none  [on_device(): lax.psum((grads[0], grads[1], grads[2], grads[3], grads[4], grads[5], val...]
    conv_general_dilated x8 -> x0, matrix products: 135 us -> none  [convolve(): lax.conv_general_dilated(inputs, kernel.astype(jnp.bfloat16), (1, 1, 1),...]
    unnamed x116 -> x43, local copies, waits for them, and re-layouts: 118 us -> 11.2 us
    psum x1 -> x0, blocking collectives: 69.4 us -> none  [on_device(): lax.psum((grads[0], grads[1], grads[2], grads[3], grads[4], grads[5], val...]
    all_to_all x3 -> x0, local copies, waits for them, and re-layouts: 28.5 us -> none  [the longest x2 14.5 us: on_device(): lax.all_to_all(initial_fields, 'gy', split_axis=3, concat_axis=2, tiled=T...]
    ppermute x12 -> x20, waiting for transfers between devices: 15.9 us -> 41.3 us  [the longest x6 18.6 us: sum_all(): mine = mine + lax.ppermute(mine, both, pairs)]
    convert_element_type x21 -> x2, local copies, waits for them, and re-layouts: 22.6 us -> 0.21 us  [banded(): jnp.pad(rows, ((0, 0), (0, ROWS - F * X), (0, 0)))]
    pallas_call x0 -> x7, Pallas kernels: none -> 18.8 us  [the longest x3 6.33 us: on_device(): call(kernel, outs, ins=[SMEM] + [VMEM] * 7, nbytes=4000000)]
  transfers between devices with their start and end apart: 15 -> 22, of which waited for: 6 -> 13; matrix products, arithmetic and copies ran while one was open for 32% -> 3% of each run, Pallas kernels for 0% -> 8%
where the time goes in v1:
time: 135 us; the launch traced here: 134 us
  starting transfers between devices  50.2 us (37%)
  waiting for transfers between devices  42.6 us (32%)
  Pallas kernels  18.8 us (14%)
  local copies, waits for them, and re-layouts  16 us (12%)
  between operations  3.48 us (3%)
  other arithmetic  3.22 us (2%)
    ppermute x6, waiting for transfers between devices, sum_all(): mine = mine + lax.ppermute(mine, both, pairs)  18.6 us
    ppermute x3, waiting for transfers between devices, exchange(): lax.ppermute(yb, 'gy', pairs(16, True))  15.2 us
    unnamed x43, local copies, waits for them, and re-layouts  11.2 us
    ppermute x3, starting transfers between devices, exchange(): lax.ppermute(xb, 'gx', pairs(8, True))  9.6 us
    ppermute x3, starting transfers between devices, exchange(): lax.ppermute(yb, 'gy', pairs(16, True))  8.55 us
    ppermute x6, starting transfers between devices, sum_all(): mine = mine + lax.ppermute(mine, both, pairs)  7.33 us
    all_to_all x1, starting transfers between devices, on_device(): lax.all_to_all(slabs, 'gy', 0, 0, tiled=True).reshape(32, 2 * F * X, Z)  6.9 us
    ppermute x1, starting transfers between devices, sum_all(): return (mine, lax.ppermute(mine, 'gy', cores))  6.81 us
  transfers between devices with their start and end apart: 22, of which 13 were waited for; matrix products, arithmetic and copies ran while one was open for 3% of the time, Pallas kernels for 8%

profile of v1, /device:TPU:1, one launch (start us, length us, event | category | flops | bytes accessed | tf_op | source)
XLA Modules:
  0.0 134.3 jit_solution(12719537799060901783)
XLA Ops:
  0.7 1.1 copy-done.1
  1.9 1.7 %shard_map.170 = (f32[16,2,40,128]{3,2,1,0:T(8,128)}, f32[5,4,2048]{2,1,0:T(4,128)S(1)}, f32[5,4,2048]{2,1,0:T(4,128)S(1)}, f32[20,2048]{1,0:T(8,128)S(1)}, f32[20,2048]{1,0:T(8,128)S(1)}) custom-call(s32[2]{0:T(128)S(1)} %pad_add_fusion.place.refs_0_, f32[20,4,2048]{2,1,0:T(4,128)S(1)} %bitcast.59), custom_call_target="tpu_custom_call" | custom-call | bytes 1500000 | tf_op jit(solution)/shard_map/pallas_call | solution.py:366
  3.6 1.4 %collective-permute-start.2 = (f32[20,2048]{1,0:T(8,128)S(1)}, f32[20,2048]{1,0:T(8,128)S(1)}, u32[]{:S(2)}, u32[]{:S(2)}) collective-permute-start(f32[20,2048]{1,0:T(8,128)S(1)} %get-tuple-element.38), channel_id=1, source_target_pairs={{0,1},{1,0},{2,3},{3,2},{4,5},{5,4},{6,7},{7,6},{8,9},{9,8},{10,11... | collective-permute-start | bytes 491528 | tf_op jit(solution)/shard_map/ppermute | solution.py:112
  5.0 3.6 %collective-permute-start.3 = (f32[20,2048]{1,0:T(8,128)S(1)}, f32[20,2048]{1,0:T(8,128)S(1)}, u32[]{:S(2)}, u32[]{:S(2)}) collective-permute-start(f32[20,2048]{1,0:T(8,128)S(1)} %get-tuple-element.39), channel_id=1, source_target_pairs={{0,15},{1,2},{2,1},{3,4},{4,3},{5,6},{6,5},{7,8},{8,7},{9,10},{10,... | collective-permute-start | bytes 491528 | tf_op jit(solution)/shard_map/ppermute | solution.py:113
  8.6 0.7 collective-permute-start
  9.3 2.9 %collective-permute-start.1 = (f32[5,4,2048]{2,1,0:T(4,128)S(1)}, f32[5,4,2048]{2,1,0:T(4,128)S(1)}, u32[]{:S(2)}, u32[]{:S(2)}) collective-permute-start(f32[5,4,2048]{2,1,0:T(4,128)S(1)} %get-tuple-element.37), channel_id=1, source_target_pairs={{0,112},{16,32},{32,16},{48,64},{64,48},{80,96},{96,80},{112,0},{1... | collective-permute-start | bytes 491528 | tf_op jit(solution)/shard_map/ppermute | solution.py:111
  12.2 6.9 %all-to-all-start.1 = ((f32[16,2,40,128]{3,2,1,0:T(8,128)}), f32[16,2,40,128]{3,2,1,0:T(8,128)S(1)}, u32[]{:S(2)}, u32[]{:S(2)}) async-start(f32[16,2,40,128]{3,2,1,0:T(8,128)} %get-tuple-element.52), calls=%async_computation.1 | async-start | bytes 1310720 | tf_op jit(solution)/shard_map/all_to_all | solution.py:367
  19.2 2.7 %collective-permute-done.refs_2_ = f32[5,4,2048]{2,1,0:T(4,128)S(1)} collective-permute-done((f32[5,4,2048]{2,1,0:T(4,128)S(1)}, f32[5,4,2048]{2,1,0:T(4,128)S(1)}, u32[]{:S(2)}, u32[]{:S(2)}) %collective-permute-start) | collective-permute-done | bytes 163872 | tf_op jit(solution)/shard_map/ppermute | solution.py:110
  21.9 1.8 %shard_map.171 = (f32[20,4,2048]{2,1,0:T(4,128)S(1)}, f32[5,4,2048]{2,1,0:T(4,128)S(1)}, f32[5,4,2048]{2,1,0:T(4,128)S(1)}, f32[20,2048]{1,0:T(8,128)S(1)}, f32[20,2048]{1,0:T(8,128)S(1)}) custom-call(s32[2]{0:T(128)S(1)} %pad_add_fusion.place.refs_0_, f32[20,4,2048]{2,1,0:T(4,128)S(1)} %bitcast.60, f32[5,4,2048]{2,1,0:T(4,128)S(1)} %collective-permute-done.refs_2_, ...), custom_call_target="tpu_custom_call" | custom-call | bytes 4000000 | tf_op jit(solution)/shard_map/pallas_call | solution.py:382
  23.8 1.9 %collective-permute-start.7 = (f32[20,2048]{1,0:T(8,128)S(1)}, f32[20,2048]{1,0:T(8,128)S(1)}, u32[]{:S(2)}, u32[]{:S(2)}) collective-permute-start(f32[20,2048]{1,0:T(8,128)S(1)} %get-tuple-element.44), channel_id=1, source_target_pairs={{0,15},{1,2},{2,1},{3,4},{4,3},{5,6},{6,5},{7,8},{8,7},{9,10},{10,... | collective-permute-start | bytes 491528 | tf_op jit(solution)/shard_map/ppermute | solution.py:113
  25.6 4.4 %collective-permute-start.5 = (f32[5,4,2048]{2,1,0:T(4,128)S(1)}, f32[5,4,2048]{2,1,0:T(4,128)S(1)}, u32[]{:S(2)}, u32[]{:S(2)}) collective-permute-start(f32[5,4,2048]{2,1,0:T(4,128)S(1)} %get-tuple-element.42), channel_id=1, source_target_pairs={{0,112},{16,32},{32,16},{48,64},{64,48},{80,96},{96,80},{112,0},{1... | collective-permute-start | bytes 491528 | tf_op jit(solution)/shard_map/ppermute | solution.py:111
  30.0 10.6 %collective-permute-done.7.refs_5_ = f32[20,2048]{1,0:T(8,128)S(1)} collective-permute-done((f32[20,2048]{1,0:T(8,128)S(1)}, f32[20,2048]{1,0:T(8,128)S(1)}, u32[]{:S(2)}, u32[]{:S(2)}) %collective-permute-start.7) | collective-permute-done | bytes 163872 | tf_op jit(solution)/shard_map/ppermute | solution.py:113
  40.6 1.8 %shard_map.172 = (f32[20,4,2048]{2,1,0:T(4,128)S(1)}, f32[5,4,2048]{2,1,0:T(4,128)S(1)}, f32[5,4,2048]{2,1,0:T(4,128)S(1)}, f32[20,2048]{1,0:T(8,128)S(1)}, f32[20,2048]{1,0:T(8,128)S(1)}) custom-call(s32[2]{0:T(128)S(1)} %pad_add_fusion.place.refs_0_, f32[20,4,2048]{2,1,0:T(4,128)S(1)} %get-tuple-element.40.refs_1_, ...), custom_call_target="tpu_custom_call" | custom-call | bytes 4000000 | tf_op jit(solution)/shard_map/pallas_call | solution.py:382
  42.5 3.1 %collective-permute-start.11 = (f32[20,2048]{1,0:T(8,128)S(1)}, f32[20,2048]{1,0:T(8,128)S(1)}, u32[]{:S(2)}, u32[]{:S(2)}) collective-permute-start(f32[20,2048]{1,0:T(8,128)S(1)} %get-tuple-element.49), channel_id=1, source_target_pairs={{0,15},{1,2},{2,1},{3,4},{4,3},{5,6},{6,5},{7,8},{8,7},{9,10},{10,... | collective-permute-start | bytes 491528 | tf_op jit(solution)/shard_map/ppermute | solution.py:113
  46.0 2.3 %collective-permute-start.9 = (f32[5,4,2048]{2,1,0:T(4,128)S(1)}, f32[5,4,2048]{2,1,0:T(4,128)S(1)}, u32[]{:S(2)}, u32[]{:S(2)}) collective-permute-start(f32[5,4,2048]{2,1,0:T(4,128)S(1)} %get-tuple-element.47), channel_id=1, source_target_pairs={{0,112},{16,32},{32,16},{48,64},{64,48},{80,96},{96,80},{112,0},{1... | collective-permute-start | bytes 491528 | tf_op jit(solution)/shard_map/ppermute | solution.py:111
  49.6 1.0 fusion.4
  50.6 4.6 %collective-permute-done.11.refs_5_ = f32[20,2048]{1,0:T(8,128)S(1)} collective-permute-done((f32[20,2048]{1,0:T(8,128)S(1)}, f32[20,2048]{1,0:T(8,128)S(1)}, u32[]{:S(2)}, u32[]{:S(2)}) %collective-permute-start.11) | collective-permute-done | bytes 163872 | tf_op jit(solution)/shard_map/ppermute | solution.py:113
  55.2 3.0 %collective-permute-done.8.refs_2_ = f32[5,4,2048]{2,1,0:T(4,128)S(1)} collective-permute-done((f32[5,4,2048]{2,1,0:T(4,128)S(1)}, f32[5,4,2048]{2,1,0:T(4,128)S(1)}, u32[]{:S(2)}, u32[]{:S(2)}) %collective-permute-start.8) | collective-permute-done | bytes 163872 | tf_op jit(solution)/shard_map/ppermute | solution.py:110
  58.2 2.8 %shard_map.173 = (f32[20,4,2048]{2,1,0:T(4,128)}, f32[16,2,40,128]{3,2,1,0:T(8,128)}) custom-call(s32[2]{0:T(128)S(1)} %pad_add_fusion.place.refs_0_, f32[20,4,2048]{2,1,0:T(4,128)S(1)} %get-tuple-element.45.refs_1_, f32[5,4,2048]{2,1,0:T(4,128)S(1)} %collective-permute-done.8.refs_2_, f32[5,4,2048]{2,1,0:T(4,128)S(1)} %collective-permute-done.9.refs_3_, ...), custom_call_target="tpu_custom_call" | custom-call | bytes 4000000 | tf_op jit(solution)/shard_map/pallas_call | solution.py:382
  61.0 6.7 %all-to-all-start = ((f32[16,2,40,128]{3,2,1,0:T(8,128)}), f32[16,2,40,128]{3,2,1,0:T(8,128)S(1)}, u32[]{:S(2)}, u32[]{:S(2)}) async-start(f32[16,2,40,128]{3,2,1,0:T(8,128)} %get-tuple-element.51), calls=%async_computation | async-start | bytes 1310720 | tf_op jit(solution)/shard_map/all_to_all | solution.py:402
  70.7 4.5 %shard_map.175 = (f32[2,24,1024]{2,1,0:T(8,128)S(1)}, bf16[2,216,1024]{2,1,0:T(8,128)(2,1)S(1)}, bf16[2,384,1280]{2,1,0:T(8,128)(2,1)}, f32[2,128,1024]{2,1,0:T(...) custom-call(s32[2]{0:T(128)S(1)} %bitcast.68, ...), custom_call_target="tpu_custom_call" | custom-call | flops 2000000000 | bytes 8000000 | tf_op jit(solution)/shard_map/pallas_call | solution.py:386
  75.3 1.0 copy-done.6
  76.3 1.0 copy-done.8
  77.2 0.8 copy-done.10
  78.1 0.7 copy-done.12
  78.8 1.3 all-to-all-done
  80.0 1.2 copy-done.7
  81.2 1.2 copy-done.9
  82.5 1.0 copy-done.11
  83.5 0.9 copy-done.13
  84.4 5.7 %shard_map.176 = (f32[144,128]{1,0:T(8,128)S(1)}, f32[144,128]{1,0:T(8,128)S(1)}) custom-call(s32[2]{0:T(128)S(1)} %pad_add_fusion.place.refs_0_, s32[2]{0:T(128)S(1)} %bitcast.69, s32[1]{0:T(128)} %bitcast.55.count, f32[32,40,128]{2,1,0:T(8,128)S(1)} %bitcast.62, f32[2,24,1024]{2,1,0:T(8,128)S(1)} %get-tuple-element.54.first_ref, ...), custom_call_target="tpu_custom_call" | custom-call | flops 4000000000 | bytes 10000000 | tf_op jit(solution)/shard_map/pallas_call | solution.py:403
  90.2 1.6 %collective-permute-start.12 = (f32[144,128]{1,0:T(8,128)S(1)}, f32[144,128]{1,0:T(8,128)S(1)}, u32[]{:S(2)}, u32[]{:S(2)}) collective-permute-start(f32[144,128]{1,0:T(8,128)S(1)} %get-tuple-element.63), channel_id=1, source_target_pairs={{0,1},{1,0},{2,3},{3,2},{4,5},{5,4},{6,7},{7,6},{8,9},{9,8},{10,11... | collective-permute-start | bytes 221192 | tf_op jit(solution)/shard_map/ppermute | solution.py:336
  91.8 0.9 collective-permute-done.12
  92.8 3.2 %collective-permute-done.13 = f32[144,128]{1,0:T(8,128)S(1)} collective-permute-done((f32[144,128]{1,0:T(8,128)S(1)}, f32[144,128]{1,0:T(8,128)S(1)}, u32[]{:S(2)}, u32[]{:S(2)}) %collective-permute-start.13) | collective-permute-done | bytes 73760 | tf_op jit(solution)/shard_map/ppermute | solution.py:338
  96.0 0.7 collective-permute-start.14
  96.7 3.8 %collective-permute-done.14 = f32[144,128]{1,0:T(8,128)S(1)} collective-permute-done((f32[144,128]{1,0:T(8,128)S(1)}, f32[144,128]{1,0:T(8,128)S(1)}, u32[]{:S(2)}, u32[]{:S(2)}) %collective-permute-start.14) | collective-permute-done | bytes 73760 | tf_op jit(solution)/shard_map/ppermute | solution.py:338
  100.6 3.2 %collective-permute-done.15 = f32[144,128]{1,0:T(8,128)S(1)} collective-permute-done((f32[144,128]{1,0:T(8,128)S(1)}, f32[144,128]{1,0:T(8,128)S(1)}, u32[]{:S(2)}, u32[]{:S(2)}) %collective-permute-start.15) | collective-permute-done | bytes 73760 | tf_op jit(solution)/shard_map/ppermute | solution.py:338
  103.9 4.4 %collective-permute-done.16 = f32[144,128]{1,0:T(8,128)S(1)} collective-permute-done((f32[144,128]{1,0:T(8,128)S(1)}, f32[144,128]{1,0:T(8,128)S(1)}, u32[]{:S(2)}, u32[]{:S(2)}) %collective-permute-start.16) | collective-permute-done | bytes 73760 | tf_op jit(solution)/shard_map/ppermute | solution.py:338
  108.3 3.9 %collective-permute-start.17 = (f32[144,128]{1,0:T(8,128)S(1)}, f32[144,128]{1,0:T(8,128)S(1)}, u32[]{:S(2)}, u32[]{:S(2)}) collective-permute-start(f32[144,128]{1,0:T(8,128)S(1)} %add.52), channel_id=1, source_target_pairs={{0,16},{1,33},{2,18},{3,35},{4,20},{5,37},{6,22},{7,39},{8,24},{9,... | collective-permute-start | bytes 221192 | tf_op jit(solution)/shard_map/ppermute | solution.py:338
  112.2 2.0 %collective-permute-done.17 = f32[144,128]{1,0:T(8,128)S(1)} collective-permute-done((f32[144,128]{1,0:T(8,128)S(1)}, f32[144,128]{1,0:T(8,128)S(1)}, u32[]{:S(2)}, u32[]{:S(2)}) %collective-permute-start.17) | collective-permute-done | bytes 73760 | tf_op jit(solution)/shard_map/ppermute | solution.py:338
  114.3 2.5 %collective-permute-start.18 = (f32[144,128]{1,0:T(8,128)S(1)}, f32[144,128]{1,0:T(8,128)S(1)}, u32[]{:S(2)}, u32[]{:S(2)}) collective-permute-start(f32[144,128]{1,0:T(8,128)S(1)} %add.53), channel_id=1, source_target_pairs={{0,18},{1,97},{2,16},{3,99},{4,22},{5,101},{6,20},{7,103},{8,26},{... | collective-permute-start | bytes 221192 | tf_op jit(solution)/shard_map/ppermute | solution.py:338
  116.8 2.0 %collective-permute-done.18 = f32[144,128]{1,0:T(8,128)S(1)} collective-permute-done((f32[144,128]{1,0:T(8,128)S(1)}, f32[144,128]{1,0:T(8,128)S(1)}, u32[]{:S(2)}, u32[]{:S(2)}) %collective-permute-start.18) | collective-permute-done | bytes 73760 | tf_op jit(solution)/shard_map/ppermute | solution.py:338
  118.8 6.8 %collective-permute-start.19 = (f32[144,128]{1,0:T(8,128)S(1)}, f32[144,128]{1,0:T(8,128)S(1)}, u32[]{:S(2)}, u32[]{:S(2)}) collective-permute-start(f32[144,128]{1,0:T(8,128)S(1)} %add.54), channel_id=1, source_target_pairs={{0,1},{1,0},{2,3},{3,2},{4,5},{5,4},{6,7},{7,6},{8,9},{9,8},{10,11... | collective-permute-start | bytes 221192 | tf_op jit(solution)/shard_map/ppermute | solution.py:339
  125.6 0.9 collective-permute-done.19
  127.3 0.7 broadcast_divide_fusion
  129.5 0.8 copy.36
  130.4 0.7 copy.37
  131.1 0.7 copy.35
  (90 shorter events, 7.6 us)
Async XLA Ops:
  0.6 21.2 %copy-start = (f32[3,4,4,2048]{3,2,1,0:T(4,128)S(1)}, f32[3,4,4,2048]{3,2,1,0:T(4,128)}, u32[]{:S(2)}) copy-start(f32[3,4,4,2048]{3,2,1,0:T(4,128)} %param.12) | copy-start | bytes 1179652
  0.7 1.1 copy-start.1
  1.8 20.0 %copy-start.2 = (f32[5,4,4,2048]{3,2,1,0:T(4,128)S(1)}, f32[5,4,4,2048]{3,2,1,0:T(4,128)}, u32[]{:S(2)}) copy-start(f32[5,4,4,2048]{3,2,1,0:T(4,128)} %param.11) | copy-start | bytes 1966084
  1.8 20.0 %copy-start.3 = (f32[4,4,2048]{2,1,0:T(4,128)S(1)}, f32[4,4,2048]{2,1,0:T(4,128)}, u32[]{:S(2)}) copy-start(f32[4,4,2048]{2,1,0:T(4,128)} %refs_7_.5) | copy-start | bytes 393220
  3.6 15.6 %collective-permute-start.2 = (f32[20,2048]{1,0:T(8,128)S(1)}, f32[20,2048]{1,0:T(8,128)S(1)}, u32[]{:S(2)}, u32[]{:S(2)}) collective-permute-start(f32[20,2048]{1,0:T(8,128)S(1)} %get-tuple-element.38), channel_id=1, source_target_pairs={{0,1},{1,0},{2,3},{3,2},{4,5},{5,4},{6,7},{7,6},{8,9},{9,8},{10,11... | collective-permute-start | bytes 491528 | tf_op jit(solution)/shard_map/ppermute | solution.py:112
  5.0 14.1 %collective-permute-start.3 = (f32[20,2048]{1,0:T(8,128)S(1)}, f32[20,2048]{1,0:T(8,128)S(1)}, u32[]{:S(2)}, u32[]{:S(2)}) collective-permute-start(f32[20,2048]{1,0:T(8,128)S(1)} %get-tuple-element.39), channel_id=1, source_target_pairs={{0,15},{1,2},{2,1},{3,4},{4,3},{5,6},{6,5},{7,8},{8,7},{9,10},{10,... | collective-permute-start | bytes 491528 | tf_op jit(solution)/shard_map/ppermute | solution.py:113
  8.6 13.3 %collective-permute-start = (f32[5,4,2048]{2,1,0:T(4,128)S(1)}, f32[5,4,2048]{2,1,0:T(4,128)S(1)}, u32[]{:S(2)}, u32[]{:S(2)}) collective-permute-start(f32[5,4,2048]{2,1,0:T(4,128)S(1)} %get-tuple-element.36), channel_id=1, source_target_pairs={{0,16},{16,0},{32,48},{48,32},{64,80},{80,64},{96,112},{112,96},{1... | collective-permute-start | bytes 491528 | tf_op jit(solution)/shard_map/ppermute | solution.py:110
  9.3 12.5 %collective-permute-start.1 = (f32[5,4,2048]{2,1,0:T(4,128)S(1)}, f32[5,4,2048]{2,1,0:T(4,128)S(1)}, u32[]{:S(2)}, u32[]{:S(2)}) collective-permute-start(f32[5,4,2048]{2,1,0:T(4,128)S(1)} %get-tuple-element.37), channel_id=1, source_target_pairs={{0,112},{16,32},{32,16},{48,64},{64,48},{80,96},{96,80},{112,0},{1... | collective-permute-start | bytes 491528 | tf_op jit(solution)/shard_map/ppermute | solution.py:111
  12.2 48.7 %all-to-all-start.1 = ((f32[16,2,40,128]{3,2,1,0:T(8,128)}), f32[16,2,40,128]{3,2,1,0:T(8,128)S(1)}, u32[]{:S(2)}, u32[]{:S(2)}) async-start(f32[16,2,40,128]{3,2,1,0:T(8,128)} %get-tuple-element.52), calls=%async_computation.1 | async-start | bytes 1310720 | tf_op jit(solution)/shard_map/all_to_all | solution.py:367
  19.1 29.2 %copy-start.15 = (f32[32,5,3,3,3]{0,4,3,2,1:T(4,128)S(1)}, f32[32,5,3,3,3]{0,4,3,2,1:T(4,128)}, u32[]{:S(2)}) copy-start(f32[32,5,3,3,3]{0,4,3,2,1:T(4,128)} %param.16) | copy-start | bytes 51844
  21.9 27.1 %copy-start.16 = (f32[5,32,3,3,3]{1,4,3,2,0:T(4,128)S(1)}, f32[5,32,3,3,3]{1,4,3,2,0:T(4,128)}, u32[]{:S(2)}) copy-start(f32[5,32,3,3,3]{1,4,3,2,0:T(4,128)} %param.20) | copy-start | bytes 51844
  23.7 6.4 %collective-permute-start.6 = (f32[20,2048]{1,0:T(8,128)S(1)}, f32[20,2048]{1,0:T(8,128)S(1)}, u32[]{:S(2)}, u32[]{:S(2)}) collective-permute-start(f32[20,2048]{1,0:T(8,128)S(1)} %get-tuple-element.43), channel_id=1, source_target_pairs={{0,1},{1,0},{2,3},{3,2},{4,5},{5,4},{6,7},{7,6},{8,9},{9,8},{10,11... | collective-permute-start | bytes 491528 | tf_op jit(solution)/shard_map/ppermute | solution.py:112
  23.8 16.9 %collective-permute-start.7 = (f32[20,2048]{1,0:T(8,128)S(1)}, f32[20,2048]{1,0:T(8,128)S(1)}, u32[]{:S(2)}, u32[]{:S(2)}) collective-permute-start(f32[20,2048]{1,0:T(8,128)S(1)} %get-tuple-element.44), channel_id=1, source_target_pairs={{0,15},{1,2},{2,1},{3,4},{4,3},{5,6},{6,5},{7,8},{8,7},{9,10},{10,... | collective-permute-start | bytes 491528 | tf_op jit(solution)/shard_map/ppermute | solution.py:113
  25.6 15.0 %collective-permute-start.4 = (f32[5,4,2048]{2,1,0:T(4,128)S(1)}, f32[5,4,2048]{2,1,0:T(4,128)S(1)}, u32[]{:S(2)}, u32[]{:S(2)}) collective-permute-start(f32[5,4,2048]{2,1,0:T(4,128)S(1)} %get-tuple-element.41), channel_id=1, source_target_pairs={{0,16},{16,0},{32,48},{48,32},{64,80},{80,64},{96,112},{112,96},{1... | collective-permute-start | bytes 491528 | tf_op jit(solution)/shard_map/ppermute | solution.py:110
  25.6 15.0 %collective-permute-start.5 = (f32[5,4,2048]{2,1,0:T(4,128)S(1)}, f32[5,4,2048]{2,1,0:T(4,128)S(1)}, u32[]{:S(2)}, u32[]{:S(2)}) collective-permute-start(f32[5,4,2048]{2,1,0:T(4,128)S(1)} %get-tuple-element.42), channel_id=1, source_target_pairs={{0,112},{16,32},{32,16},{48,64},{64,48},{80,96},{96,80},{112,0},{1... | collective-permute-start | bytes 491528 | tf_op jit(solution)/shard_map/ppermute | solution.py:111
  42.4 8.2 %collective-permute-start.10 = (f32[20,2048]{1,0:T(8,128)S(1)}, f32[20,2048]{1,0:T(8,128)S(1)}, u32[]{:S(2)}, u32[]{:S(2)}) collective-permute-start(f32[20,2048]{1,0:T(8,128)S(1)} %get-tuple-element.48), channel_id=1, source_target_pairs={{0,1},{1,0},{2,3},{3,2},{4,5},{5,4},{6,7},{7,6},{8,9},{9,8},{10,11... | collective-permute-start | bytes 491528 | tf_op jit(solution)/shard_map/ppermute | solution.py:112
  42.5 12.7 %collective-permute-start.11 = (f32[20,2048]{1,0:T(8,128)S(1)}, f32[20,2048]{1,0:T(8,128)S(1)}, u32[]{:S(2)}, u32[]{:S(2)}) collective-permute-start(f32[20,2048]{1,0:T(8,128)S(1)} %get-tuple-element.49), channel_id=1, source_target_pairs={{0,15},{1,2},{2,1},{3,4},{4,3},{5,6},{6,5},{7,8},{8,7},{9,10},{10,... | collective-permute-start | bytes 491528 | tf_op jit(solution)/shard_map/ppermute | solution.py:113
  45.7 12.6 %collective-permute-start.8 = (f32[5,4,2048]{2,1,0:T(4,128)S(1)}, f32[5,4,2048]{2,1,0:T(4,128)S(1)}, u32[]{:S(2)}, u32[]{:S(2)}) collective-permute-start(f32[5,4,2048]{2,1,0:T(4,128)S(1)} %get-tuple-element.46), channel_id=1, source_target_pairs={{0,16},{16,0},{32,48},{48,32},{64,80},{80,64},{96,112},{112,96},{1... | collective-permute-start | bytes 491528 | tf_op jit(solution)/shard_map/ppermute | solution.py:110
  46.0 12.2 %collective-permute-start.9 = (f32[5,4,2048]{2,1,0:T(4,128)S(1)}, f32[5,4,2048]{2,1,0:T(4,128)S(1)}, u32[]{:S(2)}, u32[]{:S(2)}) collective-permute-start(f32[5,4,2048]{2,1,0:T(4,128)S(1)} %get-tuple-element.47), channel_id=1, source_target_pairs={{0,112},{16,32},{32,16},{48,64},{64,48},{80,96},{96,80},{112,0},{1... | collective-permute-start | bytes 491528 | tf_op jit(solution)/shard_map/ppermute | solution.py:111
  58.2 10.0 %copy-start.14 = (bf16[5,3,3,3,32]{4,3,2,1,0:T(4,128)(2,1)S(1)}, bf16[5,3,3,3,32]{4,3,2,1,0:T(4,128)(2,1)}, u32[]{:S(2)}) copy-start(bf16[5,3,3,3,32]{4,3,2,1,0:T(4,128)(2,1)} %convert_bitcast_fusion) | copy-start | bytes 25924
  61.0 8.0 %copy-start.4 = (f32[32,32,3,3,3]{1,0,4,3,2:T(8,128)S(1)}, f32[32,32,3,3,3]{1,0,4,3,2:T(8,128)}, u32[]{:S(2)}) copy-start(f32[32,32,3,3,3]{1,0,4,3,2:T(8,128)} %param.18) | copy-start | bytes 331780
  61.0 19.0 %all-to-all-start = ((f32[16,2,40,128]{3,2,1,0:T(8,128)}), f32[16,2,40,128]{3,2,1,0:T(8,128)S(1)}, u32[]{:S(2)}, u32[]{:S(2)}) async-start(f32[16,2,40,128]{3,2,1,0:T(8,128)} %get-tuple-element.51), calls=%async_computation | async-start | bytes 1310720 | tf_op jit(solution)/shard_map/all_to_all | solution.py:402
  67.7 1.7 %copy-start.17 = (f32[32]{0:T(128)S(1)}, f32[32]{0:T(128)}, u32[]{:S(2)}) copy-start(f32[32]{0:T(128)} %param.17) | copy-start | bytes 388
  67.7 1.9 %copy-start.18 = (f32[32]{0:T(128)S(1)}, f32[32]{0:T(128)}, u32[]{:S(2)}) copy-start(f32[32]{0:T(128)} %param.19) | copy-start | bytes 388
  67.7 2.0 %copy-start.19 = (f32[5]{0:T(128)S(1)}, f32[5]{0:T(128)}, u32[]{:S(2)}) copy-start(f32[5]{0:T(128)} %param.21) | copy-start | bytes 64
  67.7 3.0 %copy-start.5 = (s32[1,1,2]{2,1,0:T(1,128)S(1)}, s32[1,1,2]{2,1,0:T(1,128)}, u32[]{:S(2)}) copy-start(s32[1,1,2]{2,1,0:T(1,128)} %param.14) | copy-start | bytes 28
  75.3 1.0 copy-start.6
  76.3 1.0 copy-start.8
  77.2 0.8 copy-start.10
  78.1 0.7 copy-start.12
  80.0 1.2 copy-start.7
  81.2 1.2 copy-start.9
  82.5 1.0 copy-start.11
  83.5 0.9 copy-start.13
  90.2 2.5 %collective-permute-start.12 = (f32[144,128]{1,0:T(8,128)S(1)}, f32[144,128]{1,0:T(8,128)S(1)}, u32[]{:S(2)}, u32[]{:S(2)}) collective-permute-start(f32[144,128]{1,0:T(8,128)S(1)} %get-tuple-element.63), channel_id=1, source_target_pairs={{0,1},{1,0},{2,3},{3,2},{4,5},{5,4},{6,7},{7,6},{8,9},{9,8},{10,11... | collective-permute-start | bytes 221192 | tf_op jit(solution)/shard_map/ppermute | solution.py:336
  92.7 3.3 %collective-permute-start.13 = (f32[144,128]{1,0:T(8,128)S(1)}, f32[144,128]{1,0:T(8,128)S(1)}, u32[]{:S(2)}, u32[]{:S(2)}) collective-permute-start(f32[144,128]{1,0:T(8,128)S(1)} %add.48), channel_id=1, source_target_pairs={{0,32},{1,5},{2,34},{3,7},{4,36},{5,1},{6,38},{7,3},{8,40},{9,13},... | collective-permute-start | bytes 221192 | tf_op jit(solution)/shard_map/ppermute | solution.py:338
  96.0 4.5 %collective-permute-start.14 = (f32[144,128]{1,0:T(8,128)S(1)}, f32[144,128]{1,0:T(8,128)S(1)}, u32[]{:S(2)}, u32[]{:S(2)}) collective-permute-start(f32[144,128]{1,0:T(8,128)S(1)} %add.49), channel_id=1, source_target_pairs={{0,96},{1,13},{2,98},{3,15},{4,100},{5,9},{6,102},{7,11},{8,104},{... | collective-permute-start | bytes 221192 | tf_op jit(solution)/shard_map/ppermute | solution.py:338
  100.5 3.3 %collective-permute-start.15 = (f32[144,128]{1,0:T(8,128)S(1)}, f32[144,128]{1,0:T(8,128)S(1)}, u32[]{:S(2)}, u32[]{:S(2)}) collective-permute-start(f32[144,128]{1,0:T(8,128)S(1)} %add.50), channel_id=1, source_target_pairs={{0,4},{1,17},{2,6},{3,19},{4,0},{5,21},{6,2},{7,23},{8,12},{9,25},... | collective-permute-start | bytes 221192 | tf_op jit(solution)/shard_map/ppermute | solution.py:338
  103.8 4.5 %collective-permute-start.16 = (f32[144,128]{1,0:T(8,128)S(1)}, f32[144,128]{1,0:T(8,128)S(1)}, u32[]{:S(2)}, u32[]{:S(2)}) collective-permute-start(f32[144,128]{1,0:T(8,128)S(1)} %add.51), channel_id=1, source_target_pairs={{0,12},{1,19},{2,14},{3,17},{4,8},{5,23},{6,10},{7,21},{8,4},{9,27... | collective-permute-start | bytes 221192 | tf_op jit(solution)/shard_map/ppermute | solution.py:338
  108.3 5.9 %collective-permute-start.17 = (f32[144,128]{1,0:T(8,128)S(1)}, f32[144,128]{1,0:T(8,128)S(1)}, u32[]{:S(2)}, u32[]{:S(2)}) collective-permute-start(f32[144,128]{1,0:T(8,128)S(1)} %add.52), channel_id=1, source_target_pairs={{0,16},{1,33},{2,18},{3,35},{4,20},{5,37},{6,22},{7,39},{8,24},{9,... | collective-permute-start | bytes 221192 | tf_op jit(solution)/shard_map/ppermute | solution.py:338
  114.3 4.5 %collective-permute-start.18 = (f32[144,128]{1,0:T(8,128)S(1)}, f32[144,128]{1,0:T(8,128)S(1)}, u32[]{:S(2)}, u32[]{:S(2)}) collective-permute-start(f32[144,128]{1,0:T(8,128)S(1)} %add.53), channel_id=1, source_target_pairs={{0,18},{1,97},{2,16},{3,99},{4,22},{5,101},{6,20},{7,103},{8,26},{... | collective-permute-start | bytes 221192 | tf_op jit(solution)/shard_map/ppermute | solution.py:338
  118.8 7.7 %collective-permute-start.19 = (f32[144,128]{1,0:T(8,128)S(1)}, f32[144,128]{1,0:T(8,128)S(1)}, u32[]{:S(2)}, u32[]{:S(2)}) collective-permute-start(f32[144,128]{1,0:T(8,128)S(1)} %add.54), channel_id=1, source_target_pairs={{0,1},{1,0},{2,3},{3,2},{4,5},{5,4},{6,7},{7,6},{8,9},{9,8},{10,11... | collective-permute-start | bytes 221192 | tf_op jit(solution)/shard_map/ppermute | solution.py:339

commit v2 on v1

--- a/solution.py
+++ b/solution.py
@@ -18,17 +18,17 @@
 F32 = jnp.float32
 VMEM = pl.BlockSpec(memory_space=pltpu.VMEM)
 SMEM = pl.BlockSpec(memory_space=pltpu.SMEM)
-LIMIT = 48 * 1024 * 1024
-
-
-def call(kernel, outs, scratch=(), flops=0, nbytes=0, ins=()):
+MIB = 1024 * 1024
+
+
+def call(kernel, outs, scratch=(), flops=0, nbytes=0, ins=(), mib=12):
     return pl.pallas_call(
         kernel,
         out_shape=[jax.ShapeDtypeStruct(s, d) for s, d in outs],
         in_specs=list(ins),
         out_specs=[VMEM] * len(outs),
         scratch_shapes=list(scratch),
-        compiler_params=pltpu.CompilerParams(vmem_limit_bytes=LIMIT),
+        compiler_params=pltpu.CompilerParams(vmem_limit_bytes=mib * MIB),
         cost_estimate=pl.CostEstimate(flops=flops, bytes_accessed=nbytes, transcendentals=0),
     )
 
@@ -53,10 +53,13 @@
         yb_ref[pl.ds(row, 1), :] = jnp.where(odd_y, tail, head)
 
 
-def start_kernel(place, u_ref, slabs_ref, xa_ref, xb_ref, ya_ref, yb_ref):
+def edges_kernel(place, u_ref, xa_ref, xb_ref, ya_ref, yb_ref):
     get = lambda row: u_ref[row]
     write_edges(get, place[0] % 2 == 1, place[1] % 2 == 1, xa_ref, xb_ref, ya_ref, yb_ref)
-    pack_slabs(get, slabs_ref)
+
+
+def slabs_kernel(u_ref, slabs_ref):
+    pack_slabs(lambda row: u_ref[row], slabs_ref)
 
 
 def step_kernel(last, place, u_ref, rxa, rxb, rya, ryb, vel_ref, dif_ref, new_ref, *outs):
@@ -240,9 +243,9 @@
 
 
 def backward_kernel(
-    place, anchors, count, slabs_ref, first_ref, taps_ref, a1_ref, d1_ref, a2_ref, d2_ref, pred_ref, w2_ref, w3_ref,
-    keep_ref, send_ref,
-    last_ref, err_ref, g_ref, b_ref, grads_ref,
+    anchors, count, slabs_ref, first_ref, taps_ref, a1_ref, d1_ref, a2_ref, d2_ref, pred_ref, w2_ref, w3_ref,
+    grads_ref,
+    last_ref, err_ref, g_ref, b_ref,
 ):
     db1 = jnp.zeros((128, 1), F32)
     db2 = jnp.zeros((128, 1), F32)
@@ -280,8 +283,10 @@
     lane = lax.broadcasted_iota(jnp.int32, (C, 128), 1)
     small1, small3 = band_sum(dw1), band_sum(dw3)
     fold = lambda v: v[0:C] + v[C : 2 * C] + v[2 * C : 3 * C] + v[3 * C : 4 * C]
-    grow = lambda v: jnp.concatenate([v, jnp.zeros((C - ROWS, 1), F32)], axis=0)
-    extras = {0: (fold(db1), fold(db2)), 1: (grow(db3), grow(loss)), 2: (jnp.full((C, 1), 1.0, F32) * count[0].astype(F32), None)}
+    by_field = [jnp.sum(db3[f * X : (f + 1) * X], axis=0, keepdims=True) for f in range(F)]
+    db3 = jnp.concatenate(by_field + [jnp.zeros((C - F, 1), F32)], axis=0)
+    loss = jnp.sum(loss, axis=0, keepdims=True) * (1.0 / CELLS)
+    extras = {0: (fold(db1), fold(db2)), 1: (db3, loss), 2: (jnp.full((C, 1), 1.0, F32) * count[0].astype(F32), None)}
     for t in range(TAPS):
         dy, dz = t // 3, t % 3
         total = jnp.zeros((C, 128), F32)
@@ -301,10 +306,31 @@
             if b is not None:
                 total = jnp.where(lane == 127, b, total)
         grads_ref[t * C : (t + 1) * C] = total
-    core = place[1] % 2
-    low, high = grads_ref[0:144], grads_ref[144:288]
-    keep_ref[...] = jnp.where(core == 0, low, high)
-    send_ref[...] = jnp.where(core == 0, high, low)
+
+
+def finish_kernel(place, mine_ref, other_ref, g1_ref, gb1_ref, g2_ref, gb2_ref, g3_ref, gb3_ref, loss_ref):
+    first = place[1] % 2 == 0
+    rows = lambda t: jnp.where(first, other_ref[t * C : (t + 1) * C], mine_ref[t * C : (t + 1) * C])
+    total = rows(2)[0:1, 126:127]
+    for t in range(TAPS):
+        dy, dz = t // 3, t % 3
+        block = rows(t) / total
+        for dx in range(3):
+            g2_ref[dx * TAPS + t] = block[:, dx * C : (dx + 1) * C]
+        turned = block.T
+        for f in range(F):
+            for dx in range(3):
+                to = (f * 3 + dx) * 3 + dy
+                at = 96 + f * 3 + dx
+                g1_ref[to, dz : dz + 1, :] = turned[at : at + 1]
+                at = 111 + f * 3 + 2 - dx
+                g3_ref[to, dz : dz + 1, :] = turned[at : at + 1]
+        if t == 0:
+            gb1_ref[...] = turned[126:127]
+            gb2_ref[...] = turned[127:128]
+        if t == 1:
+            gb3_ref[...] = turned[126:127, 0:F]
+            loss_ref[...] = turned[127:128, 0:1]
 
 
 def reduce_steps():
@@ -314,29 +340,25 @@
     def far(c):
         return 3 - c
 
-    orders = (("x", "y", "z"), ("y", "z", "x"))
     steps = []
     for n in range(6):
         pairs = []
         for gx in range(8):
-            for gy in range(16):
+            for gy in range(1, 16, 2):
                 at = {"x": gx // 2, "y": gy // 4, "z": (gy // 2 % 2) * 2 + gx % 2}
-                core = gy % 2
-                axis = orders[core][n // 2]
+                axis = "zyx"[n // 2]
                 at[axis] = (near, far)[n % 2](at[axis])
-                to = (at["x"] * 2 + at["z"] % 2) * 16 + at["y"] * 4 + (at["z"] // 2) * 2 + core
+                to = (at["x"] * 2 + at["z"] % 2) * 16 + at["y"] * 4 + (at["z"] // 2) * 2 + 1
                 pairs.append((gx * 16 + gy, to))
         steps.append(pairs)
     return steps
 
 
-def sum_all(keep, send):
-    both = ("gx", "gy")
-    cores = [(i, i ^ 1) for i in range(16)]
-    mine = keep + lax.ppermute(send, "gy", cores)
+def sum_all(mine):
+    mine = mine + lax.ppermute(mine, "gy", [(i, i + 1) for i in range(0, 16, 2)])
     for pairs in reduce_steps():
-        mine = mine + lax.ppermute(mine, both, pairs)
-    return mine, lax.ppermute(mine, "gy", cores)
+        mine = mine + lax.ppermute(mine, ("gx", "gy"), pairs)
+    return mine, lax.ppermute(mine, "gy", [(i + 1, i) for i in range(0, 16, 2)])
 
 
 def banded(w, flip):
@@ -363,7 +385,8 @@
     anchors = patch_anchor.reshape(2)
     count = patch_count.reshape(1)
 
-    slabs, *edges = call(start_kernel, [SLABS] + EDGES, ins=[SMEM, VMEM], nbytes=1_500_000)(place, u)
+    edges = call(edges_kernel, EDGES, ins=[SMEM, VMEM], nbytes=1_000_000)(place, u)
+    (slabs,) = call(slabs_kernel, [SLABS], ins=[VMEM], nbytes=1_500_000)(u)
     first_slabs = lax.all_to_all(slabs, "gy", 0, 0, tiled=True).reshape(32, 2 * F * X, Z)
 
     w2 = jnp.transpose(weight_two, (2, 3, 4, 0, 1)).reshape(27, C, C)
@@ -397,36 +420,36 @@
         ins=[SMEM] + [VMEM] * 7,
         flops=2_000_000_000,
         nbytes=8_000_000,
+        mib=24,
     )(anchors, first_slabs, w1_band.T, w2_fwd, w3_band, b1, b2, b3)
 
     last_slabs = lax.all_to_all(edges[0], "gy", 0, 0, tiled=True).reshape(32, 2 * F * X, Z)
-    keep, send = call(
+    (grads,) = call(
         backward_kernel,
-        [((144, 128), F32)] * 2,
+        [((TAPS * C, 128), F32)],
         scratch=[
             pltpu.VMEM((ROWS, PY * Z), F32),
             pltpu.VMEM((ROWS, PY * Z), F32),
             pltpu.VMEM((TAPS * ROWS, PY * Z), BF),
             pltpu.VMEM((384, (PY + 2) * Z), BF),
-            pltpu.VMEM((288, 128), F32),
         ],
-        ins=[SMEM] * 3 + [VMEM] * 10,
+        ins=[SMEM] * 2 + [VMEM] * 10,
         flops=4_000_000_000,
         nbytes=10_000_000,
-    )(place, anchors, count, last_slabs, *learned, w2_bwd, w3_band.T)
-
-    mine, other = sum_all(keep, send)
-    core = place[1] % 2
-    grads = jnp.where(core == 0, jnp.concatenate([mine, other]), jnp.concatenate([other, mine]))
-    grads = grads.reshape(TAPS, C, 128)
-    total = grads[2, 0, 126]
-    grads = grads / total
-    g2 = jnp.transpose(grads[:, :, 0:96].reshape(3, 3, C, 3, C), (2, 4, 3, 0, 1))
-    g1 = jnp.transpose(grads[:, :, 96:111].reshape(3, 3, C, F, 3), (2, 3, 4, 0, 1))
-    g3 = jnp.transpose(grads[:, :, 111:126].reshape(3, 3, C, F, 3), (3, 2, 4, 0, 1))[:, :, ::-1]
-    gb1, gb2 = grads[0, :, 126], grads[0, :, 127]
-    gb3 = grads[1, 0 : F * X, 126].reshape(F, X).sum(1)
-    loss = grads[1, 0 : F * X, 127].sum() / CELLS
+        mib=24,
+    )(anchors, count, last_slabs, *learned, w2_bwd, w3_band.T)
+
+    mine, other = sum_all(grads)
+    g1, gb1, g2, gb2, g3, gb3, loss = call(
+        finish_kernel,
+        [((45, 3, C), F32), ((1, C), F32), ((27, C, C), F32), ((1, C), F32), ((45, 3, C), F32), ((1, F), F32), ((1, 1), F32)],
+        ins=[SMEM, VMEM, VMEM],
+        nbytes=1_000_000,
+    )(place, mine, other)
+    g1 = jnp.transpose(g1.reshape(F, 3, 3, 3, C), (4, 0, 1, 2, 3))
+    g2 = jnp.transpose(g2.reshape(3, 3, 3, C, C), (3, 4, 0, 1, 2))
+    g3 = jnp.transpose(g3.reshape(F, 3, 3, 3, C), (0, 4, 1, 2, 3))
+    gb1, gb2, gb3, loss = gb1.reshape(C), gb2.reshape(C), gb3.reshape(F), loss.reshape(())
     return u.reshape(F, X, 4, 2048), g1, gb1, g2, gb2, g3, gb3, loss
 
 

time: 135 us -> 138 us (1.022)
  waiting for transfers between devices: 42.6 us -> 49.8 us
  other arithmetic: 3.22 us -> 1.33 us
  between operations: 3.48 us -> 1.69 us
    ppermute x8, waiting for transfers between devices: 20.5 us -> 28.5 us  [the longest x6 25.1 us: sum_all(): mine = mine + lax.ppermute(mine, ('gx', 'gy'), pairs)]
    ppermute x3, waiting for transfers between devices: 5.66 us -> 2.33 us  [exchange(): lax.ppermute(xa, 'gx', pairs(8, False))]
    ppermute x3, waiting for transfers between devices: 15.2 us -> 17.8 us  [exchange(): lax.ppermute(yb, 'gy', pairs(16, True))]
    ppermute x3, starting transfers between devices: 9.6 us -> 7.84 us  [exchange(): lax.ppermute(xb, 'gx', pairs(8, True))]
    unnamed x43 -> x44, local copies, waits for them, and re-layouts: 11.2 us -> 12.9 us
    pallas_call x2 -> x4, Pallas kernels: 7.44 us -> 8.44 us  [the longest x1 4.69 us: on_device(): call(backward_kernel, [((TAPS * C, 128), F32)], scratch=[pltpu.VMEM((ROWS...]
  transfers between devices with their start and end apart: 22 -> 22, of which waited for: 13 -> 13; matrix products, arithmetic and copies ran while one was open for 3% -> 4% of each run, Pallas kernels for 8% -> 8%
where the time goes in v2:
time: 138 us
  waiting for transfers between devices  49.8 us (36%)
  starting transfers between devices  49.4 us (36%)
  Pallas kernels  18.7 us (14%)
  local copies, waits for them, and re-layouts  16.7 us (12%)
  between operations  1.69 us (1%)
    ppermute x6, waiting for transfers between devices, sum_all(): mine = mine + lax.ppermute(mine, ('gx', 'gy'), pairs)  25.1 us
    ppermute x3, waiting for transfers between devices, exchange(): lax.ppermute(yb, 'gy', pairs(16, True))  17.8 us
    ppermute x6, starting transfers between devices, sum_all(): mine = mine + lax.ppermute(mine, ('gx', 'gy'), pairs)  13.8 us
    unnamed x44, local copies, waits for them, and re-layouts  12.9 us
    ppermute x3, starting transfers between devices, exchange(): lax.ppermute(yb, 'gy', pairs(16, True))  9.08 us
    ppermute x3, starting transfers between devices, exchange(): lax.ppermute(xb, 'gx', pairs(8, True))  7.84 us
    all_to_all x1, starting transfers between devices, on_device(): lax.all_to_all(slabs, 'gy', 0, 0, tiled=True).reshape(32, 2 * F * X, Z)  6.81 us
    pallas_call x3, Pallas kernels, on_device(): call(kernel, outs, ins=[SMEM] + [VMEM] * 7, nbytes=4000000)  6.51 us
  transfers between devices with their start and end apart: 22, of which 13 were waited for; matrix products, arithmetic and copies ran while one was open for 4% of the time, Pallas kernels for 8%

profile of v2, /device:TPU:1, one launch (start us, length us, event | category | flops | bytes accessed | tf_op | source)
XLA Modules:
  0.0 137.6 jit_solution(8992975871407969179)
XLA Ops:
  0.7 1.1 copy-done
  2.6 1.5 %collective-permute-start.2 = (f32[20,2048]{1,0:T(8,128)S(1)}, f32[20,2048]{1,0:T(8,128)S(1)}, u32[]{:S(2)}, u32[]{:S(2)}) collective-permute-start(f32[20,2048]{1,0:T(8,128)S(1)} %get-tuple-element.42), channel_id=1, source_target_pairs={{0,1},{1,0},{2,3},{3,2},{4,5},{5,4},{6,7},{7,6},{8,9},{9,8},{10,11... | collective-permute-start | bytes 491528 | tf_op jit(solution)/shard_map/ppermute | solution.py:115
  4.1 3.7 %collective-permute-start.3 = (f32[20,2048]{1,0:T(8,128)S(1)}, f32[20,2048]{1,0:T(8,128)S(1)}, u32[]{:S(2)}, u32[]{:S(2)}) collective-permute-start(f32[20,2048]{1,0:T(8,128)S(1)} %get-tuple-element.43), channel_id=1, source_target_pairs={{0,15},{1,2},{2,1},{3,4},{4,3},{5,6},{6,5},{7,8},{8,7},{9,10},{10,... | collective-permute-start | bytes 491528 | tf_op jit(solution)/shard_map/ppermute | solution.py:116
  8.5 2.9 %collective-permute-start.1 = (f32[5,4,2048]{2,1,0:T(4,128)S(1)}, f32[5,4,2048]{2,1,0:T(4,128)S(1)}, u32[]{:S(2)}, u32[]{:S(2)}) collective-permute-start(f32[5,4,2048]{2,1,0:T(4,128)S(1)} %get-tuple-element.41), channel_id=1, source_target_pairs={{0,112},{16,32},{32,16},{48,64},{64,48},{80,96},{96,80},{112,0},{1... | collective-permute-start | bytes 491528 | tf_op jit(solution)/shard_map/ppermute | solution.py:114
  11.4 1.1 copy-done.1
  12.5 1.2 shard_map.174
  13.7 6.8 %all-to-all-start.1 = ((f32[16,2,40,128]{3,2,1,0:T(8,128)}), f32[16,2,40,128]{3,2,1,0:T(8,128)S(1)}, u32[]{:S(2)}, u32[]{:S(2)}) async-start(f32[16,2,40,128]{3,2,1,0:T(8,128)} %shard_map.174), calls=%async_computation.1 | async-start | bytes 1310720 | tf_op jit(solution)/shard_map/all_to_all | solution.py:390
  20.7 1.8 %shard_map.171 = (f32[20,4,2048]{2,1,0:T(4,128)S(1)}, f32[5,4,2048]{2,1,0:T(4,128)S(1)}, f32[5,4,2048]{2,1,0:T(4,128)S(1)}, f32[20,2048]{1,0:T(8,128)S(1)}, f32[20,2048]{1,0:T(8,128)S(1)}) custom-call(s32[2]{0:T(128)S(1)} %pad_add_fusion.place.refs_0_, f32[20,4,2048]{2,1,0:T(4,128)S(1)} %bitcast.57, f32[5,4,2048]{2,1,0:T(4,128)S(1)} %collective-permute-done.refs_2_, ...), custom_call_target="tpu_custom_call" | custom-call | bytes 4000000 | tf_op jit(solution)/shard_map/pallas_call | solution.py:405
  22.8 2.9 %collective-permute-start.7 = (f32[20,2048]{1,0:T(8,128)S(1)}, f32[20,2048]{1,0:T(8,128)S(1)}, u32[]{:S(2)}, u32[]{:S(2)}) collective-permute-start(f32[20,2048]{1,0:T(8,128)S(1)} %get-tuple-element.48), channel_id=1, source_target_pairs={{0,15},{1,2},{2,1},{3,4},{4,3},{5,6},{6,5},{7,8},{8,7},{9,10},{10,... | collective-permute-start | bytes 491528 | tf_op jit(solution)/shard_map/ppermute | solution.py:116
  25.8 2.6 %collective-permute-start.5 = (f32[5,4,2048]{2,1,0:T(4,128)S(1)}, f32[5,4,2048]{2,1,0:T(4,128)S(1)}, u32[]{:S(2)}, u32[]{:S(2)}) collective-permute-start(f32[5,4,2048]{2,1,0:T(4,128)S(1)} %get-tuple-element.46), channel_id=1, source_target_pairs={{0,112},{16,32},{32,16},{48,64},{64,48},{80,96},{96,80},{112,0},{1... | collective-permute-start | bytes 491528 | tf_op jit(solution)/shard_map/ppermute | solution.py:114
  28.4 13.3 %collective-permute-done.7.refs_5_ = f32[20,2048]{1,0:T(8,128)S(1)} collective-permute-done((f32[20,2048]{1,0:T(8,128)S(1)}, f32[20,2048]{1,0:T(8,128)S(1)}, u32[]{:S(2)}, u32[]{:S(2)}) %collective-permute-start.7) | collective-permute-done | bytes 163872 | tf_op jit(solution)/shard_map/ppermute | solution.py:116
  41.7 1.8 %shard_map.172 = (f32[20,4,2048]{2,1,0:T(4,128)S(1)}, f32[5,4,2048]{2,1,0:T(4,128)S(1)}, f32[5,4,2048]{2,1,0:T(4,128)S(1)}, f32[20,2048]{1,0:T(8,128)S(1)}, f32[20,2048]{1,0:T(8,128)S(1)}) custom-call(s32[2]{0:T(128)S(1)} %pad_add_fusion.place.refs_0_, f32[20,4,2048]{2,1,0:T(4,128)S(1)} %get-tuple-element.44.refs_1_, ...), custom_call_target="tpu_custom_call" | custom-call | bytes 4000000 | tf_op jit(solution)/shard_map/pallas_call | solution.py:405
  43.7 2.5 %collective-permute-start.11 = (f32[20,2048]{1,0:T(8,128)S(1)}, f32[20,2048]{1,0:T(8,128)S(1)}, u32[]{:S(2)}, u32[]{:S(2)}) collective-permute-start(f32[20,2048]{1,0:T(8,128)S(1)} %get-tuple-element.53), channel_id=1, source_target_pairs={{0,15},{1,2},{2,1},{3,4},{4,3},{5,6},{6,5},{7,8},{8,7},{9,10},{10,... | collective-permute-start | bytes 491528 | tf_op jit(solution)/shard_map/ppermute | solution.py:116
  46.9 2.3 %collective-permute-start.9 = (f32[5,4,2048]{2,1,0:T(4,128)S(1)}, f32[5,4,2048]{2,1,0:T(4,128)S(1)}, u32[]{:S(2)}, u32[]{:S(2)}) collective-permute-start(f32[5,4,2048]{2,1,0:T(4,128)S(1)} %get-tuple-element.51), channel_id=1, source_target_pairs={{0,112},{16,32},{32,16},{48,64},{64,48},{80,96},{96,80},{112,0},{1... | collective-permute-start | bytes 491528 | tf_op jit(solution)/shard_map/ppermute | solution.py:114
  49.9 1.5 %rev.8 = bf16[5,3,3,3,32]{4,3,2,1,0:T(4,128)(2,1)} reverse(f32[5,3,3,3,32]{4,3,2,1,0:T(4,128)} %bitcast.71), dimensions={1} | reverse | bytes 25920 | tf_op jit(solution)/shard_map/rev | solution.py:368
  51.4 1.0 fusion.4
  52.4 4.5 %collective-permute-done.11.refs_5_ = f32[20,2048]{1,0:T(8,128)S(1)} collective-permute-done((f32[20,2048]{1,0:T(8,128)S(1)}, f32[20,2048]{1,0:T(8,128)S(1)}, u32[]{:S(2)}, u32[]{:S(2)}) %collective-permute-start.11) | collective-permute-done | bytes 163872 | tf_op jit(solution)/shard_map/ppermute | solution.py:116
  56.9 2.2 %collective-permute-done.8.refs_2_ = f32[5,4,2048]{2,1,0:T(4,128)S(1)} collective-permute-done((f32[5,4,2048]{2,1,0:T(4,128)S(1)}, f32[5,4,2048]{2,1,0:T(4,128)S(1)}, u32[]{:S(2)}, u32[]{:S(2)}) %collective-permute-start.8) | collective-permute-done | bytes 163872 | tf_op jit(solution)/shard_map/ppermute | solution.py:113
  59.1 2.8 %shard_map.173 = (f32[20,4,2048]{2,1,0:T(4,128)}, f32[16,2,40,128]{3,2,1,0:T(8,128)}) custom-call(s32[2]{0:T(128)S(1)} %pad_add_fusion.place.refs_0_, f32[20,4,2048]{2,1,0:T(4,128)S(1)} %get-tuple-element.49.refs_1_, f32[5,4,2048]{2,1,0:T(4,128)S(1)} %collective-permute-done.8.refs_2_, f32[5,4,2048]{2,1,0:T(4,128)S(1)} %collective-permute-done.9.refs_3_, ...), custom_call_target="tpu_custom_call" | custom-call | bytes 4000000 | tf_op jit(solution)/shard_map/pallas_call | solution.py:405
  61.9 5.8 %all-to-all-start = ((f32[16,2,40,128]{3,2,1,0:T(8,128)}), f32[16,2,40,128]{3,2,1,0:T(8,128)S(1)}, u32[]{:S(2)}, u32[]{:S(2)}) async-start(f32[16,2,40,128]{3,2,1,0:T(8,128)} %get-tuple-element.55), calls=%async_computation | async-start | bytes 1310720 | tf_op jit(solution)/shard_map/all_to_all | solution.py:426
  70.8 3.3 %shard_map.176 = (f32[2,24,1024]{2,1,0:T(8,128)S(1)}, bf16[2,216,1024]{2,1,0:T(8,128)(2,1)S(1)}, bf16[2,384,1280]{2,1,0:T(8,128)(2,1)S(1)}, f32[2,128,1024]{2,1,...) custom-call(s32[2]{0:T(128)S(1)} %bitcast.68, ...), custom_call_target="tpu_custom_call" | custom-call | flops 2000000000 | bytes 8000000 | tf_op jit(solution)/shard_map/pallas_call | solution.py:409
  74.1 1.3 copy-done.7
  75.4 1.0 copy-done.9
  76.4 1.0 copy-done.11
  78.9 1.2 all-to-all-done
  80.1 1.5 %copy-done.8 = bf16[2,384,1280]{2,1,0:T(8,128)(2,1)S(1)} copy-done((bf16[2,384,1280]{2,1,0:T(8,128)(2,1)S(1)}, bf16[2,384,1280]{2,1,0:T(8,128)(2,1)}, u32[]{:S(2)}) %copy-start.8) | copy-done | bytes 1966104
  81.6 1.2 copy-done.10
  82.8 1.2 copy-done.12
  84.1 1.0 copy-done.14
  85.1 0.9 copy-done.16
  86.0 4.7 %shard_map.177 = f32[288,128]{1,0:T(8,128)S(1)} custom-call(s32[2]{0:T(128)S(1)} %bitcast.69, s32[1]{0:T(128)} %bitcast.54.count, f32[32,40,128]{2,1,0:T(8,128)S(1)} %bitcast.62, f32[2,24,1024]{2,1,0:T(8,128)S(1)} %get-tuple-element.57.first_ref, bf16[2,216,1024]{2,1,0:T(8,128)(2,1)S(1)} %get-tuple-element.58.taps_ref, bf16[2,384,1280]{2,1,0:T(8,128)(2,1)S(1)} %copy-done.8, ...), custom_call_target="tpu_custom_call" | custom-call | flops 4000000000 | bytes 10000000 | tf_op jit(solution)/shard_map/pallas_call | solution.py:427
  90.7 1.3 collective-permute-start.12
  92.0 2.4 %collective-permute-done.12 = f32[288,128]{1,0:T(8,128)S(1)} collective-permute-done((f32[288,128]{1,0:T(8,128)S(1)}, f32[288,128]{1,0:T(8,128)S(1)}, u32[]{:S(2)}, u32[]{:S(2)}) %collective-permute-start.12) | collective-permute-done | bytes 147488 | tf_op jit(solution)/shard_map/ppermute | solution.py:358
  94.4 1.9 %collective-permute-start.13 = (f32[288,128]{1,0:T(8,128)S(1)}, f32[288,128]{1,0:T(8,128)S(1)}, u32[]{:S(2)}, u32[]{:S(2)}) collective-permute-start(f32[288,128]{1,0:T(8,128)S(1)} %add.43), channel_id=1, source_target_pairs={{1,17},{3,19},{5,21},{7,23},{9,25},{11,27},{13,29},{15,31},{17,1},... | collective-permute-start | bytes 442376 | tf_op jit(solution)/shard_map/ppermute | solution.py:360
  96.4 4.0 %collective-permute-done.13 = f32[288,128]{1,0:T(8,128)S(1)} collective-permute-done((f32[288,128]{1,0:T(8,128)S(1)}, f32[288,128]{1,0:T(8,128)S(1)}, u32[]{:S(2)}, u32[]{:S(2)}) %collective-permute-start.13) | collective-permute-done | bytes 147488 | tf_op jit(solution)/shard_map/ppermute | solution.py:360
  100.3 2.2 %collective-permute-start.14 = (f32[288,128]{1,0:T(8,128)S(1)}, f32[288,128]{1,0:T(8,128)S(1)}, u32[]{:S(2)}, u32[]{:S(2)}) collective-permute-start(f32[288,128]{1,0:T(8,128)S(1)} %add.44), channel_id=1, source_target_pairs={{1,19},{3,17},{5,23},{7,21},{9,27},{11,25},{13,31},{15,29},{17,3},... | collective-permute-start | bytes 442376 | tf_op jit(solution)/shard_map/ppermute | solution.py:360
  102.5 4.9 %collective-permute-done.14 = f32[288,128]{1,0:T(8,128)S(1)} collective-permute-done((f32[288,128]{1,0:T(8,128)S(1)}, f32[288,128]{1,0:T(8,128)S(1)}, u32[]{:S(2)}, u32[]{:S(2)}) %collective-permute-start.14) | collective-permute-done | bytes 147488 | tf_op jit(solution)/shard_map/ppermute | solution.py:360
  107.5 1.9 %collective-permute-start.15 = (f32[288,128]{1,0:T(8,128)S(1)}, f32[288,128]{1,0:T(8,128)S(1)}, u32[]{:S(2)}, u32[]{:S(2)}) collective-permute-start(f32[288,128]{1,0:T(8,128)S(1)} %add.45), channel_id=1, source_target_pairs={{1,5},{3,7},{5,1},{7,3},{9,13},{11,15},{13,9},{15,11},{17,21},{19,... | collective-permute-start | bytes 442376 | tf_op jit(solution)/shard_map/ppermute | solution.py:360
  109.4 4.0 %collective-permute-done.15 = f32[288,128]{1,0:T(8,128)S(1)} collective-permute-done((f32[288,128]{1,0:T(8,128)S(1)}, f32[288,128]{1,0:T(8,128)S(1)}, u32[]{:S(2)}, u32[]{:S(2)}) %collective-permute-start.15) | collective-permute-done | bytes 147488 | tf_op jit(solution)/shard_map/ppermute | solution.py:360
  113.4 2.9 %collective-permute-start.16 = (f32[288,128]{1,0:T(8,128)S(1)}, f32[288,128]{1,0:T(8,128)S(1)}, u32[]{:S(2)}, u32[]{:S(2)}) collective-permute-start(f32[288,128]{1,0:T(8,128)S(1)} %add.46), channel_id=1, source_target_pairs={{1,13},{3,15},{5,9},{7,11},{9,5},{11,7},{13,1},{15,3},{17,29},{19,... | collective-permute-start | bytes 442376 | tf_op jit(solution)/shard_map/ppermute | solution.py:360
  116.3 4.2 %collective-permute-done.16 = f32[288,128]{1,0:T(8,128)S(1)} collective-permute-done((f32[288,128]{1,0:T(8,128)S(1)}, f32[288,128]{1,0:T(8,128)S(1)}, u32[]{:S(2)}, u32[]{:S(2)}) %collective-permute-start.16) | collective-permute-done | bytes 147488 | tf_op jit(solution)/shard_map/ppermute | solution.py:360
  120.5 1.9 %collective-permute-start.17 = (f32[288,128]{1,0:T(8,128)S(1)}, f32[288,128]{1,0:T(8,128)S(1)}, u32[]{:S(2)}, u32[]{:S(2)}) collective-permute-start(f32[288,128]{1,0:T(8,128)S(1)} %add.47), channel_id=1, source_target_pairs={{1,33},{3,35},{5,37},{7,39},{9,41},{11,43},{13,45},{15,47},{17,49}... | collective-permute-start | bytes 442376 | tf_op jit(solution)/shard_map/ppermute | solution.py:360
  122.4 4.0 %collective-permute-done.17 = f32[288,128]{1,0:T(8,128)S(1)} collective-permute-done((f32[288,128]{1,0:T(8,128)S(1)}, f32[288,128]{1,0:T(8,128)S(1)}, u32[]{:S(2)}, u32[]{:S(2)}) %collective-permute-start.17) | collective-permute-done | bytes 147488 | tf_op jit(solution)/shard_map/ppermute | solution.py:360
  126.4 3.0 %collective-permute-start.18 = (f32[288,128]{1,0:T(8,128)S(1)}, f32[288,128]{1,0:T(8,128)S(1)}, u32[]{:S(2)}, u32[]{:S(2)}) collective-permute-start(f32[288,128]{1,0:T(8,128)S(1)} %add.48), channel_id=1, source_target_pairs={{1,97},{3,99},{5,101},{7,103},{9,105},{11,107},{13,109},{15,111},{... | collective-permute-start | bytes 442376 | tf_op jit(solution)/shard_map/ppermute | solution.py:360
  129.4 4.1 %collective-permute-done.18 = f32[288,128]{1,0:T(8,128)S(1)} collective-permute-done((f32[288,128]{1,0:T(8,128)S(1)}, f32[288,128]{1,0:T(8,128)S(1)}, u32[]{:S(2)}, u32[]{:S(2)}) %collective-permute-start.18) | collective-permute-done | bytes 147488 | tf_op jit(solution)/shard_map/ppermute | solution.py:360
  133.5 1.3 collective-permute-start.19
  134.8 1.0 collective-permute-done.19.other_ref
  135.8 1.8 %shard_map.178 = (f32[45,3,32]{2,1,0:T(4,128)}, f32[1,32]{1,0:T(1,128)}, f32[27,32,32]{2,1,0:T(8,128)}, f32[1,32]{1,0:T(1,128)}, f32[45,3,32]{2,1,0:T(4,128)}, /*index=5*/f32[1,5]{1,0:T(1,128)}, f32[1,1]{1,0:T(1,128)}) custom-call(s32[2]{0:T(128)S(1)} %pad_add_fusion.place.refs_0_, f32[288,128]{1,0:T(8,128)S(1)} %add.49.mine_ref, ...), custom_call_target="tpu_custom_call" | custom-call | bytes 1000000 | tf_op jit(solution)/shard_map/pallas_call | solution.py:443
  (79 shorter events, 7.4 us)
Async XLA Ops:
  0.7 1.1 copy-start
  1.8 18.9 %copy-start.2 = (f32[5,4,4,2048]{3,2,1,0:T(4,128)S(1)}, f32[5,4,4,2048]{3,2,1,0:T(4,128)}, u32[]{:S(2)}) copy-start(f32[5,4,4,2048]{3,2,1,0:T(4,128)} %param.11) | copy-start | bytes 1966084
  2.6 17.9 %collective-permute-start.2 = (f32[20,2048]{1,0:T(8,128)S(1)}, f32[20,2048]{1,0:T(8,128)S(1)}, u32[]{:S(2)}, u32[]{:S(2)}) collective-permute-start(f32[20,2048]{1,0:T(8,128)S(1)} %get-tuple-element.42), channel_id=1, source_target_pairs={{0,1},{1,0},{2,3},{3,2},{4,5},{5,4},{6,7},{7,6},{8,9},{9,8},{10,11... | collective-permute-start | bytes 491528 | tf_op jit(solution)/shard_map/ppermute | solution.py:115
  4.1 16.4 %collective-permute-start.3 = (f32[20,2048]{1,0:T(8,128)S(1)}, f32[20,2048]{1,0:T(8,128)S(1)}, u32[]{:S(2)}, u32[]{:S(2)}) collective-permute-start(f32[20,2048]{1,0:T(8,128)S(1)} %get-tuple-element.43), channel_id=1, source_target_pairs={{0,15},{1,2},{2,1},{3,4},{4,3},{5,6},{6,5},{7,8},{8,7},{9,10},{10,... | collective-permute-start | bytes 491528 | tf_op jit(solution)/shard_map/ppermute | solution.py:116
  7.7 12.9 %collective-permute-start = (f32[5,4,2048]{2,1,0:T(4,128)S(1)}, f32[5,4,2048]{2,1,0:T(4,128)S(1)}, u32[]{:S(2)}, u32[]{:S(2)}) collective-permute-start(f32[5,4,2048]{2,1,0:T(4,128)S(1)} %get-tuple-element.40), channel_id=1, source_target_pairs={{0,16},{16,0},{32,48},{48,32},{64,80},{80,64},{96,112},{112,96},{1... | collective-permute-start | bytes 491528 | tf_op jit(solution)/shard_map/ppermute | solution.py:113
  8.5 12.2 %collective-permute-start.1 = (f32[5,4,2048]{2,1,0:T(4,128)S(1)}, f32[5,4,2048]{2,1,0:T(4,128)S(1)}, u32[]{:S(2)}, u32[]{:S(2)}) collective-permute-start(f32[5,4,2048]{2,1,0:T(4,128)S(1)} %get-tuple-element.41), channel_id=1, source_target_pairs={{0,112},{16,32},{32,16},{48,64},{64,48},{80,96},{96,80},{112,0},{1... | collective-permute-start | bytes 491528 | tf_op jit(solution)/shard_map/ppermute | solution.py:114
  11.4 1.1 copy-start.1
  12.5 8.2 %copy-start.3 = (f32[3,4,4,2048]{3,2,1,0:T(4,128)S(1)}, f32[3,4,4,2048]{3,2,1,0:T(4,128)}, u32[]{:S(2)}) copy-start(f32[3,4,4,2048]{3,2,1,0:T(4,128)} %param.12) | copy-start | bytes 1179652
  12.5 8.2 %copy-start.4 = (f32[4,4,2048]{2,1,0:T(4,128)S(1)}, f32[4,4,2048]{2,1,0:T(4,128)}, u32[]{:S(2)}) copy-start(f32[4,4,2048]{2,1,0:T(4,128)} %refs_7_.5) | copy-start | bytes 393220
  13.7 48.3 %all-to-all-start.1 = ((f32[16,2,40,128]{3,2,1,0:T(8,128)}), f32[16,2,40,128]{3,2,1,0:T(8,128)S(1)}, u32[]{:S(2)}, u32[]{:S(2)}) async-start(f32[16,2,40,128]{3,2,1,0:T(8,128)} %shard_map.174), calls=%async_computation.1 | async-start | bytes 1310720 | tf_op jit(solution)/shard_map/all_to_all | solution.py:390
  20.5 28.8 %copy-start.18 = (f32[32,5,3,3,3]{0,4,3,2,1:T(4,128)S(1)}, f32[32,5,3,3,3]{0,4,3,2,1:T(4,128)}, u32[]{:S(2)}) copy-start(f32[32,5,3,3,3]{0,4,3,2,1:T(4,128)} %param.16) | copy-start | bytes 51844
  22.5 5.9 %collective-permute-start.6 = (f32[20,2048]{1,0:T(8,128)S(1)}, f32[20,2048]{1,0:T(8,128)S(1)}, u32[]{:S(2)}, u32[]{:S(2)}) collective-permute-start(f32[20,2048]{1,0:T(8,128)S(1)} %get-tuple-element.47), channel_id=1, source_target_pairs={{0,1},{1,0},{2,3},{3,2},{4,5},{5,4},{6,7},{7,6},{8,9},{9,8},{10,11... | collective-permute-start | bytes 491528 | tf_op jit(solution)/shard_map/ppermute | solution.py:115
  22.8 18.9 %collective-permute-start.7 = (f32[20,2048]{1,0:T(8,128)S(1)}, f32[20,2048]{1,0:T(8,128)S(1)}, u32[]{:S(2)}, u32[]{:S(2)}) collective-permute-start(f32[20,2048]{1,0:T(8,128)S(1)} %get-tuple-element.48), channel_id=1, source_target_pairs={{0,15},{1,2},{2,1},{3,4},{4,3},{5,6},{6,5},{7,8},{8,7},{9,10},{10,... | collective-permute-start | bytes 491528 | tf_op jit(solution)/shard_map/ppermute | solution.py:116
  25.8 15.9 %collective-permute-start.4 = (f32[5,4,2048]{2,1,0:T(4,128)S(1)}, f32[5,4,2048]{2,1,0:T(4,128)S(1)}, u32[]{:S(2)}, u32[]{:S(2)}) collective-permute-start(f32[5,4,2048]{2,1,0:T(4,128)S(1)} %get-tuple-element.45), channel_id=1, source_target_pairs={{0,16},{16,0},{32,48},{48,32},{64,80},{80,64},{96,112},{112,96},{1... | collective-permute-start | bytes 491528 | tf_op jit(solution)/shard_map/ppermute | solution.py:113
  25.8 15.9 %collective-permute-start.5 = (f32[5,4,2048]{2,1,0:T(4,128)S(1)}, f32[5,4,2048]{2,1,0:T(4,128)S(1)}, u32[]{:S(2)}, u32[]{:S(2)}) collective-permute-start(f32[5,4,2048]{2,1,0:T(4,128)S(1)} %get-tuple-element.46), channel_id=1, source_target_pairs={{0,112},{16,32},{32,16},{48,64},{64,48},{80,96},{96,80},{112,0},{1... | collective-permute-start | bytes 491528 | tf_op jit(solution)/shard_map/ppermute | solution.py:114
  43.6 8.9 %collective-permute-start.10 = (f32[20,2048]{1,0:T(8,128)S(1)}, f32[20,2048]{1,0:T(8,128)S(1)}, u32[]{:S(2)}, u32[]{:S(2)}) collective-permute-start(f32[20,2048]{1,0:T(8,128)S(1)} %get-tuple-element.52), channel_id=1, source_target_pairs={{0,1},{1,0},{2,3},{3,2},{4,5},{5,4},{6,7},{7,6},{8,9},{9,8},{10,11... | collective-permute-start | bytes 491528 | tf_op jit(solution)/shard_map/ppermute | solution.py:115
  43.7 13.3 %collective-permute-start.11 = (f32[20,2048]{1,0:T(8,128)S(1)}, f32[20,2048]{1,0:T(8,128)S(1)}, u32[]{:S(2)}, u32[]{:S(2)}) collective-permute-start(f32[20,2048]{1,0:T(8,128)S(1)} %get-tuple-element.53), channel_id=1, source_target_pairs={{0,15},{1,2},{2,1},{3,4},{4,3},{5,6},{6,5},{7,8},{8,7},{9,10},{10,... | collective-permute-start | bytes 491528 | tf_op jit(solution)/shard_map/ppermute | solution.py:116
  46.1 13.0 %collective-permute-start.8 = (f32[5,4,2048]{2,1,0:T(4,128)S(1)}, f32[5,4,2048]{2,1,0:T(4,128)S(1)}, u32[]{:S(2)}, u32[]{:S(2)}) collective-permute-start(f32[5,4,2048]{2,1,0:T(4,128)S(1)} %get-tuple-element.50), channel_id=1, source_target_pairs={{0,16},{16,0},{32,48},{48,32},{64,80},{80,64},{96,112},{112,96},{1... | collective-permute-start | bytes 491528 | tf_op jit(solution)/shard_map/ppermute | solution.py:113
  46.9 12.2 %collective-permute-start.9 = (f32[5,4,2048]{2,1,0:T(4,128)S(1)}, f32[5,4,2048]{2,1,0:T(4,128)S(1)}, u32[]{:S(2)}, u32[]{:S(2)}) collective-permute-start(f32[5,4,2048]{2,1,0:T(4,128)S(1)} %get-tuple-element.51), channel_id=1, source_target_pairs={{0,112},{16,32},{32,16},{48,64},{64,48},{80,96},{96,80},{112,0},{1... | collective-permute-start | bytes 491528 | tf_op jit(solution)/shard_map/ppermute | solution.py:114
  59.1 9.2 %copy-start.17 = (bf16[5,3,3,3,32]{4,3,2,1,0:T(4,128)(2,1)S(1)}, bf16[5,3,3,3,32]{4,3,2,1,0:T(4,128)(2,1)}, u32[]{:S(2)}) copy-start(bf16[5,3,3,3,32]{4,3,2,1,0:T(4,128)(2,1)} %convert_bitcast_fusion) | copy-start | bytes 25924
  61.9 7.1 %copy-start.5 = (f32[32,32,3,3,3]{1,0,4,3,2:T(8,128)S(1)}, f32[32,32,3,3,3]{1,0,4,3,2:T(8,128)}, u32[]{:S(2)}) copy-start(f32[32,32,3,3,3]{1,0,4,3,2:T(8,128)} %param.18) | copy-start | bytes 331780
  61.9 18.1 %all-to-all-start = ((f32[16,2,40,128]{3,2,1,0:T(8,128)}), f32[16,2,40,128]{3,2,1,0:T(8,128)S(1)}, u32[]{:S(2)}, u32[]{:S(2)}) async-start(f32[16,2,40,128]{3,2,1,0:T(8,128)} %get-tuple-element.55), calls=%async_computation | async-start | bytes 1310720 | tf_op jit(solution)/shard_map/all_to_all | solution.py:426
  67.7 1.8 %copy-start.19 = (f32[32]{0:T(128)S(1)}, f32[32]{0:T(128)}, u32[]{:S(2)}) copy-start(f32[32]{0:T(128)} %param.17) | copy-start | bytes 388
  67.7 1.9 %copy-start.20 = (f32[32]{0:T(128)S(1)}, f32[32]{0:T(128)}, u32[]{:S(2)}) copy-start(f32[32]{0:T(128)} %param.19) | copy-start | bytes 388
  67.8 2.0 %copy-start.21 = (f32[5]{0:T(128)S(1)}, f32[5]{0:T(128)}, u32[]{:S(2)}) copy-start(f32[5]{0:T(128)} %param.21) | copy-start | bytes 64
  67.8 3.0 %copy-start.6 = (s32[1,1,2]{2,1,0:T(1,128)S(1)}, s32[1,1,2]{2,1,0:T(1,128)}, u32[]{:S(2)}) copy-start(s32[1,1,2]{2,1,0:T(1,128)} %param.14) | copy-start | bytes 28
  74.1 1.3 copy-start.7
  75.4 1.0 copy-start.9
  76.4 1.0 copy-start.11
  77.4 0.8 copy-start.13
  78.2 0.7 copy-start.15
  80.1 1.5 %copy-start.8 = (bf16[2,384,1280]{2,1,0:T(8,128)(2,1)S(1)}, bf16[2,384,1280]{2,1,0:T(8,128)(2,1)}, u32[]{:S(2)}) copy-start(bf16[2,384,1280]{2,1,0:T(8,128)(2,1)} %copy-done.7) | copy-start | bytes 5898244
  81.6 1.2 copy-start.10
  82.8 1.2 copy-start.12
  84.1 1.0 copy-start.14
  85.1 0.9 copy-start.16
  90.7 3.7 %collective-permute-start.12 = (f32[288,128]{1,0:T(8,128)S(1)}, f32[288,128]{1,0:T(8,128)S(1)}, u32[]{:S(2)}, u32[]{:S(2)}) collective-permute-start(f32[288,128]{1,0:T(8,128)S(1)} %shard_map.177), channel_id=1, source_target_pairs={{0,1},{2,3},{4,5},{6,7},{8,9},{10,11},{12,13},{14,15},{16,17},{18,... | collective-permute-start | bytes 442376 | tf_op jit(solution)/shard_map/ppermute | solution.py:358
  94.4 5.9 %collective-permute-start.13 = (f32[288,128]{1,0:T(8,128)S(1)}, f32[288,128]{1,0:T(8,128)S(1)}, u32[]{:S(2)}, u32[]{:S(2)}) collective-permute-start(f32[288,128]{1,0:T(8,128)S(1)} %add.43), channel_id=1, source_target_pairs={{1,17},{3,19},{5,21},{7,23},{9,25},{11,27},{13,29},{15,31},{17,1},... | collective-permute-start | bytes 442376 | tf_op jit(solution)/shard_map/ppermute | solution.py:360
  100.3 7.1 %collective-permute-start.14 = (f32[288,128]{1,0:T(8,128)S(1)}, f32[288,128]{1,0:T(8,128)S(1)}, u32[]{:S(2)}, u32[]{:S(2)}) collective-permute-start(f32[288,128]{1,0:T(8,128)S(1)} %add.44), channel_id=1, source_target_pairs={{1,19},{3,17},{5,23},{7,21},{9,27},{11,25},{13,31},{15,29},{17,3},... | collective-permute-start | bytes 442376 | tf_op jit(solution)/shard_map/ppermute | solution.py:360
  107.5 5.9 %collective-permute-start.15 = (f32[288,128]{1,0:T(8,128)S(1)}, f32[288,128]{1,0:T(8,128)S(1)}, u32[]{:S(2)}, u32[]{:S(2)}) collective-permute-start(f32[288,128]{1,0:T(8,128)S(1)} %add.45), channel_id=1, source_target_pairs={{1,5},{3,7},{5,1},{7,3},{9,13},{11,15},{13,9},{15,11},{17,21},{19,... | collective-permute-start | bytes 442376 | tf_op jit(solution)/shard_map/ppermute | solution.py:360
  113.4 7.1 %collective-permute-start.16 = (f32[288,128]{1,0:T(8,128)S(1)}, f32[288,128]{1,0:T(8,128)S(1)}, u32[]{:S(2)}, u32[]{:S(2)}) collective-permute-start(f32[288,128]{1,0:T(8,128)S(1)} %add.46), channel_id=1, source_target_pairs={{1,13},{3,15},{5,9},{7,11},{9,5},{11,7},{13,1},{15,3},{17,29},{19,... | collective-permute-start | bytes 442376 | tf_op jit(solution)/shard_map/ppermute | solution.py:360
  120.5 5.9 %collective-permute-start.17 = (f32[288,128]{1,0:T(8,128)S(1)}, f32[288,128]{1,0:T(8,128)S(1)}, u32[]{:S(2)}, u32[]{:S(2)}) collective-permute-start(f32[288,128]{1,0:T(8,128)S(1)} %add.47), channel_id=1, source_target_pairs={{1,33},{3,35},{5,37},{7,39},{9,41},{11,43},{13,45},{15,47},{17,49}... | collective-permute-start | bytes 442376 | tf_op jit(solution)/shard_map/ppermute | solution.py:360
  126.4 7.1 %collective-permute-start.18 = (f32[288,128]{1,0:T(8,128)S(1)}, f32[288,128]{1,0:T(8,128)S(1)}, u32[]{:S(2)}, u32[]{:S(2)}) collective-permute-start(f32[288,128]{1,0:T(8,128)S(1)} %add.48), channel_id=1, source_target_pairs={{1,97},{3,99},{5,101},{7,103},{9,105},{11,107},{13,109},{15,111},{... | collective-permute-start | bytes 442376 | tf_op jit(solution)/shard_map/ppermute | solution.py:360
  133.5 2.3 %collective-permute-start.19 = (f32[288,128]{1,0:T(8,128)S(1)}, f32[288,128]{1,0:T(8,128)S(1)}, u32[]{:S(2)}, u32[]{:S(2)}) collective-permute-start(f32[288,128]{1,0:T(8,128)S(1)} %add.49.mine_ref), channel_id=1, source_target_pairs={{1,0},{3,2},{5,4},{7,6},{9,8},{11,10},{13,12},{15,14},{17,16},{19,... | collective-permute-start | bytes 442376 | tf_op jit(solution)/shard_map/ppermute | solution.py:361

commit v3 on v2

--- a/solution.py
+++ b/solution.py
@@ -12,21 +12,24 @@
 PY = 8
 Z = 128
 ROWS = 24
+HALF = 144
 TAPS = 9
+TALL = 224
 CELLS = 20480.0
 BF = jnp.bfloat16
 F32 = jnp.float32
 VMEM = pl.BlockSpec(memory_space=pltpu.VMEM)
 SMEM = pl.BlockSpec(memory_space=pltpu.SMEM)
+HBM = pl.BlockSpec(memory_space=pltpu.HBM)
 MIB = 1024 * 1024
 
 
-def call(kernel, outs, scratch=(), flops=0, nbytes=0, ins=(), mib=12):
+def call(kernel, outs, scratch=(), flops=0, nbytes=0, ins=(), mib=12, out_space=None):
     return pl.pallas_call(
         kernel,
         out_shape=[jax.ShapeDtypeStruct(s, d) for s, d in outs],
         in_specs=list(ins),
-        out_specs=[VMEM] * len(outs),
+        out_specs=[out_space or VMEM] * len(outs),
         scratch_shapes=list(scratch),
         compiler_params=pltpu.CompilerParams(vmem_limit_bytes=mib * MIB),
         cost_estimate=pl.CostEstimate(flops=flops, bytes_accessed=nbytes, transcendentals=0),
@@ -62,36 +65,51 @@
     pack_slabs(lambda row: u_ref[row], slabs_ref)
 
 
-def step_kernel(last, place, u_ref, rxa, rxb, rya, ryb, vel_ref, dif_ref, new_ref, *outs):
-    gx, gy = place[0], place[1]
-    odd_x, odd_y = gx % 2 == 1, gy % 2 == 1
+def inner_kernel(u_ref, vel_ref, dif_ref, part_ref):
     lane = lax.broadcasted_iota(jnp.int32, (4, 2048), 1)
     not_first, not_last = lane > 0, lane < 2047
+    zero_row = jnp.zeros((1, 2048), F32)
     for x in range(X):
         v0, v1, v2, dif = vel_ref[x], vel_ref[X + x], vel_ref[2 * X + x], dif_ref[x]
         for f in range(F):
             row = f * X + x
             middle = u_ref[row]
-            if x < X - 1:
-                x_plus = u_ref[row + 1]
-            else:
-                x_plus = jnp.where(odd_x, rxb[f], rxa[f])
-                x_plus = jnp.where(gx == 7, 0.0, x_plus)
-            if x > 0:
-                x_minus = u_ref[row - 1]
-            else:
-                x_minus = jnp.where(odd_x, rxa[f], rxb[f])
-                x_minus = jnp.where(gx == 0, 0.0, x_minus)
-            a, b = rya[pl.ds(row, 1), :], ryb[pl.ds(row, 1), :]
-            above = jnp.where(gy == 15, 0.0, jnp.where(odd_y, b, a))
-            below = jnp.where(gy == 0, 0.0, jnp.where(odd_y, a, b))
-            y_plus = jnp.concatenate([middle[1:4], above], axis=0)
-            y_minus = jnp.concatenate([below, middle[0:3]], axis=0)
+            x_plus = u_ref[row + 1] if x < X - 1 else 0.0
+            x_minus = u_ref[row - 1] if x > 0 else 0.0
+            y_plus = jnp.concatenate([middle[1:4], zero_row], axis=0)
+            y_minus = jnp.concatenate([zero_row, middle[0:3]], axis=0)
             z_plus = jnp.where(not_last, pltpu.roll(middle, 2047, 1), 0.0)
             z_minus = jnp.where(not_first, pltpu.roll(middle, 1, 1), 0.0)
             carried = v0 * (x_plus - x_minus) + v1 * (y_plus - y_minus) + v2 * (z_plus - z_minus)
             spread = x_plus + x_minus + y_plus + y_minus + z_plus + z_minus - 6.0 * middle
-            new_ref[row] = middle - 0.5 * carried + dif * spread
+            part_ref[row] = middle - 0.5 * carried + dif * spread
+
+
+def outer_kernel(last, place, part_ref, rxa, rxb, rya, ryb, vel_ref, dif_ref, new_ref, *outs):
+    gx, gy = place[0], place[1]
+    odd_x, odd_y = gx % 2 == 1, gy % 2 == 1
+    y_at = lax.broadcasted_iota(jnp.int32, (4, 2048), 0)
+    up_on = (y_at == 3) & (gy != 15)
+    down_on = (y_at == 0) & (gy != 0)
+    for x in range(X):
+        v0, v1, dif = vel_ref[x], vel_ref[X + x], dif_ref[x]
+        up = jnp.where(up_on, dif - 0.5 * v1, 0.0)
+        down = jnp.where(down_on, dif + 0.5 * v1, 0.0)
+        side = None
+        if x == X - 1:
+            side = jnp.where(gx == 7, 0.0, dif - 0.5 * v0)
+        if x == 0:
+            side = jnp.where(gx == 0, 0.0, dif + 0.5 * v0)
+        from_a = jnp.where(odd_y, down, up)
+        from_b = jnp.where(odd_y, up, down)
+        for f in range(F):
+            row = f * X + x
+            new = part_ref[row] + rya[pl.ds(row, 1), :] * from_a + ryb[pl.ds(row, 1), :] * from_b
+            if x == X - 1:
+                new = new + jnp.where(odd_x, rxb[f], rxa[f]) * side
+            if x == 0:
+                new = new + jnp.where(odd_x, rxa[f], rxb[f]) * side
+            new_ref[row] = new
     get = lambda row: new_ref[row]
     if last:
         pack_slabs(get, outs[0])
@@ -144,6 +162,7 @@
             at = k + sign * (dy - 1)
             for dz in range(3):
                 parts.append(shifted[at][dz] if 0 <= at < PY else zero)
+        parts.append(jnp.zeros((TALL - TAPS * rows, Z), F32))
         out_ref[:, k * Z : (k + 1) * Z] = jnp.concatenate(parts, axis=0).astype(BF)
 
 
@@ -188,25 +207,53 @@
             bwd_ref[dy, :, dz * 128 : (dz + 1) * 128] = block.T.astype(BF)
 
 
+KEPT = [
+    ((2, ROWS, PY * Z), F32),
+    ((2, TALL, PY * Z), BF),
+    ((2, 384, (PY + 2) * Z), BF),
+    ((2, 128, PY * Z), F32),
+    ((2, 128, PY * Z), BF),
+    ((2, 128, PY * Z), F32),
+    ((2, ROWS, PY * Z), F32),
+]
+SAVED = len(KEPT)
+HELD = [pltpu.VMEM(s, d) for s, d in KEPT] + [pltpu.SemaphoreType.DMA((SAVED, 2))]
+
+
 def forward_kernel(
     anchors, slabs_ref, w1_ref, w2_ref, w3_ref, b1_ref, b2_ref, b3_ref,
-    first_ref, taps_ref, a1_ref, d1_ref, a2_ref, d2_ref, pred_ref,
+    *refs,
 ):
+    kept, held, sems = refs[:SAVED], refs[SAVED : 2 * SAVED], refs[2 * SAVED]
+    first_ref, taps_ref, a1_ref, d1_ref, a2_ref, d2_ref, pred_ref = held
+    copies = []
+
+    def keep(n, p):
+        copy = pltpu.make_async_copy(held[n].at[p], kept[n].at[p], sems.at[n, p])
+        copy.start()
+        copies.append(copy)
+
     for p in range(2):
         patch_rows(slabs_ref, anchors[p], first_ref.at[p])
         fill_taps(first_ref.at[p], taps_ref.at[p], 1)
+        keep(0, p)
+        keep(1, p)
         y1 = dot(w1_ref[...], taps_ref[p])
         act, slope = activate(y1 + b1_ref[...])
         d1_ref[p] = slope
         clear_ends(a1_ref.at[p])
         for k in range(PY):
             fill_z(act[:, k * Z : (k + 1) * Z], k, a1_ref.at[p], 1)
+        keep(2, p)
+        keep(3, p)
         y2 = b2_ref[...] + dot(w2_ref[0], a1_ref[p, :, 0 : PY * Z])
         for dy in range(1, 3):
             y2 = y2 + dot(w2_ref[dy], a1_ref[p, :, dy * Z : (dy + PY) * Z])
         act, slope = activate(y2)
         d2_ref[p] = slope
         a2_ref[p] = act.astype(BF)
+        keep(4, p)
+        keep(5, p)
         terms = dot(w3_ref[...], a2_ref[p])
         lane = lax.broadcasted_iota(jnp.int32, (ROWS, Z), 1)
         for k in range(PY):
@@ -221,6 +268,9 @@
                         part = term if part is None else part + term
                 out = out + z_shifted(part, dz - 1, lane)
             pred_ref[p, :, k * Z : (k + 1) * Z] = out
+        keep(6, p)
+    for copy in copies:
+        copy.wait()
 
 
 def band_sum(full):
@@ -228,7 +278,7 @@
     total = None
     for x in range(X):
         block = full[x * C : (x + 1) * C]
-        block = jnp.concatenate([block, jnp.zeros((C, 256 - TAPS * ROWS), F32)], axis=1)
+        block = jnp.concatenate([block, jnp.zeros((C, 256 - TALL), F32)], axis=1)
         moved = pltpu.roll(block, (1 - x) % 256, 1)
         e = lane % 4
         ok = (e < 3) & (x + e - 1 >= 0) & (x + e - 1 < X) & (lane < TAPS * ROWS)
@@ -243,21 +293,30 @@
 
 
 def backward_kernel(
-    anchors, count, slabs_ref, first_ref, taps_ref, a1_ref, d1_ref, a2_ref, d2_ref, pred_ref, w2_ref, w3_ref,
-    grads_ref,
-    last_ref, err_ref, g_ref, b_ref,
+    place, anchors, count, slabs_ref, w2_ref, w3_ref, *refs,
 ):
+    kept, (keep_ref, send_ref) = refs[:SAVED], refs[SAVED : SAVED + 2]
+    held, sems = refs[SAVED + 2 : 2 * SAVED + 2], refs[2 * SAVED + 2]
+    last_ref, err_ref, g_ref, b_ref, grads_ref = refs[2 * SAVED + 3 :]
+    first_ref, taps_ref, a1_ref, d1_ref, a2_ref, d2_ref, pred_ref = held
+    copies = {}
+    for p in range(2):
+        for n in (6, 0, 4, 5, 2, 3, 1):
+            copies[n, p] = pltpu.make_async_copy(kept[n].at[p], held[n].at[p], sems.at[n, p])
+            copies[n, p].start()
     db1 = jnp.zeros((128, 1), F32)
     db2 = jnp.zeros((128, 1), F32)
     db3 = jnp.zeros((ROWS, 1), F32)
     loss = jnp.zeros((ROWS, 1), F32)
-    dw1 = jnp.zeros((128, TAPS * ROWS), F32)
-    dw3 = jnp.zeros((128, TAPS * ROWS), F32)
+    dw1 = jnp.zeros((128, TALL), F32)
+    dw3 = jnp.zeros((128, TALL), F32)
     dw2 = [jnp.zeros((128, 384), F32) for _ in range(3)]
     clear_ends(b_ref)
     for p in range(2):
         live = jnp.where(p < count[0], 1.0, 0.0).astype(F32)
         patch_rows(slabs_ref, anchors[p], last_ref)
+        copies[6, p].wait()
+        copies[0, p].wait()
         err = pred_ref[p] - (last_ref[...] - first_ref[p])
         loss = loss + live * jnp.sum(err * err, axis=1, keepdims=True)
         err = err * (live * (2.0 / CELLS))
@@ -265,19 +324,24 @@
         db3 = db3 + jnp.sum(err, axis=1, keepdims=True)
         fill_taps(err_ref, g_ref, -1)
         da2 = dot(w3_ref[...], g_ref[...])
+        copies[4, p].wait()
         dw3 = dw3 + dot_t(a2_ref[p], g_ref[...])
+        copies[5, p].wait()
         dy2 = da2 * d2_ref[p]
         db2 = db2 + jnp.sum(dy2, axis=1, keepdims=True)
         for k in range(PY):
             fill_z(dy2[:, k * Z : (k + 1) * Z], k, b_ref, -1)
         middle = b_ref[128:256, Z : (PY + 1) * Z]
         da1 = None
+        copies[2, p].wait()
         for dy in range(3):
             dw2[dy] = dw2[dy] + dot_t(middle, a1_ref[p, :, dy * Z : (dy + PY) * Z])
             term = dot(w2_ref[dy], b_ref[:, (2 - dy) * Z : (2 - dy + PY) * Z])
             da1 = term if da1 is None else da1 + term
+        copies[3, p].wait()
         dy1 = da1 * d1_ref[p]
         db1 = db1 + jnp.sum(dy1, axis=1, keepdims=True)
+        copies[1, p].wait()
         dw1 = dw1 + dot_t(dy1.astype(BF), taps_ref[p])
 
     lane = lax.broadcasted_iota(jnp.int32, (C, 128), 1)
@@ -306,11 +370,20 @@
             if b is not None:
                 total = jnp.where(lane == 127, b, total)
         grads_ref[t * C : (t + 1) * C] = total
-
-
-def finish_kernel(place, mine_ref, other_ref, g1_ref, gb1_ref, g2_ref, gb2_ref, g3_ref, gb3_ref, loss_ref):
-    first = place[1] % 2 == 0
-    rows = lambda t: jnp.where(first, other_ref[t * C : (t + 1) * C], mine_ref[t * C : (t + 1) * C])
+    second = place[1] % 2 == 1
+    low, high = grads_ref[0:HALF], grads_ref[HALF:]
+    keep_ref[...] = jnp.where(second, high, low)
+    send_ref[...] = jnp.where(second, low, high)
+
+
+def finish_kernel(
+    place, mine_ref, other_ref, g1_ref, gb1_ref, g2_ref, gb2_ref, g3_ref, gb3_ref, loss_ref, grads_ref
+):
+    second = place[1] % 2 == 1
+    mine, other = mine_ref[...], other_ref[...]
+    grads_ref[0:HALF] = jnp.where(second, other, mine)
+    grads_ref[HALF:] = jnp.where(second, mine, other)
+    rows = lambda t: grads_ref[t * C : (t + 1) * C]
     total = rows(2)[0:1, 126:127]
     for t in range(TAPS):
         dy, dz = t // 3, t % 3
@@ -344,21 +417,22 @@
     for n in range(6):
         pairs = []
         for gx in range(8):
-            for gy in range(1, 16, 2):
+            for gy in range(16):
                 at = {"x": gx // 2, "y": gy // 4, "z": (gy // 2 % 2) * 2 + gx % 2}
                 axis = "zyx"[n // 2]
                 at[axis] = (near, far)[n % 2](at[axis])
-                to = (at["x"] * 2 + at["z"] % 2) * 16 + at["y"] * 4 + (at["z"] // 2) * 2 + 1
+                to = (at["x"] * 2 + at["z"] % 2) * 16 + at["y"] * 4 + (at["z"] // 2) * 2 + gy % 2
                 pairs.append((gx * 16 + gy, to))
         steps.append(pairs)
     return steps
 
 
-def sum_all(mine):
-    mine = mine + lax.ppermute(mine, "gy", [(i, i + 1) for i in range(0, 16, 2)])
+def sum_all(keep, send):
+    cores = [(i, i ^ 1) for i in range(16)]
+    mine = keep + lax.ppermute(send, "gy", cores)
     for pairs in reduce_steps():
         mine = mine + lax.ppermute(mine, ("gx", "gy"), pairs)
-    return mine, lax.ppermute(mine, "gy", [(i + 1, i) for i in range(0, 16, 2)])
+    return mine, lax.ppermute(mine, "gy", cores)
 
 
 def banded(w, flip):
@@ -372,7 +446,8 @@
         bands.append(padded[:, 1 : X + 1])
     all_x = jnp.stack(bands, axis=4)
     rows = jnp.transpose(all_x, (2, 3, 0, 1, 4, 5)).reshape(TAPS, F * X, X * C)
-    return jnp.pad(rows, ((0, 0), (0, ROWS - F * X), (0, 0))).reshape(TAPS * ROWS, X * C).astype(BF)
+    rows = jnp.pad(rows, ((0, 0), (0, ROWS - F * X), (0, 0))).reshape(TAPS * ROWS, X * C)
+    return jnp.pad(rows, ((0, TALL - TAPS * ROWS), (0, 0))).astype(BF)
 
 
 def on_device(
@@ -401,51 +476,48 @@
         last = step == STEPS - 1
         outs = [((F * X, 4, 2048), F32)] + ([SLABS] if last else EDGES)
         received = exchange(edges)
-        kernel = lambda *refs, last=last: step_kernel(last, *refs)
-        u, *edges = call(kernel, outs, ins=[SMEM] + [VMEM] * 7, nbytes=4_000_000)(
-            place, u, *received, vel, diffusivity
+        (part,) = call(inner_kernel, [((F * X, 4, 2048), F32)], ins=[VMEM] * 3, nbytes=4_000_000)(u, vel, diffusivity)
+        kernel = lambda *refs, last=last: outer_kernel(last, *refs)
+        u, *edges = call(kernel, outs, ins=[SMEM] + [VMEM] * 7, nbytes=3_000_000)(
+            place, part, *received, vel, diffusivity
         )
 
     learned = call(
         forward_kernel,
-        [
-            ((2, ROWS, PY * Z), F32),
-            ((2, TAPS * ROWS, PY * Z), BF),
-            ((2, 384, (PY + 2) * Z), BF),
-            ((2, 128, PY * Z), F32),
-            ((2, 128, PY * Z), BF),
-            ((2, 128, PY * Z), F32),
-            ((2, ROWS, PY * Z), F32),
-        ],
+        KEPT,
+        scratch=HELD,
         ins=[SMEM] + [VMEM] * 7,
         flops=2_000_000_000,
         nbytes=8_000_000,
         mib=24,
+        out_space=HBM,
     )(anchors, first_slabs, w1_band.T, w2_fwd, w3_band, b1, b2, b3)
 
     last_slabs = lax.all_to_all(edges[0], "gy", 0, 0, tiled=True).reshape(32, 2 * F * X, Z)
-    (grads,) = call(
+    keep, send = call(
         backward_kernel,
-        [((TAPS * C, 128), F32)],
-        scratch=[
+        [((HALF, 128), F32)] * 2,
+        scratch=HELD
+        + [
             pltpu.VMEM((ROWS, PY * Z), F32),
             pltpu.VMEM((ROWS, PY * Z), F32),
-            pltpu.VMEM((TAPS * ROWS, PY * Z), BF),
+            pltpu.VMEM((TALL, PY * Z), BF),
             pltpu.VMEM((384, (PY + 2) * Z), BF),
+            pltpu.VMEM((2 * HALF, 128), F32),
         ],
-        ins=[SMEM] * 2 + [VMEM] * 10,
+        ins=[SMEM] * 3 + [VMEM] * 3 + [HBM] * SAVED,
         flops=4_000_000_000,
         nbytes=10_000_000,
         mib=24,
-    )(anchors, count, last_slabs, *learned, w2_bwd, w3_band.T)
-
-    mine, other = sum_all(grads)
+    )(place, anchors, count, last_slabs, w2_bwd, w3_band.T, *learned)
+
     g1, gb1, g2, gb2, g3, gb3, loss = call(
         finish_kernel,
         [((45, 3, C), F32), ((1, C), F32), ((27, C, C), F32), ((1, C), F32), ((45, 3, C), F32), ((1, F), F32), ((1, 1), F32)],
+        scratch=[pltpu.VMEM((2 * HALF, 128), F32)],
         ins=[SMEM, VMEM, VMEM],
         nbytes=1_000_000,
-    )(place, mine, other)
+    )(place, *sum_all(keep, send))
     g1 = jnp.transpose(g1.reshape(F, 3, 3, 3, C), (4, 0, 1, 2, 3))
     g2 = jnp.transpose(g2.reshape(3, 3, 3, C, C), (3, 4, 0, 1, 2))
     g3 = jnp.transpose(g3.reshape(F, 3, 3, 3, C), (0, 4, 1, 2, 3))

time: 138 us -> 129 us (0.935)
  waiting for transfers between devices: 49.8 us -> 36.2 us
  Pallas kernels: 18.7 us -> 27.8 us
  local copies, waits for them, and re-layouts: 16.7 us -> 12.6 us
    ppermute x6, waiting for transfers between devices: 25.1 us -> 15.9 us  [sum_all(): mine = mine + lax.ppermute(mine, ('gx', 'gy'), pairs)]
    pallas_call x5 -> x8, Pallas kernels: 14.5 us -> 23.6 us  [the longest x1 8.86 us: on_device(): call(backward_kernel, [((HALF, 128), F32)] * 2, scratch=HELD + [pltpu.VME...]
    ppermute x6, starting transfers between devices: 13.8 us -> 7.46 us  [sum_all(): mine = mine + lax.ppermute(mine, ('gx', 'gy'), pairs)]
    ppermute x2, starting transfers between devices: 2.59 us -> 8.74 us  [the longest x1 7.33 us: sum_all(): return (mine, lax.ppermute(mine, 'gy', cores))]
    ppermute x3, waiting for transfers between devices: 17.8 us -> 14.7 us  [exchange(): lax.ppermute(yb, 'gy', pairs(16, True))]
    unnamed x44 -> x45, local copies, waits for them, and re-layouts: 12.9 us -> 10.6 us
    ppermute x2, waiting for transfers between devices: 3.36 us -> 1.83 us  [the longest x1 0.91 us: sum_all(): mine = keep + lax.ppermute(send, 'gy', cores)]
    rev x1, local copies, waits for them, and re-layouts: 1.53 us -> 0.02 us  [banded(): w_ = w[:, ::-1]]
  transfers between devices with their start and end apart: 22 -> 22, of which waited for: 13 -> 13; matrix products, arithmetic and copies ran while one was open for 4% -> 2% of each run, Pallas kernels for 8% -> 13%
where the time goes in v3:
time: 129 us
  starting transfers between devices  49.7 us (39%)
  waiting for transfers between devices  36.2 us (28%)
  Pallas kernels  27.8 us (22%)
  local copies, waits for them, and re-layouts  12.6 us (10%)
  between operations  1.74 us (1%)
    ppermute x6, waiting for transfers between devices, sum_all(): mine = mine + lax.ppermute(mine, ('gx', 'gy'), pairs)  15.9 us
    ppermute x3, waiting for transfers between devices, exchange(): lax.ppermute(yb, 'gy', pairs(16, True))  14.7 us
    unnamed x45, local copies, waits for them, and re-layouts  10.6 us
    ppermute x3, starting transfers between devices, exchange(): lax.ppermute(yb, 'gy', pairs(16, True))  9.54 us
    pallas_call x1, Pallas kernels, on_device(): call(backward_kernel, [((HALF, 128), F32)] * 2, scratch=HELD + [pltpu.VME...  8.86 us
    ppermute x3, starting transfers between devices, exchange(): lax.ppermute(xb, 'gx', pairs(8, True))  8.29 us
    ppermute x6, starting transfers between devices, sum_all(): mine = mine + lax.ppermute(mine, ('gx', 'gy'), pairs)  7.46 us
    ppermute x1, starting transfers between devices, sum_all(): return (mine, lax.ppermute(mine, 'gy', cores))  7.33 us
  transfers between devices with their start and end apart: 22, of which 13 were waited for; matrix products, arithmetic and copies ran while one was open for 2% of the time, Pallas kernels for 13%

profile of v3, /device:TPU:1, one launch (start us, length us, event | category | flops | bytes accessed | tf_op | source)
XLA Modules:
  0.0 128.7 jit_solution(15756861657994924646)
XLA Ops:
  0.7 1.1 copy-done.1
  1.8 0.8 shard_map.171
  2.6 1.5 %collective-permute-start.2 = (f32[20,2048]{1,0:T(8,128)S(1)}, f32[20,2048]{1,0:T(8,128)S(1)}, u32[]{:S(2)}, u32[]{:S(2)}) collective-permute-start(f32[20,2048]{1,0:T(8,128)S(1)} %get-tuple-element.44), channel_id=1, source_target_pairs={{0,1},{1,0},{2,3},{3,2},{4,5},{5,4},{6,7},{7,6},{8,9},{9,8},{10,11... | collective-permute-start | bytes 491528 | tf_op jit(solution)/shard_map/ppermute | solution.py:133
  4.1 3.7 %collective-permute-start.3 = (f32[20,2048]{1,0:T(8,128)S(1)}, f32[20,2048]{1,0:T(8,128)S(1)}, u32[]{:S(2)}, u32[]{:S(2)}) collective-permute-start(f32[20,2048]{1,0:T(8,128)S(1)} %get-tuple-element.45), channel_id=1, source_target_pairs={{0,15},{1,2},{2,1},{3,4},{4,3},{5,6},{6,5},{7,8},{8,7},{9,10},{10,... | collective-permute-start | bytes 491528 | tf_op jit(solution)/shard_map/ppermute | solution.py:134
  7.8 0.7 collective-permute-start
  8.5 2.9 %collective-permute-start.1 = (f32[5,4,2048]{2,1,0:T(4,128)S(1)}, f32[5,4,2048]{2,1,0:T(4,128)S(1)}, u32[]{:S(2)}, u32[]{:S(2)}) collective-permute-start(f32[5,4,2048]{2,1,0:T(4,128)S(1)} %get-tuple-element.43), channel_id=1, source_target_pairs={{0,112},{16,32},{32,16},{48,64},{64,48},{80,96},{96,80},{112,0},{1... | collective-permute-start | bytes 491528 | tf_op jit(solution)/shard_map/ppermute | solution.py:132
  11.4 1.2 shard_map.178
  12.6 6.8 %all-to-all-start.1 = ((f32[16,2,40,128]{3,2,1,0:T(8,128)}), f32[16,2,40,128]{3,2,1,0:T(8,128)S(1)}, u32[]{:S(2)}, u32[]{:S(2)}) async-start(f32[16,2,40,128]{3,2,1,0:T(8,128)} %shard_map.178), calls=%async_computation.1 | async-start | bytes 1310720 | tf_op jit(solution)/shard_map/all_to_all | solution.py:465
  19.5 1.0 shard_map.170.refs_1_
  20.9 1.9 %shard_map.172 = (f32[20,4,2048]{2,1,0:T(4,128)S(1)}, f32[5,4,2048]{2,1,0:T(4,128)}, f32[5,4,2048]{2,1,0:T(4,128)}, f32[20,2048]{1,0:T(8,128)}, f32[20,2048]{1,0:T(8,128)S(1)}) custom-call(s32[2]{0:T(128)S(1)} %pad_add_fusion.place.refs_0_, f32[20,4,2048]{2,1,0:T(4,128)S(1)} %shard_map.170.refs_1_, f32[5,4,2048]{2,1,0:T(4,128)S(1)} %collective-permute-done.refs_2_, ...), custom_call_target="tpu_custom_call" | custom-call | bytes 3000000 | tf_op jit(solution)/shard_map/pallas_call | solution.py:481
  22.8 2.9 %collective-permute-start.7 = (f32[20,2048]{1,0:T(8,128)S(1)}, f32[20,2048]{1,0:T(8,128)S(1)}, u32[]{:S(2)}, u32[]{:S(2)}) collective-permute-start(f32[20,2048]{1,0:T(8,128)S(1)} %get-tuple-element.50), channel_id=1, source_target_pairs={{0,15},{1,2},{2,1},{3,4},{4,3},{5,6},{6,5},{7,8},{8,7},{9,10},{10,... | collective-permute-start | bytes 491528 | tf_op jit(solution)/shard_map/ppermute | solution.py:134
  25.7 2.6 %collective-permute-start.5 = (f32[5,4,2048]{2,1,0:T(4,128)}, f32[5,4,2048]{2,1,0:T(4,128)S(1)}, u32[]{:S(2)}, u32[]{:S(2)}) collective-permute-start(f32[5,4,2048]{2,1,0:T(4,128)} %get-tuple-element.48), channel_id=1, source_target_pairs={{0,112},{16,32},{32,16},{48,64},{64,48},{80,96},{96,80},{112,0},{1... | collective-permute-start | bytes 491528 | tf_op jit(solution)/shard_map/ppermute | solution.py:132
  28.4 1.0 shard_map.173.refs_1_
  29.4 10.7 %collective-permute-done.7.refs_5_ = f32[20,2048]{1,0:T(8,128)S(1)} collective-permute-done((f32[20,2048]{1,0:T(8,128)S(1)}, f32[20,2048]{1,0:T(8,128)S(1)}, u32[]{:S(2)}, u32[]{:S(2)}) %collective-permute-start.7) | collective-permute-done | bytes 163872 | tf_op jit(solution)/shard_map/ppermute | solution.py:134
  40.5 1.8 %shard_map.174 = (f32[20,4,2048]{2,1,0:T(4,128)S(1)}, f32[5,4,2048]{2,1,0:T(4,128)}, f32[5,4,2048]{2,1,0:T(4,128)}, f32[20,2048]{1,0:T(8,128)}, f32[20,2048]{1,0:T(8,128)S(1)}) custom-call(s32[2]{0:T(128)S(1)} %pad_add_fusion.place.refs_0_, f32[20,4,2048]{2,1,0:T(4,128)S(1)} %shard_map.173.refs_1_, f32[5,4,2048]{2,1,0:T(4,128)S(1)} %collective-permute-done.4.refs_2_, ...), custom_call_target="tpu_custom_call" | custom-call | bytes 3000000 | tf_op jit(solution)/shard_map/pallas_call | solution.py:481
  42.3 3.0 %collective-permute-start.11 = (f32[20,2048]{1,0:T(8,128)S(1)}, f32[20,2048]{1,0:T(8,128)S(1)}, u32[]{:S(2)}, u32[]{:S(2)}) collective-permute-start(f32[20,2048]{1,0:T(8,128)S(1)} %get-tuple-element.55), channel_id=1, source_target_pairs={{0,15},{1,2},{2,1},{3,4},{4,3},{5,6},{6,5},{7,8},{8,7},{9,10},{10,... | collective-permute-start | bytes 491528 | tf_op jit(solution)/shard_map/ppermute | solution.py:134
  45.7 2.8 %collective-permute-start.9 = (f32[5,4,2048]{2,1,0:T(4,128)}, f32[5,4,2048]{2,1,0:T(4,128)S(1)}, u32[]{:S(2)}, u32[]{:S(2)}) collective-permute-start(f32[5,4,2048]{2,1,0:T(4,128)} %get-tuple-element.53), channel_id=1, source_target_pairs={{0,112},{16,32},{32,16},{48,64},{64,48},{80,96},{96,80},{112,0},{1... | collective-permute-start | bytes 491528 | tf_op jit(solution)/shard_map/ppermute | solution.py:132
  49.2 0.7 fusion.4
  49.9 1.0 shard_map.175.refs_1_
  51.0 4.0 %collective-permute-done.11.refs_5_ = f32[20,2048]{1,0:T(8,128)S(1)} collective-permute-done((f32[20,2048]{1,0:T(8,128)S(1)}, f32[20,2048]{1,0:T(8,128)S(1)}, u32[]{:S(2)}, u32[]{:S(2)}) %collective-permute-start.11) | collective-permute-done | bytes 163872 | tf_op jit(solution)/shard_map/ppermute | solution.py:134
  55.0 2.9 %collective-permute-done.8.refs_2_ = f32[5,4,2048]{2,1,0:T(4,128)S(1)} collective-permute-done((f32[5,4,2048]{2,1,0:T(4,128)}, f32[5,4,2048]{2,1,0:T(4,128)S(1)}, u32[]{:S(2)}, u32[]{:S(2)}) %collective-permute-start.8) | collective-permute-done | bytes 163872 | tf_op jit(solution)/shard_map/ppermute | solution.py:131
  57.9 2.2 %shard_map.176 = (f32[20,4,2048]{2,1,0:T(4,128)}, f32[16,2,40,128]{3,2,1,0:T(8,128)}) custom-call(s32[2]{0:T(128)S(1)} %pad_add_fusion.place.refs_0_, f32[20,4,2048]{2,1,0:T(4,128)S(1)} %shard_map.175.refs_1_, f32[5,4,2048]{2,1,0:T(4,128)S(1)} %collective-permute-done.8.refs_2_, f32[5,4,2048]{2,1,0:T(4,128)S(1)} %collective-permute-done.9.refs_3_, ...), custom_call_target="tpu_custom_call" | custom-call | bytes 3000000 | tf_op jit(solution)/shard_map/pallas_call | solution.py:481
  60.1 6.2 %all-to-all-start = ((f32[16,2,40,128]{3,2,1,0:T(8,128)}), f32[16,2,40,128]{3,2,1,0:T(8,128)S(1)}, u32[]{:S(2)}, u32[]{:S(2)}) async-start(f32[16,2,40,128]{3,2,1,0:T(8,128)} %get-tuple-element.57), calls=%async_computation | async-start | bytes 1310720 | tf_op jit(solution)/shard_map/all_to_all | solution.py:496
  68.7 6.0 %shard_map.179 = (f32[2,24,1024]{2,1,0:T(8,128)S(1)}, bf16[2,224,1024]{2,1,0:T(8,128)(2,1)S(1)}, bf16[2,384,1280]{2,1,0:T(8,128)(2,1)S(1)}, f32[2,128,1024]{2,1,...) custom-call(s32[2]{0:T(128)S(1)} %bitcast.69, ...), custom_call_target="tpu_custom_call" | custom-call | flops 2000000000 | bytes 8000000 | tf_op jit(solution)/shard_map/pallas_call | solution.py:485
  74.7 1.3 %copy-done.6 = bf16[2,384,1280]{2,1,0:T(8,128)(2,1)} copy-done((bf16[2,384,1280]{2,1,0:T(8,128)(2,1)}, bf16[2,384,1280]{2,1,0:T(8,128)(2,1)S(1)}, u32[]{:S(2)}) %copy-start.6) | copy-done | bytes 1966104
  76.0 1.0 copy-done.8
  77.0 1.0 copy-done.10
  78.0 0.9 copy-done.12
  78.9 1.5 %copy-done.7 = bf16[2,384,1280]{2,1,0:T(8,128)(2,1)S(1)} copy-done((bf16[2,384,1280]{2,1,0:T(8,128)(2,1)S(1)}, bf16[2,384,1280]{2,1,0:T(8,128)(2,1)}, u32[]{:S(2)}) %copy-start.7) | copy-done | bytes 1966104
  80.4 1.2 copy-done.9
  81.7 1.2 copy-done.11
  82.9 1.2 copy-done.13
  84.1 8.9 %shard_map.180 = (f32[144,128]{1,0:T(8,128)S(1)}, f32[144,128]{1,0:T(8,128)S(1)}) custom-call(s32[2]{0:T(128)S(1)} %pad_add_fusion.place.refs_0_, s32[2]{0:T(128)S(1)} %bitcast.70, s32[1]{0:T(128)} %bitcast.56.count, f32[32,40,128]{2,1,0:T(8,128)S(1)} %bitcast.67, bf16[3,128,384]{2,1,0:T(8,128)(2,1)S(1)} %get-tuple-element.58.w2_ref, ...), custom_call_target="tpu_custom_call" | custom-call | flops 4000000000 | bytes 10000000 | tf_op jit(solution)/shard_map/pallas_call | solution.py:497
  92.9 1.4 %collective-permute-start.12 = (f32[144,128]{1,0:T(8,128)S(1)}, f32[144,128]{1,0:T(8,128)S(1)}, u32[]{:S(2)}, u32[]{:S(2)}) collective-permute-start(f32[144,128]{1,0:T(8,128)S(1)} %get-tuple-element.68), channel_id=1, source_target_pairs={{0,1},{1,0},{2,3},{3,2},{4,5},{5,4},{6,7},{7,6},{8,9},{9,8},{10,11... | collective-permute-start | bytes 221192 | tf_op jit(solution)/shard_map/ppermute | solution.py:432
  94.4 0.9 collective-permute-done.12
  95.4 3.2 %collective-permute-done.13 = f32[144,128]{1,0:T(8,128)S(1)} collective-permute-done((f32[144,128]{1,0:T(8,128)S(1)}, f32[144,128]{1,0:T(8,128)S(1)}, u32[]{:S(2)}, u32[]{:S(2)}) %collective-permute-start.13) | collective-permute-done | bytes 73760 | tf_op jit(solution)/shard_map/ppermute | solution.py:434
  98.6 1.4 %collective-permute-start.14 = (f32[144,128]{1,0:T(8,128)S(1)}, f32[144,128]{1,0:T(8,128)S(1)}, u32[]{:S(2)}, u32[]{:S(2)}) collective-permute-start(f32[144,128]{1,0:T(8,128)S(1)} %add.48), channel_id=1, source_target_pairs={{0,18},{1,19},{2,16},{3,17},{4,22},{5,23},{6,20},{7,21},{8,26},{9,... | collective-permute-start | bytes 221192 | tf_op jit(solution)/shard_map/ppermute | solution.py:434
  100.0 3.1 %collective-permute-done.14 = f32[144,128]{1,0:T(8,128)S(1)} collective-permute-done((f32[144,128]{1,0:T(8,128)S(1)}, f32[144,128]{1,0:T(8,128)S(1)}, u32[]{:S(2)}, u32[]{:S(2)}) %collective-permute-start.14) | collective-permute-done | bytes 73760 | tf_op jit(solution)/shard_map/ppermute | solution.py:434
  103.6 2.8 %collective-permute-done.15 = f32[144,128]{1,0:T(8,128)S(1)} collective-permute-done((f32[144,128]{1,0:T(8,128)S(1)}, f32[144,128]{1,0:T(8,128)S(1)}, u32[]{:S(2)}, u32[]{:S(2)}) %collective-permute-start.15) | collective-permute-done | bytes 73760 | tf_op jit(solution)/shard_map/ppermute | solution.py:434
  106.4 1.7 %collective-permute-start.16 = (f32[144,128]{1,0:T(8,128)S(1)}, f32[144,128]{1,0:T(8,128)S(1)}, u32[]{:S(2)}, u32[]{:S(2)}) collective-permute-start(f32[144,128]{1,0:T(8,128)S(1)} %add.50), channel_id=1, source_target_pairs={{0,12},{1,13},{2,14},{3,15},{4,8},{5,9},{6,10},{7,11},{8,4},{9,5},... | collective-permute-start | bytes 221192 | tf_op jit(solution)/shard_map/ppermute | solution.py:434
  108.1 2.8 %collective-permute-done.16 = f32[144,128]{1,0:T(8,128)S(1)} collective-permute-done((f32[144,128]{1,0:T(8,128)S(1)}, f32[144,128]{1,0:T(8,128)S(1)}, u32[]{:S(2)}, u32[]{:S(2)}) %collective-permute-start.16) | collective-permute-done | bytes 73760 | tf_op jit(solution)/shard_map/ppermute | solution.py:434
  110.9 1.4 %collective-permute-start.17 = (f32[144,128]{1,0:T(8,128)S(1)}, f32[144,128]{1,0:T(8,128)S(1)}, u32[]{:S(2)}, u32[]{:S(2)}) collective-permute-start(f32[144,128]{1,0:T(8,128)S(1)} %add.51), channel_id=1, source_target_pairs={{0,32},{1,33},{2,34},{3,35},{4,36},{5,37},{6,38},{7,39},{8,40},{9,... | collective-permute-start | bytes 221192 | tf_op jit(solution)/shard_map/ppermute | solution.py:434
  112.2 1.9 %collective-permute-done.17 = f32[144,128]{1,0:T(8,128)S(1)} collective-permute-done((f32[144,128]{1,0:T(8,128)S(1)}, f32[144,128]{1,0:T(8,128)S(1)}, u32[]{:S(2)}, u32[]{:S(2)}) %collective-permute-start.17) | collective-permute-done | bytes 73760 | tf_op jit(solution)/shard_map/ppermute | solution.py:434
  114.2 2.4 %collective-permute-start.18 = (f32[144,128]{1,0:T(8,128)S(1)}, f32[144,128]{1,0:T(8,128)S(1)}, u32[]{:S(2)}, u32[]{:S(2)}) collective-permute-start(f32[144,128]{1,0:T(8,128)S(1)} %add.52), channel_id=1, source_target_pairs={{0,96},{1,97},{2,98},{3,99},{4,100},{5,101},{6,102},{7,103},{8,104... | collective-permute-start | bytes 221192 | tf_op jit(solution)/shard_map/ppermute | solution.py:434
  116.6 2.1 %collective-permute-done.18 = f32[144,128]{1,0:T(8,128)S(1)} collective-permute-done((f32[144,128]{1,0:T(8,128)S(1)}, f32[144,128]{1,0:T(8,128)S(1)}, u32[]{:S(2)}, u32[]{:S(2)}) %collective-permute-start.18) | collective-permute-done | bytes 73760 | tf_op jit(solution)/shard_map/ppermute | solution.py:434
  118.7 7.3 %collective-permute-start.19 = (f32[144,128]{1,0:T(8,128)S(1)}, f32[144,128]{1,0:T(8,128)S(1)}, u32[]{:S(2)}, u32[]{:S(2)}) collective-permute-start(f32[144,128]{1,0:T(8,128)S(1)} %add.53.mine_ref), channel_id=1, source_target_pairs={{0,1},{1,0},{2,3},{3,2},{4,5},{5,4},{6,7},{7,6},{8,9},{9,8},{10,11... | collective-permute-start | bytes 221192 | tf_op jit(solution)/shard_map/ppermute | solution.py:435
  126.0 0.9 collective-permute-done.19.other_ref
  126.9 1.8 %shard_map.181 = (f32[45,3,32]{2,1,0:T(4,128)}, f32[1,32]{1,0:T(1,128)}, f32[27,32,32]{2,1,0:T(8,128)}, f32[1,32]{1,0:T(1,128)}, f32[45,3,32]{2,1,0:T(4,128)}, /*index=5*/f32[1,5]{1,0:T(1,128)}, f32[1,1]{1,0:T(1,128)}) custom-call(s32[2]{0:T(128)S(1)} %pad_add_fusion.place.refs_0_, f32[144,128]{1,0:T(8,128)S(1)} %add.53.mine_ref, ...), custom_call_target="tpu_custom_call" | custom-call | bytes 1000000 | tf_op jit(solution)/shard_map/pallas_call | solution.py:514
  (86 shorter events, 4.4 us)
Async XLA Ops:
  0.6 18.8 %copy-start = (f32[3,4,4,2048]{3,2,1,0:T(4,128)S(1)}, f32[3,4,4,2048]{3,2,1,0:T(4,128)}, u32[]{:S(2)}) copy-start(f32[3,4,4,2048]{3,2,1,0:T(4,128)} %param.12) | copy-start | bytes 1179652
  0.7 1.1 copy-start.1
  1.8 17.6 %copy-start.2 = (f32[5,4,4,2048]{3,2,1,0:T(4,128)S(1)}, f32[5,4,4,2048]{3,2,1,0:T(4,128)}, u32[]{:S(2)}) copy-start(f32[5,4,4,2048]{3,2,1,0:T(4,128)} %param.11) | copy-start | bytes 1966084
  1.8 17.6 %copy-start.3 = (f32[4,4,2048]{2,1,0:T(4,128)S(1)}, f32[4,4,2048]{2,1,0:T(4,128)}, u32[]{:S(2)}) copy-start(f32[4,4,2048]{2,1,0:T(4,128)} %refs_7_.5) | copy-start | bytes 393220
  2.6 17.9 %collective-permute-start.2 = (f32[20,2048]{1,0:T(8,128)S(1)}, f32[20,2048]{1,0:T(8,128)S(1)}, u32[]{:S(2)}, u32[]{:S(2)}) collective-permute-start(f32[20,2048]{1,0:T(8,128)S(1)} %get-tuple-element.44), channel_id=1, source_target_pairs={{0,1},{1,0},{2,3},{3,2},{4,5},{5,4},{6,7},{7,6},{8,9},{9,8},{10,11... | collective-permute-start | bytes 491528 | tf_op jit(solution)/shard_map/ppermute | solution.py:133
  4.1 16.4 %collective-permute-start.3 = (f32[20,2048]{1,0:T(8,128)S(1)}, f32[20,2048]{1,0:T(8,128)S(1)}, u32[]{:S(2)}, u32[]{:S(2)}) collective-permute-start(f32[20,2048]{1,0:T(8,128)S(1)} %get-tuple-element.45), channel_id=1, source_target_pairs={{0,15},{1,2},{2,1},{3,4},{4,3},{5,6},{6,5},{7,8},{8,7},{9,10},{10,... | collective-permute-start | bytes 491528 | tf_op jit(solution)/shard_map/ppermute | solution.py:134
  7.8 13.1 %collective-permute-start = (f32[5,4,2048]{2,1,0:T(4,128)S(1)}, f32[5,4,2048]{2,1,0:T(4,128)S(1)}, u32[]{:S(2)}, u32[]{:S(2)}) collective-permute-start(f32[5,4,2048]{2,1,0:T(4,128)S(1)} %get-tuple-element.42), channel_id=1, source_target_pairs={{0,16},{16,0},{32,48},{48,32},{64,80},{80,64},{96,112},{112,96},{1... | collective-permute-start | bytes 491528 | tf_op jit(solution)/shard_map/ppermute | solution.py:131
  8.5 12.4 %collective-permute-start.1 = (f32[5,4,2048]{2,1,0:T(4,128)S(1)}, f32[5,4,2048]{2,1,0:T(4,128)S(1)}, u32[]{:S(2)}, u32[]{:S(2)}) collective-permute-start(f32[5,4,2048]{2,1,0:T(4,128)S(1)} %get-tuple-element.43), channel_id=1, source_target_pairs={{0,112},{16,32},{32,16},{48,64},{64,48},{80,96},{96,80},{112,0},{1... | collective-permute-start | bytes 491528 | tf_op jit(solution)/shard_map/ppermute | solution.py:132
  12.6 47.5 %all-to-all-start.1 = ((f32[16,2,40,128]{3,2,1,0:T(8,128)}), f32[16,2,40,128]{3,2,1,0:T(8,128)S(1)}, u32[]{:S(2)}, u32[]{:S(2)}) async-start(f32[16,2,40,128]{3,2,1,0:T(8,128)} %shard_map.178), calls=%async_computation.1 | async-start | bytes 1310720 | tf_op jit(solution)/shard_map/all_to_all | solution.py:465
  19.4 8.8 %copy-start.17 = (f32[32,5,3,3,3]{0,4,3,2,1:T(4,128)S(1)}, f32[32,5,3,3,3]{0,4,3,2,1:T(4,128)}, u32[]{:S(2)}) copy-start(f32[32,5,3,3,3]{0,4,3,2,1:T(4,128)} %param.16) | copy-start | bytes 51844
  19.5 8.8 %copy-start.18 = (f32[5,32,3,3,3]{1,4,3,2,0:T(4,128)S(1)}, f32[5,32,3,3,3]{1,4,3,2,0:T(4,128)}, u32[]{:S(2)}) copy-start(f32[5,32,3,3,3]{1,4,3,2,0:T(4,128)} %param.20) | copy-start | bytes 51844
  22.8 6.6 %collective-permute-start.6 = (f32[20,2048]{1,0:T(8,128)}, f32[20,2048]{1,0:T(8,128)S(1)}, u32[]{:S(2)}, u32[]{:S(2)}) collective-permute-start(f32[20,2048]{1,0:T(8,128)} %get-tuple-element.49), channel_id=1, source_target_pairs={{0,1},{1,0},{2,3},{3,2},{4,5},{5,4},{6,7},{7,6},{8,9},{9,8},{10,11... | collective-permute-start | bytes 491528 | tf_op jit(solution)/shard_map/ppermute | solution.py:133
  22.8 17.3 %collective-permute-start.7 = (f32[20,2048]{1,0:T(8,128)S(1)}, f32[20,2048]{1,0:T(8,128)S(1)}, u32[]{:S(2)}, u32[]{:S(2)}) collective-permute-start(f32[20,2048]{1,0:T(8,128)S(1)} %get-tuple-element.50), channel_id=1, source_target_pairs={{0,15},{1,2},{2,1},{3,4},{4,3},{5,6},{6,5},{7,8},{8,7},{9,10},{10,... | collective-permute-start | bytes 491528 | tf_op jit(solution)/shard_map/ppermute | solution.py:134
  25.7 14.8 %collective-permute-start.4 = (f32[5,4,2048]{2,1,0:T(4,128)}, f32[5,4,2048]{2,1,0:T(4,128)S(1)}, u32[]{:S(2)}, u32[]{:S(2)}) collective-permute-start(f32[5,4,2048]{2,1,0:T(4,128)} %get-tuple-element.47), channel_id=1, source_target_pairs={{0,16},{16,0},{32,48},{48,32},{64,80},{80,64},{96,112},{112,96},{1... | collective-permute-start | bytes 491528 | tf_op jit(solution)/shard_map/ppermute | solution.py:131
  25.7 14.8 %collective-permute-start.5 = (f32[5,4,2048]{2,1,0:T(4,128)}, f32[5,4,2048]{2,1,0:T(4,128)S(1)}, u32[]{:S(2)}, u32[]{:S(2)}) collective-permute-start(f32[5,4,2048]{2,1,0:T(4,128)} %get-tuple-element.48), channel_id=1, source_target_pairs={{0,112},{16,32},{32,16},{48,64},{64,48},{80,96},{96,80},{112,0},{1... | collective-permute-start | bytes 491528 | tf_op jit(solution)/shard_map/ppermute | solution.py:132
  42.3 8.7 %collective-permute-start.10 = (f32[20,2048]{1,0:T(8,128)}, f32[20,2048]{1,0:T(8,128)S(1)}, u32[]{:S(2)}, u32[]{:S(2)}) collective-permute-start(f32[20,2048]{1,0:T(8,128)} %get-tuple-element.54), channel_id=1, source_target_pairs={{0,1},{1,0},{2,3},{3,2},{4,5},{5,4},{6,7},{7,6},{8,9},{9,8},{10,11... | collective-permute-start | bytes 491528 | tf_op jit(solution)/shard_map/ppermute | solution.py:133
  42.3 12.7 %collective-permute-start.11 = (f32[20,2048]{1,0:T(8,128)S(1)}, f32[20,2048]{1,0:T(8,128)S(1)}, u32[]{:S(2)}, u32[]{:S(2)}) collective-permute-start(f32[20,2048]{1,0:T(8,128)S(1)} %get-tuple-element.55), channel_id=1, source_target_pairs={{0,15},{1,2},{2,1},{3,4},{4,3},{5,6},{6,5},{7,8},{8,7},{9,10},{10,... | collective-permute-start | bytes 491528 | tf_op jit(solution)/shard_map/ppermute | solution.py:134
  45.3 12.6 %collective-permute-start.8 = (f32[5,4,2048]{2,1,0:T(4,128)}, f32[5,4,2048]{2,1,0:T(4,128)S(1)}, u32[]{:S(2)}, u32[]{:S(2)}) collective-permute-start(f32[5,4,2048]{2,1,0:T(4,128)} %get-tuple-element.52), channel_id=1, source_target_pairs={{0,16},{16,0},{32,48},{48,32},{64,80},{80,64},{96,112},{112,96},{1... | collective-permute-start | bytes 491528 | tf_op jit(solution)/shard_map/ppermute | solution.py:131
  45.7 12.2 %collective-permute-start.9 = (f32[5,4,2048]{2,1,0:T(4,128)}, f32[5,4,2048]{2,1,0:T(4,128)S(1)}, u32[]{:S(2)}, u32[]{:S(2)}) collective-permute-start(f32[5,4,2048]{2,1,0:T(4,128)} %get-tuple-element.53), channel_id=1, source_target_pairs={{0,112},{16,32},{32,16},{48,64},{64,48},{80,96},{96,80},{112,0},{1... | collective-permute-start | bytes 491528 | tf_op jit(solution)/shard_map/ppermute | solution.py:132
  50.9 15.4 %copy-start.14 = (bf16[5,4,3,3,1,32]{5,3,2,1,0,4:T(4,128)(2,1)S(1)}, bf16[5,4,3,3,1,32]{5,3,2,1,0,4:T(4,128)(2,1)}, u32[]{:S(2)}) copy-start(bf16[5,4,3,3,1,32]{5,3,2,1,0,4:T(4,128)(2,1)} %get-tuple-element.76) | copy-start | bytes 34564
  50.9 15.4 %copy-start.15 = (bf16[5,4,3,3,1,32]{5,3,2,1,0,4:T(4,128)(2,1)S(1)}, bf16[5,4,3,3,1,32]{5,3,2,1,0,4:T(4,128)(2,1)}, u32[]{:S(2)}) copy-start(bf16[5,4,3,3,1,32]{5,3,2,1,0,4:T(4,128)(2,1)} %get-tuple-element.77) | copy-start | bytes 34564
  50.9 15.4 %copy-start.16 = (bf16[5,4,3,3,1,32]{5,3,2,1,0,4:T(4,128)(2,1)S(1)}, bf16[5,4,3,3,1,32]{5,3,2,1,0,4:T(4,128)(2,1)}, u32[]{:S(2)}) copy-start(bf16[5,4,3,3,1,32]{5,3,2,1,0,4:T(4,128)(2,1)} %get-tuple-element.78) | copy-start | bytes 34564
  51.0 16.1 %copy-start.4 = (f32[32,32,3,3,3]{1,0,4,3,2:T(8,128)S(1)}, f32[32,32,3,3,3]{1,0,4,3,2:T(8,128)}, u32[]{:S(2)}) copy-start(f32[32,32,3,3,3]{1,0,4,3,2:T(8,128)} %param.18) | copy-start | bytes 331780
  60.1 7.4 %copy-start.19 = (f32[32]{0:T(128)S(1)}, f32[32]{0:T(128)}, u32[]{:S(2)}) copy-start(f32[32]{0:T(128)} %param.17) | copy-start | bytes 388
  60.1 7.5 %copy-start.20 = (f32[32]{0:T(128)S(1)}, f32[32]{0:T(128)}, u32[]{:S(2)}) copy-start(f32[32]{0:T(128)} %param.19) | copy-start | bytes 388
  60.1 7.7 %copy-start.21 = (f32[5]{0:T(128)S(1)}, f32[5]{0:T(128)}, u32[]{:S(2)}) copy-start(f32[5]{0:T(128)} %param.21) | copy-start | bytes 64
  60.1 8.6 %copy-start.5 = (s32[1,1,2]{2,1,0:T(1,128)S(1)}, s32[1,1,2]{2,1,0:T(1,128)}, u32[]{:S(2)}) copy-start(s32[1,1,2]{2,1,0:T(1,128)} %param.14) | copy-start | bytes 28
  60.1 18.8 %all-to-all-start = ((f32[16,2,40,128]{3,2,1,0:T(8,128)}), f32[16,2,40,128]{3,2,1,0:T(8,128)S(1)}, u32[]{:S(2)}, u32[]{:S(2)}) async-start(f32[16,2,40,128]{3,2,1,0:T(8,128)} %get-tuple-element.57), calls=%async_computation | async-start | bytes 1310720 | tf_op jit(solution)/shard_map/all_to_all | solution.py:496
  74.7 1.3 %copy-start.6 = (bf16[2,384,1280]{2,1,0:T(8,128)(2,1)}, bf16[2,384,1280]{2,1,0:T(8,128)(2,1)S(1)}, u32[]{:S(2)}) copy-start(bf16[2,384,1280]{2,1,0:T(8,128)(2,1)S(1)} %get-tuple-element.62.refs_2_) | copy-start | bytes 5898244
  76.0 1.0 copy-start.8
  77.0 1.0 copy-start.10
  78.0 0.9 copy-start.12
  78.9 1.5 %copy-start.7 = (bf16[2,384,1280]{2,1,0:T(8,128)(2,1)S(1)}, bf16[2,384,1280]{2,1,0:T(8,128)(2,1)}, u32[]{:S(2)}) copy-start(bf16[2,384,1280]{2,1,0:T(8,128)(2,1)} %copy-done.6) | copy-start | bytes 5898244
  80.4 1.2 copy-start.9
  81.7 1.2 copy-start.11
  82.9 1.2 copy-start.13
  92.9 2.3 %collective-permute-start.12 = (f32[144,128]{1,0:T(8,128)S(1)}, f32[144,128]{1,0:T(8,128)S(1)}, u32[]{:S(2)}, u32[]{:S(2)}) collective-permute-start(f32[144,128]{1,0:T(8,128)S(1)} %get-tuple-element.68), channel_id=1, source_target_pairs={{0,1},{1,0},{2,3},{3,2},{4,5},{5,4},{6,7},{7,6},{8,9},{9,8},{10,11... | collective-permute-start | bytes 221192 | tf_op jit(solution)/shard_map/ppermute | solution.py:432
  95.3 3.3 %collective-permute-start.13 = (f32[144,128]{1,0:T(8,128)S(1)}, f32[144,128]{1,0:T(8,128)S(1)}, u32[]{:S(2)}, u32[]{:S(2)}) collective-permute-start(f32[144,128]{1,0:T(8,128)S(1)} %add.47), channel_id=1, source_target_pairs={{0,16},{1,17},{2,18},{3,19},{4,20},{5,21},{6,22},{7,23},{8,24},{9,... | collective-permute-start | bytes 221192 | tf_op jit(solution)/shard_map/ppermute | solution.py:434
  98.6 4.5 %collective-permute-start.14 = (f32[144,128]{1,0:T(8,128)S(1)}, f32[144,128]{1,0:T(8,128)S(1)}, u32[]{:S(2)}, u32[]{:S(2)}) collective-permute-start(f32[144,128]{1,0:T(8,128)S(1)} %add.48), channel_id=1, source_target_pairs={{0,18},{1,19},{2,16},{3,17},{4,22},{5,23},{6,20},{7,21},{8,26},{9,... | collective-permute-start | bytes 221192 | tf_op jit(solution)/shard_map/ppermute | solution.py:434
  103.1 3.3 %collective-permute-start.15 = (f32[144,128]{1,0:T(8,128)S(1)}, f32[144,128]{1,0:T(8,128)S(1)}, u32[]{:S(2)}, u32[]{:S(2)}) collective-permute-start(f32[144,128]{1,0:T(8,128)S(1)} %add.49), channel_id=1, source_target_pairs={{0,4},{1,5},{2,6},{3,7},{4,0},{5,1},{6,2},{7,3},{8,12},{9,13},{10,... | collective-permute-start | bytes 221192 | tf_op jit(solution)/shard_map/ppermute | solution.py:434
  106.4 4.5 %collective-permute-start.16 = (f32[144,128]{1,0:T(8,128)S(1)}, f32[144,128]{1,0:T(8,128)S(1)}, u32[]{:S(2)}, u32[]{:S(2)}) collective-permute-start(f32[144,128]{1,0:T(8,128)S(1)} %add.50), channel_id=1, source_target_pairs={{0,12},{1,13},{2,14},{3,15},{4,8},{5,9},{6,10},{7,11},{8,4},{9,5},... | collective-permute-start | bytes 221192 | tf_op jit(solution)/shard_map/ppermute | solution.py:434
  110.9 3.3 %collective-permute-start.17 = (f32[144,128]{1,0:T(8,128)S(1)}, f32[144,128]{1,0:T(8,128)S(1)}, u32[]{:S(2)}, u32[]{:S(2)}) collective-permute-start(f32[144,128]{1,0:T(8,128)S(1)} %add.51), channel_id=1, source_target_pairs={{0,32},{1,33},{2,34},{3,35},{4,36},{5,37},{6,38},{7,39},{8,40},{9,... | collective-permute-start | bytes 221192 | tf_op jit(solution)/shard_map/ppermute | solution.py:434
  114.2 4.5 %collective-permute-start.18 = (f32[144,128]{1,0:T(8,128)S(1)}, f32[144,128]{1,0:T(8,128)S(1)}, u32[]{:S(2)}, u32[]{:S(2)}) collective-permute-start(f32[144,128]{1,0:T(8,128)S(1)} %add.52), channel_id=1, source_target_pairs={{0,96},{1,97},{2,98},{3,99},{4,100},{5,101},{6,102},{7,103},{8,104... | collective-permute-start | bytes 221192 | tf_op jit(solution)/shard_map/ppermute | solution.py:434
  118.7 8.2 %collective-permute-start.19 = (f32[144,128]{1,0:T(8,128)S(1)}, f32[144,128]{1,0:T(8,128)S(1)}, u32[]{:S(2)}, u32[]{:S(2)}) collective-permute-start(f32[144,128]{1,0:T(8,128)S(1)} %add.53.mine_ref), channel_id=1, source_target_pairs={{0,1},{1,0},{2,3},{3,2},{4,5},{5,4},{6,7},{7,6},{8,9},{9,8},{10,11... | collective-permute-start | bytes 221192 | tf_op jit(solution)/shard_map/ppermute | solution.py:435

commit v4 on v3

--- a/solution.py
+++ b/solution.py
@@ -151,11 +151,11 @@
     return jnp.where(lane == (Z - 1 if dz > 0 else 0), 0.0, moved)
 
 
-def fill_taps(cells_ref, out_ref, sign):
-    rows = cells_ref.shape[0]
+def fill_taps(cells, out_ref, sign):
+    rows = cells.shape[0]
     lane = lax.broadcasted_iota(jnp.int32, (rows, Z), 1)
     zero = jnp.zeros((rows, Z), F32)
-    shifted = [[z_shifted(cells_ref[:, k * Z : (k + 1) * Z], sign * (dz - 1), lane) for dz in range(3)] for k in range(PY)]
+    shifted = [[z_shifted(cells[:, k * Z : (k + 1) * Z], sign * (dz - 1), lane) for dz in range(3)] for k in range(PY)]
     for k in range(PY):
         parts = []
         for dy in range(3):
@@ -207,57 +207,61 @@
             bwd_ref[dy, :, dz * 128 : (dz + 1) * 128] = block.T.astype(BF)
 
 
-KEPT = [
-    ((2, ROWS, PY * Z), F32),
-    ((2, TALL, PY * Z), BF),
-    ((2, 384, (PY + 2) * Z), BF),
-    ((2, 128, PY * Z), F32),
-    ((2, 128, PY * Z), BF),
-    ((2, 128, PY * Z), F32),
-    ((2, ROWS, PY * Z), F32),
-]
-SAVED = len(KEPT)
-HELD = [pltpu.VMEM(s, d) for s, d in KEPT] + [pltpu.SemaphoreType.DMA((SAVED, 2))]
+PARTS = 80
+AT = {"sum": (0, PARTS), "first": (80, 32), "a1": (112, 128), "a2": (240, 128), "d1": (368, 128), "d2": (496, 128)}
+KEPT = ((2, 16384, PY * Z), BF)
+NAMES = ("sum", "d2", "a2", "a1", "first", "d1")
+HELD = [pltpu.VMEM((2, AT[name][1], PY * Z), BF) for name in NAMES] + [pltpu.SemaphoreType.DMA((len(NAMES), 2))]
+
+
+def transfers(kept_ref, held, sems):
+    out = {}
+    for n, name in enumerate(NAMES):
+        for p in range(2):
+            start, size = AT[name]
+            out[name, p] = (kept_ref.at[p, pl.ds(start, size)], held[n].at[p], sems.at[n, p])
+    return out
 
 
 def forward_kernel(
-    anchors, slabs_ref, w1_ref, w2_ref, w3_ref, b1_ref, b2_ref, b3_ref,
-    *refs,
+    anchors, slabs_ref, w1_ref, w2_ref, w3_ref, b1_ref, b2_ref, b3_ref, kept_ref, *refs,
 ):
-    kept, held, sems = refs[:SAVED], refs[SAVED : 2 * SAVED], refs[2 * SAVED]
-    first_ref, taps_ref, a1_ref, d1_ref, a2_ref, d2_ref, pred_ref = held
+    held, sems, (first_ref, taps_ref, a1_ref) = refs[: len(NAMES)], refs[len(NAMES)], refs[len(NAMES) + 1 :]
+    sum_ref, d2_ref, a2_ref, a1_kept, cells_ref, d1_ref = held
+    plan = transfers(kept_ref, held, sems)
     copies = []
 
-    def keep(n, p):
-        copy = pltpu.make_async_copy(held[n].at[p], kept[n].at[p], sems.at[n, p])
-        copy.start()
-        copies.append(copy)
+    def keep(name, p):
+        to, of, sem = plan[name, p]
+        copies.append(pltpu.make_async_copy(of, to, sem))
+        copies[-1].start()
 
     for p in range(2):
         patch_rows(slabs_ref, anchors[p], first_ref.at[p])
-        fill_taps(first_ref.at[p], taps_ref.at[p], 1)
-        keep(0, p)
-        keep(1, p)
+        cells_ref[p] = jnp.concatenate([first_ref[p], jnp.zeros((32 - ROWS, PY * Z), F32)], axis=0).astype(BF)
+        keep("first", p)
+        fill_taps(first_ref[p], taps_ref.at[p], 1)
         y1 = dot(w1_ref[...], taps_ref[p])
         act, slope = activate(y1 + b1_ref[...])
-        d1_ref[p] = slope
+        d1_ref[p] = slope.astype(BF)
+        keep("d1", p)
+        a1_kept[p] = act.astype(BF)
+        keep("a1", p)
         clear_ends(a1_ref.at[p])
         for k in range(PY):
             fill_z(act[:, k * Z : (k + 1) * Z], k, a1_ref.at[p], 1)
-        keep(2, p)
-        keep(3, p)
         y2 = b2_ref[...] + dot(w2_ref[0], a1_ref[p, :, 0 : PY * Z])
         for dy in range(1, 3):
             y2 = y2 + dot(w2_ref[dy], a1_ref[p, :, dy * Z : (dy + PY) * Z])
         act, slope = activate(y2)
-        d2_ref[p] = slope
+        d2_ref[p] = slope.astype(BF)
         a2_ref[p] = act.astype(BF)
-        keep(4, p)
-        keep(5, p)
+        keep("d2", p)
+        keep("a2", p)
         terms = dot(w3_ref[...], a2_ref[p])
         lane = lax.broadcasted_iota(jnp.int32, (ROWS, Z), 1)
         for k in range(PY):
-            out = b3_ref[...] + jnp.zeros((ROWS, Z), F32)
+            out = b3_ref[...] + first_ref[p, :, k * Z : (k + 1) * Z]
             for dz in range(3):
                 part = None
                 for dy in range(3):
@@ -267,8 +271,12 @@
                         term = terms[t : t + ROWS, at * Z : (at + 1) * Z]
                         part = term if part is None else part + term
                 out = out + z_shifted(part, dz - 1, lane)
-            pred_ref[p, :, k * Z : (k + 1) * Z] = out
-        keep(6, p)
+            high = out.astype(BF).astype(F32)
+            mid = (out - high).astype(BF).astype(F32)
+            low = out - high - mid
+            pad = jnp.zeros((PARTS - 3 * ROWS, Z), F32)
+            sum_ref[p, :, k * Z : (k + 1) * Z] = jnp.concatenate([high, mid, low, pad], axis=0).astype(BF)
+        keep("sum", p)
     for copy in copies:
         copy.wait()
 
@@ -292,18 +300,15 @@
     return out
 
 
-def backward_kernel(
-    place, anchors, count, slabs_ref, w2_ref, w3_ref, *refs,
-):
-    kept, (keep_ref, send_ref) = refs[:SAVED], refs[SAVED : SAVED + 2]
-    held, sems = refs[SAVED + 2 : 2 * SAVED + 2], refs[2 * SAVED + 2]
-    last_ref, err_ref, g_ref, b_ref, grads_ref = refs[2 * SAVED + 3 :]
-    first_ref, taps_ref, a1_ref, d1_ref, a2_ref, d2_ref, pred_ref = held
-    copies = {}
+def backward_kernel(place, anchors, count, slabs_ref, w2_ref, w3_ref, kept_ref, keep_ref, send_ref, *refs):
+    held, sems = refs[: len(NAMES)], refs[len(NAMES)]
+    last_ref, taps_ref, a1_ref, g_ref, b_ref, grads_ref = refs[len(NAMES) + 1 :]
+    sum_ref, d2_ref, a2_ref, a1_kept, cells_ref, d1_ref = held
+    plan = transfers(kept_ref, held, sems)
+    copies = {key: pltpu.make_async_copy(of, to, sem) for key, (of, to, sem) in plan.items()}
     for p in range(2):
-        for n in (6, 0, 4, 5, 2, 3, 1):
-            copies[n, p] = pltpu.make_async_copy(kept[n].at[p], held[n].at[p], sems.at[n, p])
-            copies[n, p].start()
+        for name in NAMES:
+            copies[name, p].start()
     db1 = jnp.zeros((128, 1), F32)
     db2 = jnp.zeros((128, 1), F32)
     db3 = jnp.zeros((ROWS, 1), F32)
@@ -311,37 +316,41 @@
     dw1 = jnp.zeros((128, TALL), F32)
     dw3 = jnp.zeros((128, TALL), F32)
     dw2 = [jnp.zeros((128, 384), F32) for _ in range(3)]
-    clear_ends(b_ref)
+    for name in NAMES[:3]:
+        for p in range(2):
+            copies[name, p].wait()
     for p in range(2):
         live = jnp.where(p < count[0], 1.0, 0.0).astype(F32)
-        patch_rows(slabs_ref, anchors[p], last_ref)
-        copies[6, p].wait()
-        copies[0, p].wait()
-        err = pred_ref[p] - (last_ref[...] - first_ref[p])
+        patch_rows(slabs_ref, anchors[p], last_ref.at[p])
+        parts = sum_ref[p].astype(F32)
+        err = parts[0:ROWS] + parts[ROWS : 2 * ROWS] + parts[2 * ROWS : 3 * ROWS] - last_ref[p]
         loss = loss + live * jnp.sum(err * err, axis=1, keepdims=True)
         err = err * (live * (2.0 / CELLS))
-        err_ref[...] = err
         db3 = db3 + jnp.sum(err, axis=1, keepdims=True)
-        fill_taps(err_ref, g_ref, -1)
-        da2 = dot(w3_ref[...], g_ref[...])
-        copies[4, p].wait()
-        dw3 = dw3 + dot_t(a2_ref[p], g_ref[...])
-        copies[5, p].wait()
-        dy2 = da2 * d2_ref[p]
+        fill_taps(err, g_ref.at[p], -1)
+        da2 = dot(w3_ref[...], g_ref[p])
+        dw3 = dw3 + dot_t(a2_ref[p], g_ref[p])
+        dy2 = da2 * d2_ref[p].astype(F32)
         db2 = db2 + jnp.sum(dy2, axis=1, keepdims=True)
+        clear_ends(b_ref.at[p])
         for k in range(PY):
-            fill_z(dy2[:, k * Z : (k + 1) * Z], k, b_ref, -1)
-        middle = b_ref[128:256, Z : (PY + 1) * Z]
+            fill_z(dy2[:, k * Z : (k + 1) * Z], k, b_ref.at[p], -1)
+    for name in NAMES[3:]:
+        for p in range(2):
+            copies[name, p].wait()
+    for p in range(2):
+        clear_ends(a1_ref.at[p])
+        for k in range(PY):
+            fill_z(a1_kept[p, :, k * Z : (k + 1) * Z].astype(F32), k, a1_ref.at[p], 1)
+        fill_taps(cells_ref[p].astype(F32)[0:ROWS], taps_ref.at[p], 1)
+        middle = b_ref[p, 128:256, Z : (PY + 1) * Z]
         da1 = None
-        copies[2, p].wait()
         for dy in range(3):
             dw2[dy] = dw2[dy] + dot_t(middle, a1_ref[p, :, dy * Z : (dy + PY) * Z])
-            term = dot(w2_ref[dy], b_ref[:, (2 - dy) * Z : (2 - dy + PY) * Z])
+            term = dot(w2_ref[dy], b_ref[p, :, (2 - dy) * Z : (2 - dy + PY) * Z])
             da1 = term if da1 is None else da1 + term
-        copies[3, p].wait()
-        dy1 = da1 * d1_ref[p]
+        dy1 = da1 * d1_ref[p].astype(F32)
         db1 = db1 + jnp.sum(dy1, axis=1, keepdims=True)
-        copies[1, p].wait()
         dw1 = dw1 + dot_t(dy1.astype(BF), taps_ref[p])
 
     lane = lax.broadcasted_iota(jnp.int32, (C, 128), 1)
@@ -482,10 +491,15 @@
             place, part, *received, vel, diffusivity
         )
 
-    learned = call(
+    (kept,) = call(
         forward_kernel,
-        KEPT,
-        scratch=HELD,
+        [KEPT],
+        scratch=HELD
+        + [
+            pltpu.VMEM((2, ROWS, PY * Z), F32),
+            pltpu.VMEM((2, TALL, PY * Z), BF),
+            pltpu.VMEM((2, 384, (PY + 2) * Z), BF),
+        ],
         ins=[SMEM] + [VMEM] * 7,
         flops=2_000_000_000,
         nbytes=8_000_000,
@@ -499,17 +513,18 @@
         [((HALF, 128), F32)] * 2,
         scratch=HELD
         + [
-            pltpu.VMEM((ROWS, PY * Z), F32),
-            pltpu.VMEM((ROWS, PY * Z), F32),
-            pltpu.VMEM((TALL, PY * Z), BF),
-            pltpu.VMEM((384, (PY + 2) * Z), BF),
+            pltpu.VMEM((2, ROWS, PY * Z), F32),
+            pltpu.VMEM((2, TALL, PY * Z), BF),
+            pltpu.VMEM((2, 384, (PY + 2) * Z), BF),
+            pltpu.VMEM((2, TALL, PY * Z), BF),
+            pltpu.VMEM((2, 384, (PY + 2) * Z), BF),
             pltpu.VMEM((2 * HALF, 128), F32),
         ],
-        ins=[SMEM] * 3 + [VMEM] * 3 + [HBM] * SAVED,
+        ins=[SMEM] * 3 + [VMEM] * 3 + [HBM],
         flops=4_000_000_000,
         nbytes=10_000_000,
         mib=24,
-    )(place, anchors, count, last_slabs, w2_bwd, w3_band.T, *learned)
+    )(place, anchors, count, last_slabs, w2_bwd, w3_band.T, kept)
 
     g1, gb1, g2, gb2, g3, gb3, loss = call(
         finish_kernel,

time: 129 us -> 124 us (0.961)
  Pallas kernels: 27.8 us -> 22.2 us
  starting transfers between devices: 49.7 us -> 45.2 us
  local copies, waits for them, and re-layouts: 12.6 us -> 15.7 us
    ppermute x3, waiting for transfers between devices: 14.7 us -> 9.76 us  [exchange(): lax.ppermute(yb, 'gy', pairs(16, True))]
    ppermute x6, starting transfers between devices: 7.46 us -> 2.85 us  [sum_all(): mine = mine + lax.ppermute(mine, ('gx', 'gy'), pairs)]
    ppermute x6, waiting for transfers between devices: 15.9 us -> 20.5 us  [sum_all(): mine = mine + lax.ppermute(mine, ('gx', 'gy'), pairs)]
    pallas_call x1, Pallas kernels: 8.86 us -> 6.49 us  [on_device(): call(backward_kernel, [((HALF, 128), F32)] * 2, scratch=HELD + [pltpu.VME...]
    all_to_all x1, waiting for transfers between devices: 0.01 us -> 2.07 us  [on_device(): lax.all_to_all(edges[0], 'gy', 0, 0, tiled=True).reshape(32, 2 * F * X, Z)]
    ppermute x3, starting transfers between devices: 8.29 us -> 6.51 us  [exchange(): lax.ppermute(xb, 'gx', pairs(8, True))]
    pallas_call x1, Pallas kernels: 5.98 us -> 4.34 us  [on_device(): call(forward_kernel, [KEPT], scratch=HELD + [pltpu.VMEM((2, ROWS, PY * Z)...]
    pallas_call x3, Pallas kernels: 5.87 us -> 4.5 us  [on_device(): call(kernel, outs, ins=[SMEM] + [VMEM] * 7, nbytes=3000000)]
  transfers between devices with their start and end apart: 22 -> 22, of which waited for: 13 -> 13; matrix products, arithmetic and copies ran while one was open for 2% -> 5% of each run, Pallas kernels for 13% -> 11%
where the time goes in v4:
time: 124 us; the launch traced here: 123 us
  starting transfers between devices  45.2 us (36%)
  waiting for transfers between devices  36.5 us (29%)
  Pallas kernels  22.2 us (18%)
  local copies, waits for them, and re-layouts  15.7 us (13%)
  between operations  1.65 us (1%)
  other arithmetic  1.55 us (1%)
    ppermute x6, waiting for transfers between devices, sum_all(): mine = mine + lax.ppermute(mine, ('gx', 'gy'), pairs)  20.5 us
    unnamed x27, local copies, waits for them, and re-layouts  11.5 us
    ppermute x3, waiting for transfers between devices, exchange(): lax.ppermute(yb, 'gy', pairs(16, True))  9.76 us
    ppermute x3, starting transfers between devices, exchange(): lax.ppermute(yb, 'gy', pairs(16, True))  8.64 us
    all_to_all x1, starting transfers between devices, on_device(): lax.all_to_all(edges[0], 'gy', 0, 0, tiled=True).reshape(32, 2 * F * X, Z)  7.57 us
    ppermute x1, starting transfers between devices, sum_all(): return (mine, lax.ppermute(mine, 'gy', cores))  7.33 us
    all_to_all x1, starting transfers between devices, on_device(): lax.all_to_all(slabs, 'gy', 0, 0, tiled=True).reshape(32, 2 * F * X, Z)  6.81 us
    ppermute x3, starting transfers between devices, exchange(): lax.ppermute(xb, 'gx', pairs(8, True))  6.51 us
  transfers between devices with their start and end apart: 22, of which 13 were waited for; matrix products, arithmetic and copies ran while one was open for 5% of the time, Pallas kernels for 11%

profile of v4, /device:TPU:1, one launch (start us, length us, event | category | flops | bytes accessed | tf_op | source)
XLA Modules:
  0.0 122.8 jit_solution(3601840984159774709)
XLA Ops:
  0.7 1.1 copy-done.4
  2.6 1.5 %collective-permute-start.2 = (f32[20,2048]{1,0:T(8,128)S(1)}, f32[20,2048]{1,0:T(8,128)S(1)}, u32[]{:S(2)}, u32[]{:S(2)}) collective-permute-start(f32[20,2048]{1,0:T(8,128)S(1)} %get-tuple-element.37), channel_id=1, source_target_pairs={{0,1},{1,0},{2,3},{3,2},{4,5},{5,4},{6,7},{7,6},{8,9},{9,8},{10,11... | collective-permute-start | bytes 491528 | tf_op jit(solution)/shard_map/ppermute | solution.py:133
  4.1 3.7 %collective-permute-start.3 = (f32[20,2048]{1,0:T(8,128)S(1)}, f32[20,2048]{1,0:T(8,128)S(1)}, u32[]{:S(2)}, u32[]{:S(2)}) collective-permute-start(f32[20,2048]{1,0:T(8,128)S(1)} %get-tuple-element.38), channel_id=1, source_target_pairs={{0,15},{1,2},{2,1},{3,4},{4,3},{5,6},{6,5},{7,8},{8,7},{9,10},{10,... | collective-permute-start | bytes 491528 | tf_op jit(solution)/shard_map/ppermute | solution.py:134
  8.5 2.9 %collective-permute-start.1 = (f32[5,4,2048]{2,1,0:T(4,128)S(1)}, f32[5,4,2048]{2,1,0:T(4,128)S(1)}, u32[]{:S(2)}, u32[]{:S(2)}) collective-permute-start(f32[5,4,2048]{2,1,0:T(4,128)S(1)} %get-tuple-element.36), channel_id=1, source_target_pairs={{0,112},{16,32},{32,16},{48,64},{64,48},{80,96},{96,80},{112,0},{1... | collective-permute-start | bytes 491528 | tf_op jit(solution)/shard_map/ppermute | solution.py:132
  11.4 1.2 shard_map.178
  12.6 6.8 %all-to-all-start.1 = ((f32[16,2,40,128]{3,2,1,0:T(8,128)}), f32[16,2,40,128]{3,2,1,0:T(8,128)S(1)}, u32[]{:S(2)}, u32[]{:S(2)}) async-start(f32[16,2,40,128]{3,2,1,0:T(8,128)} %shard_map.178), calls=%async_computation.1 | async-start | bytes 1310720 | tf_op jit(solution)/shard_map/all_to_all | solution.py:474
  19.4 1.0 copy-done
  20.4 1.1 copy-done.5
  21.5 0.9 copy-done.6
  22.4 0.9 shard_map.170.refs_1_
  23.3 1.0 copy-done.1
  24.3 0.9 copy-done.7
  25.2 1.2 shard_map.172
  26.7 3.1 %collective-permute-start.7 = (f32[20,2048]{1,0:T(8,128)S(1)}, f32[20,2048]{1,0:T(8,128)S(1)}, u32[]{:S(2)}, u32[]{:S(2)}) collective-permute-start(f32[20,2048]{1,0:T(8,128)S(1)} %get-tuple-element.43), channel_id=1, source_target_pairs={{0,15},{1,2},{2,1},{3,4},{4,3},{5,6},{6,5},{7,8},{8,7},{9,10},{10,... | collective-permute-start | bytes 491528 | tf_op jit(solution)/shard_map/ppermute | solution.py:134
  29.8 1.7 %collective-permute-start.5 = (f32[5,4,2048]{2,1,0:T(4,128)S(1)}, f32[5,4,2048]{2,1,0:T(4,128)S(1)}, u32[]{:S(2)}, u32[]{:S(2)}) collective-permute-start(f32[5,4,2048]{2,1,0:T(4,128)S(1)} %get-tuple-element.41), channel_id=1, source_target_pairs={{0,112},{16,32},{32,16},{48,64},{64,48},{80,96},{96,80},{112,0},{1... | collective-permute-start | bytes 491528 | tf_op jit(solution)/shard_map/ppermute | solution.py:132
  31.5 0.9 convert_bitcast_fusion
  32.4 0.9 rev.8
  33.4 1.0 copy-done.2
  34.4 0.9 copy-done.8
  35.3 0.9 shard_map.173.refs_1_
  36.2 5.3 %collective-permute-done.7.refs_5_ = f32[20,2048]{1,0:T(8,128)S(1)} collective-permute-done((f32[20,2048]{1,0:T(8,128)S(1)}, f32[20,2048]{1,0:T(8,128)S(1)}, u32[]{:S(2)}, u32[]{:S(2)}) %collective-permute-start.7) | collective-permute-done | bytes 163872 | tf_op jit(solution)/shard_map/ppermute | solution.py:134
  41.6 1.2 shard_map.174
  43.3 1.9 %collective-permute-start.11 = (f32[20,2048]{1,0:T(8,128)S(1)}, f32[20,2048]{1,0:T(8,128)S(1)}, u32[]{:S(2)}, u32[]{:S(2)}) collective-permute-start(f32[20,2048]{1,0:T(8,128)S(1)} %get-tuple-element.48), channel_id=1, source_target_pairs={{0,15},{1,2},{2,1},{3,4},{4,3},{5,6},{6,5},{7,8},{8,7},{9,10},{10,... | collective-permute-start | bytes 491528 | tf_op jit(solution)/shard_map/ppermute | solution.py:134
  45.3 0.8 collective-permute-start.8
  46.0 1.9 %collective-permute-start.9 = (f32[5,4,2048]{2,1,0:T(4,128)S(1)}, f32[5,4,2048]{2,1,0:T(4,128)S(1)}, u32[]{:S(2)}, u32[]{:S(2)}) collective-permute-start(f32[5,4,2048]{2,1,0:T(4,128)S(1)} %get-tuple-element.46), channel_id=1, source_target_pairs={{0,112},{16,32},{32,16},{48,64},{64,48},{80,96},{96,80},{112,0},{1... | collective-permute-start | bytes 491528 | tf_op jit(solution)/shard_map/ppermute | solution.py:132
  48.7 1.0 copy-done.3
  49.7 0.9 copy-done.9
  50.6 0.9 shard_map.175.refs_1_
  51.5 4.4 %collective-permute-done.11.refs_5_ = f32[20,2048]{1,0:T(8,128)S(1)} collective-permute-done((f32[20,2048]{1,0:T(8,128)S(1)}, f32[20,2048]{1,0:T(8,128)S(1)}, u32[]{:S(2)}, u32[]{:S(2)}) %collective-permute-start.11) | collective-permute-done | bytes 163872 | tf_op jit(solution)/shard_map/ppermute | solution.py:134
  56.0 2.2 %collective-permute-done.8.refs_2_ = f32[5,4,2048]{2,1,0:T(4,128)S(1)} collective-permute-done((f32[5,4,2048]{2,1,0:T(4,128)S(1)}, f32[5,4,2048]{2,1,0:T(4,128)S(1)}, u32[]{:S(2)}, u32[]{:S(2)}) %collective-permute-start.8) | collective-permute-done | bytes 163872 | tf_op jit(solution)/shard_map/ppermute | solution.py:131
  58.2 2.2 %shard_map.176 = (f32[20,4,2048]{2,1,0:T(4,128)}, f32[16,2,40,128]{3,2,1,0:T(8,128)}) custom-call(s32[2]{0:T(128)S(1)} %pad_add_fusion.place.refs_0_, f32[20,4,2048]{2,1,0:T(4,128)S(1)} %shard_map.175.refs_1_, f32[5,4,2048]{2,1,0:T(4,128)S(1)} %collective-permute-done.8.refs_2_, f32[5,4,2048]{2,1,0:T(4,128)S(1)} %collective-permute-done.9.refs_3_, ...), custom_call_target="tpu_custom_call" | custom-call | bytes 3000000 | tf_op jit(solution)/shard_map/pallas_call | solution.py:490
  60.4 7.6 %all-to-all-start = ((f32[16,2,40,128]{3,2,1,0:T(8,128)}), f32[16,2,40,128]{3,2,1,0:T(8,128)S(1)}, u32[]{:S(2)}, u32[]{:S(2)}) async-start(f32[16,2,40,128]{3,2,1,0:T(8,128)} %get-tuple-element.50), calls=%async_computation | async-start | bytes 1310720 | tf_op jit(solution)/shard_map/all_to_all | solution.py:510
  68.6 1.0 copy-done.10
  73.9 4.3 %shard_map.179.kept_ref = bf16[2,16384,1024]{2,1,0:T(8,128)(2,1)} custom-call(s32[2]{0:T(128)S(1)} %bitcast.69, f32[32,40,128]{2,1,0:T(8,128)S(1)} %bitcast.66, bf16[128,224]{1,0:T(8,128)(2,1)S(1)} %pad_bitcast_fusion.w1_ref, bf16[3,128,384]{2,1,0:T(8,128)(2,1)S(1)} %get-tuple-element.52.w2_ref, bf16[224,128]{1,0:T(8,128)(2,1)S(1)} %pad.63.clone.w3_ref, ...), custom_call_target="tpu_custom_call" | custom-call | flops 2000000000 | bytes 8000000 | tf_op jit(solution)/shard_map/pallas_call | solution.py:494
  78.2 2.1 %all-to-all-done = f32[16,2,40,128]{3,2,1,0:T(8,128)S(1)} async-done(((f32[16,2,40,128]{3,2,1,0:T(8,128)}), f32[16,2,40,128]{3,2,1,0:T(8,128)S(1)}, u32[]{:S(2)}, u32[]{:S(2)}) %all-to-all-start) | async-done | bytes 655392 | tf_op jit(solution)/shard_map/all_to_all | solution.py:510
  80.3 6.5 %shard_map.180 = (f32[144,128]{1,0:T(8,128)S(1)}, f32[144,128]{1,0:T(8,128)S(1)}) custom-call(s32[2]{0:T(128)S(1)} %pad_add_fusion.place.refs_0_, s32[2]{0:T(128)S(1)} %bitcast.70, s32[1]{0:T(128)} %bitcast.56.count, f32[32,40,128]{2,1,0:T(8,128)S(1)} %bitcast.67, bf16[3,128,384]{2,1,0:T(8,128)(2,1)S(1)} %get-tuple-element.51.w2_ref, ...), custom_call_target="tpu_custom_call" | custom-call | flops 4000000000 | bytes 10000000 | tf_op jit(solution)/shard_map/pallas_call | solution.py:511
  86.8 1.6 %collective-permute-start.12 = (f32[144,128]{1,0:T(8,128)S(1)}, f32[144,128]{1,0:T(8,128)S(1)}, u32[]{:S(2)}, u32[]{:S(2)}) collective-permute-start(f32[144,128]{1,0:T(8,128)S(1)} %get-tuple-element.54), channel_id=1, source_target_pairs={{0,1},{1,0},{2,3},{3,2},{4,5},{5,4},{6,7},{7,6},{8,9},{9,8},{10,11... | collective-permute-start | bytes 221192 | tf_op jit(solution)/shard_map/ppermute | solution.py:441
  88.4 0.9 collective-permute-done.12
  89.4 3.2 %collective-permute-done.13 = f32[144,128]{1,0:T(8,128)S(1)} collective-permute-done((f32[144,128]{1,0:T(8,128)S(1)}, f32[144,128]{1,0:T(8,128)S(1)}, u32[]{:S(2)}, u32[]{:S(2)}) %collective-permute-start.13) | collective-permute-done | bytes 73760 | tf_op jit(solution)/shard_map/ppermute | solution.py:443
  92.7 4.4 %collective-permute-done.14 = f32[144,128]{1,0:T(8,128)S(1)} collective-permute-done((f32[144,128]{1,0:T(8,128)S(1)}, f32[144,128]{1,0:T(8,128)S(1)}, u32[]{:S(2)}, u32[]{:S(2)}) %collective-permute-start.14) | collective-permute-done | bytes 73760 | tf_op jit(solution)/shard_map/ppermute | solution.py:443
  97.2 3.2 %collective-permute-done.15 = f32[144,128]{1,0:T(8,128)S(1)} collective-permute-done((f32[144,128]{1,0:T(8,128)S(1)}, f32[144,128]{1,0:T(8,128)S(1)}, u32[]{:S(2)}, u32[]{:S(2)}) %collective-permute-start.15) | collective-permute-done | bytes 73760 | tf_op jit(solution)/shard_map/ppermute | solution.py:443
  101.1 3.8 %collective-permute-done.16 = f32[144,128]{1,0:T(8,128)S(1)} collective-permute-done((f32[144,128]{1,0:T(8,128)S(1)}, f32[144,128]{1,0:T(8,128)S(1)}, u32[]{:S(2)}, u32[]{:S(2)}) %collective-permute-start.16) | collective-permute-done | bytes 73760 | tf_op jit(solution)/shard_map/ppermute | solution.py:443
  105.5 2.8 %collective-permute-done.17 = f32[144,128]{1,0:T(8,128)S(1)} collective-permute-done((f32[144,128]{1,0:T(8,128)S(1)}, f32[144,128]{1,0:T(8,128)S(1)}, u32[]{:S(2)}, u32[]{:S(2)}) %collective-permute-start.17) | collective-permute-done | bytes 73760 | tf_op jit(solution)/shard_map/ppermute | solution.py:443
  108.3 1.4 %collective-permute-start.18 = (f32[144,128]{1,0:T(8,128)S(1)}, f32[144,128]{1,0:T(8,128)S(1)}, u32[]{:S(2)}, u32[]{:S(2)}) collective-permute-start(f32[144,128]{1,0:T(8,128)S(1)} %add.52), channel_id=1, source_target_pairs={{0,96},{1,97},{2,98},{3,99},{4,100},{5,101},{6,102},{7,103},{8,104... | collective-permute-start | bytes 221192 | tf_op jit(solution)/shard_map/ppermute | solution.py:443
  109.7 3.1 %collective-permute-done.18 = f32[144,128]{1,0:T(8,128)S(1)} collective-permute-done((f32[144,128]{1,0:T(8,128)S(1)}, f32[144,128]{1,0:T(8,128)S(1)}, u32[]{:S(2)}, u32[]{:S(2)}) %collective-permute-start.18) | collective-permute-done | bytes 73760 | tf_op jit(solution)/shard_map/ppermute | solution.py:443
  112.8 7.3 %collective-permute-start.19 = (f32[144,128]{1,0:T(8,128)S(1)}, f32[144,128]{1,0:T(8,128)S(1)}, u32[]{:S(2)}, u32[]{:S(2)}) collective-permute-start(f32[144,128]{1,0:T(8,128)S(1)} %add.53.mine_ref), channel_id=1, source_target_pairs={{0,1},{1,0},{2,3},{3,2},{4,5},{5,4},{6,7},{7,6},{8,9},{9,8},{10,11... | collective-permute-start | bytes 221192 | tf_op jit(solution)/shard_map/ppermute | solution.py:444
  120.1 0.9 collective-permute-done.19.other_ref
  121.0 1.8 %shard_map.181 = (f32[45,3,32]{2,1,0:T(4,128)}, f32[1,32]{1,0:T(1,128)}, f32[27,32,32]{2,1,0:T(8,128)}, f32[1,32]{1,0:T(1,128)}, f32[45,3,32]{2,1,0:T(4,128)}, /*index=5*/f32[1,5]{1,0:T(1,128)}, f32[1,1]{1,0:T(1,128)}) custom-call(s32[2]{0:T(128)S(1)} %pad_add_fusion.place.refs_0_, f32[144,128]{1,0:T(8,128)S(1)} %add.53.mine_ref, ...), custom_call_target="tpu_custom_call" | custom-call | bytes 1000000 | tf_op jit(solution)/shard_map/pallas_call | solution.py:529
  (68 shorter events, 9.1 us)
Async XLA Ops:
  0.6 79.7 %copy-start.12 = (s32[1,1,2]{2,1,0:T(1,128)S(1)}, s32[1,1,2]{2,1,0:T(1,128)}, u32[]{:S(2)}) copy-start(s32[1,1,2]{2,1,0:T(1,128)} %param.14) | copy-start | bytes 28
  0.7 1.1 copy-start.4
  2.6 20.7 %collective-permute-start.2 = (f32[20,2048]{1,0:T(8,128)S(1)}, f32[20,2048]{1,0:T(8,128)S(1)}, u32[]{:S(2)}, u32[]{:S(2)}) collective-permute-start(f32[20,2048]{1,0:T(8,128)S(1)} %get-tuple-element.37), channel_id=1, source_target_pairs={{0,1},{1,0},{2,3},{3,2},{4,5},{5,4},{6,7},{7,6},{8,9},{9,8},{10,11... | collective-permute-start | bytes 491528 | tf_op jit(solution)/shard_map/ppermute | solution.py:133
  4.1 19.2 %collective-permute-start.3 = (f32[20,2048]{1,0:T(8,128)S(1)}, f32[20,2048]{1,0:T(8,128)S(1)}, u32[]{:S(2)}, u32[]{:S(2)}) collective-permute-start(f32[20,2048]{1,0:T(8,128)S(1)} %get-tuple-element.38), channel_id=1, source_target_pairs={{0,15},{1,2},{2,1},{3,4},{4,3},{5,6},{6,5},{7,8},{8,7},{9,10},{10,... | collective-permute-start | bytes 491528 | tf_op jit(solution)/shard_map/ppermute | solution.py:134
  7.7 15.6 %collective-permute-start = (f32[5,4,2048]{2,1,0:T(4,128)S(1)}, f32[5,4,2048]{2,1,0:T(4,128)S(1)}, u32[]{:S(2)}, u32[]{:S(2)}) collective-permute-start(f32[5,4,2048]{2,1,0:T(4,128)S(1)} %get-tuple-element.35), channel_id=1, source_target_pairs={{0,16},{16,0},{32,48},{48,32},{64,80},{80,64},{96,112},{112,96},{1... | collective-permute-start | bytes 491528 | tf_op jit(solution)/shard_map/ppermute | solution.py:131
  8.5 14.8 %collective-permute-start.1 = (f32[5,4,2048]{2,1,0:T(4,128)S(1)}, f32[5,4,2048]{2,1,0:T(4,128)S(1)}, u32[]{:S(2)}, u32[]{:S(2)}) collective-permute-start(f32[5,4,2048]{2,1,0:T(4,128)S(1)} %get-tuple-element.36), channel_id=1, source_target_pairs={{0,112},{16,32},{32,16},{48,64},{64,48},{80,96},{96,80},{112,0},{1... | collective-permute-start | bytes 491528 | tf_op jit(solution)/shard_map/ppermute | solution.py:132
  12.6 47.8 %all-to-all-start.1 = ((f32[16,2,40,128]{3,2,1,0:T(8,128)}), f32[16,2,40,128]{3,2,1,0:T(8,128)S(1)}, u32[]{:S(2)}, u32[]{:S(2)}) async-start(f32[16,2,40,128]{3,2,1,0:T(8,128)} %shard_map.178), calls=%async_computation.1 | async-start | bytes 1310720 | tf_op jit(solution)/shard_map/all_to_all | solution.py:474
  19.4 1.0 copy-start
  20.4 1.1 copy-start.5
  21.5 0.9 copy-start.6
  23.3 1.0 copy-start.1
  24.3 0.9 copy-start.7
  26.4 9.8 %collective-permute-start.6 = (f32[20,2048]{1,0:T(8,128)S(1)}, f32[20,2048]{1,0:T(8,128)S(1)}, u32[]{:S(2)}, u32[]{:S(2)}) collective-permute-start(f32[20,2048]{1,0:T(8,128)S(1)} %get-tuple-element.42), channel_id=1, source_target_pairs={{0,1},{1,0},{2,3},{3,2},{4,5},{5,4},{6,7},{7,6},{8,9},{9,8},{10,11... | collective-permute-start | bytes 491528 | tf_op jit(solution)/shard_map/ppermute | solution.py:133
  26.7 14.8 %collective-permute-start.7 = (f32[20,2048]{1,0:T(8,128)S(1)}, f32[20,2048]{1,0:T(8,128)S(1)}, u32[]{:S(2)}, u32[]{:S(2)}) collective-permute-start(f32[20,2048]{1,0:T(8,128)S(1)} %get-tuple-element.43), channel_id=1, source_target_pairs={{0,15},{1,2},{2,1},{3,4},{4,3},{5,6},{6,5},{7,8},{8,7},{9,10},{10,... | collective-permute-start | bytes 491528 | tf_op jit(solution)/shard_map/ppermute | solution.py:134
  29.8 11.9 %collective-permute-start.4 = (f32[5,4,2048]{2,1,0:T(4,128)S(1)}, f32[5,4,2048]{2,1,0:T(4,128)S(1)}, u32[]{:S(2)}, u32[]{:S(2)}) collective-permute-start(f32[5,4,2048]{2,1,0:T(4,128)S(1)} %get-tuple-element.40), channel_id=1, source_target_pairs={{0,16},{16,0},{32,48},{48,32},{64,80},{80,64},{96,112},{112,96},{1... | collective-permute-start | bytes 491528 | tf_op jit(solution)/shard_map/ppermute | solution.py:131
  29.8 11.9 %collective-permute-start.5 = (f32[5,4,2048]{2,1,0:T(4,128)S(1)}, f32[5,4,2048]{2,1,0:T(4,128)S(1)}, u32[]{:S(2)}, u32[]{:S(2)}) collective-permute-start(f32[5,4,2048]{2,1,0:T(4,128)S(1)} %get-tuple-element.41), channel_id=1, source_target_pairs={{0,112},{16,32},{32,16},{48,64},{64,48},{80,96},{96,80},{112,0},{1... | collective-permute-start | bytes 491528 | tf_op jit(solution)/shard_map/ppermute | solution.py:132
  33.4 1.0 copy-start.2
  34.4 0.9 copy-start.8
  42.8 8.7 %collective-permute-start.10 = (f32[20,2048]{1,0:T(8,128)S(1)}, f32[20,2048]{1,0:T(8,128)S(1)}, u32[]{:S(2)}, u32[]{:S(2)}) collective-permute-start(f32[20,2048]{1,0:T(8,128)S(1)} %get-tuple-element.47), channel_id=1, source_target_pairs={{0,1},{1,0},{2,3},{3,2},{4,5},{5,4},{6,7},{7,6},{8,9},{9,8},{10,11... | collective-permute-start | bytes 491528 | tf_op jit(solution)/shard_map/ppermute | solution.py:133
  43.3 12.6 %collective-permute-start.11 = (f32[20,2048]{1,0:T(8,128)S(1)}, f32[20,2048]{1,0:T(8,128)S(1)}, u32[]{:S(2)}, u32[]{:S(2)}) collective-permute-start(f32[20,2048]{1,0:T(8,128)S(1)} %get-tuple-element.48), channel_id=1, source_target_pairs={{0,15},{1,2},{2,1},{3,4},{4,3},{5,6},{6,5},{7,8},{8,7},{9,10},{10,... | collective-permute-start | bytes 491528 | tf_op jit(solution)/shard_map/ppermute | solution.py:134
  45.3 13.0 %collective-permute-start.8 = (f32[5,4,2048]{2,1,0:T(4,128)S(1)}, f32[5,4,2048]{2,1,0:T(4,128)S(1)}, u32[]{:S(2)}, u32[]{:S(2)}) collective-permute-start(f32[5,4,2048]{2,1,0:T(4,128)S(1)} %get-tuple-element.45), channel_id=1, source_target_pairs={{0,16},{16,0},{32,48},{48,32},{64,80},{80,64},{96,112},{112,96},{1... | collective-permute-start | bytes 491528 | tf_op jit(solution)/shard_map/ppermute | solution.py:131
  46.0 12.2 %collective-permute-start.9 = (f32[5,4,2048]{2,1,0:T(4,128)S(1)}, f32[5,4,2048]{2,1,0:T(4,128)S(1)}, u32[]{:S(2)}, u32[]{:S(2)}) collective-permute-start(f32[5,4,2048]{2,1,0:T(4,128)S(1)} %get-tuple-element.46), channel_id=1, source_target_pairs={{0,112},{16,32},{32,16},{48,64},{64,48},{80,96},{96,80},{112,0},{1... | collective-permute-start | bytes 491528 | tf_op jit(solution)/shard_map/ppermute | solution.py:132
  48.7 1.0 copy-start.3
  49.7 0.9 copy-start.9
  60.4 19.9 %all-to-all-start = ((f32[16,2,40,128]{3,2,1,0:T(8,128)}), f32[16,2,40,128]{3,2,1,0:T(8,128)S(1)}, u32[]{:S(2)}, u32[]{:S(2)}) async-start(f32[16,2,40,128]{3,2,1,0:T(8,128)} %get-tuple-element.50), calls=%async_computation | async-start | bytes 1310720 | tf_op jit(solution)/shard_map/all_to_all | solution.py:510
  68.6 1.0 copy-start.10
  73.2 0.7 copy-start.11
  86.8 2.5 %collective-permute-start.12 = (f32[144,128]{1,0:T(8,128)S(1)}, f32[144,128]{1,0:T(8,128)S(1)}, u32[]{:S(2)}, u32[]{:S(2)}) collective-permute-start(f32[144,128]{1,0:T(8,128)S(1)} %get-tuple-element.54), channel_id=1, source_target_pairs={{0,1},{1,0},{2,3},{3,2},{4,5},{5,4},{6,7},{7,6},{8,9},{9,8},{10,11... | collective-permute-start | bytes 221192 | tf_op jit(solution)/shard_map/ppermute | solution.py:441
  89.3 3.3 %collective-permute-start.13 = (f32[144,128]{1,0:T(8,128)S(1)}, f32[144,128]{1,0:T(8,128)S(1)}, u32[]{:S(2)}, u32[]{:S(2)}) collective-permute-start(f32[144,128]{1,0:T(8,128)S(1)} %add.47), channel_id=1, source_target_pairs={{0,16},{1,17},{2,18},{3,19},{4,20},{5,21},{6,22},{7,23},{8,24},{9,... | collective-permute-start | bytes 221192 | tf_op jit(solution)/shard_map/ppermute | solution.py:443
  92.6 4.5 %collective-permute-start.14 = (f32[144,128]{1,0:T(8,128)S(1)}, f32[144,128]{1,0:T(8,128)S(1)}, u32[]{:S(2)}, u32[]{:S(2)}) collective-permute-start(f32[144,128]{1,0:T(8,128)S(1)} %add.48), channel_id=1, source_target_pairs={{0,18},{1,19},{2,16},{3,17},{4,22},{5,23},{6,20},{7,21},{8,26},{9,... | collective-permute-start | bytes 221192 | tf_op jit(solution)/shard_map/ppermute | solution.py:443
  97.2 3.3 %collective-permute-start.15 = (f32[144,128]{1,0:T(8,128)S(1)}, f32[144,128]{1,0:T(8,128)S(1)}, u32[]{:S(2)}, u32[]{:S(2)}) collective-permute-start(f32[144,128]{1,0:T(8,128)S(1)} %add.49), channel_id=1, source_target_pairs={{0,4},{1,5},{2,6},{3,7},{4,0},{5,1},{6,2},{7,3},{8,12},{9,13},{10,... | collective-permute-start | bytes 221192 | tf_op jit(solution)/shard_map/ppermute | solution.py:443
  100.4 4.5 %collective-permute-start.16 = (f32[144,128]{1,0:T(8,128)S(1)}, f32[144,128]{1,0:T(8,128)S(1)}, u32[]{:S(2)}, u32[]{:S(2)}) collective-permute-start(f32[144,128]{1,0:T(8,128)S(1)} %add.50), channel_id=1, source_target_pairs={{0,12},{1,13},{2,14},{3,15},{4,8},{5,9},{6,10},{7,11},{8,4},{9,5},... | collective-permute-start | bytes 221192 | tf_op jit(solution)/shard_map/ppermute | solution.py:443
  105.0 3.3 %collective-permute-start.17 = (f32[144,128]{1,0:T(8,128)S(1)}, f32[144,128]{1,0:T(8,128)S(1)}, u32[]{:S(2)}, u32[]{:S(2)}) collective-permute-start(f32[144,128]{1,0:T(8,128)S(1)} %add.51), channel_id=1, source_target_pairs={{0,32},{1,33},{2,34},{3,35},{4,36},{5,37},{6,38},{7,39},{8,40},{9,... | collective-permute-start | bytes 221192 | tf_op jit(solution)/shard_map/ppermute | solution.py:443
  108.3 4.5 %collective-permute-start.18 = (f32[144,128]{1,0:T(8,128)S(1)}, f32[144,128]{1,0:T(8,128)S(1)}, u32[]{:S(2)}, u32[]{:S(2)}) collective-permute-start(f32[144,128]{1,0:T(8,128)S(1)} %add.52), channel_id=1, source_target_pairs={{0,96},{1,97},{2,98},{3,99},{4,100},{5,101},{6,102},{7,103},{8,104... | collective-permute-start | bytes 221192 | tf_op jit(solution)/shard_map/ppermute | solution.py:443
  112.8 8.2 %collective-permute-start.19 = (f32[144,128]{1,0:T(8,128)S(1)}, f32[144,128]{1,0:T(8,128)S(1)}, u32[]{:S(2)}, u32[]{:S(2)}) collective-permute-start(f32[144,128]{1,0:T(8,128)S(1)} %add.53.mine_ref), channel_id=1, source_target_pairs={{0,1},{1,0},{2,3},{3,2},{4,5},{5,4},{6,7},{7,6},{8,9},{9,8},{10,11... | collective-permute-start | bytes 221192 | tf_op jit(solution)/shard_map/ppermute | solution.py:444

commit v5 on v4

--- a/solution.py
+++ b/solution.py
@@ -21,7 +21,9 @@
 VMEM = pl.BlockSpec(memory_space=pltpu.VMEM)
 SMEM = pl.BlockSpec(memory_space=pltpu.SMEM)
 HBM = pl.BlockSpec(memory_space=pltpu.HBM)
+ANY = pl.BlockSpec(memory_space=pl.ANY)
 MIB = 1024 * 1024
+BESIDE = 6_000_000_000
 
 
 def call(kernel, outs, scratch=(), flops=0, nbytes=0, ins=(), mib=12, out_space=None):
@@ -52,8 +54,9 @@
     for row in range(F * X):
         cells = get(row)
         head, tail = cells[0:1], cells[3:4]
-        ya_ref[pl.ds(row, 1), :] = jnp.where(odd_y, head, tail)
-        yb_ref[pl.ds(row, 1), :] = jnp.where(odd_y, tail, head)
+        f, x = row // X, row % X
+        ya_ref[f, x : x + 1, :] = jnp.where(odd_y, head, tail)
+        yb_ref[f, x : x + 1, :] = jnp.where(odd_y, tail, head)
 
 
 def edges_kernel(place, u_ref, xa_ref, xb_ref, ya_ref, yb_ref):
@@ -104,7 +107,7 @@
         from_b = jnp.where(odd_y, up, down)
         for f in range(F):
             row = f * X + x
-            new = part_ref[row] + rya[pl.ds(row, 1), :] * from_a + ryb[pl.ds(row, 1), :] * from_b
+            new = part_ref[row] + rya[f, x : x + 1, :] * from_a + ryb[f, x : x + 1, :] * from_b
             if x == X - 1:
                 new = new + jnp.where(odd_x, rxb[f], rxa[f]) * side
             if x == 0:
@@ -117,7 +120,7 @@
         write_edges(get, odd_x, odd_y, *outs)
 
 
-EDGES = [((F, X, 2048), F32)] * 2 + [((F * X, 2048), F32)] * 2
+EDGES = [((F, X, 2048), F32)] * 4
 SLABS = ((16, 2, 2 * F * X, Z), F32)
 
 
@@ -191,7 +194,33 @@
     return y * sig, sig * (1.0 + y * (1.0 - sig))
 
 
-def bands_kernel(w2_ref, fwd_ref, bwd_ref):
+def band_rows(w_ref, flip, out_ref):
+    out_ref[...] = jnp.zeros_like(out_ref)
+    zero = jnp.zeros((1, C), F32)
+    for t in range(TAPS):
+        for f in range(F):
+            for to in range(X):
+                parts = []
+                for x in range(X):
+                    dx = x - to + 1 if flip else to - x + 1
+                    parts.append(w_ref[(f * 3 + dx) * 3 + t // 3, t % 3 : t % 3 + 1, :] if 0 <= dx < 3 else zero)
+                out_ref[pl.ds(t * ROWS + f * X + to, 1), :] = jnp.concatenate(parts, axis=1)
+
+
+def prepare_kernel(*refs):
+    params, outs, rows_ref, held, sems = refs[:6], refs[6:12], refs[12], refs[13:19], refs[19]
+    w1_ref, w2_ref, w3_ref, b1_ref, b2_ref, b3_ref = held
+    w1_out, fwd_ref, bwd_ref, w3_out, w3_turned, bias_ref = outs
+    copies = [pltpu.make_async_copy(params[n], held[n], sems.at[n]) for n in range(6)]
+    for copy in copies:
+        copy.start()
+    for copy in copies:
+        copy.wait()
+    band_rows(w1_ref, False, rows_ref)
+    w1_out[...] = rows_ref[...].T[:, 0:TALL].astype(BF)
+    band_rows(w3_ref, True, rows_ref)
+    w3_out[...] = rows_ref[0:TALL].astype(BF)
+    w3_turned[...] = rows_ref[...].T[:, 0:TALL].astype(BF)
     zero = jnp.zeros((C, C), F32)
     for dy in range(3):
         for dz in range(3):
@@ -205,6 +234,12 @@
             block = jnp.concatenate(rows, axis=0)
             fwd_ref[dy, :, dz * 128 : (dz + 1) * 128] = block.astype(BF)
             bwd_ref[dy, :, dz * 128 : (dz + 1) * 128] = block.T.astype(BF)
+    lane = lax.broadcasted_iota(jnp.int32, (1, 128), 1)
+    third = jnp.zeros((1, 128), F32)
+    for f in range(F):
+        third = jnp.where(lane // X == f, b3_ref[:, f : f + 1], third)
+    rows = [jnp.concatenate([b1_ref[...]] * X, axis=1), jnp.concatenate([b2_ref[...]] * X, axis=1), third]
+    bias_ref[...] = jnp.concatenate(rows + [jnp.zeros((125, 128), F32)], axis=0).T
 
 
 PARTS = 80
@@ -224,8 +259,9 @@
 
 
 def forward_kernel(
-    anchors, slabs_ref, w1_ref, w2_ref, w3_ref, b1_ref, b2_ref, b3_ref, kept_ref, *refs,
+    anchors, slabs_ref, w1_ref, w2_ref, w3_ref, bias_ref, kept_ref, *refs,
 ):
+    b1, b2, b3 = bias_ref[:, 0:1], bias_ref[:, 1:2], bias_ref[0:ROWS, 2:3]
     held, sems, (first_ref, taps_ref, a1_ref) = refs[: len(NAMES)], refs[len(NAMES)], refs[len(NAMES) + 1 :]
     sum_ref, d2_ref, a2_ref, a1_kept, cells_ref, d1_ref = held
     plan = transfers(kept_ref, held, sems)
@@ -242,7 +278,7 @@
         keep("first", p)
         fill_taps(first_ref[p], taps_ref.at[p], 1)
         y1 = dot(w1_ref[...], taps_ref[p])
-        act, slope = activate(y1 + b1_ref[...])
+        act, slope = activate(y1 + b1)
         d1_ref[p] = slope.astype(BF)
         keep("d1", p)
         a1_kept[p] = act.astype(BF)
@@ -250,7 +286,7 @@
         clear_ends(a1_ref.at[p])
         for k in range(PY):
             fill_z(act[:, k * Z : (k + 1) * Z], k, a1_ref.at[p], 1)
-        y2 = b2_ref[...] + dot(w2_ref[0], a1_ref[p, :, 0 : PY * Z])
+        y2 = b2 + dot(w2_ref[0], a1_ref[p, :, 0 : PY * Z])
         for dy in range(1, 3):
             y2 = y2 + dot(w2_ref[dy], a1_ref[p, :, dy * Z : (dy + PY) * Z])
         act, slope = activate(y2)
@@ -261,7 +297,7 @@
         terms = dot(w3_ref[...], a2_ref[p])
         lane = lax.broadcasted_iota(jnp.int32, (ROWS, Z), 1)
         for k in range(PY):
-            out = b3_ref[...] + first_ref[p, :, k * Z : (k + 1) * Z]
+            out = b3 + first_ref[p, :, k * Z : (k + 1) * Z]
             for dz in range(3):
                 part = None
                 for dy in range(3):
@@ -281,6 +317,11 @@
         copy.wait()
 
 
+def half_of(place):
+    gx, gy = place[0], place[1]
+    return (gx // 2 + gx + gy // 4 + gy) % 2
+
+
 def band_sum(full):
     lane = lax.broadcasted_iota(jnp.int32, (C, 256), 1)
     total = None
@@ -316,9 +357,8 @@
     dw1 = jnp.zeros((128, TALL), F32)
     dw3 = jnp.zeros((128, TALL), F32)
     dw2 = [jnp.zeros((128, 384), F32) for _ in range(3)]
-    for name in NAMES[:3]:
-        for p in range(2):
-            copies[name, p].wait()
+    for p in range(2):
+        copies["sum", p].wait()
     for p in range(2):
         live = jnp.where(p < count[0], 1.0, 0.0).astype(F32)
         patch_rows(slabs_ref, anchors[p], last_ref.at[p])
@@ -328,6 +368,10 @@
         err = err * (live * (2.0 / CELLS))
         db3 = db3 + jnp.sum(err, axis=1, keepdims=True)
         fill_taps(err, g_ref.at[p], -1)
+    for name in NAMES[1:]:
+        for p in range(2):
+            copies[name, p].wait()
+    for p in range(2):
         da2 = dot(w3_ref[...], g_ref[p])
         dw3 = dw3 + dot_t(a2_ref[p], g_ref[p])
         dy2 = da2 * d2_ref[p].astype(F32)
@@ -335,10 +379,6 @@
         clear_ends(b_ref.at[p])
         for k in range(PY):
             fill_z(dy2[:, k * Z : (k + 1) * Z], k, b_ref.at[p], -1)
-    for name in NAMES[3:]:
-        for p in range(2):
-            copies[name, p].wait()
-    for p in range(2):
         clear_ends(a1_ref.at[p])
         for k in range(PY):
             fill_z(a1_kept[p, :, k * Z : (k + 1) * Z].astype(F32), k, a1_ref.at[p], 1)
@@ -379,7 +419,7 @@
             if b is not None:
                 total = jnp.where(lane == 127, b, total)
         grads_ref[t * C : (t + 1) * C] = total
-    second = place[1] % 2 == 1
+    second = half_of(place) == 1
     low, high = grads_ref[0:HALF], grads_ref[HALF:]
     keep_ref[...] = jnp.where(second, high, low)
     send_ref[...] = jnp.where(second, low, high)
@@ -388,15 +428,15 @@
 def finish_kernel(
     place, mine_ref, other_ref, g1_ref, gb1_ref, g2_ref, gb2_ref, g3_ref, gb3_ref, loss_ref, grads_ref
 ):
-    second = place[1] % 2 == 1
-    mine, other = mine_ref[...], other_ref[...]
-    grads_ref[0:HALF] = jnp.where(second, other, mine)
-    grads_ref[HALF:] = jnp.where(second, mine, other)
+    second = half_of(place) == 1
+    at = jnp.where(second, HALF, 0)
+    grads_ref[pl.ds(pl.multiple_of(at, 8), HALF)] = mine_ref[...]
+    grads_ref[pl.ds(pl.multiple_of(HALF - at, 8), HALF)] = other_ref[...]
     rows = lambda t: grads_ref[t * C : (t + 1) * C]
-    total = rows(2)[0:1, 126:127]
+    scale = 1.0 / rows(2)[0:1, 126:127]
     for t in range(TAPS):
         dy, dz = t // 3, t % 3
-        block = rows(t) / total
+        block = rows(t) * scale
         for dx in range(3):
             g2_ref[dx * TAPS + t] = block[:, dx * C : (dx + 1) * C]
         turned = block.T
@@ -415,7 +455,7 @@
             loss_ref[...] = turned[127:128, 0:1]
 
 
-def reduce_steps():
+def reduce_steps(order):
     def near(c):
         return c ^ 1
 
@@ -428,9 +468,9 @@
         for gx in range(8):
             for gy in range(16):
                 at = {"x": gx // 2, "y": gy // 4, "z": (gy // 2 % 2) * 2 + gx % 2}
-                axis = "zyx"[n // 2]
+                axis = order[n // 2]
                 at[axis] = (near, far)[n % 2](at[axis])
-                to = (at["x"] * 2 + at["z"] % 2) * 16 + at["y"] * 4 + (at["z"] // 2) * 2 + gy % 2
+                to = (at["x"] * 2 + at["z"] % 2) * 16 + at["y"] * 4 + (at["z"] // 2) * 2 + (gy + 1) % 2
                 pairs.append((gx * 16 + gy, to))
         steps.append(pairs)
     return steps
@@ -439,24 +479,12 @@
 def sum_all(keep, send):
     cores = [(i, i ^ 1) for i in range(16)]
     mine = keep + lax.ppermute(send, "gy", cores)
-    for pairs in reduce_steps():
-        mine = mine + lax.ppermute(mine, ("gx", "gy"), pairs)
+    parts = [mine[: HALF // 2], mine[HALF // 2 :]]
+    for pairs in zip(reduce_steps("zyx"), reduce_steps("xzy")):
+        moved = [lax.ppermute(part, ("gx", "gy"), p) for part, p in zip(parts, pairs)]
+        parts = [part + m for part, m in zip(parts, moved)]
+    mine = jnp.concatenate(parts)
     return mine, lax.ppermute(mine, "gy", cores)
-
-
-def banded(w, flip):
-    bands = []
-    for x in range(X):
-        if flip:
-            w_ = w[:, ::-1]
-        else:
-            w_ = w
-        padded = jnp.pad(w_, ((0, 0), (x, X - 1 - x), (0, 0), (0, 0), (0, 0)))
-        bands.append(padded[:, 1 : X + 1])
-    all_x = jnp.stack(bands, axis=4)
-    rows = jnp.transpose(all_x, (2, 3, 0, 1, 4, 5)).reshape(TAPS, F * X, X * C)
-    rows = jnp.pad(rows, ((0, 0), (0, ROWS - F * X), (0, 0))).reshape(TAPS * ROWS, X * C)
-    return jnp.pad(rows, ((0, TALL - TAPS * ROWS), (0, 0))).astype(BF)
 
 
 def on_device(
@@ -470,24 +498,40 @@
     count = patch_count.reshape(1)
 
     edges = call(edges_kernel, EDGES, ins=[SMEM, VMEM], nbytes=1_000_000)(place, u)
+    params = (
+        jnp.transpose(weight_one, (1, 2, 3, 4, 0)).reshape(45, 3, C),
+        jnp.transpose(weight_two, (2, 3, 4, 0, 1)).reshape(27, C, C),
+        jnp.transpose(weight_three, (0, 2, 3, 4, 1)).reshape(45, 3, C),
+        bias_one.reshape(1, C),
+        bias_two.reshape(1, C),
+        bias_three.reshape(1, F),
+    )
     (slabs,) = call(slabs_kernel, [SLABS], ins=[VMEM], nbytes=1_500_000)(u)
     first_slabs = lax.all_to_all(slabs, "gy", 0, 0, tiled=True).reshape(32, 2 * F * X, Z)
-
-    w2 = jnp.transpose(weight_two, (2, 3, 4, 0, 1)).reshape(27, C, C)
-    w2_fwd, w2_bwd = call(bands_kernel, [((3, 128, 384), BF)] * 2, ins=[VMEM], nbytes=1_000_000)(w2)
-    w1_band = banded(jnp.transpose(weight_one, (1, 2, 3, 4, 0)), False)
-    w3_band = banded(jnp.transpose(weight_three, (0, 2, 3, 4, 1)), True)
-    b1 = jnp.tile(bias_one, X).reshape(128, 1)
-    b2 = jnp.tile(bias_two, X).reshape(128, 1)
-    b3 = jnp.pad(jnp.repeat(bias_three, X), (0, ROWS - F * X)).reshape(ROWS, 1)
+    w1_band, w2_fwd, w2_bwd, w3_band, w3_turned, biases = call(
+        prepare_kernel,
+        [
+            ((128, TALL), BF),
+            ((3, 128, 384), BF),
+            ((3, 128, 384), BF),
+            ((TALL, 128), BF),
+            ((128, TALL), BF),
+            ((128, 128), F32),
+        ],
+        scratch=[pltpu.VMEM((256, 128), F32)]
+        + [pltpu.VMEM(p.shape, F32) for p in params]
+        + [pltpu.SemaphoreType.DMA((len(params),))],
+        ins=[ANY] * len(params),
+        nbytes=1_000_000,
+    )(*params)
 
     for step in range(STEPS):
         last = step == STEPS - 1
         outs = [((F * X, 4, 2048), F32)] + ([SLABS] if last else EDGES)
         received = exchange(edges)
-        (part,) = call(inner_kernel, [((F * X, 4, 2048), F32)], ins=[VMEM] * 3, nbytes=4_000_000)(u, vel, diffusivity)
+        (part,) = call(inner_kernel, [((F * X, 4, 2048), F32)], ins=[VMEM] * 3, nbytes=4_000_000, flops=BESIDE)(u, vel, diffusivity)
         kernel = lambda *refs, last=last: outer_kernel(last, *refs)
-        u, *edges = call(kernel, outs, ins=[SMEM] + [VMEM] * 7, nbytes=3_000_000)(
+        u, *edges = call(kernel, outs, ins=[SMEM] + [VMEM] * 7, nbytes=3_000_000, flops=BESIDE)(
             place, part, *received, vel, diffusivity
         )
 
@@ -500,12 +544,12 @@
             pltpu.VMEM((2, TALL, PY * Z), BF),
             pltpu.VMEM((2, 384, (PY + 2) * Z), BF),
         ],
-        ins=[SMEM] + [VMEM] * 7,
+        ins=[SMEM] + [VMEM] * 5,
         flops=2_000_000_000,
         nbytes=8_000_000,
         mib=24,
         out_space=HBM,
-    )(anchors, first_slabs, w1_band.T, w2_fwd, w3_band, b1, b2, b3)
+    )(anchors, first_slabs, w1_band, w2_fwd, w3_band, biases)
 
     last_slabs = lax.all_to_all(edges[0], "gy", 0, 0, tiled=True).reshape(32, 2 * F * X, Z)
     keep, send = call(
@@ -524,7 +568,7 @@
         flops=4_000_000_000,
         nbytes=10_000_000,
         mib=24,
-    )(place, anchors, count, last_slabs, w2_bwd, w3_band.T, kept)
+    )(place, anchors, count, last_slabs, w2_bwd, w3_turned, kept)
 
     g1, gb1, g2, gb2, g3, gb3, loss = call(
         finish_kernel,

time: 124 us -> 116 us (0.935)
  local copies, waits for them, and re-layouts: 15.7 us -> 6 us
  waiting for transfers between devices: 36.5 us -> 42 us
  starting transfers between devices: 45.2 us -> 43.2 us
  other arithmetic: 1.55 us -> 0.17 us
    ppermute x6 -> x12, starting transfers between devices: 2.85 us -> 10.3 us  [sum_all(): lax.ppermute(part, ('gx', 'gy'), p)]
    ppermute x1, starting transfers between devices: 7.33 us -> 0.47 us  [sum_all(): return (mine, lax.ppermute(mine, 'gy', cores))]
    unnamed x27 -> x26, local copies, waits for them, and re-layouts: 11.5 us -> 6 us
    ppermute x6 -> x12, waiting for transfers between devices: 20.5 us -> 15.8 us  [sum_all(): lax.ppermute(part, ('gx', 'gy'), p)]
    ppermute x3, waiting for transfers between devices: 9.76 us -> 13.4 us  [exchange(): lax.ppermute(yb, 'gy', pairs(16, True))]
    all_to_all x1, waiting for transfers between devices: 2.07 us -> 5.46 us  [on_device(): lax.all_to_all(edges[0], 'gy', 0, 0, tiled=True).reshape(32, 2 * F * X, Z)]
    ppermute x3, waiting for transfers between devices: 2.37 us -> 5.46 us  [exchange(): lax.ppermute(xa, 'gx', pairs(8, False))]
    another operation x6 -> x0, local copies, waits for them, and re-layouts: 1.66 us -> none  [the longest x2 0.76 us: on_device(): b2 = jnp.tile(bias_two, X).reshape(128, 1)]
  transfers between devices with their start and end apart: 22 -> 28, of which waited for: 13 -> 17; matrix products, arithmetic and copies ran while one was open for 5% -> 0% of each run, Pallas kernels for 11% -> 12%
where the time goes in v5:
time: 116 us
  starting transfers between devices  43.2 us (37%)
  waiting for transfers between devices  42 us (36%)
  Pallas kernels  23 us (20%)
  local copies, waits for them, and re-layouts  6 us (5%)
  between operations  1.56 us (1%)
    ppermute x12, waiting for transfers between devices, sum_all(): lax.ppermute(part, ('gx', 'gy'), p)  15.8 us
    ppermute x3, waiting for transfers between devices, exchange(): lax.ppermute(yb, 'gy', pairs(16, True))  13.4 us
    ppermute x12, starting transfers between devices, sum_all(): lax.ppermute(part, ('gx', 'gy'), p)  10.3 us
    ppermute x3, starting transfers between devices, exchange(): lax.ppermute(yb, 'gy', pairs(16, True))  7.72 us
    all_to_all x1, starting transfers between devices, on_device(): lax.all_to_all(edges[0], 'gy', 0, 0, tiled=True).reshape(32, 2 * F * X, Z)  6.46 us
    all_to_all x1, starting transfers between devices, on_device(): lax.all_to_all(slabs, 'gy', 0, 0, tiled=True).reshape(32, 2 * F * X, Z)  6.34 us
    pallas_call x1, Pallas kernels, on_device(): call(backward_kernel, [((HALF, 128), F32)] * 2, scratch=HELD + [pltpu.VME...  6.33 us
    unnamed x26, local copies, waits for them, and re-layouts  6 us
  transfers between devices with their start and end apart: 28, of which 17 were waited for; matrix products, arithmetic and copies ran while one was open for 0% of the time, Pallas kernels for 12%

profile of v5, /device:TPU:1, one launch (start us, length us, event | category | flops | bytes accessed | tf_op | source)
XLA Modules:
  0.0 115.9 jit_solution(10673852197917707792)
XLA Ops:
  0.7 1.1 copy-done
  1.8 0.7 shard_map.171
  2.6 2.5 %collective-permute-start = (f32[5,4,2048]{2,1,0:T(4,128)S(1)}, f32[5,4,2048]{2,1,0:T(4,128)S(1)}, u32[]{:S(2)}, u32[]{:S(2)}) collective-permute-start(f32[5,4,2048]{2,1,0:T(4,128)S(1)} %get-tuple-element.39), channel_id=1, source_target_pairs={{0,16},{16,0},{32,48},{48,32},{64,80},{80,64},{96,112},{112,96},{1... | collective-permute-start | bytes 491528 | tf_op jit(solution)/shard_map/ppermute | solution.py:134
  5.1 2.3 %collective-permute-start.1 = (f32[5,4,2048]{2,1,0:T(4,128)S(1)}, f32[5,4,2048]{2,1,0:T(4,128)S(1)}, u32[]{:S(2)}, u32[]{:S(2)}) collective-permute-start(f32[5,4,2048]{2,1,0:T(4,128)S(1)} %get-tuple-element.40), channel_id=1, source_target_pairs={{0,112},{16,32},{32,16},{48,64},{64,48},{80,96},{96,80},{112,0},{1... | collective-permute-start | bytes 491528 | tf_op jit(solution)/shard_map/ppermute | solution.py:135
  7.4 1.0 collective-permute-start.2
  8.4 3.5 %collective-permute-start.3 = (f32[5,4,2048]{2,1,0:T(4,128)S(1)}, f32[5,4,2048]{2,1,0:T(4,128)S(1)}, u32[]{:S(2)}, u32[]{:S(2)}) collective-permute-start(f32[5,4,2048]{2,1,0:T(4,128)S(1)} %get-tuple-element.42), channel_id=1, source_target_pairs={{0,15},{1,2},{2,1},{3,4},{4,3},{5,6},{6,5},{7,8},{8,7},{9,10},{10,... | collective-permute-start | bytes 491528 | tf_op jit(solution)/shard_map/ppermute | solution.py:137
  11.8 1.2 %shard_map.178 = f32[16,2,40,128]{3,2,1,0:T(8,128)} custom-call(f32[20,4,2048]{2,1,0:T(4,128)S(1)} %bitcast.37), custom_call_target="tpu_custom_call" | custom-call | bytes 1500000 | tf_op jit(solution)/shard_map/pallas_call | solution.py:509
  13.0 6.3 %all-to-all-start.1 = ((f32[16,2,40,128]{3,2,1,0:T(8,128)}), f32[16,2,40,128]{3,2,1,0:T(8,128)S(1)}, u32[]{:S(2)}, u32[]{:S(2)}) async-start(f32[16,2,40,128]{3,2,1,0:T(8,128)} %shard_map.178), calls=%async_computation.1 | async-start | bytes 1310720 | tf_op jit(solution)/shard_map/all_to_all | solution.py:510
  19.4 1.1 copy-done.1
  20.5 1.0 copy-done.9
  21.5 0.9 copy-done.11
  22.4 0.9 shard_map.170.refs_1_
  23.4 1.0 copy-done.10
  24.4 0.9 copy-done.12
  25.3 1.0 shard_map.172
  26.4 1.7 %collective-permute-start.5 = (f32[5,4,2048]{2,1,0:T(4,128)S(1)}, f32[5,4,2048]{2,1,0:T(4,128)S(1)}, u32[]{:S(2)}, u32[]{:S(2)}) collective-permute-start(f32[5,4,2048]{2,1,0:T(4,128)S(1)} %get-tuple-element.45), channel_id=1, source_target_pairs={{0,112},{16,32},{32,16},{48,64},{64,48},{80,96},{96,80},{112,0},{1... | collective-permute-start | bytes 491528 | tf_op jit(solution)/shard_map/ppermute | solution.py:135
  28.1 0.8 collective-permute-start.6
  28.9 2.9 %collective-permute-start.7 = (f32[5,4,2048]{2,1,0:T(4,128)S(1)}, f32[5,4,2048]{2,1,0:T(4,128)S(1)}, u32[]{:S(2)}, u32[]{:S(2)}) collective-permute-start(f32[5,4,2048]{2,1,0:T(4,128)S(1)} %get-tuple-element.47), channel_id=1, source_target_pairs={{0,15},{1,2},{2,1},{3,4},{4,3},{5,6},{6,5},{7,8},{8,7},{9,10},{10,... | collective-permute-start | bytes 491528 | tf_op jit(solution)/shard_map/ppermute | solution.py:137
  31.8 0.9 shard_map.173.refs_1_
  32.7 5.5 %collective-permute-done.4.refs_2_ = f32[5,4,2048]{2,1,0:T(4,128)S(1)} collective-permute-done((f32[5,4,2048]{2,1,0:T(4,128)S(1)}, f32[5,4,2048]{2,1,0:T(4,128)S(1)}, u32[]{:S(2)}, u32[]{:S(2)}) %collective-permute-start.4) | collective-permute-done | bytes 163872 | tf_op jit(solution)/shard_map/ppermute | solution.py:134
  38.2 4.4 %collective-permute-done.7.refs_5_ = f32[5,4,2048]{2,1,0:T(4,128)S(1)} collective-permute-done((f32[5,4,2048]{2,1,0:T(4,128)S(1)}, f32[5,4,2048]{2,1,0:T(4,128)S(1)}, u32[]{:S(2)}, u32[]{:S(2)}) %collective-permute-start.7) | collective-permute-done | bytes 163872 | tf_op jit(solution)/shard_map/ppermute | solution.py:137
  42.6 1.0 shard_map.174
  43.7 1.3 %collective-permute-start.11 = (f32[5,4,2048]{2,1,0:T(4,128)S(1)}, f32[5,4,2048]{2,1,0:T(4,128)S(1)}, u32[]{:S(2)}, u32[]{:S(2)}) collective-permute-start(f32[5,4,2048]{2,1,0:T(4,128)S(1)} %get-tuple-element.52), channel_id=1, source_target_pairs={{0,15},{1,2},{2,1},{3,4},{4,3},{5,6},{6,5},{7,8},{8,7},{9,10},{10,... | collective-permute-start | bytes 491528 | tf_op jit(solution)/shard_map/ppermute | solution.py:137
  45.0 1.8 %collective-permute-start.9 = (f32[5,4,2048]{2,1,0:T(4,128)S(1)}, f32[5,4,2048]{2,1,0:T(4,128)S(1)}, u32[]{:S(2)}, u32[]{:S(2)}) collective-permute-start(f32[5,4,2048]{2,1,0:T(4,128)S(1)} %get-tuple-element.50), channel_id=1, source_target_pairs={{0,112},{16,32},{32,16},{48,64},{64,48},{80,96},{96,80},{112,0},{1... | collective-permute-start | bytes 491528 | tf_op jit(solution)/shard_map/ppermute | solution.py:135
  46.8 0.9 shard_map.175.refs_1_
  47.7 9.0 %collective-permute-done.11.refs_5_ = f32[5,4,2048]{2,1,0:T(4,128)S(1)} collective-permute-done((f32[5,4,2048]{2,1,0:T(4,128)S(1)}, f32[5,4,2048]{2,1,0:T(4,128)S(1)}, u32[]{:S(2)}, u32[]{:S(2)}) %collective-permute-start.11) | collective-permute-done | bytes 163872 | tf_op jit(solution)/shard_map/ppermute | solution.py:137
  56.7 2.1 %shard_map.176 = (f32[20,4,2048]{2,1,0:T(4,128)}, f32[16,2,40,128]{3,2,1,0:T(8,128)}) custom-call(s32[2]{0:T(128)S(1)} %pad_add_fusion.place.refs_0_, f32[20,4,2048]{2,1,0:T(4,128)S(1)} %shard_map.175.refs_1_, f32[5,4,2048]{2,1,0:T(4,128)S(1)} %collective-permute-done.8.refs_2_, f32[5,4,2048]{2,1,0:T(4,128)S(1)} %collective-permute-done.9.refs_3_, ...), custom_call_target="tpu_custom_call" | custom-call | flops 6000000000 | bytes 3000000 | tf_op jit(solution)/shard_map/pallas_call | solution.py:534
  58.8 6.5 %all-to-all-start = ((f32[16,2,40,128]{3,2,1,0:T(8,128)}), f32[16,2,40,128]{3,2,1,0:T(8,128)S(1)}, u32[]{:S(2)}, u32[]{:S(2)}) async-start(f32[16,2,40,128]{3,2,1,0:T(8,128)} %get-tuple-element.54), calls=%async_computation | async-start | bytes 1310720 | tf_op jit(solution)/shard_map/all_to_all | solution.py:554
  66.0 1.7 %shard_map.177 = (bf16[128,224]{1,0:T(8,128)(2,1)S(1)}, bf16[3,128,384]{2,1,0:T(8,128)(2,1)S(1)}, bf16[3,128,384]{2,1,0:T(8,128)(2,1)S(1)}, bf16[224,128]{1,0:T(...) custom-call(f32[45,3,32]{2,1,0:T(4,128)S(1)} %bitcast.41, f32[27,32,32]{2,1,0:T(8,128)S(1)} %bitcast.40, ...), custom_call_target="tpu_custom_call" | custom-call | bytes 1000000 | tf_op jit(solution)/shard_map/pallas_call | solution.py:511
  67.7 4.4 %shard_map.179.kept_ref = bf16[2,16384,1024]{2,1,0:T(8,128)(2,1)} custom-call(s32[2]{0:T(128)S(1)} %bitcast.43, f32[32,40,128]{2,1,0:T(8,128)S(1)} %bitcast.39, bf16[128,224]{1,0:T(8,128)(2,1)S(1)} %get-tuple-element.57.w1_ref, bf16[3,128,384]{2,1,0:T(8,128)(2,1)S(1)} %get-tuple-element.58.w2_ref, bf16[224,128]{1,0:T(8,128)(2,1)S(1)} %get-tuple-element.59.w3_ref, ...), custom_call_target="tpu_custom_call" | custom-call | flops 2000000000 | bytes 8000000 | tf_op jit(solution)/shard_map/pallas_call | solution.py:538
  72.1 5.5 %all-to-all-done = f32[16,2,40,128]{3,2,1,0:T(8,128)S(1)} async-done(((f32[16,2,40,128]{3,2,1,0:T(8,128)}), f32[16,2,40,128]{3,2,1,0:T(8,128)S(1)}, u32[]{:S(2)}, u32[]{:S(2)}) %all-to-all-start) | async-done | bytes 655392 | tf_op jit(solution)/shard_map/all_to_all | solution.py:554
  77.6 6.3 %shard_map.180 = (f32[144,128]{1,0:T(8,128)S(1)}, f32[144,128]{1,0:T(8,128)S(1)}) custom-call(s32[2]{0:T(128)S(1)} %pad_add_fusion.place.refs_0_, s32[2]{0:T(128)S(1)} %bitcast.44, s32[1]{0:T(128)} %bitcast.34.count, f32[32,40,128]{2,1,0:T(8,128)S(1)} %bitcast.35, bf16[3,128,384]{2,1,0:T(8,128)(2,1)S(1)} %get-tuple-element.55.w2_ref, ...), custom_call_target="tpu_custom_call" | custom-call | flops 4000000000 | bytes 10000000 | tf_op jit(solution)/shard_map/pallas_call | solution.py:555
  83.9 1.6 %collective-permute-start.12 = (f32[144,128]{1,0:T(8,128)S(1)}, f32[144,128]{1,0:T(8,128)S(1)}, u32[]{:S(2)}, u32[]{:S(2)}) collective-permute-start(f32[144,128]{1,0:T(8,128)S(1)} %get-tuple-element.62), channel_id=1, source_target_pairs={{0,1},{1,0},{2,3},{3,2},{4,5},{5,4},{6,7},{7,6},{8,9},{9,8},{10,11... | collective-permute-start | bytes 221192 | tf_op jit(solution)/shard_map/ppermute | solution.py:481
  85.6 0.9 collective-permute-done.12
  86.8 0.8 collective-permute-start.19
  87.5 2.5 %collective-permute-done.13 = f32[72,128]{1,0:T(8,128)S(1)} collective-permute-done((f32[72,128]{1,0:T(8,128)S(1)}, f32[72,128]{1,0:T(8,128)S(1)}, u32[]{:S(2)}, u32[]{:S(2)}) %collective-permute-start.13) | collective-permute-done | bytes 36896 | tf_op jit(solution)/shard_map/ppermute | solution.py:484
  91.6 3.5 %collective-permute-done.14 = f32[72,128]{1,0:T(8,128)S(1)} collective-permute-done((f32[72,128]{1,0:T(8,128)S(1)}, f32[72,128]{1,0:T(8,128)S(1)}, u32[]{:S(2)}, u32[]{:S(2)}) %collective-permute-start.14) | collective-permute-done | bytes 36896 | tf_op jit(solution)/shard_map/ppermute | solution.py:484
  95.5 1.0 collective-permute-start.21
  96.5 2.2 %collective-permute-done.15 = f32[72,128]{1,0:T(8,128)S(1)} collective-permute-done((f32[72,128]{1,0:T(8,128)S(1)}, f32[72,128]{1,0:T(8,128)S(1)}, u32[]{:S(2)}, u32[]{:S(2)}) %collective-permute-start.15) | collective-permute-done | bytes 36896 | tf_op jit(solution)/shard_map/ppermute | solution.py:484
  99.0 2.2 %collective-permute-start.22 = (f32[72,128]{1,0:T(8,128)S(1)}, f32[72,128]{1,0:T(8,128)S(1)}, u32[]{:S(2)}, u32[]{:S(2)}) collective-permute-start(f32[72,128]{1,0:T(8,128)S(1)} %add.48), channel_id=1, source_target_pairs={{0,19},{1,18},{2,17},{3,16},{4,23},{5,22},{6,21},{7,20},{8,27},{9,... | collective-permute-start | bytes 110600 | tf_op jit(solution)/shard_map/ppermute | solution.py:484
  101.2 2.1 %collective-permute-done.16 = f32[72,128]{1,0:T(8,128)S(1)} collective-permute-done((f32[72,128]{1,0:T(8,128)S(1)}, f32[72,128]{1,0:T(8,128)S(1)}, u32[]{:S(2)}, u32[]{:S(2)}) %collective-permute-start.16) | collective-permute-done | bytes 36896 | tf_op jit(solution)/shard_map/ppermute | solution.py:484
  104.2 1.2 collective-permute-start.23
  105.3 1.3 %collective-permute-done.17 = f32[72,128]{1,0:T(8,128)S(1)} collective-permute-done((f32[72,128]{1,0:T(8,128)S(1)}, f32[72,128]{1,0:T(8,128)S(1)}, u32[]{:S(2)}, u32[]{:S(2)}) %collective-permute-start.17) | collective-permute-done | bytes 36896 | tf_op jit(solution)/shard_map/ppermute | solution.py:484
  108.0 2.2 %collective-permute-start.24 = (f32[72,128]{1,0:T(8,128)S(1)}, f32[72,128]{1,0:T(8,128)S(1)}, u32[]{:S(2)}, u32[]{:S(2)}) collective-permute-start(f32[72,128]{1,0:T(8,128)S(1)} %add.50), channel_id=1, source_target_pairs={{0,13},{1,12},{2,15},{3,14},{4,9},{5,8},{6,11},{7,10},{8,5},{9,4},... | collective-permute-start | bytes 110600 | tf_op jit(solution)/shard_map/ppermute | solution.py:484
  110.2 1.1 collective-permute-done.18
  111.3 1.4 %collective-permute-done.24 = f32[72,128]{1,0:T(8,128)S(1)} collective-permute-done((f32[72,128]{1,0:T(8,128)S(1)}, f32[72,128]{1,0:T(8,128)S(1)}, u32[]{:S(2)}, u32[]{:S(2)}) %collective-permute-start.24) | collective-permute-done | bytes 36896 | tf_op jit(solution)/shard_map/ppermute | solution.py:484
  113.2 0.9 collective-permute-done.25.other_ref
  114.1 1.8 %shard_map.181 = (f32[45,3,32]{2,1,0:T(4,128)}, f32[1,32]{1,0:T(1,128)}, f32[27,32,32]{2,1,0:T(8,128)}, f32[1,32]{1,0:T(1,128)}, f32[45,3,32]{2,1,0:T(4,128)}, /*index=5*/f32[1,5]{1,0:T(1,128)}, f32[1,1]{1,0:T(1,128)}) custom-call(s32[2]{0:T(128)S(1)} %pad_add_fusion.place.refs_0_, f32[144,128]{1,0:T(8,128)S(1)} %pad_maximum_fusion.mine_ref, ...), custom_call_target="tpu_custom_call" | custom-call | bytes 1000000 | tf_op jit(solution)/shard_map/pallas_call | solution.py:573
  (61 shorter events, 5.5 us)
Async XLA Ops:
  0.7 1.1 copy-start
  2.6 20.8 %collective-permute-start = (f32[5,4,2048]{2,1,0:T(4,128)S(1)}, f32[5,4,2048]{2,1,0:T(4,128)S(1)}, u32[]{:S(2)}, u32[]{:S(2)}) collective-permute-start(f32[5,4,2048]{2,1,0:T(4,128)S(1)} %get-tuple-element.39), channel_id=1, source_target_pairs={{0,16},{16,0},{32,48},{48,32},{64,80},{80,64},{96,112},{112,96},{1... | collective-permute-start | bytes 491528 | tf_op jit(solution)/shard_map/ppermute | solution.py:134
  5.1 18.2 %collective-permute-start.1 = (f32[5,4,2048]{2,1,0:T(4,128)S(1)}, f32[5,4,2048]{2,1,0:T(4,128)S(1)}, u32[]{:S(2)}, u32[]{:S(2)}) collective-permute-start(f32[5,4,2048]{2,1,0:T(4,128)S(1)} %get-tuple-element.40), channel_id=1, source_target_pairs={{0,112},{16,32},{32,16},{48,64},{64,48},{80,96},{96,80},{112,0},{1... | collective-permute-start | bytes 491528 | tf_op jit(solution)/shard_map/ppermute | solution.py:135
  7.4 15.9 %collective-permute-start.2 = (f32[5,4,2048]{2,1,0:T(4,128)S(1)}, f32[5,4,2048]{2,1,0:T(4,128)S(1)}, u32[]{:S(2)}, u32[]{:S(2)}) collective-permute-start(f32[5,4,2048]{2,1,0:T(4,128)S(1)} %get-tuple-element.41), channel_id=1, source_target_pairs={{0,1},{1,0},{2,3},{3,2},{4,5},{5,4},{6,7},{7,6},{8,9},{9,8},{10,11... | collective-permute-start | bytes 491528 | tf_op jit(solution)/shard_map/ppermute | solution.py:136
  8.4 15.0 %collective-permute-start.3 = (f32[5,4,2048]{2,1,0:T(4,128)S(1)}, f32[5,4,2048]{2,1,0:T(4,128)S(1)}, u32[]{:S(2)}, u32[]{:S(2)}) collective-permute-start(f32[5,4,2048]{2,1,0:T(4,128)S(1)} %get-tuple-element.42), channel_id=1, source_target_pairs={{0,15},{1,2},{2,1},{3,4},{4,3},{5,6},{6,5},{7,8},{8,7},{9,10},{10,... | collective-permute-start | bytes 491528 | tf_op jit(solution)/shard_map/ppermute | solution.py:137
  13.0 45.8 %all-to-all-start.1 = ((f32[16,2,40,128]{3,2,1,0:T(8,128)}), f32[16,2,40,128]{3,2,1,0:T(8,128)S(1)}, u32[]{:S(2)}, u32[]{:S(2)}) async-start(f32[16,2,40,128]{3,2,1,0:T(8,128)} %shard_map.178), calls=%async_computation.1 | async-start | bytes 1310720 | tf_op jit(solution)/shard_map/all_to_all | solution.py:510
  19.4 1.1 copy-start.1
  20.5 1.0 copy-start.9
  21.5 0.9 copy-start.11
  22.4 43.6 %copy-start.2 = (f32[32,32,3,3,3]{1,0,4,3,2:T(8,128)S(1)}, f32[32,32,3,3,3]{1,0,4,3,2:T(8,128)}, u32[]{:S(2)}) copy-start(f32[32,32,3,3,3]{1,0,4,3,2:T(8,128)} %param.18) | copy-start | bytes 331780
  22.4 43.6 %copy-start.3 = (f32[32,5,3,3,3]{0,4,3,2,1:T(4,128)S(1)}, f32[32,5,3,3,3]{0,4,3,2,1:T(4,128)}, u32[]{:S(2)}) copy-start(f32[32,5,3,3,3]{0,4,3,2,1:T(4,128)} %param.16) | copy-start | bytes 51844
  22.4 43.6 %copy-start.4 = (f32[5,32,3,3,3]{1,4,3,2,0:T(4,128)S(1)}, f32[5,32,3,3,3]{1,4,3,2,0:T(4,128)}, u32[]{:S(2)}) copy-start(f32[5,32,3,3,3]{1,4,3,2,0:T(4,128)} %param.20) | copy-start | bytes 51844
  22.4 43.6 %copy-start.6 = (f32[32]{0:T(128)S(1)}, f32[32]{0:T(128)}, u32[]{:S(2)}) copy-start(f32[32]{0:T(128)} %param.17) | copy-start | bytes 388
  22.4 43.6 %copy-start.7 = (f32[32]{0:T(128)S(1)}, f32[32]{0:T(128)}, u32[]{:S(2)}) copy-start(f32[32]{0:T(128)} %param.19) | copy-start | bytes 388
  22.4 43.6 %copy-start.8 = (f32[5]{0:T(128)S(1)}, f32[5]{0:T(128)}, u32[]{:S(2)}) copy-start(f32[5]{0:T(128)} %param.21) | copy-start | bytes 64
  22.4 45.3 %copy-start.5 = (s32[1,1,2]{2,1,0:T(1,128)S(1)}, s32[1,1,2]{2,1,0:T(1,128)}, u32[]{:S(2)}) copy-start(s32[1,1,2]{2,1,0:T(1,128)} %param.14) | copy-start | bytes 28
  23.4 1.0 copy-start.10
  24.4 0.9 copy-start.12
  26.3 11.9 %collective-permute-start.4 = (f32[5,4,2048]{2,1,0:T(4,128)S(1)}, f32[5,4,2048]{2,1,0:T(4,128)S(1)}, u32[]{:S(2)}, u32[]{:S(2)}) collective-permute-start(f32[5,4,2048]{2,1,0:T(4,128)S(1)} %get-tuple-element.44), channel_id=1, source_target_pairs={{0,16},{16,0},{32,48},{48,32},{64,80},{80,64},{96,112},{112,96},{1... | collective-permute-start | bytes 491528 | tf_op jit(solution)/shard_map/ppermute | solution.py:134
  26.4 11.8 %collective-permute-start.5 = (f32[5,4,2048]{2,1,0:T(4,128)S(1)}, f32[5,4,2048]{2,1,0:T(4,128)S(1)}, u32[]{:S(2)}, u32[]{:S(2)}) collective-permute-start(f32[5,4,2048]{2,1,0:T(4,128)S(1)} %get-tuple-element.45), channel_id=1, source_target_pairs={{0,112},{16,32},{32,16},{48,64},{64,48},{80,96},{96,80},{112,0},{1... | collective-permute-start | bytes 491528 | tf_op jit(solution)/shard_map/ppermute | solution.py:135
  28.1 10.1 %collective-permute-start.6 = (f32[5,4,2048]{2,1,0:T(4,128)S(1)}, f32[5,4,2048]{2,1,0:T(4,128)S(1)}, u32[]{:S(2)}, u32[]{:S(2)}) collective-permute-start(f32[5,4,2048]{2,1,0:T(4,128)S(1)} %get-tuple-element.46), channel_id=1, source_target_pairs={{0,1},{1,0},{2,3},{3,2},{4,5},{5,4},{6,7},{7,6},{8,9},{9,8},{10,11... | collective-permute-start | bytes 491528 | tf_op jit(solution)/shard_map/ppermute | solution.py:136
  28.9 13.7 %collective-permute-start.7 = (f32[5,4,2048]{2,1,0:T(4,128)S(1)}, f32[5,4,2048]{2,1,0:T(4,128)S(1)}, u32[]{:S(2)}, u32[]{:S(2)}) collective-permute-start(f32[5,4,2048]{2,1,0:T(4,128)S(1)} %get-tuple-element.47), channel_id=1, source_target_pairs={{0,15},{1,2},{2,1},{3,4},{4,3},{5,6},{6,5},{7,8},{8,7},{9,10},{10,... | collective-permute-start | bytes 491528 | tf_op jit(solution)/shard_map/ppermute | solution.py:137
  43.6 4.1 %collective-permute-start.10 = (f32[5,4,2048]{2,1,0:T(4,128)S(1)}, f32[5,4,2048]{2,1,0:T(4,128)S(1)}, u32[]{:S(2)}, u32[]{:S(2)}) collective-permute-start(f32[5,4,2048]{2,1,0:T(4,128)S(1)} %get-tuple-element.51), channel_id=1, source_target_pairs={{0,1},{1,0},{2,3},{3,2},{4,5},{5,4},{6,7},{7,6},{8,9},{9,8},{10,11... | collective-permute-start | bytes 491528 | tf_op jit(solution)/shard_map/ppermute | solution.py:136
  43.7 13.0 %collective-permute-start.11 = (f32[5,4,2048]{2,1,0:T(4,128)S(1)}, f32[5,4,2048]{2,1,0:T(4,128)S(1)}, u32[]{:S(2)}, u32[]{:S(2)}) collective-permute-start(f32[5,4,2048]{2,1,0:T(4,128)S(1)} %get-tuple-element.52), channel_id=1, source_target_pairs={{0,15},{1,2},{2,1},{3,4},{4,3},{5,6},{6,5},{7,8},{8,7},{9,10},{10,... | collective-permute-start | bytes 491528 | tf_op jit(solution)/shard_map/ppermute | solution.py:137
  45.0 11.7 %collective-permute-start.8 = (f32[5,4,2048]{2,1,0:T(4,128)S(1)}, f32[5,4,2048]{2,1,0:T(4,128)S(1)}, u32[]{:S(2)}, u32[]{:S(2)}) collective-permute-start(f32[5,4,2048]{2,1,0:T(4,128)S(1)} %get-tuple-element.49), channel_id=1, source_target_pairs={{0,16},{16,0},{32,48},{48,32},{64,80},{80,64},{96,112},{112,96},{1... | collective-permute-start | bytes 491528 | tf_op jit(solution)/shard_map/ppermute | solution.py:134
  45.0 11.7 %collective-permute-start.9 = (f32[5,4,2048]{2,1,0:T(4,128)S(1)}, f32[5,4,2048]{2,1,0:T(4,128)S(1)}, u32[]{:S(2)}, u32[]{:S(2)}) collective-permute-start(f32[5,4,2048]{2,1,0:T(4,128)S(1)} %get-tuple-element.50), channel_id=1, source_target_pairs={{0,112},{16,32},{32,16},{48,64},{64,48},{80,96},{96,80},{112,0},{1... | collective-permute-start | bytes 491528 | tf_op jit(solution)/shard_map/ppermute | solution.py:135
  58.8 18.8 %all-to-all-start = ((f32[16,2,40,128]{3,2,1,0:T(8,128)}), f32[16,2,40,128]{3,2,1,0:T(8,128)S(1)}, u32[]{:S(2)}, u32[]{:S(2)}) async-start(f32[16,2,40,128]{3,2,1,0:T(8,128)} %get-tuple-element.54), calls=%async_computation | async-start | bytes 1310720 | tf_op jit(solution)/shard_map/all_to_all | solution.py:554
  83.9 2.5 %collective-permute-start.12 = (f32[144,128]{1,0:T(8,128)S(1)}, f32[144,128]{1,0:T(8,128)S(1)}, u32[]{:S(2)}, u32[]{:S(2)}) collective-permute-start(f32[144,128]{1,0:T(8,128)S(1)} %get-tuple-element.62), channel_id=1, source_target_pairs={{0,1},{1,0},{2,3},{3,2},{4,5},{5,4},{6,7},{7,6},{8,9},{9,8},{10,11... | collective-permute-start | bytes 221192 | tf_op jit(solution)/shard_map/ppermute | solution.py:481
  86.5 3.5 %collective-permute-start.13 = (f32[72,128]{1,0:T(8,128)S(1)}, f32[72,128]{1,0:T(8,128)S(1)}, u32[]{:S(2)}, u32[]{:S(2)}) collective-permute-start(f32[72,128]{1,0:T(8,128)S(1)} %get-tuple-element.72), channel_id=1, source_target_pairs={{0,17},{1,16},{2,19},{3,18},{4,21},{5,20},{6,23},{7,22},{8,25},{9,... | collective-permute-start | bytes 110600 | tf_op jit(solution)/shard_map/ppermute | solution.py:484
  86.8 3.4 %collective-permute-start.19 = (f32[72,128]{1,0:T(8,128)S(1)}, f32[72,128]{1,0:T(8,128)S(1)}, u32[]{:S(2)}, u32[]{:S(2)}) collective-permute-start(f32[72,128]{1,0:T(8,128)S(1)} %get-tuple-element.73), channel_id=1, source_target_pairs={{0,33},{1,32},{2,35},{3,34},{4,37},{5,36},{6,39},{7,38},{8,41},{9,... | collective-permute-start | bytes 110600 | tf_op jit(solution)/shard_map/ppermute | solution.py:484
  90.2 5.0 %collective-permute-start.14 = (f32[72,128]{1,0:T(8,128)S(1)}, f32[72,128]{1,0:T(8,128)S(1)}, u32[]{:S(2)}, u32[]{:S(2)}) collective-permute-start(f32[72,128]{1,0:T(8,128)S(1)} %get-tuple-element.70), channel_id=1, source_target_pairs={{0,19},{1,18},{2,17},{3,16},{4,23},{5,22},{6,21},{7,20},{8,27},{9,... | collective-permute-start | bytes 110600 | tf_op jit(solution)/shard_map/ppermute | solution.py:484
  90.9 4.6 %collective-permute-start.20 = (f32[72,128]{1,0:T(8,128)S(1)}, f32[72,128]{1,0:T(8,128)S(1)}, u32[]{:S(2)}, u32[]{:S(2)}) collective-permute-start(f32[72,128]{1,0:T(8,128)S(1)} %get-tuple-element.71), channel_id=1, source_target_pairs={{0,97},{1,96},{2,99},{3,98},{4,101},{5,100},{6,103},{7,102},{8,105... | collective-permute-start | bytes 110600 | tf_op jit(solution)/shard_map/ppermute | solution.py:484
  95.1 3.5 %collective-permute-start.15 = (f32[72,128]{1,0:T(8,128)S(1)}, f32[72,128]{1,0:T(8,128)S(1)}, u32[]{:S(2)}, u32[]{:S(2)}) collective-permute-start(f32[72,128]{1,0:T(8,128)S(1)} %add.41), channel_id=1, source_target_pairs={{0,5},{1,4},{2,7},{3,6},{4,1},{5,0},{6,3},{7,2},{8,13},{9,12},{10,... | collective-permute-start | bytes 110600 | tf_op jit(solution)/shard_map/ppermute | solution.py:484
  95.5 3.5 %collective-permute-start.21 = (f32[72,128]{1,0:T(8,128)S(1)}, f32[72,128]{1,0:T(8,128)S(1)}, u32[]{:S(2)}, u32[]{:S(2)}) collective-permute-start(f32[72,128]{1,0:T(8,128)S(1)} %add.47), channel_id=1, source_target_pairs={{0,17},{1,16},{2,19},{3,18},{4,21},{5,20},{6,23},{7,22},{8,25},{9,... | collective-permute-start | bytes 110600 | tf_op jit(solution)/shard_map/ppermute | solution.py:484
  98.7 4.6 %collective-permute-start.16 = (f32[72,128]{1,0:T(8,128)S(1)}, f32[72,128]{1,0:T(8,128)S(1)}, u32[]{:S(2)}, u32[]{:S(2)}) collective-permute-start(f32[72,128]{1,0:T(8,128)S(1)} %add.42), channel_id=1, source_target_pairs={{0,13},{1,12},{2,15},{3,14},{4,9},{5,8},{6,11},{7,10},{8,5},{9,4},... | collective-permute-start | bytes 110600 | tf_op jit(solution)/shard_map/ppermute | solution.py:484
  99.0 5.2 %collective-permute-start.22 = (f32[72,128]{1,0:T(8,128)S(1)}, f32[72,128]{1,0:T(8,128)S(1)}, u32[]{:S(2)}, u32[]{:S(2)}) collective-permute-start(f32[72,128]{1,0:T(8,128)S(1)} %add.48), channel_id=1, source_target_pairs={{0,19},{1,18},{2,17},{3,16},{4,23},{5,22},{6,21},{7,20},{8,27},{9,... | collective-permute-start | bytes 110600 | tf_op jit(solution)/shard_map/ppermute | solution.py:484
  103.3 3.4 %collective-permute-start.17 = (f32[72,128]{1,0:T(8,128)S(1)}, f32[72,128]{1,0:T(8,128)S(1)}, u32[]{:S(2)}, u32[]{:S(2)}) collective-permute-start(f32[72,128]{1,0:T(8,128)S(1)} %add.43), channel_id=1, source_target_pairs={{0,33},{1,32},{2,35},{3,34},{4,37},{5,36},{6,39},{7,38},{8,41},{9,... | collective-permute-start | bytes 110600 | tf_op jit(solution)/shard_map/ppermute | solution.py:484
  104.2 3.8 %collective-permute-start.23 = (f32[72,128]{1,0:T(8,128)S(1)}, f32[72,128]{1,0:T(8,128)S(1)}, u32[]{:S(2)}, u32[]{:S(2)}) collective-permute-start(f32[72,128]{1,0:T(8,128)S(1)} %add.49), channel_id=1, source_target_pairs={{0,5},{1,4},{2,7},{3,6},{4,1},{5,0},{6,3},{7,2},{8,13},{9,12},{10,... | collective-permute-start | bytes 110600 | tf_op jit(solution)/shard_map/ppermute | solution.py:484
  106.7 4.6 %collective-permute-start.18 = (f32[72,128]{1,0:T(8,128)S(1)}, f32[72,128]{1,0:T(8,128)S(1)}, u32[]{:S(2)}, u32[]{:S(2)}) collective-permute-start(f32[72,128]{1,0:T(8,128)S(1)} %add.44), channel_id=1, source_target_pairs={{0,97},{1,96},{2,99},{3,98},{4,101},{5,100},{6,103},{7,102},{8,105... | collective-permute-start | bytes 110600 | tf_op jit(solution)/shard_map/ppermute | solution.py:484
  108.0 4.7 %collective-permute-start.24 = (f32[72,128]{1,0:T(8,128)S(1)}, f32[72,128]{1,0:T(8,128)S(1)}, u32[]{:S(2)}, u32[]{:S(2)}) collective-permute-start(f32[72,128]{1,0:T(8,128)S(1)} %add.50), channel_id=1, source_target_pairs={{0,13},{1,12},{2,15},{3,14},{4,9},{5,8},{6,11},{7,10},{8,5},{9,4},... | collective-permute-start | bytes 110600 | tf_op jit(solution)/shard_map/ppermute | solution.py:484
  112.7 1.4 %collective-permute-start.25 = (f32[144,128]{1,0:T(8,128)S(1)}, f32[144,128]{1,0:T(8,128)S(1)}, u32[]{:S(2)}, u32[]{:S(2)}) collective-permute-start(f32[144,128]{1,0:T(8,128)S(1)} %pad_maximum_fusion.mine_ref), channel_id=1, source_target_pairs={{0,1},{1,0},{2,3},{3,2},{4,5},{5,4},{6,7},{7,6},{8,9},{9,8},{10,11... | collective-permute-start | bytes 221192 | tf_op jit(solution)/shard_map/ppermute | solution.py:487

commit v6 on v5

--- a/solution.py
+++ b/solution.py
@@ -88,7 +88,9 @@
             part_ref[row] = middle - 0.5 * carried + dif * spread
 
 
-def outer_kernel(last, place, part_ref, rxa, rxb, rya, ryb, vel_ref, dif_ref, new_ref, *outs):
+def outer_kernel(last, place, part_ref, *refs):
+    rxa, rxb, rya, ryb = refs[2:4] + refs[0:2] if last else refs[0:4]
+    vel_ref, dif_ref, new_ref, *outs = refs[4:]
     gx, gy = place[0], place[1]
     odd_x, odd_y = gx % 2 == 1, gy % 2 == 1
     y_at = lax.broadcasted_iota(jnp.int32, (4, 2048), 0)
@@ -124,18 +126,15 @@
 SLABS = ((16, 2, 2 * F * X, Z), F32)
 
 
-def exchange(edges):
+def exchange(edges, y_first):
     def pairs(n, second):
         partner = lambda i: (i ^ 1) if not second else ((i + 1) if i % 2 else (i - 1)) % n
         return [(i, partner(i)) for i in range(n)]
 
     xa, xb, ya, yb = edges
-    return (
-        lax.ppermute(xa, "gx", pairs(8, False)),
-        lax.ppermute(xb, "gx", pairs(8, True)),
-        lax.ppermute(ya, "gy", pairs(16, False)),
-        lax.ppermute(yb, "gy", pairs(16, True)),
-    )
+    along_x = lambda: [lax.ppermute(xa, "gx", pairs(8, False)), lax.ppermute(xb, "gx", pairs(8, True))]
+    along_y = lambda: [lax.ppermute(ya, "gy", pairs(16, False)), lax.ppermute(yb, "gy", pairs(16, True))]
+    return along_y() + along_x() if y_first else along_x() + along_y()
 
 
 def patch_rows(slabs_ref, anchor, out_ref):
@@ -528,7 +527,7 @@
     for step in range(STEPS):
         last = step == STEPS - 1
         outs = [((F * X, 4, 2048), F32)] + ([SLABS] if last else EDGES)
-        received = exchange(edges)
+        received = exchange(edges, last)
         (part,) = call(inner_kernel, [((F * X, 4, 2048), F32)], ins=[VMEM] * 3, nbytes=4_000_000, flops=BESIDE)(u, vel, diffusivity)
         kernel = lambda *refs, last=last: outer_kernel(last, *refs)
         u, *edges = call(kernel, outs, ins=[SMEM] + [VMEM] * 7, nbytes=3_000_000, flops=BESIDE)(

time: 116 us -> 114 us (0.983)
  starting transfers between devices: 43.2 us -> 41.2 us
    ppermute x3, waiting for transfers between devices: 13.4 us -> 6.07 us  [exchange(): lax.ppermute(yb, 'gy', pairs(16, True))]
    ppermute x3, waiting for transfers between devices: 5.46 us -> 10.7 us  [exchange(): lax.ppermute(xa, 'gx', pairs(8, False))]
    ppermute x12, waiting for transfers between devices: 15.8 us -> 17.8 us  [sum_all(): lax.ppermute(part, ('gx', 'gy'), p)]
    all_to_all x1, starting transfers between devices: 6.46 us -> 5.18 us  [on_device(): lax.all_to_all(edges[0], 'gy', 0, 0, tiled=True).reshape(32, 2 * F * X, Z)]
  transfers between devices with their start and end apart: 28 -> 28, of which waited for: 17 -> 18; matrix products, arithmetic and copies ran while one was open for 0% -> 0% of each run, Pallas kernels for 12% -> 12%
where the time goes in v6:
time: 114 us
  waiting for transfers between devices  41.9 us (37%)
  starting transfers between devices  41.2 us (36%)
  Pallas kernels  23.1 us (20%)
  local copies, waits for them, and re-layouts  6 us (5%)
  between operations  1.56 us (1%)
    ppermute x12, waiting for transfers between devices, sum_all(): lax.ppermute(part, ('gx', 'gy'), p)  17.8 us
    ppermute x3, waiting for transfers between devices, exchange(): lax.ppermute(xa, 'gx', pairs(8, False))  10.7 us
    ppermute x12, starting transfers between devices, sum_all(): lax.ppermute(part, ('gx', 'gy'), p)  9.17 us
    ppermute x3, starting transfers between devices, exchange(): lax.ppermute(yb, 'gy', pairs(16, True))  8.22 us
    all_to_all x1, starting transfers between devices, on_device(): lax.all_to_all(slabs, 'gy', 0, 0, tiled=True).reshape(32, 2 * F * X, Z)  6.34 us
    pallas_call x1, Pallas kernels, on_device(): call(backward_kernel, [((HALF, 128), F32)] * 2, scratch=HELD + [pltpu.VME...  6.33 us
    ppermute x3, waiting for transfers between devices, exchange(): lax.ppermute(yb, 'gy', pairs(16, True))  6.07 us
    unnamed x26, local copies, waits for them, and re-layouts  6 us
  transfers between devices with their start and end apart: 28, of which 18 were waited for; matrix products, arithmetic and copies ran while one was open for 0% of the time, Pallas kernels for 12%

profile of v6, /device:TPU:1, one launch (start us, length us, event | category | flops | bytes accessed | tf_op | source)
XLA Modules:
  0.0 113.9 jit_solution(11428152187109646293)
XLA Ops:
  0.7 1.1 copy-done
  2.6 2.5 %collective-permute-start = (f32[5,4,2048]{2,1,0:T(4,128)S(1)}, f32[5,4,2048]{2,1,0:T(4,128)S(1)}, u32[]{:S(2)}, u32[]{:S(2)}) collective-permute-start(f32[5,4,2048]{2,1,0:T(4,128)S(1)} %get-tuple-element.39), channel_id=1, source_target_pairs={{0,16},{16,0},{32,48},{48,32},{64,80},{80,64},{96,112},{112,96},{1... | collective-permute-start | bytes 491528 | tf_op jit(solution)/shard_map/ppermute | solution.py:135
  5.1 2.3 %collective-permute-start.1 = (f32[5,4,2048]{2,1,0:T(4,128)S(1)}, f32[5,4,2048]{2,1,0:T(4,128)S(1)}, u32[]{:S(2)}, u32[]{:S(2)}) collective-permute-start(f32[5,4,2048]{2,1,0:T(4,128)S(1)} %get-tuple-element.40), channel_id=1, source_target_pairs={{0,112},{16,32},{32,16},{48,64},{64,48},{80,96},{96,80},{112,0},{1... | collective-permute-start | bytes 491528 | tf_op jit(solution)/shard_map/ppermute | solution.py:135
  7.4 1.0 collective-permute-start.2
  8.4 3.5 %collective-permute-start.3 = (f32[5,4,2048]{2,1,0:T(4,128)S(1)}, f32[5,4,2048]{2,1,0:T(4,128)S(1)}, u32[]{:S(2)}, u32[]{:S(2)}) collective-permute-start(f32[5,4,2048]{2,1,0:T(4,128)S(1)} %get-tuple-element.42), channel_id=1, source_target_pairs={{0,15},{1,2},{2,1},{3,4},{4,3},{5,6},{6,5},{7,8},{8,7},{9,10},{10,... | collective-permute-start | bytes 491528 | tf_op jit(solution)/shard_map/ppermute | solution.py:136
  11.8 1.2 %shard_map.178 = f32[16,2,40,128]{3,2,1,0:T(8,128)} custom-call(f32[20,4,2048]{2,1,0:T(4,128)S(1)} %bitcast.37), custom_call_target="tpu_custom_call" | custom-call | bytes 1500000 | tf_op jit(solution)/shard_map/pallas_call | solution.py:508
  13.0 6.3 %all-to-all-start.1 = ((f32[16,2,40,128]{3,2,1,0:T(8,128)}), f32[16,2,40,128]{3,2,1,0:T(8,128)S(1)}, u32[]{:S(2)}, u32[]{:S(2)}) async-start(f32[16,2,40,128]{3,2,1,0:T(8,128)} %shard_map.178), calls=%async_computation.1 | async-start | bytes 1310720 | tf_op jit(solution)/shard_map/all_to_all | solution.py:509
  19.4 1.1 copy-done.1
  20.5 1.0 copy-done.9
  21.5 0.9 copy-done.11
  22.4 0.9 shard_map.170.refs_1_
  23.4 1.0 copy-done.10
  24.4 0.9 copy-done.12
  25.3 1.0 shard_map.172
  26.4 1.7 %collective-permute-start.5 = (f32[5,4,2048]{2,1,0:T(4,128)S(1)}, f32[5,4,2048]{2,1,0:T(4,128)S(1)}, u32[]{:S(2)}, u32[]{:S(2)}) collective-permute-start(f32[5,4,2048]{2,1,0:T(4,128)S(1)} %get-tuple-element.45), channel_id=1, source_target_pairs={{0,112},{16,32},{32,16},{48,64},{64,48},{80,96},{96,80},{112,0},{1... | collective-permute-start | bytes 491528 | tf_op jit(solution)/shard_map/ppermute | solution.py:135
  28.9 2.9 %collective-permute-start.7 = (f32[5,4,2048]{2,1,0:T(4,128)S(1)}, f32[5,4,2048]{2,1,0:T(4,128)S(1)}, u32[]{:S(2)}, u32[]{:S(2)}) collective-permute-start(f32[5,4,2048]{2,1,0:T(4,128)S(1)} %get-tuple-element.47), channel_id=1, source_target_pairs={{0,15},{1,2},{2,1},{3,4},{4,3},{5,6},{6,5},{7,8},{8,7},{9,10},{10,... | collective-permute-start | bytes 491528 | tf_op jit(solution)/shard_map/ppermute | solution.py:136
  31.8 0.9 shard_map.173.refs_1_
  32.7 5.5 %collective-permute-done.4.refs_2_ = f32[5,4,2048]{2,1,0:T(4,128)S(1)} collective-permute-done((f32[5,4,2048]{2,1,0:T(4,128)S(1)}, f32[5,4,2048]{2,1,0:T(4,128)S(1)}, u32[]{:S(2)}, u32[]{:S(2)}) %collective-permute-start.4) | collective-permute-done | bytes 163872 | tf_op jit(solution)/shard_map/ppermute | solution.py:135
  38.2 4.4 %collective-permute-done.7.refs_5_ = f32[5,4,2048]{2,1,0:T(4,128)S(1)} collective-permute-done((f32[5,4,2048]{2,1,0:T(4,128)S(1)}, f32[5,4,2048]{2,1,0:T(4,128)S(1)}, u32[]{:S(2)}, u32[]{:S(2)}) %collective-permute-start.7) | collective-permute-done | bytes 163872 | tf_op jit(solution)/shard_map/ppermute | solution.py:136
  42.6 1.0 shard_map.174
  43.7 1.7 %collective-permute-start.11 = (f32[5,4,2048]{2,1,0:T(4,128)S(1)}, f32[5,4,2048]{2,1,0:T(4,128)S(1)}, u32[]{:S(2)}, u32[]{:S(2)}) collective-permute-start(f32[5,4,2048]{2,1,0:T(4,128)S(1)} %get-tuple-element.52), channel_id=1, source_target_pairs={{0,112},{16,32},{32,16},{48,64},{64,48},{80,96},{96,80},{112,0},{1... | collective-permute-start | bytes 491528 | tf_op jit(solution)/shard_map/ppermute | solution.py:135
  45.4 1.8 %collective-permute-start.9 = (f32[5,4,2048]{2,1,0:T(4,128)S(1)}, f32[5,4,2048]{2,1,0:T(4,128)S(1)}, u32[]{:S(2)}, u32[]{:S(2)}) collective-permute-start(f32[5,4,2048]{2,1,0:T(4,128)S(1)} %get-tuple-element.50), channel_id=1, source_target_pairs={{0,15},{1,2},{2,1},{3,4},{4,3},{5,6},{6,5},{7,8},{8,7},{9,10},{10,... | collective-permute-start | bytes 491528 | tf_op jit(solution)/shard_map/ppermute | solution.py:136
  47.2 0.9 shard_map.175.refs_1_
  48.1 5.3 %collective-permute-done.10.refs_4_ = f32[5,4,2048]{2,1,0:T(4,128)S(1)} collective-permute-done((f32[5,4,2048]{2,1,0:T(4,128)S(1)}, f32[5,4,2048]{2,1,0:T(4,128)S(1)}, u32[]{:S(2)}, u32[]{:S(2)}) %collective-permute-start.10) | collective-permute-done | bytes 163872 | tf_op jit(solution)/shard_map/ppermute | solution.py:135
  53.4 1.7 %collective-permute-done.9.refs_3_ = f32[5,4,2048]{2,1,0:T(4,128)S(1)} collective-permute-done((f32[5,4,2048]{2,1,0:T(4,128)S(1)}, f32[5,4,2048]{2,1,0:T(4,128)S(1)}, u32[]{:S(2)}, u32[]{:S(2)}) %collective-permute-start.9) | collective-permute-done | bytes 163872 | tf_op jit(solution)/shard_map/ppermute | solution.py:136
  55.1 2.1 %shard_map.176 = (f32[20,4,2048]{2,1,0:T(4,128)}, f32[16,2,40,128]{3,2,1,0:T(8,128)}) custom-call(s32[2]{0:T(128)S(1)} %pad_add_fusion.place.refs_0_, f32[20,4,2048]{2,1,0:T(4,128)S(1)} %shard_map.175.refs_1_, f32[5,4,2048]{2,1,0:T(4,128)S(1)} %collective-permute-done.8.refs_2_, f32[5,4,2048]{2,1,0:T(4,128)S(1)} %collective-permute-done.9.refs_3_, ...), custom_call_target="tpu_custom_call" | custom-call | flops 6000000000 | bytes 3000000 | tf_op jit(solution)/shard_map/pallas_call | solution.py:533
  57.2 5.2 %all-to-all-start = ((f32[16,2,40,128]{3,2,1,0:T(8,128)}), f32[16,2,40,128]{3,2,1,0:T(8,128)S(1)}, u32[]{:S(2)}, u32[]{:S(2)}) async-start(f32[16,2,40,128]{3,2,1,0:T(8,128)} %get-tuple-element.54), calls=%async_computation | async-start | bytes 1310720 | tf_op jit(solution)/shard_map/all_to_all | solution.py:553
  63.1 1.7 %shard_map.177 = (bf16[128,224]{1,0:T(8,128)(2,1)S(1)}, bf16[3,128,384]{2,1,0:T(8,128)(2,1)S(1)}, bf16[3,128,384]{2,1,0:T(8,128)(2,1)S(1)}, bf16[224,128]{1,0:T(...) custom-call(f32[45,3,32]{2,1,0:T(4,128)S(1)} %bitcast.41, f32[27,32,32]{2,1,0:T(8,128)S(1)} %bitcast.40, ...), custom_call_target="tpu_custom_call" | custom-call | bytes 1000000 | tf_op jit(solution)/shard_map/pallas_call | solution.py:510
  64.8 4.4 %shard_map.179.kept_ref = bf16[2,16384,1024]{2,1,0:T(8,128)(2,1)} custom-call(s32[2]{0:T(128)S(1)} %bitcast.43, f32[32,40,128]{2,1,0:T(8,128)S(1)} %bitcast.39, bf16[128,224]{1,0:T(8,128)(2,1)S(1)} %get-tuple-element.57.w1_ref, bf16[3,128,384]{2,1,0:T(8,128)(2,1)S(1)} %get-tuple-element.58.w2_ref, bf16[224,128]{1,0:T(8,128)(2,1)S(1)} %get-tuple-element.59.w3_ref, ...), custom_call_target="tpu_custom_call" | custom-call | flops 2000000000 | bytes 8000000 | tf_op jit(solution)/shard_map/pallas_call | solution.py:537
  69.2 5.5 %all-to-all-done = f32[16,2,40,128]{3,2,1,0:T(8,128)S(1)} async-done(((f32[16,2,40,128]{3,2,1,0:T(8,128)}), f32[16,2,40,128]{3,2,1,0:T(8,128)S(1)}, u32[]{:S(2)}, u32[]{:S(2)}) %all-to-all-start) | async-done | bytes 655392 | tf_op jit(solution)/shard_map/all_to_all | solution.py:553
  74.7 6.3 %shard_map.180 = (f32[144,128]{1,0:T(8,128)S(1)}, f32[144,128]{1,0:T(8,128)S(1)}) custom-call(s32[2]{0:T(128)S(1)} %pad_add_fusion.place.refs_0_, s32[2]{0:T(128)S(1)} %bitcast.44, s32[1]{0:T(128)} %bitcast.34.count, f32[32,40,128]{2,1,0:T(8,128)S(1)} %bitcast.35, bf16[3,128,384]{2,1,0:T(8,128)(2,1)S(1)} %get-tuple-element.55.w2_ref, ...), custom_call_target="tpu_custom_call" | custom-call | flops 4000000000 | bytes 10000000 | tf_op jit(solution)/shard_map/pallas_call | solution.py:554
  81.0 1.6 %collective-permute-start.12 = (f32[144,128]{1,0:T(8,128)S(1)}, f32[144,128]{1,0:T(8,128)S(1)}, u32[]{:S(2)}, u32[]{:S(2)}) collective-permute-start(f32[144,128]{1,0:T(8,128)S(1)} %get-tuple-element.62), channel_id=1, source_target_pairs={{0,1},{1,0},{2,3},{3,2},{4,5},{5,4},{6,7},{7,6},{8,9},{9,8},{10,11... | collective-permute-start | bytes 221192 | tf_op jit(solution)/shard_map/ppermute | solution.py:480
  82.7 0.9 collective-permute-done.12
  83.6 1.5 %collective-permute-start.13 = (f32[72,128]{1,0:T(8,128)S(1)}, f32[72,128]{1,0:T(8,128)S(1)}, u32[]{:S(2)}, u32[]{:S(2)}) collective-permute-start(f32[72,128]{1,0:T(8,128)S(1)} %get-tuple-element.72), channel_id=1, source_target_pairs={{0,17},{1,16},{2,19},{3,18},{4,21},{5,20},{6,23},{7,22},{8,25},{9,... | collective-permute-start | bytes 110600 | tf_op jit(solution)/shard_map/ppermute | solution.py:483
  85.3 1.9 %collective-permute-done.13 = f32[72,128]{1,0:T(8,128)S(1)} collective-permute-done((f32[72,128]{1,0:T(8,128)S(1)}, f32[72,128]{1,0:T(8,128)S(1)}, u32[]{:S(2)}, u32[]{:S(2)}) %collective-permute-start.13) | collective-permute-done | bytes 36896 | tf_op jit(solution)/shard_map/ppermute | solution.py:483
  87.1 1.4 %collective-permute-done.19 = f32[72,128]{1,0:T(8,128)S(1)} collective-permute-done((f32[72,128]{1,0:T(8,128)S(1)}, f32[72,128]{1,0:T(8,128)S(1)}, u32[]{:S(2)}, u32[]{:S(2)}) %collective-permute-start.19) | collective-permute-done | bytes 36896 | tf_op jit(solution)/shard_map/ppermute | solution.py:483
  89.3 3.9 %collective-permute-done.14 = f32[72,128]{1,0:T(8,128)S(1)} collective-permute-done((f32[72,128]{1,0:T(8,128)S(1)}, f32[72,128]{1,0:T(8,128)S(1)}, u32[]{:S(2)}, u32[]{:S(2)}) %collective-permute-start.14) | collective-permute-done | bytes 36896 | tf_op jit(solution)/shard_map/ppermute | solution.py:483
  93.9 2.7 %collective-permute-done.15 = f32[72,128]{1,0:T(8,128)S(1)} collective-permute-done((f32[72,128]{1,0:T(8,128)S(1)}, f32[72,128]{1,0:T(8,128)S(1)}, u32[]{:S(2)}, u32[]{:S(2)}) %collective-permute-start.15) | collective-permute-done | bytes 36896 | tf_op jit(solution)/shard_map/ppermute | solution.py:483
  97.2 2.4 %collective-permute-start.22 = (f32[72,128]{1,0:T(8,128)S(1)}, f32[72,128]{1,0:T(8,128)S(1)}, u32[]{:S(2)}, u32[]{:S(2)}) collective-permute-start(f32[72,128]{1,0:T(8,128)S(1)} %add.48), channel_id=1, source_target_pairs={{0,19},{1,18},{2,17},{3,16},{4,23},{5,22},{6,21},{7,20},{8,27},{9,... | collective-permute-start | bytes 110600 | tf_op jit(solution)/shard_map/ppermute | solution.py:483
  99.7 1.5 %collective-permute-done.16 = f32[72,128]{1,0:T(8,128)S(1)} collective-permute-done((f32[72,128]{1,0:T(8,128)S(1)}, f32[72,128]{1,0:T(8,128)S(1)}, u32[]{:S(2)}, u32[]{:S(2)}) %collective-permute-start.16) | collective-permute-done | bytes 36896 | tf_op jit(solution)/shard_map/ppermute | solution.py:483
  101.3 1.2 %collective-permute-done.22 = f32[72,128]{1,0:T(8,128)S(1)} collective-permute-done((f32[72,128]{1,0:T(8,128)S(1)}, f32[72,128]{1,0:T(8,128)S(1)}, u32[]{:S(2)}, u32[]{:S(2)}) %collective-permute-start.22) | collective-permute-done | bytes 36896 | tf_op jit(solution)/shard_map/ppermute | solution.py:483
  103.1 1.4 %collective-permute-done.17 = f32[72,128]{1,0:T(8,128)S(1)} collective-permute-done((f32[72,128]{1,0:T(8,128)S(1)}, f32[72,128]{1,0:T(8,128)S(1)}, u32[]{:S(2)}, u32[]{:S(2)}) %collective-permute-start.17) | collective-permute-done | bytes 36896 | tf_op jit(solution)/shard_map/ppermute | solution.py:483
  105.2 0.8 collective-permute-done.23
  106.0 1.7 %collective-permute-start.24 = (f32[72,128]{1,0:T(8,128)S(1)}, f32[72,128]{1,0:T(8,128)S(1)}, u32[]{:S(2)}, u32[]{:S(2)}) collective-permute-start(f32[72,128]{1,0:T(8,128)S(1)} %add.50), channel_id=1, source_target_pairs={{0,13},{1,12},{2,15},{3,14},{4,9},{5,8},{6,11},{7,10},{8,5},{9,4},... | collective-permute-start | bytes 110600 | tf_op jit(solution)/shard_map/ppermute | solution.py:483
  107.7 1.4 %collective-permute-done.18 = f32[72,128]{1,0:T(8,128)S(1)} collective-permute-done((f32[72,128]{1,0:T(8,128)S(1)}, f32[72,128]{1,0:T(8,128)S(1)}, u32[]{:S(2)}, u32[]{:S(2)}) %collective-permute-start.18) | collective-permute-done | bytes 36896 | tf_op jit(solution)/shard_map/ppermute | solution.py:483
  109.2 1.5 %collective-permute-done.24 = f32[72,128]{1,0:T(8,128)S(1)} collective-permute-done((f32[72,128]{1,0:T(8,128)S(1)}, f32[72,128]{1,0:T(8,128)S(1)}, u32[]{:S(2)}, u32[]{:S(2)}) %collective-permute-start.24) | collective-permute-done | bytes 36896 | tf_op jit(solution)/shard_map/ppermute | solution.py:483
  111.2 0.9 collective-permute-done.25.other_ref
  112.1 1.8 %shard_map.181 = (f32[45,3,32]{2,1,0:T(4,128)}, f32[1,32]{1,0:T(1,128)}, f32[27,32,32]{2,1,0:T(8,128)}, f32[1,32]{1,0:T(1,128)}, f32[45,3,32]{2,1,0:T(4,128)}, /*index=5*/f32[1,5]{1,0:T(1,128)}, f32[1,1]{1,0:T(1,128)}) custom-call(s32[2]{0:T(128)S(1)} %pad_add_fusion.place.refs_0_, f32[144,128]{1,0:T(8,128)S(1)} %pad_maximum_fusion.mine_ref, ...), custom_call_target="tpu_custom_call" | custom-call | bytes 1000000 | tf_op jit(solution)/shard_map/pallas_call | solution.py:572
  (61 shorter events, 6.0 us)
Async XLA Ops:
  0.7 1.1 copy-start
  2.6 20.8 %collective-permute-start = (f32[5,4,2048]{2,1,0:T(4,128)S(1)}, f32[5,4,2048]{2,1,0:T(4,128)S(1)}, u32[]{:S(2)}, u32[]{:S(2)}) collective-permute-start(f32[5,4,2048]{2,1,0:T(4,128)S(1)} %get-tuple-element.39), channel_id=1, source_target_pairs={{0,16},{16,0},{32,48},{48,32},{64,80},{80,64},{96,112},{112,96},{1... | collective-permute-start | bytes 491528 | tf_op jit(solution)/shard_map/ppermute | solution.py:135
  5.1 18.2 %collective-permute-start.1 = (f32[5,4,2048]{2,1,0:T(4,128)S(1)}, f32[5,4,2048]{2,1,0:T(4,128)S(1)}, u32[]{:S(2)}, u32[]{:S(2)}) collective-permute-start(f32[5,4,2048]{2,1,0:T(4,128)S(1)} %get-tuple-element.40), channel_id=1, source_target_pairs={{0,112},{16,32},{32,16},{48,64},{64,48},{80,96},{96,80},{112,0},{1... | collective-permute-start | bytes 491528 | tf_op jit(solution)/shard_map/ppermute | solution.py:135
  7.4 15.9 %collective-permute-start.2 = (f32[5,4,2048]{2,1,0:T(4,128)S(1)}, f32[5,4,2048]{2,1,0:T(4,128)S(1)}, u32[]{:S(2)}, u32[]{:S(2)}) collective-permute-start(f32[5,4,2048]{2,1,0:T(4,128)S(1)} %get-tuple-element.41), channel_id=1, source_target_pairs={{0,1},{1,0},{2,3},{3,2},{4,5},{5,4},{6,7},{7,6},{8,9},{9,8},{10,11... | collective-permute-start | bytes 491528 | tf_op jit(solution)/shard_map/ppermute | solution.py:136
  8.4 15.0 %collective-permute-start.3 = (f32[5,4,2048]{2,1,0:T(4,128)S(1)}, f32[5,4,2048]{2,1,0:T(4,128)S(1)}, u32[]{:S(2)}, u32[]{:S(2)}) collective-permute-start(f32[5,4,2048]{2,1,0:T(4,128)S(1)} %get-tuple-element.42), channel_id=1, source_target_pairs={{0,15},{1,2},{2,1},{3,4},{4,3},{5,6},{6,5},{7,8},{8,7},{9,10},{10,... | collective-permute-start | bytes 491528 | tf_op jit(solution)/shard_map/ppermute | solution.py:136
  13.0 44.2 %all-to-all-start.1 = ((f32[16,2,40,128]{3,2,1,0:T(8,128)}), f32[16,2,40,128]{3,2,1,0:T(8,128)S(1)}, u32[]{:S(2)}, u32[]{:S(2)}) async-start(f32[16,2,40,128]{3,2,1,0:T(8,128)} %shard_map.178), calls=%async_computation.1 | async-start | bytes 1310720 | tf_op jit(solution)/shard_map/all_to_all | solution.py:509
  19.4 1.1 copy-start.1
  20.5 1.0 copy-start.9
  21.5 0.9 copy-start.11
  22.4 40.7 %copy-start.2 = (f32[32,32,3,3,3]{1,0,4,3,2:T(8,128)S(1)}, f32[32,32,3,3,3]{1,0,4,3,2:T(8,128)}, u32[]{:S(2)}) copy-start(f32[32,32,3,3,3]{1,0,4,3,2:T(8,128)} %param.18) | copy-start | bytes 331780
  22.4 40.7 %copy-start.3 = (f32[32,5,3,3,3]{0,4,3,2,1:T(4,128)S(1)}, f32[32,5,3,3,3]{0,4,3,2,1:T(4,128)}, u32[]{:S(2)}) copy-start(f32[32,5,3,3,3]{0,4,3,2,1:T(4,128)} %param.16) | copy-start | bytes 51844
  22.4 40.7 %copy-start.4 = (f32[5,32,3,3,3]{1,4,3,2,0:T(4,128)S(1)}, f32[5,32,3,3,3]{1,4,3,2,0:T(4,128)}, u32[]{:S(2)}) copy-start(f32[5,32,3,3,3]{1,4,3,2,0:T(4,128)} %param.20) | copy-start | bytes 51844
  22.4 40.7 %copy-start.6 = (f32[32]{0:T(128)S(1)}, f32[32]{0:T(128)}, u32[]{:S(2)}) copy-start(f32[32]{0:T(128)} %param.17) | copy-start | bytes 388
  22.4 40.7 %copy-start.7 = (f32[32]{0:T(128)S(1)}, f32[32]{0:T(128)}, u32[]{:S(2)}) copy-start(f32[32]{0:T(128)} %param.19) | copy-start | bytes 388
  22.4 40.7 %copy-start.8 = (f32[5]{0:T(128)S(1)}, f32[5]{0:T(128)}, u32[]{:S(2)}) copy-start(f32[5]{0:T(128)} %param.21) | copy-start | bytes 64
  22.4 42.4 %copy-start.5 = (s32[1,1,2]{2,1,0:T(1,128)S(1)}, s32[1,1,2]{2,1,0:T(1,128)}, u32[]{:S(2)}) copy-start(s32[1,1,2]{2,1,0:T(1,128)} %param.14) | copy-start | bytes 28
  23.4 1.0 copy-start.10
  24.4 0.9 copy-start.12
  26.3 11.9 %collective-permute-start.4 = (f32[5,4,2048]{2,1,0:T(4,128)S(1)}, f32[5,4,2048]{2,1,0:T(4,128)S(1)}, u32[]{:S(2)}, u32[]{:S(2)}) collective-permute-start(f32[5,4,2048]{2,1,0:T(4,128)S(1)} %get-tuple-element.44), channel_id=1, source_target_pairs={{0,16},{16,0},{32,48},{48,32},{64,80},{80,64},{96,112},{112,96},{1... | collective-permute-start | bytes 491528 | tf_op jit(solution)/shard_map/ppermute | solution.py:135
  26.4 11.8 %collective-permute-start.5 = (f32[5,4,2048]{2,1,0:T(4,128)S(1)}, f32[5,4,2048]{2,1,0:T(4,128)S(1)}, u32[]{:S(2)}, u32[]{:S(2)}) collective-permute-start(f32[5,4,2048]{2,1,0:T(4,128)S(1)} %get-tuple-element.45), channel_id=1, source_target_pairs={{0,112},{16,32},{32,16},{48,64},{64,48},{80,96},{96,80},{112,0},{1... | collective-permute-start | bytes 491528 | tf_op jit(solution)/shard_map/ppermute | solution.py:135
  28.1 10.1 %collective-permute-start.6 = (f32[5,4,2048]{2,1,0:T(4,128)S(1)}, f32[5,4,2048]{2,1,0:T(4,128)S(1)}, u32[]{:S(2)}, u32[]{:S(2)}) collective-permute-start(f32[5,4,2048]{2,1,0:T(4,128)S(1)} %get-tuple-element.46), channel_id=1, source_target_pairs={{0,1},{1,0},{2,3},{3,2},{4,5},{5,4},{6,7},{7,6},{8,9},{9,8},{10,11... | collective-permute-start | bytes 491528 | tf_op jit(solution)/shard_map/ppermute | solution.py:136
  28.9 13.7 %collective-permute-start.7 = (f32[5,4,2048]{2,1,0:T(4,128)S(1)}, f32[5,4,2048]{2,1,0:T(4,128)S(1)}, u32[]{:S(2)}, u32[]{:S(2)}) collective-permute-start(f32[5,4,2048]{2,1,0:T(4,128)S(1)} %get-tuple-element.47), channel_id=1, source_target_pairs={{0,15},{1,2},{2,1},{3,4},{4,3},{5,6},{6,5},{7,8},{8,7},{9,10},{10,... | collective-permute-start | bytes 491528 | tf_op jit(solution)/shard_map/ppermute | solution.py:136
  43.6 9.8 %collective-permute-start.10 = (f32[5,4,2048]{2,1,0:T(4,128)S(1)}, f32[5,4,2048]{2,1,0:T(4,128)S(1)}, u32[]{:S(2)}, u32[]{:S(2)}) collective-permute-start(f32[5,4,2048]{2,1,0:T(4,128)S(1)} %get-tuple-element.51), channel_id=1, source_target_pairs={{0,16},{16,0},{32,48},{48,32},{64,80},{80,64},{96,112},{112,96},{1... | collective-permute-start | bytes 491528 | tf_op jit(solution)/shard_map/ppermute | solution.py:135
  43.7 9.7 %collective-permute-start.11 = (f32[5,4,2048]{2,1,0:T(4,128)S(1)}, f32[5,4,2048]{2,1,0:T(4,128)S(1)}, u32[]{:S(2)}, u32[]{:S(2)}) collective-permute-start(f32[5,4,2048]{2,1,0:T(4,128)S(1)} %get-tuple-element.52), channel_id=1, source_target_pairs={{0,112},{16,32},{32,16},{48,64},{64,48},{80,96},{96,80},{112,0},{1... | collective-permute-start | bytes 491528 | tf_op jit(solution)/shard_map/ppermute | solution.py:135
  45.4 8.0 %collective-permute-start.8 = (f32[5,4,2048]{2,1,0:T(4,128)S(1)}, f32[5,4,2048]{2,1,0:T(4,128)S(1)}, u32[]{:S(2)}, u32[]{:S(2)}) collective-permute-start(f32[5,4,2048]{2,1,0:T(4,128)S(1)} %get-tuple-element.49), channel_id=1, source_target_pairs={{0,1},{1,0},{2,3},{3,2},{4,5},{5,4},{6,7},{7,6},{8,9},{9,8},{10,11... | collective-permute-start | bytes 491528 | tf_op jit(solution)/shard_map/ppermute | solution.py:136
  45.4 9.7 %collective-permute-start.9 = (f32[5,4,2048]{2,1,0:T(4,128)S(1)}, f32[5,4,2048]{2,1,0:T(4,128)S(1)}, u32[]{:S(2)}, u32[]{:S(2)}) collective-permute-start(f32[5,4,2048]{2,1,0:T(4,128)S(1)} %get-tuple-element.50), channel_id=1, source_target_pairs={{0,15},{1,2},{2,1},{3,4},{4,3},{5,6},{6,5},{7,8},{8,7},{9,10},{10,... | collective-permute-start | bytes 491528 | tf_op jit(solution)/shard_map/ppermute | solution.py:136
  57.2 17.5 %all-to-all-start = ((f32[16,2,40,128]{3,2,1,0:T(8,128)}), f32[16,2,40,128]{3,2,1,0:T(8,128)S(1)}, u32[]{:S(2)}, u32[]{:S(2)}) async-start(f32[16,2,40,128]{3,2,1,0:T(8,128)} %get-tuple-element.54), calls=%async_computation | async-start | bytes 1310720 | tf_op jit(solution)/shard_map/all_to_all | solution.py:553
  81.0 2.5 %collective-permute-start.12 = (f32[144,128]{1,0:T(8,128)S(1)}, f32[144,128]{1,0:T(8,128)S(1)}, u32[]{:S(2)}, u32[]{:S(2)}) collective-permute-start(f32[144,128]{1,0:T(8,128)S(1)} %get-tuple-element.62), channel_id=1, source_target_pairs={{0,1},{1,0},{2,3},{3,2},{4,5},{5,4},{6,7},{7,6},{8,9},{9,8},{10,11... | collective-permute-start | bytes 221192 | tf_op jit(solution)/shard_map/ppermute | solution.py:480
  83.6 3.5 %collective-permute-start.13 = (f32[72,128]{1,0:T(8,128)S(1)}, f32[72,128]{1,0:T(8,128)S(1)}, u32[]{:S(2)}, u32[]{:S(2)}) collective-permute-start(f32[72,128]{1,0:T(8,128)S(1)} %get-tuple-element.72), channel_id=1, source_target_pairs={{0,17},{1,16},{2,19},{3,18},{4,21},{5,20},{6,23},{7,22},{8,25},{9,... | collective-permute-start | bytes 110600 | tf_op jit(solution)/shard_map/ppermute | solution.py:483
  85.1 3.4 %collective-permute-start.19 = (f32[72,128]{1,0:T(8,128)S(1)}, f32[72,128]{1,0:T(8,128)S(1)}, u32[]{:S(2)}, u32[]{:S(2)}) collective-permute-start(f32[72,128]{1,0:T(8,128)S(1)} %get-tuple-element.73), channel_id=1, source_target_pairs={{0,33},{1,32},{2,35},{3,34},{4,37},{5,36},{6,39},{7,38},{8,41},{9,... | collective-permute-start | bytes 110600 | tf_op jit(solution)/shard_map/ppermute | solution.py:483
  88.5 4.7 %collective-permute-start.14 = (f32[72,128]{1,0:T(8,128)S(1)}, f32[72,128]{1,0:T(8,128)S(1)}, u32[]{:S(2)}, u32[]{:S(2)}) collective-permute-start(f32[72,128]{1,0:T(8,128)S(1)} %get-tuple-element.70), channel_id=1, source_target_pairs={{0,19},{1,18},{2,17},{3,16},{4,23},{5,22},{6,21},{7,20},{8,27},{9,... | collective-permute-start | bytes 110600 | tf_op jit(solution)/shard_map/ppermute | solution.py:483
  88.6 4.7 %collective-permute-start.20 = (f32[72,128]{1,0:T(8,128)S(1)}, f32[72,128]{1,0:T(8,128)S(1)}, u32[]{:S(2)}, u32[]{:S(2)}) collective-permute-start(f32[72,128]{1,0:T(8,128)S(1)} %get-tuple-element.71), channel_id=1, source_target_pairs={{0,97},{1,96},{2,99},{3,98},{4,101},{5,100},{6,103},{7,102},{8,105... | collective-permute-start | bytes 110600 | tf_op jit(solution)/shard_map/ppermute | solution.py:483
  93.2 3.4 %collective-permute-start.15 = (f32[72,128]{1,0:T(8,128)S(1)}, f32[72,128]{1,0:T(8,128)S(1)}, u32[]{:S(2)}, u32[]{:S(2)}) collective-permute-start(f32[72,128]{1,0:T(8,128)S(1)} %add.41), channel_id=1, source_target_pairs={{0,5},{1,4},{2,7},{3,6},{4,1},{5,0},{6,3},{7,2},{8,13},{9,12},{10,... | collective-permute-start | bytes 110600 | tf_op jit(solution)/shard_map/ppermute | solution.py:483
  93.3 3.9 %collective-permute-start.21 = (f32[72,128]{1,0:T(8,128)S(1)}, f32[72,128]{1,0:T(8,128)S(1)}, u32[]{:S(2)}, u32[]{:S(2)}) collective-permute-start(f32[72,128]{1,0:T(8,128)S(1)} %add.47), channel_id=1, source_target_pairs={{0,17},{1,16},{2,19},{3,18},{4,21},{5,20},{6,23},{7,22},{8,25},{9,... | collective-permute-start | bytes 110600 | tf_op jit(solution)/shard_map/ppermute | solution.py:483
  96.6 4.6 %collective-permute-start.16 = (f32[72,128]{1,0:T(8,128)S(1)}, f32[72,128]{1,0:T(8,128)S(1)}, u32[]{:S(2)}, u32[]{:S(2)}) collective-permute-start(f32[72,128]{1,0:T(8,128)S(1)} %add.42), channel_id=1, source_target_pairs={{0,13},{1,12},{2,15},{3,14},{4,9},{5,8},{6,11},{7,10},{8,5},{9,4},... | collective-permute-start | bytes 110600 | tf_op jit(solution)/shard_map/ppermute | solution.py:483
  97.2 5.3 %collective-permute-start.22 = (f32[72,128]{1,0:T(8,128)S(1)}, f32[72,128]{1,0:T(8,128)S(1)}, u32[]{:S(2)}, u32[]{:S(2)}) collective-permute-start(f32[72,128]{1,0:T(8,128)S(1)} %add.48), channel_id=1, source_target_pairs={{0,19},{1,18},{2,17},{3,16},{4,23},{5,22},{6,21},{7,20},{8,27},{9,... | collective-permute-start | bytes 110600 | tf_op jit(solution)/shard_map/ppermute | solution.py:483
  101.2 3.4 %collective-permute-start.17 = (f32[72,128]{1,0:T(8,128)S(1)}, f32[72,128]{1,0:T(8,128)S(1)}, u32[]{:S(2)}, u32[]{:S(2)}) collective-permute-start(f32[72,128]{1,0:T(8,128)S(1)} %add.43), channel_id=1, source_target_pairs={{0,33},{1,32},{2,35},{3,34},{4,37},{5,36},{6,39},{7,38},{8,41},{9,... | collective-permute-start | bytes 110600 | tf_op jit(solution)/shard_map/ppermute | solution.py:483
  102.5 3.5 %collective-permute-start.23 = (f32[72,128]{1,0:T(8,128)S(1)}, f32[72,128]{1,0:T(8,128)S(1)}, u32[]{:S(2)}, u32[]{:S(2)}) collective-permute-start(f32[72,128]{1,0:T(8,128)S(1)} %add.49), channel_id=1, source_target_pairs={{0,5},{1,4},{2,7},{3,6},{4,1},{5,0},{6,3},{7,2},{8,13},{9,12},{10,... | collective-permute-start | bytes 110600 | tf_op jit(solution)/shard_map/ppermute | solution.py:483
  104.6 4.6 %collective-permute-start.18 = (f32[72,128]{1,0:T(8,128)S(1)}, f32[72,128]{1,0:T(8,128)S(1)}, u32[]{:S(2)}, u32[]{:S(2)}) collective-permute-start(f32[72,128]{1,0:T(8,128)S(1)} %add.44), channel_id=1, source_target_pairs={{0,97},{1,96},{2,99},{3,98},{4,101},{5,100},{6,103},{7,102},{8,105... | collective-permute-start | bytes 110600 | tf_op jit(solution)/shard_map/ppermute | solution.py:483
  106.0 4.7 %collective-permute-start.24 = (f32[72,128]{1,0:T(8,128)S(1)}, f32[72,128]{1,0:T(8,128)S(1)}, u32[]{:S(2)}, u32[]{:S(2)}) collective-permute-start(f32[72,128]{1,0:T(8,128)S(1)} %add.50), channel_id=1, source_target_pairs={{0,13},{1,12},{2,15},{3,14},{4,9},{5,8},{6,11},{7,10},{8,5},{9,4},... | collective-permute-start | bytes 110600 | tf_op jit(solution)/shard_map/ppermute | solution.py:483
  110.7 1.4 %collective-permute-start.25 = (f32[144,128]{1,0:T(8,128)S(1)}, f32[144,128]{1,0:T(8,128)S(1)}, u32[]{:S(2)}, u32[]{:S(2)}) collective-permute-start(f32[144,128]{1,0:T(8,128)S(1)} %pad_maximum_fusion.mine_ref), channel_id=1, source_target_pairs={{0,1},{1,0},{2,3},{3,2},{4,5},{5,4},{6,7},{7,6},{8,9},{9,8},{10,11... | collective-permute-start | bytes 221192 | tf_op jit(solution)/shard_map/ppermute | solution.py:486

commit v7 on v6

--- a/solution.py
+++ b/solution.py
@@ -89,7 +89,7 @@
 
 
 def outer_kernel(last, place, part_ref, *refs):
-    rxa, rxb, rya, ryb = refs[2:4] + refs[0:2] if last else refs[0:4]
+    rxa, rxb, ryb, rya = refs[2:4] + refs[0:2] if last else refs[0:4]
     vel_ref, dif_ref, new_ref, *outs = refs[4:]
     gx, gy = place[0], place[1]
     odd_x, odd_y = gx % 2 == 1, gy % 2 == 1
@@ -133,7 +133,7 @@
 
     xa, xb, ya, yb = edges
     along_x = lambda: [lax.ppermute(xa, "gx", pairs(8, False)), lax.ppermute(xb, "gx", pairs(8, True))]
-    along_y = lambda: [lax.ppermute(ya, "gy", pairs(16, False)), lax.ppermute(yb, "gy", pairs(16, True))]
+    along_y = lambda: [lax.ppermute(yb, "gy", pairs(16, True)), lax.ppermute(ya, "gy", pairs(16, False))]
     return along_y() + along_x() if y_first else along_x() + along_y()
 
 

time: 114 us -> 113 us (level)
  waiting for transfers between devices: 41.9 us -> 38.1 us
  starting transfers between devices: 41.2 us -> 43.8 us
    all_to_all x1, starting transfers between devices: 6.34 us -> 3.49 us  [on_device(): lax.all_to_all(slabs, 'gy', 0, 0, tiled=True).reshape(32, 2 * F * X, Z)]
    ppermute x3, starting transfers between devices: 1.76 us -> 3.64 us  [exchange(): lax.ppermute(ya, 'gy', pairs(16, False))]
    ppermute x3, waiting for transfers between devices: 10.7 us -> 8.93 us  [exchange(): lax.ppermute(xa, 'gx', pairs(8, False))]
    ppermute x12, waiting for transfers between devices: 17.8 us -> 16 us  [sum_all(): lax.ppermute(part, ('gx', 'gy'), p)]
    ppermute x12, starting transfers between devices: 9.17 us -> 11 us  [sum_all(): lax.ppermute(part, ('gx', 'gy'), p)]
    ppermute x3, starting transfers between devices: 8.22 us -> 9.62 us  [exchange(): lax.ppermute(yb, 'gy', pairs(16, True))]
  transfers between devices with their start and end apart: 28 -> 28, of which waited for: 18 -> 18; matrix products, arithmetic and copies ran while one was open for 0% -> 0% of each run, Pallas kernels for 12% -> 13%
where the time goes in v7:
time: 113 us
  starting transfers between devices  43.8 us (39%)
  waiting for transfers between devices  38.1 us (34%)
  Pallas kernels  23.1 us (20%)
  local copies, waits for them, and re-layouts  6 us (5%)
  between operations  1.57 us (1%)
    ppermute x12, waiting for transfers between devices, sum_all(): lax.ppermute(part, ('gx', 'gy'), p)  16 us
    ppermute x12, starting transfers between devices, sum_all(): lax.ppermute(part, ('gx', 'gy'), p)  11 us
    ppermute x3, starting transfers between devices, exchange(): lax.ppermute(yb, 'gy', pairs(16, True))  9.62 us
    ppermute x3, waiting for transfers between devices, exchange(): lax.ppermute(xa, 'gx', pairs(8, False))  8.93 us
    pallas_call x1, Pallas kernels, on_device(): call(backward_kernel, [((HALF, 128), F32)] * 2, scratch=HELD + [pltpu.VME...  6.33 us
    unnamed x26, local copies, waits for them, and re-layouts  6 us
    ppermute x3, starting transfers between devices, exchange(): lax.ppermute(xb, 'gx', pairs(8, True))  5.97 us
    ppermute x3, waiting for transfers between devices, exchange(): lax.ppermute(yb, 'gy', pairs(16, True))  5.89 us
  transfers between devices with their start and end apart: 28, of which 18 were waited for; matrix products, arithmetic and copies ran while one was open for 0% of the time, Pallas kernels for 13%

profile of v7, /device:TPU:1, one launch (start us, length us, event | category | flops | bytes accessed | tf_op | source)
XLA Modules:
  0.0 112.7 jit_solution(11774322333081335756)
XLA Ops:
  0.7 1.1 copy-done
  2.6 2.5 %collective-permute-start = (f32[5,4,2048]{2,1,0:T(4,128)S(1)}, f32[5,4,2048]{2,1,0:T(4,128)S(1)}, u32[]{:S(2)}, u32[]{:S(2)}) collective-permute-start(f32[5,4,2048]{2,1,0:T(4,128)S(1)} %get-tuple-element.39), channel_id=1, source_target_pairs={{0,16},{16,0},{32,48},{48,32},{64,80},{80,64},{96,112},{112,96},{1... | collective-permute-start | bytes 491528 | tf_op jit(solution)/shard_map/ppermute | solution.py:135
  5.1 2.3 %collective-permute-start.1 = (f32[5,4,2048]{2,1,0:T(4,128)S(1)}, f32[5,4,2048]{2,1,0:T(4,128)S(1)}, u32[]{:S(2)}, u32[]{:S(2)}) collective-permute-start(f32[5,4,2048]{2,1,0:T(4,128)S(1)} %get-tuple-element.40), channel_id=1, source_target_pairs={{0,112},{16,32},{32,16},{48,64},{64,48},{80,96},{96,80},{112,0},{1... | collective-permute-start | bytes 491528 | tf_op jit(solution)/shard_map/ppermute | solution.py:135
  7.4 4.5 %collective-permute-start.2 = (f32[5,4,2048]{2,1,0:T(4,128)S(1)}, f32[5,4,2048]{2,1,0:T(4,128)S(1)}, u32[]{:S(2)}, u32[]{:S(2)}) collective-permute-start(f32[5,4,2048]{2,1,0:T(4,128)S(1)} %get-tuple-element.41), channel_id=1, source_target_pairs={{0,15},{1,2},{2,1},{3,4},{4,3},{5,6},{6,5},{7,8},{8,7},{9,10},{10,... | collective-permute-start | bytes 491528 | tf_op jit(solution)/shard_map/ppermute | solution.py:136
  11.8 1.7 %collective-permute-start.3 = (f32[5,4,2048]{2,1,0:T(4,128)S(1)}, f32[5,4,2048]{2,1,0:T(4,128)S(1)}, u32[]{:S(2)}, u32[]{:S(2)}) collective-permute-start(f32[5,4,2048]{2,1,0:T(4,128)S(1)} %get-tuple-element.42), channel_id=1, source_target_pairs={{0,1},{1,0},{2,3},{3,2},{4,5},{5,4},{6,7},{7,6},{8,9},{9,8},{10,11... | collective-permute-start | bytes 491528 | tf_op jit(solution)/shard_map/ppermute | solution.py:136
  13.6 1.2 %shard_map.178 = f32[16,2,40,128]{3,2,1,0:T(8,128)} custom-call(f32[20,4,2048]{2,1,0:T(4,128)S(1)} %bitcast.37), custom_call_target="tpu_custom_call" | custom-call | bytes 1500000 | tf_op jit(solution)/shard_map/pallas_call | solution.py:508
  14.8 3.5 %all-to-all-start.1 = ((f32[16,2,40,128]{3,2,1,0:T(8,128)}), f32[16,2,40,128]{3,2,1,0:T(8,128)S(1)}, u32[]{:S(2)}, u32[]{:S(2)}) async-start(f32[16,2,40,128]{3,2,1,0:T(8,128)} %shard_map.178), calls=%async_computation.1 | async-start | bytes 1310720 | tf_op jit(solution)/shard_map/all_to_all | solution.py:509
  18.3 1.1 copy-done.1
  19.3 1.0 copy-done.9
  20.3 0.9 copy-done.11
  21.3 0.9 shard_map.170.refs_1_
  22.3 1.0 copy-done.10
  23.2 0.9 copy-done.12
  24.1 1.0 shard_map.172
  25.3 1.7 %collective-permute-start.5 = (f32[5,4,2048]{2,1,0:T(4,128)S(1)}, f32[5,4,2048]{2,1,0:T(4,128)S(1)}, u32[]{:S(2)}, u32[]{:S(2)}) collective-permute-start(f32[5,4,2048]{2,1,0:T(4,128)S(1)} %get-tuple-element.45), channel_id=1, source_target_pairs={{0,112},{16,32},{32,16},{48,64},{64,48},{80,96},{96,80},{112,0},{1... | collective-permute-start | bytes 491528 | tf_op jit(solution)/shard_map/ppermute | solution.py:135
  27.0 3.6 %collective-permute-start.6 = (f32[5,4,2048]{2,1,0:T(4,128)S(1)}, f32[5,4,2048]{2,1,0:T(4,128)S(1)}, u32[]{:S(2)}, u32[]{:S(2)}) collective-permute-start(f32[5,4,2048]{2,1,0:T(4,128)S(1)} %get-tuple-element.46), channel_id=1, source_target_pairs={{0,15},{1,2},{2,1},{3,4},{4,3},{5,6},{6,5},{7,8},{8,7},{9,10},{10,... | collective-permute-start | bytes 491528 | tf_op jit(solution)/shard_map/ppermute | solution.py:136
  30.6 1.9 %collective-permute-start.7 = (f32[5,4,2048]{2,1,0:T(4,128)S(1)}, f32[5,4,2048]{2,1,0:T(4,128)S(1)}, u32[]{:S(2)}, u32[]{:S(2)}) collective-permute-start(f32[5,4,2048]{2,1,0:T(4,128)S(1)} %get-tuple-element.47), channel_id=1, source_target_pairs={{0,1},{1,0},{2,3},{3,2},{4,5},{5,4},{6,7},{7,6},{8,9},{9,8},{10,11... | collective-permute-start | bytes 491528 | tf_op jit(solution)/shard_map/ppermute | solution.py:136
  33.4 3.9 %collective-permute-done.4.refs_2_ = f32[5,4,2048]{2,1,0:T(4,128)S(1)} collective-permute-done((f32[5,4,2048]{2,1,0:T(4,128)S(1)}, f32[5,4,2048]{2,1,0:T(4,128)S(1)}, u32[]{:S(2)}, u32[]{:S(2)}) %collective-permute-start.4) | collective-permute-done | bytes 163872 | tf_op jit(solution)/shard_map/ppermute | solution.py:135
  37.3 4.0 %collective-permute-done.6.refs_4_ = f32[5,4,2048]{2,1,0:T(4,128)S(1)} collective-permute-done((f32[5,4,2048]{2,1,0:T(4,128)S(1)}, f32[5,4,2048]{2,1,0:T(4,128)S(1)}, u32[]{:S(2)}, u32[]{:S(2)}) %collective-permute-start.6) | collective-permute-done | bytes 163872 | tf_op jit(solution)/shard_map/ppermute | solution.py:136
  41.3 1.1 shard_map.174
  42.5 1.9 %collective-permute-start.11 = (f32[5,4,2048]{2,1,0:T(4,128)S(1)}, f32[5,4,2048]{2,1,0:T(4,128)S(1)}, u32[]{:S(2)}, u32[]{:S(2)}) collective-permute-start(f32[5,4,2048]{2,1,0:T(4,128)S(1)} %get-tuple-element.52), channel_id=1, source_target_pairs={{0,112},{16,32},{32,16},{48,64},{64,48},{80,96},{96,80},{112,0},{1... | collective-permute-start | bytes 491528 | tf_op jit(solution)/shard_map/ppermute | solution.py:135
  44.4 1.6 %collective-permute-start.8 = (f32[5,4,2048]{2,1,0:T(4,128)S(1)}, f32[5,4,2048]{2,1,0:T(4,128)S(1)}, u32[]{:S(2)}, u32[]{:S(2)}) collective-permute-start(f32[5,4,2048]{2,1,0:T(4,128)S(1)} %get-tuple-element.49), channel_id=1, source_target_pairs={{0,15},{1,2},{2,1},{3,4},{4,3},{5,6},{6,5},{7,8},{8,7},{9,10},{10,... | collective-permute-start | bytes 491528 | tf_op jit(solution)/shard_map/ppermute | solution.py:136
  46.0 0.9 shard_map.175.refs_1_
  46.9 5.0 %collective-permute-done.10.refs_4_ = f32[5,4,2048]{2,1,0:T(4,128)S(1)} collective-permute-done((f32[5,4,2048]{2,1,0:T(4,128)S(1)}, f32[5,4,2048]{2,1,0:T(4,128)S(1)}, u32[]{:S(2)}, u32[]{:S(2)}) %collective-permute-start.10) | collective-permute-done | bytes 163872 | tf_op jit(solution)/shard_map/ppermute | solution.py:135
  51.9 1.9 %collective-permute-done.8.refs_2_ = f32[5,4,2048]{2,1,0:T(4,128)S(1)} collective-permute-done((f32[5,4,2048]{2,1,0:T(4,128)S(1)}, f32[5,4,2048]{2,1,0:T(4,128)S(1)}, u32[]{:S(2)}, u32[]{:S(2)}) %collective-permute-start.8) | collective-permute-done | bytes 163872 | tf_op jit(solution)/shard_map/ppermute | solution.py:136
  53.8 2.1 %shard_map.176 = (f32[20,4,2048]{2,1,0:T(4,128)}, f32[16,2,40,128]{3,2,1,0:T(8,128)}) custom-call(s32[2]{0:T(128)S(1)} %pad_add_fusion.place.refs_0_, f32[20,4,2048]{2,1,0:T(4,128)S(1)} %shard_map.175.refs_1_, f32[5,4,2048]{2,1,0:T(4,128)S(1)} %collective-permute-done.8.refs_2_, f32[5,4,2048]{2,1,0:T(4,128)S(1)} %collective-permute-done.9.refs_3_, ...), custom_call_target="tpu_custom_call" | custom-call | flops 6000000000 | bytes 3000000 | tf_op jit(solution)/shard_map/pallas_call | solution.py:533
  55.9 5.3 %all-to-all-start = ((f32[16,2,40,128]{3,2,1,0:T(8,128)}), f32[16,2,40,128]{3,2,1,0:T(8,128)S(1)}, u32[]{:S(2)}, u32[]{:S(2)}) async-start(f32[16,2,40,128]{3,2,1,0:T(8,128)} %get-tuple-element.54), calls=%async_computation | async-start | bytes 1310720 | tf_op jit(solution)/shard_map/all_to_all | solution.py:553
  61.9 1.7 %shard_map.177 = (bf16[128,224]{1,0:T(8,128)(2,1)S(1)}, bf16[3,128,384]{2,1,0:T(8,128)(2,1)S(1)}, bf16[3,128,384]{2,1,0:T(8,128)(2,1)S(1)}, bf16[224,128]{1,0:T(...) custom-call(f32[45,3,32]{2,1,0:T(4,128)S(1)} %bitcast.41, f32[27,32,32]{2,1,0:T(8,128)S(1)} %bitcast.40, ...), custom_call_target="tpu_custom_call" | custom-call | bytes 1000000 | tf_op jit(solution)/shard_map/pallas_call | solution.py:510
  63.6 4.4 %shard_map.179.kept_ref = bf16[2,16384,1024]{2,1,0:T(8,128)(2,1)} custom-call(s32[2]{0:T(128)S(1)} %bitcast.43, f32[32,40,128]{2,1,0:T(8,128)S(1)} %bitcast.39, bf16[128,224]{1,0:T(8,128)(2,1)S(1)} %get-tuple-element.57.w1_ref, bf16[3,128,384]{2,1,0:T(8,128)(2,1)S(1)} %get-tuple-element.58.w2_ref, bf16[224,128]{1,0:T(8,128)(2,1)S(1)} %get-tuple-element.59.w3_ref, ...), custom_call_target="tpu_custom_call" | custom-call | flops 2000000000 | bytes 8000000 | tf_op jit(solution)/shard_map/pallas_call | solution.py:537
  68.0 5.5 %all-to-all-done = f32[16,2,40,128]{3,2,1,0:T(8,128)S(1)} async-done(((f32[16,2,40,128]{3,2,1,0:T(8,128)}), f32[16,2,40,128]{3,2,1,0:T(8,128)S(1)}, u32[]{:S(2)}, u32[]{:S(2)}) %all-to-all-start) | async-done | bytes 655392 | tf_op jit(solution)/shard_map/all_to_all | solution.py:553
  73.5 6.3 %shard_map.180 = (f32[144,128]{1,0:T(8,128)S(1)}, f32[144,128]{1,0:T(8,128)S(1)}) custom-call(s32[2]{0:T(128)S(1)} %pad_add_fusion.place.refs_0_, s32[2]{0:T(128)S(1)} %bitcast.44, s32[1]{0:T(128)} %bitcast.34.count, f32[32,40,128]{2,1,0:T(8,128)S(1)} %bitcast.35, bf16[3,128,384]{2,1,0:T(8,128)(2,1)S(1)} %get-tuple-element.55.w2_ref, ...), custom_call_target="tpu_custom_call" | custom-call | flops 4000000000 | bytes 10000000 | tf_op jit(solution)/shard_map/pallas_call | solution.py:554
  79.8 1.6 %collective-permute-start.12 = (f32[144,128]{1,0:T(8,128)S(1)}, f32[144,128]{1,0:T(8,128)S(1)}, u32[]{:S(2)}, u32[]{:S(2)}) collective-permute-start(f32[144,128]{1,0:T(8,128)S(1)} %get-tuple-element.62), channel_id=1, source_target_pairs={{0,1},{1,0},{2,3},{3,2},{4,5},{5,4},{6,7},{7,6},{8,9},{9,8},{10,11... | collective-permute-start | bytes 221192 | tf_op jit(solution)/shard_map/ppermute | solution.py:480
  81.4 0.9 collective-permute-done.12
  82.4 1.5 %collective-permute-start.13 = (f32[72,128]{1,0:T(8,128)S(1)}, f32[72,128]{1,0:T(8,128)S(1)}, u32[]{:S(2)}, u32[]{:S(2)}) collective-permute-start(f32[72,128]{1,0:T(8,128)S(1)} %get-tuple-element.72), channel_id=1, source_target_pairs={{0,17},{1,16},{2,19},{3,18},{4,21},{5,20},{6,23},{7,22},{8,25},{9,... | collective-permute-start | bytes 110600 | tf_op jit(solution)/shard_map/ppermute | solution.py:483
  84.6 1.3 %collective-permute-done.13 = f32[72,128]{1,0:T(8,128)S(1)} collective-permute-done((f32[72,128]{1,0:T(8,128)S(1)}, f32[72,128]{1,0:T(8,128)S(1)}, u32[]{:S(2)}, u32[]{:S(2)}) %collective-permute-start.13) | collective-permute-done | bytes 36896 | tf_op jit(solution)/shard_map/ppermute | solution.py:483
  85.9 1.4 %collective-permute-done.19 = f32[72,128]{1,0:T(8,128)S(1)} collective-permute-done((f32[72,128]{1,0:T(8,128)S(1)}, f32[72,128]{1,0:T(8,128)S(1)}, u32[]{:S(2)}, u32[]{:S(2)}) %collective-permute-start.19) | collective-permute-done | bytes 36896 | tf_op jit(solution)/shard_map/ppermute | solution.py:483
  87.4 1.0 collective-permute-start.20
  88.4 3.6 %collective-permute-done.14 = f32[72,128]{1,0:T(8,128)S(1)} collective-permute-done((f32[72,128]{1,0:T(8,128)S(1)}, f32[72,128]{1,0:T(8,128)S(1)}, u32[]{:S(2)}, u32[]{:S(2)}) %collective-permute-start.14) | collective-permute-done | bytes 36896 | tf_op jit(solution)/shard_map/ppermute | solution.py:483
  92.6 2.7 %collective-permute-done.15 = f32[72,128]{1,0:T(8,128)S(1)} collective-permute-done((f32[72,128]{1,0:T(8,128)S(1)}, f32[72,128]{1,0:T(8,128)S(1)}, u32[]{:S(2)}, u32[]{:S(2)}) %collective-permute-start.15) | collective-permute-done | bytes 36896 | tf_op jit(solution)/shard_map/ppermute | solution.py:483
  96.0 2.4 %collective-permute-start.22 = (f32[72,128]{1,0:T(8,128)S(1)}, f32[72,128]{1,0:T(8,128)S(1)}, u32[]{:S(2)}, u32[]{:S(2)}) collective-permute-start(f32[72,128]{1,0:T(8,128)S(1)} %add.48), channel_id=1, source_target_pairs={{0,19},{1,18},{2,17},{3,16},{4,23},{5,22},{6,21},{7,20},{8,27},{9,... | collective-permute-start | bytes 110600 | tf_op jit(solution)/shard_map/ppermute | solution.py:483
  98.4 1.5 %collective-permute-done.16 = f32[72,128]{1,0:T(8,128)S(1)} collective-permute-done((f32[72,128]{1,0:T(8,128)S(1)}, f32[72,128]{1,0:T(8,128)S(1)}, u32[]{:S(2)}, u32[]{:S(2)}) %collective-permute-start.16) | collective-permute-done | bytes 36896 | tf_op jit(solution)/shard_map/ppermute | solution.py:483
  101.9 1.4 %collective-permute-done.17 = f32[72,128]{1,0:T(8,128)S(1)} collective-permute-done((f32[72,128]{1,0:T(8,128)S(1)}, f32[72,128]{1,0:T(8,128)S(1)}, u32[]{:S(2)}, u32[]{:S(2)}) %collective-permute-start.17) | collective-permute-done | bytes 36896 | tf_op jit(solution)/shard_map/ppermute | solution.py:483
  103.4 0.9 collective-permute-start.18
  104.8 1.7 %collective-permute-start.24 = (f32[72,128]{1,0:T(8,128)S(1)}, f32[72,128]{1,0:T(8,128)S(1)}, u32[]{:S(2)}, u32[]{:S(2)}) collective-permute-start(f32[72,128]{1,0:T(8,128)S(1)} %add.50), channel_id=1, source_target_pairs={{0,13},{1,12},{2,15},{3,14},{4,9},{5,8},{6,11},{7,10},{8,5},{9,4},... | collective-permute-start | bytes 110600 | tf_op jit(solution)/shard_map/ppermute | solution.py:483
  106.5 1.4 %collective-permute-done.18 = f32[72,128]{1,0:T(8,128)S(1)} collective-permute-done((f32[72,128]{1,0:T(8,128)S(1)}, f32[72,128]{1,0:T(8,128)S(1)}, u32[]{:S(2)}, u32[]{:S(2)}) %collective-permute-start.18) | collective-permute-done | bytes 36896 | tf_op jit(solution)/shard_map/ppermute | solution.py:483
  108.0 1.5 %collective-permute-done.24 = f32[72,128]{1,0:T(8,128)S(1)} collective-permute-done((f32[72,128]{1,0:T(8,128)S(1)}, f32[72,128]{1,0:T(8,128)S(1)}, u32[]{:S(2)}, u32[]{:S(2)}) %collective-permute-start.24) | collective-permute-done | bytes 36896 | tf_op jit(solution)/shard_map/ppermute | solution.py:483
  110.0 0.9 collective-permute-done.25.other_ref
  110.9 1.8 %shard_map.181 = (f32[45,3,32]{2,1,0:T(4,128)}, f32[1,32]{1,0:T(1,128)}, f32[27,32,32]{2,1,0:T(8,128)}, f32[1,32]{1,0:T(1,128)}, f32[45,3,32]{2,1,0:T(4,128)}, /*index=5*/f32[1,5]{1,0:T(1,128)}, f32[1,1]{1,0:T(1,128)}) custom-call(s32[2]{0:T(128)S(1)} %pad_add_fusion.place.refs_0_, f32[144,128]{1,0:T(8,128)S(1)} %pad_maximum_fusion.mine_ref, ...), custom_call_target="tpu_custom_call" | custom-call | bytes 1000000 | tf_op jit(solution)/shard_map/pallas_call | solution.py:572
  (61 shorter events, 7.0 us)
Async XLA Ops:
  0.7 1.1 copy-start
  2.6 19.6 %collective-permute-start = (f32[5,4,2048]{2,1,0:T(4,128)S(1)}, f32[5,4,2048]{2,1,0:T(4,128)S(1)}, u32[]{:S(2)}, u32[]{:S(2)}) collective-permute-start(f32[5,4,2048]{2,1,0:T(4,128)S(1)} %get-tuple-element.39), channel_id=1, source_target_pairs={{0,16},{16,0},{32,48},{48,32},{64,80},{80,64},{96,112},{112,96},{1... | collective-permute-start | bytes 491528 | tf_op jit(solution)/shard_map/ppermute | solution.py:135
  5.1 17.1 %collective-permute-start.1 = (f32[5,4,2048]{2,1,0:T(4,128)S(1)}, f32[5,4,2048]{2,1,0:T(4,128)S(1)}, u32[]{:S(2)}, u32[]{:S(2)}) collective-permute-start(f32[5,4,2048]{2,1,0:T(4,128)S(1)} %get-tuple-element.40), channel_id=1, source_target_pairs={{0,112},{16,32},{32,16},{48,64},{64,48},{80,96},{96,80},{112,0},{1... | collective-permute-start | bytes 491528 | tf_op jit(solution)/shard_map/ppermute | solution.py:135
  7.4 14.8 %collective-permute-start.2 = (f32[5,4,2048]{2,1,0:T(4,128)S(1)}, f32[5,4,2048]{2,1,0:T(4,128)S(1)}, u32[]{:S(2)}, u32[]{:S(2)}) collective-permute-start(f32[5,4,2048]{2,1,0:T(4,128)S(1)} %get-tuple-element.41), channel_id=1, source_target_pairs={{0,15},{1,2},{2,1},{3,4},{4,3},{5,6},{6,5},{7,8},{8,7},{9,10},{10,... | collective-permute-start | bytes 491528 | tf_op jit(solution)/shard_map/ppermute | solution.py:136
  11.8 10.4 %collective-permute-start.3 = (f32[5,4,2048]{2,1,0:T(4,128)S(1)}, f32[5,4,2048]{2,1,0:T(4,128)S(1)}, u32[]{:S(2)}, u32[]{:S(2)}) collective-permute-start(f32[5,4,2048]{2,1,0:T(4,128)S(1)} %get-tuple-element.42), channel_id=1, source_target_pairs={{0,1},{1,0},{2,3},{3,2},{4,5},{5,4},{6,7},{7,6},{8,9},{9,8},{10,11... | collective-permute-start | bytes 491528 | tf_op jit(solution)/shard_map/ppermute | solution.py:136
  14.8 41.1 %all-to-all-start.1 = ((f32[16,2,40,128]{3,2,1,0:T(8,128)}), f32[16,2,40,128]{3,2,1,0:T(8,128)S(1)}, u32[]{:S(2)}, u32[]{:S(2)}) async-start(f32[16,2,40,128]{3,2,1,0:T(8,128)} %shard_map.178), calls=%async_computation.1 | async-start | bytes 1310720 | tf_op jit(solution)/shard_map/all_to_all | solution.py:509
  18.3 1.1 copy-start.1
  19.3 1.0 copy-start.9
  20.3 0.9 copy-start.11
  21.2 40.6 %copy-start.2 = (f32[32,32,3,3,3]{1,0,4,3,2:T(8,128)S(1)}, f32[32,32,3,3,3]{1,0,4,3,2:T(8,128)}, u32[]{:S(2)}) copy-start(f32[32,32,3,3,3]{1,0,4,3,2:T(8,128)} %param.18) | copy-start | bytes 331780
  21.2 40.6 %copy-start.3 = (f32[32,5,3,3,3]{0,4,3,2,1:T(4,128)S(1)}, f32[32,5,3,3,3]{0,4,3,2,1:T(4,128)}, u32[]{:S(2)}) copy-start(f32[32,5,3,3,3]{0,4,3,2,1:T(4,128)} %param.16) | copy-start | bytes 51844
  21.3 40.6 %copy-start.4 = (f32[5,32,3,3,3]{1,4,3,2,0:T(4,128)S(1)}, f32[5,32,3,3,3]{1,4,3,2,0:T(4,128)}, u32[]{:S(2)}) copy-start(f32[5,32,3,3,3]{1,4,3,2,0:T(4,128)} %param.20) | copy-start | bytes 51844
  21.3 40.6 %copy-start.6 = (f32[32]{0:T(128)S(1)}, f32[32]{0:T(128)}, u32[]{:S(2)}) copy-start(f32[32]{0:T(128)} %param.17) | copy-start | bytes 388
  21.3 40.6 %copy-start.7 = (f32[32]{0:T(128)S(1)}, f32[32]{0:T(128)}, u32[]{:S(2)}) copy-start(f32[32]{0:T(128)} %param.19) | copy-start | bytes 388
  21.3 40.6 %copy-start.8 = (f32[5]{0:T(128)S(1)}, f32[5]{0:T(128)}, u32[]{:S(2)}) copy-start(f32[5]{0:T(128)} %param.21) | copy-start | bytes 64
  21.3 42.3 %copy-start.5 = (s32[1,1,2]{2,1,0:T(1,128)S(1)}, s32[1,1,2]{2,1,0:T(1,128)}, u32[]{:S(2)}) copy-start(s32[1,1,2]{2,1,0:T(1,128)} %param.14) | copy-start | bytes 28
  22.2 1.0 copy-start.10
  23.2 0.9 copy-start.12
  25.2 12.2 %collective-permute-start.4 = (f32[5,4,2048]{2,1,0:T(4,128)S(1)}, f32[5,4,2048]{2,1,0:T(4,128)S(1)}, u32[]{:S(2)}, u32[]{:S(2)}) collective-permute-start(f32[5,4,2048]{2,1,0:T(4,128)S(1)} %get-tuple-element.44), channel_id=1, source_target_pairs={{0,16},{16,0},{32,48},{48,32},{64,80},{80,64},{96,112},{112,96},{1... | collective-permute-start | bytes 491528 | tf_op jit(solution)/shard_map/ppermute | solution.py:135
  25.3 12.1 %collective-permute-start.5 = (f32[5,4,2048]{2,1,0:T(4,128)S(1)}, f32[5,4,2048]{2,1,0:T(4,128)S(1)}, u32[]{:S(2)}, u32[]{:S(2)}) collective-permute-start(f32[5,4,2048]{2,1,0:T(4,128)S(1)} %get-tuple-element.45), channel_id=1, source_target_pairs={{0,112},{16,32},{32,16},{48,64},{64,48},{80,96},{96,80},{112,0},{1... | collective-permute-start | bytes 491528 | tf_op jit(solution)/shard_map/ppermute | solution.py:135
  27.0 14.3 %collective-permute-start.6 = (f32[5,4,2048]{2,1,0:T(4,128)S(1)}, f32[5,4,2048]{2,1,0:T(4,128)S(1)}, u32[]{:S(2)}, u32[]{:S(2)}) collective-permute-start(f32[5,4,2048]{2,1,0:T(4,128)S(1)} %get-tuple-element.46), channel_id=1, source_target_pairs={{0,15},{1,2},{2,1},{3,4},{4,3},{5,6},{6,5},{7,8},{8,7},{9,10},{10,... | collective-permute-start | bytes 491528 | tf_op jit(solution)/shard_map/ppermute | solution.py:136
  30.6 10.7 %collective-permute-start.7 = (f32[5,4,2048]{2,1,0:T(4,128)S(1)}, f32[5,4,2048]{2,1,0:T(4,128)S(1)}, u32[]{:S(2)}, u32[]{:S(2)}) collective-permute-start(f32[5,4,2048]{2,1,0:T(4,128)S(1)} %get-tuple-element.47), channel_id=1, source_target_pairs={{0,1},{1,0},{2,3},{3,2},{4,5},{5,4},{6,7},{7,6},{8,9},{9,8},{10,11... | collective-permute-start | bytes 491528 | tf_op jit(solution)/shard_map/ppermute | solution.py:136
  42.4 9.5 %collective-permute-start.10 = (f32[5,4,2048]{2,1,0:T(4,128)S(1)}, f32[5,4,2048]{2,1,0:T(4,128)S(1)}, u32[]{:S(2)}, u32[]{:S(2)}) collective-permute-start(f32[5,4,2048]{2,1,0:T(4,128)S(1)} %get-tuple-element.51), channel_id=1, source_target_pairs={{0,16},{16,0},{32,48},{48,32},{64,80},{80,64},{96,112},{112,96},{1... | collective-permute-start | bytes 491528 | tf_op jit(solution)/shard_map/ppermute | solution.py:135
  42.5 9.4 %collective-permute-start.11 = (f32[5,4,2048]{2,1,0:T(4,128)S(1)}, f32[5,4,2048]{2,1,0:T(4,128)S(1)}, u32[]{:S(2)}, u32[]{:S(2)}) collective-permute-start(f32[5,4,2048]{2,1,0:T(4,128)S(1)} %get-tuple-element.52), channel_id=1, source_target_pairs={{0,112},{16,32},{32,16},{48,64},{64,48},{80,96},{96,80},{112,0},{1... | collective-permute-start | bytes 491528 | tf_op jit(solution)/shard_map/ppermute | solution.py:135
  44.4 9.4 %collective-permute-start.8 = (f32[5,4,2048]{2,1,0:T(4,128)S(1)}, f32[5,4,2048]{2,1,0:T(4,128)S(1)}, u32[]{:S(2)}, u32[]{:S(2)}) collective-permute-start(f32[5,4,2048]{2,1,0:T(4,128)S(1)} %get-tuple-element.49), channel_id=1, source_target_pairs={{0,15},{1,2},{2,1},{3,4},{4,3},{5,6},{6,5},{7,8},{8,7},{9,10},{10,... | collective-permute-start | bytes 491528 | tf_op jit(solution)/shard_map/ppermute | solution.py:136
  46.0 7.8 %collective-permute-start.9 = (f32[5,4,2048]{2,1,0:T(4,128)S(1)}, f32[5,4,2048]{2,1,0:T(4,128)S(1)}, u32[]{:S(2)}, u32[]{:S(2)}) collective-permute-start(f32[5,4,2048]{2,1,0:T(4,128)S(1)} %get-tuple-element.50), channel_id=1, source_target_pairs={{0,1},{1,0},{2,3},{3,2},{4,5},{5,4},{6,7},{7,6},{8,9},{9,8},{10,11... | collective-permute-start | bytes 491528 | tf_op jit(solution)/shard_map/ppermute | solution.py:136
  55.9 17.6 %all-to-all-start = ((f32[16,2,40,128]{3,2,1,0:T(8,128)}), f32[16,2,40,128]{3,2,1,0:T(8,128)S(1)}, u32[]{:S(2)}, u32[]{:S(2)}) async-start(f32[16,2,40,128]{3,2,1,0:T(8,128)} %get-tuple-element.54), calls=%async_computation | async-start | bytes 1310720 | tf_op jit(solution)/shard_map/all_to_all | solution.py:553
  79.8 2.5 %collective-permute-start.12 = (f32[144,128]{1,0:T(8,128)S(1)}, f32[144,128]{1,0:T(8,128)S(1)}, u32[]{:S(2)}, u32[]{:S(2)}) collective-permute-start(f32[144,128]{1,0:T(8,128)S(1)} %get-tuple-element.62), channel_id=1, source_target_pairs={{0,1},{1,0},{2,3},{3,2},{4,5},{5,4},{6,7},{7,6},{8,9},{9,8},{10,11... | collective-permute-start | bytes 221192 | tf_op jit(solution)/shard_map/ppermute | solution.py:480
  82.4 3.5 %collective-permute-start.13 = (f32[72,128]{1,0:T(8,128)S(1)}, f32[72,128]{1,0:T(8,128)S(1)}, u32[]{:S(2)}, u32[]{:S(2)}) collective-permute-start(f32[72,128]{1,0:T(8,128)S(1)} %get-tuple-element.72), channel_id=1, source_target_pairs={{0,17},{1,16},{2,19},{3,18},{4,21},{5,20},{6,23},{7,22},{8,25},{9,... | collective-permute-start | bytes 110600 | tf_op jit(solution)/shard_map/ppermute | solution.py:483
  83.9 3.4 %collective-permute-start.19 = (f32[72,128]{1,0:T(8,128)S(1)}, f32[72,128]{1,0:T(8,128)S(1)}, u32[]{:S(2)}, u32[]{:S(2)}) collective-permute-start(f32[72,128]{1,0:T(8,128)S(1)} %get-tuple-element.73), channel_id=1, source_target_pairs={{0,33},{1,32},{2,35},{3,34},{4,37},{5,36},{6,39},{7,38},{8,41},{9,... | collective-permute-start | bytes 110600 | tf_op jit(solution)/shard_map/ppermute | solution.py:483
  87.3 4.7 %collective-permute-start.14 = (f32[72,128]{1,0:T(8,128)S(1)}, f32[72,128]{1,0:T(8,128)S(1)}, u32[]{:S(2)}, u32[]{:S(2)}) collective-permute-start(f32[72,128]{1,0:T(8,128)S(1)} %get-tuple-element.70), channel_id=1, source_target_pairs={{0,19},{1,18},{2,17},{3,16},{4,23},{5,22},{6,21},{7,20},{8,27},{9,... | collective-permute-start | bytes 110600 | tf_op jit(solution)/shard_map/ppermute | solution.py:483
  87.4 4.7 %collective-permute-start.20 = (f32[72,128]{1,0:T(8,128)S(1)}, f32[72,128]{1,0:T(8,128)S(1)}, u32[]{:S(2)}, u32[]{:S(2)}) collective-permute-start(f32[72,128]{1,0:T(8,128)S(1)} %get-tuple-element.71), channel_id=1, source_target_pairs={{0,97},{1,96},{2,99},{3,98},{4,101},{5,100},{6,103},{7,102},{8,105... | collective-permute-start | bytes 110600 | tf_op jit(solution)/shard_map/ppermute | solution.py:483
  92.0 3.4 %collective-permute-start.15 = (f32[72,128]{1,0:T(8,128)S(1)}, f32[72,128]{1,0:T(8,128)S(1)}, u32[]{:S(2)}, u32[]{:S(2)}) collective-permute-start(f32[72,128]{1,0:T(8,128)S(1)} %add.41), channel_id=1, source_target_pairs={{0,5},{1,4},{2,7},{3,6},{4,1},{5,0},{6,3},{7,2},{8,13},{9,12},{10,... | collective-permute-start | bytes 110600 | tf_op jit(solution)/shard_map/ppermute | solution.py:483
  92.1 3.9 %collective-permute-start.21 = (f32[72,128]{1,0:T(8,128)S(1)}, f32[72,128]{1,0:T(8,128)S(1)}, u32[]{:S(2)}, u32[]{:S(2)}) collective-permute-start(f32[72,128]{1,0:T(8,128)S(1)} %add.47), channel_id=1, source_target_pairs={{0,17},{1,16},{2,19},{3,18},{4,21},{5,20},{6,23},{7,22},{8,25},{9,... | collective-permute-start | bytes 110600 | tf_op jit(solution)/shard_map/ppermute | solution.py:483
  95.4 4.6 %collective-permute-start.16 = (f32[72,128]{1,0:T(8,128)S(1)}, f32[72,128]{1,0:T(8,128)S(1)}, u32[]{:S(2)}, u32[]{:S(2)}) collective-permute-start(f32[72,128]{1,0:T(8,128)S(1)} %add.42), channel_id=1, source_target_pairs={{0,13},{1,12},{2,15},{3,14},{4,9},{5,8},{6,11},{7,10},{8,5},{9,4},... | collective-permute-start | bytes 110600 | tf_op jit(solution)/shard_map/ppermute | solution.py:483
  96.0 5.3 %collective-permute-start.22 = (f32[72,128]{1,0:T(8,128)S(1)}, f32[72,128]{1,0:T(8,128)S(1)}, u32[]{:S(2)}, u32[]{:S(2)}) collective-permute-start(f32[72,128]{1,0:T(8,128)S(1)} %add.48), channel_id=1, source_target_pairs={{0,19},{1,18},{2,17},{3,16},{4,23},{5,22},{6,21},{7,20},{8,27},{9,... | collective-permute-start | bytes 110600 | tf_op jit(solution)/shard_map/ppermute | solution.py:483
  100.0 3.4 %collective-permute-start.17 = (f32[72,128]{1,0:T(8,128)S(1)}, f32[72,128]{1,0:T(8,128)S(1)}, u32[]{:S(2)}, u32[]{:S(2)}) collective-permute-start(f32[72,128]{1,0:T(8,128)S(1)} %add.43), channel_id=1, source_target_pairs={{0,33},{1,32},{2,35},{3,34},{4,37},{5,36},{6,39},{7,38},{8,41},{9,... | collective-permute-start | bytes 110600 | tf_op jit(solution)/shard_map/ppermute | solution.py:483
  101.3 3.5 %collective-permute-start.23 = (f32[72,128]{1,0:T(8,128)S(1)}, f32[72,128]{1,0:T(8,128)S(1)}, u32[]{:S(2)}, u32[]{:S(2)}) collective-permute-start(f32[72,128]{1,0:T(8,128)S(1)} %add.49), channel_id=1, source_target_pairs={{0,5},{1,4},{2,7},{3,6},{4,1},{5,0},{6,3},{7,2},{8,13},{9,12},{10,... | collective-permute-start | bytes 110600 | tf_op jit(solution)/shard_map/ppermute | solution.py:483
  103.4 4.6 %collective-permute-start.18 = (f32[72,128]{1,0:T(8,128)S(1)}, f32[72,128]{1,0:T(8,128)S(1)}, u32[]{:S(2)}, u32[]{:S(2)}) collective-permute-start(f32[72,128]{1,0:T(8,128)S(1)} %add.44), channel_id=1, source_target_pairs={{0,97},{1,96},{2,99},{3,98},{4,101},{5,100},{6,103},{7,102},{8,105... | collective-permute-start | bytes 110600 | tf_op jit(solution)/shard_map/ppermute | solution.py:483
  104.8 4.7 %collective-permute-start.24 = (f32[72,128]{1,0:T(8,128)S(1)}, f32[72,128]{1,0:T(8,128)S(1)}, u32[]{:S(2)}, u32[]{:S(2)}) collective-permute-start(f32[72,128]{1,0:T(8,128)S(1)} %add.50), channel_id=1, source_target_pairs={{0,13},{1,12},{2,15},{3,14},{4,9},{5,8},{6,11},{7,10},{8,5},{9,4},... | collective-permute-start | bytes 110600 | tf_op jit(solution)/shard_map/ppermute | solution.py:483
  109.5 1.4 %collective-permute-start.25 = (f32[144,128]{1,0:T(8,128)S(1)}, f32[144,128]{1,0:T(8,128)S(1)}, u32[]{:S(2)}, u32[]{:S(2)}) collective-permute-start(f32[144,128]{1,0:T(8,128)S(1)} %pad_maximum_fusion.mine_ref), channel_id=1, source_target_pairs={{0,1},{1,0},{2,3},{3,2},{4,5},{5,4},{6,7},{7,6},{8,9},{9,8},{10,11... | collective-permute-start | bytes 221192 | tf_op jit(solution)/shard_map/ppermute | solution.py:486

commit v8 on v7

--- a/solution.py
+++ b/solution.py
@@ -357,10 +357,13 @@
     dw3 = jnp.zeros((128, TALL), F32)
     dw2 = [jnp.zeros((128, 384), F32) for _ in range(3)]
     for p in range(2):
+        patch_rows(slabs_ref, anchors[p], last_ref.at[p])
+        clear_ends(b_ref.at[p])
+        clear_ends(a1_ref.at[p])
+    for p in range(2):
         copies["sum", p].wait()
     for p in range(2):
         live = jnp.where(p < count[0], 1.0, 0.0).astype(F32)
-        patch_rows(slabs_ref, anchors[p], last_ref.at[p])
         parts = sum_ref[p].astype(F32)
         err = parts[0:ROWS] + parts[ROWS : 2 * ROWS] + parts[2 * ROWS : 3 * ROWS] - last_ref[p]
         loss = loss + live * jnp.sum(err * err, axis=1, keepdims=True)
@@ -375,10 +378,8 @@
         dw3 = dw3 + dot_t(a2_ref[p], g_ref[p])
         dy2 = da2 * d2_ref[p].astype(F32)
         db2 = db2 + jnp.sum(dy2, axis=1, keepdims=True)
-        clear_ends(b_ref.at[p])
         for k in range(PY):
             fill_z(dy2[:, k * Z : (k + 1) * Z], k, b_ref.at[p], -1)
-        clear_ends(a1_ref.at[p])
         for k in range(PY):
             fill_z(a1_kept[p, :, k * Z : (k + 1) * Z].astype(F32), k, a1_ref.at[p], 1)
         fill_taps(cells_ref[p].astype(F32)[0:ROWS], taps_ref.at[p], 1)

time: 113 us -> 113 us (level)
  no operation moved by 1% of the time
where the time goes in v8:
time: 113 us
  starting transfers between devices  43.8 us (39%)
  waiting for transfers between devices  38.1 us (34%)
  Pallas kernels  23 us (20%)
  local copies, waits for them, and re-layouts  6 us (5%)
  between operations  1.57 us (1%)
    ppermute x12, waiting for transfers between devices, sum_all(): lax.ppermute(part, ('gx', 'gy'), p)  16 us
    ppermute x12, starting transfers between devices, sum_all(): lax.ppermute(part, ('gx', 'gy'), p)  11 us
    ppermute x3, starting transfers between devices, exchange(): lax.ppermute(yb, 'gy', pairs(16, True))  9.62 us
    ppermute x3, waiting for transfers between devices, exchange(): lax.ppermute(xa, 'gx', pairs(8, False))  8.93 us
    pallas_call x1, Pallas kernels, on_device(): call(backward_kernel, [((HALF, 128), F32)] * 2, scratch=HELD + [pltpu.VME...  6.29 us
    unnamed x26, local copies, waits for them, and re-layouts  6 us
    ppermute x3, starting transfers between devices, exchange(): lax.ppermute(xb, 'gx', pairs(8, True))  5.97 us
    ppermute x3, waiting for transfers between devices, exchange(): lax.ppermute(yb, 'gy', pairs(16, True))  5.89 us
  transfers between devices with their start and end apart: 28, of which 18 were waited for; matrix products, arithmetic and copies ran while one was open for 0% of the time, Pallas kernels for 13%

profile of v8, /device:TPU:1, one launch (start us, length us, event | category | flops | bytes accessed | tf_op | source)
XLA Modules:
  0.0 112.6 jit_solution(9033418675647526500)
XLA Ops:
  0.7 1.1 copy-done
  2.6 2.5 %collective-permute-start = (f32[5,4,2048]{2,1,0:T(4,128)S(1)}, f32[5,4,2048]{2,1,0:T(4,128)S(1)}, u32[]{:S(2)}, u32[]{:S(2)}) collective-permute-start(f32[5,4,2048]{2,1,0:T(4,128)S(1)} %get-tuple-element.39), channel_id=1, source_target_pairs={{0,16},{16,0},{32,48},{48,32},{64,80},{80,64},{96,112},{112,96},{1... | collective-permute-start | bytes 491528 | tf_op jit(solution)/shard_map/ppermute | solution.py:135
  5.1 2.3 %collective-permute-start.1 = (f32[5,4,2048]{2,1,0:T(4,128)S(1)}, f32[5,4,2048]{2,1,0:T(4,128)S(1)}, u32[]{:S(2)}, u32[]{:S(2)}) collective-permute-start(f32[5,4,2048]{2,1,0:T(4,128)S(1)} %get-tuple-element.40), channel_id=1, source_target_pairs={{0,112},{16,32},{32,16},{48,64},{64,48},{80,96},{96,80},{112,0},{1... | collective-permute-start | bytes 491528 | tf_op jit(solution)/shard_map/ppermute | solution.py:135
  7.4 4.5 %collective-permute-start.2 = (f32[5,4,2048]{2,1,0:T(4,128)S(1)}, f32[5,4,2048]{2,1,0:T(4,128)S(1)}, u32[]{:S(2)}, u32[]{:S(2)}) collective-permute-start(f32[5,4,2048]{2,1,0:T(4,128)S(1)} %get-tuple-element.41), channel_id=1, source_target_pairs={{0,15},{1,2},{2,1},{3,4},{4,3},{5,6},{6,5},{7,8},{8,7},{9,10},{10,... | collective-permute-start | bytes 491528 | tf_op jit(solution)/shard_map/ppermute | solution.py:136
  11.8 1.7 %collective-permute-start.3 = (f32[5,4,2048]{2,1,0:T(4,128)S(1)}, f32[5,4,2048]{2,1,0:T(4,128)S(1)}, u32[]{:S(2)}, u32[]{:S(2)}) collective-permute-start(f32[5,4,2048]{2,1,0:T(4,128)S(1)} %get-tuple-element.42), channel_id=1, source_target_pairs={{0,1},{1,0},{2,3},{3,2},{4,5},{5,4},{6,7},{7,6},{8,9},{9,8},{10,11... | collective-permute-start | bytes 491528 | tf_op jit(solution)/shard_map/ppermute | solution.py:136
  13.6 1.2 %shard_map.178 = f32[16,2,40,128]{3,2,1,0:T(8,128)} custom-call(f32[20,4,2048]{2,1,0:T(4,128)S(1)} %bitcast.37), custom_call_target="tpu_custom_call" | custom-call | bytes 1500000 | tf_op jit(solution)/shard_map/pallas_call | solution.py:509
  14.8 3.5 %all-to-all-start.1 = ((f32[16,2,40,128]{3,2,1,0:T(8,128)}), f32[16,2,40,128]{3,2,1,0:T(8,128)S(1)}, u32[]{:S(2)}, u32[]{:S(2)}) async-start(f32[16,2,40,128]{3,2,1,0:T(8,128)} %shard_map.178), calls=%async_computation.1 | async-start | bytes 1310720 | tf_op jit(solution)/shard_map/all_to_all | solution.py:510
  18.3 1.1 copy-done.1
  19.3 1.0 copy-done.9
  20.3 0.9 copy-done.11
  21.3 0.9 shard_map.170.refs_1_
  22.3 1.0 copy-done.10
  23.2 0.9 copy-done.12
  24.1 1.0 shard_map.172
  25.3 1.7 %collective-permute-start.5 = (f32[5,4,2048]{2,1,0:T(4,128)S(1)}, f32[5,4,2048]{2,1,0:T(4,128)S(1)}, u32[]{:S(2)}, u32[]{:S(2)}) collective-permute-start(f32[5,4,2048]{2,1,0:T(4,128)S(1)} %get-tuple-element.45), channel_id=1, source_target_pairs={{0,112},{16,32},{32,16},{48,64},{64,48},{80,96},{96,80},{112,0},{1... | collective-permute-start | bytes 491528 | tf_op jit(solution)/shard_map/ppermute | solution.py:135
  27.0 3.6 %collective-permute-start.6 = (f32[5,4,2048]{2,1,0:T(4,128)S(1)}, f32[5,4,2048]{2,1,0:T(4,128)S(1)}, u32[]{:S(2)}, u32[]{:S(2)}) collective-permute-start(f32[5,4,2048]{2,1,0:T(4,128)S(1)} %get-tuple-element.46), channel_id=1, source_target_pairs={{0,15},{1,2},{2,1},{3,4},{4,3},{5,6},{6,5},{7,8},{8,7},{9,10},{10,... | collective-permute-start | bytes 491528 | tf_op jit(solution)/shard_map/ppermute | solution.py:136
  30.6 1.9 %collective-permute-start.7 = (f32[5,4,2048]{2,1,0:T(4,128)S(1)}, f32[5,4,2048]{2,1,0:T(4,128)S(1)}, u32[]{:S(2)}, u32[]{:S(2)}) collective-permute-start(f32[5,4,2048]{2,1,0:T(4,128)S(1)} %get-tuple-element.47), channel_id=1, source_target_pairs={{0,1},{1,0},{2,3},{3,2},{4,5},{5,4},{6,7},{7,6},{8,9},{9,8},{10,11... | collective-permute-start | bytes 491528 | tf_op jit(solution)/shard_map/ppermute | solution.py:136
  33.4 3.9 %collective-permute-done.4.refs_2_ = f32[5,4,2048]{2,1,0:T(4,128)S(1)} collective-permute-done((f32[5,4,2048]{2,1,0:T(4,128)S(1)}, f32[5,4,2048]{2,1,0:T(4,128)S(1)}, u32[]{:S(2)}, u32[]{:S(2)}) %collective-permute-start.4) | collective-permute-done | bytes 163872 | tf_op jit(solution)/shard_map/ppermute | solution.py:135
  37.3 4.0 %collective-permute-done.6.refs_4_ = f32[5,4,2048]{2,1,0:T(4,128)S(1)} collective-permute-done((f32[5,4,2048]{2,1,0:T(4,128)S(1)}, f32[5,4,2048]{2,1,0:T(4,128)S(1)}, u32[]{:S(2)}, u32[]{:S(2)}) %collective-permute-start.6) | collective-permute-done | bytes 163872 | tf_op jit(solution)/shard_map/ppermute | solution.py:136
  41.3 1.1 shard_map.174
  42.5 1.9 %collective-permute-start.11 = (f32[5,4,2048]{2,1,0:T(4,128)S(1)}, f32[5,4,2048]{2,1,0:T(4,128)S(1)}, u32[]{:S(2)}, u32[]{:S(2)}) collective-permute-start(f32[5,4,2048]{2,1,0:T(4,128)S(1)} %get-tuple-element.52), channel_id=1, source_target_pairs={{0,112},{16,32},{32,16},{48,64},{64,48},{80,96},{96,80},{112,0},{1... | collective-permute-start | bytes 491528 | tf_op jit(solution)/shard_map/ppermute | solution.py:135
  44.4 1.6 %collective-permute-start.8 = (f32[5,4,2048]{2,1,0:T(4,128)S(1)}, f32[5,4,2048]{2,1,0:T(4,128)S(1)}, u32[]{:S(2)}, u32[]{:S(2)}) collective-permute-start(f32[5,4,2048]{2,1,0:T(4,128)S(1)} %get-tuple-element.49), channel_id=1, source_target_pairs={{0,15},{1,2},{2,1},{3,4},{4,3},{5,6},{6,5},{7,8},{8,7},{9,10},{10,... | collective-permute-start | bytes 491528 | tf_op jit(solution)/shard_map/ppermute | solution.py:136
  46.0 0.9 shard_map.175.refs_1_
  46.9 5.0 %collective-permute-done.10.refs_4_ = f32[5,4,2048]{2,1,0:T(4,128)S(1)} collective-permute-done((f32[5,4,2048]{2,1,0:T(4,128)S(1)}, f32[5,4,2048]{2,1,0:T(4,128)S(1)}, u32[]{:S(2)}, u32[]{:S(2)}) %collective-permute-start.10) | collective-permute-done | bytes 163872 | tf_op jit(solution)/shard_map/ppermute | solution.py:135
  51.9 1.9 %collective-permute-done.8.refs_2_ = f32[5,4,2048]{2,1,0:T(4,128)S(1)} collective-permute-done((f32[5,4,2048]{2,1,0:T(4,128)S(1)}, f32[5,4,2048]{2,1,0:T(4,128)S(1)}, u32[]{:S(2)}, u32[]{:S(2)}) %collective-permute-start.8) | collective-permute-done | bytes 163872 | tf_op jit(solution)/shard_map/ppermute | solution.py:136
  53.8 2.1 %shard_map.176 = (f32[20,4,2048]{2,1,0:T(4,128)}, f32[16,2,40,128]{3,2,1,0:T(8,128)}) custom-call(s32[2]{0:T(128)S(1)} %pad_add_fusion.place.refs_0_, f32[20,4,2048]{2,1,0:T(4,128)S(1)} %shard_map.175.refs_1_, f32[5,4,2048]{2,1,0:T(4,128)S(1)} %collective-permute-done.8.refs_2_, f32[5,4,2048]{2,1,0:T(4,128)S(1)} %collective-permute-done.9.refs_3_, ...), custom_call_target="tpu_custom_call" | custom-call | flops 6000000000 | bytes 3000000 | tf_op jit(solution)/shard_map/pallas_call | solution.py:534
  55.9 5.3 %all-to-all-start = ((f32[16,2,40,128]{3,2,1,0:T(8,128)}), f32[16,2,40,128]{3,2,1,0:T(8,128)S(1)}, u32[]{:S(2)}, u32[]{:S(2)}) async-start(f32[16,2,40,128]{3,2,1,0:T(8,128)} %get-tuple-element.54), calls=%async_computation | async-start | bytes 1310720 | tf_op jit(solution)/shard_map/all_to_all | solution.py:554
  61.9 1.7 %shard_map.177 = (bf16[128,224]{1,0:T(8,128)(2,1)S(1)}, bf16[3,128,384]{2,1,0:T(8,128)(2,1)S(1)}, bf16[3,128,384]{2,1,0:T(8,128)(2,1)S(1)}, bf16[224,128]{1,0:T(...) custom-call(f32[45,3,32]{2,1,0:T(4,128)S(1)} %bitcast.41, f32[27,32,32]{2,1,0:T(8,128)S(1)} %bitcast.40, ...), custom_call_target="tpu_custom_call" | custom-call | bytes 1000000 | tf_op jit(solution)/shard_map/pallas_call | solution.py:511
  63.6 4.4 %shard_map.179.kept_ref = bf16[2,16384,1024]{2,1,0:T(8,128)(2,1)} custom-call(s32[2]{0:T(128)S(1)} %bitcast.43, f32[32,40,128]{2,1,0:T(8,128)S(1)} %bitcast.39, bf16[128,224]{1,0:T(8,128)(2,1)S(1)} %get-tuple-element.57.w1_ref, bf16[3,128,384]{2,1,0:T(8,128)(2,1)S(1)} %get-tuple-element.58.w2_ref, bf16[224,128]{1,0:T(8,128)(2,1)S(1)} %get-tuple-element.59.w3_ref, ...), custom_call_target="tpu_custom_call" | custom-call | flops 2000000000 | bytes 8000000 | tf_op jit(solution)/shard_map/pallas_call | solution.py:538
  68.0 5.5 %all-to-all-done = f32[16,2,40,128]{3,2,1,0:T(8,128)S(1)} async-done(((f32[16,2,40,128]{3,2,1,0:T(8,128)}), f32[16,2,40,128]{3,2,1,0:T(8,128)S(1)}, u32[]{:S(2)}, u32[]{:S(2)}) %all-to-all-start) | async-done | bytes 655392 | tf_op jit(solution)/shard_map/all_to_all | solution.py:554
  73.5 6.3 %shard_map.180 = (f32[144,128]{1,0:T(8,128)S(1)}, f32[144,128]{1,0:T(8,128)S(1)}) custom-call(s32[2]{0:T(128)S(1)} %pad_add_fusion.place.refs_0_, s32[2]{0:T(128)S(1)} %bitcast.44, s32[1]{0:T(128)} %bitcast.34.count, f32[32,40,128]{2,1,0:T(8,128)S(1)} %bitcast.35, bf16[3,128,384]{2,1,0:T(8,128)(2,1)S(1)} %get-tuple-element.55.w2_ref, ...), custom_call_target="tpu_custom_call" | custom-call | flops 4000000000 | bytes 10000000 | tf_op jit(solution)/shard_map/pallas_call | solution.py:555
  79.8 1.6 %collective-permute-start.12 = (f32[144,128]{1,0:T(8,128)S(1)}, f32[144,128]{1,0:T(8,128)S(1)}, u32[]{:S(2)}, u32[]{:S(2)}) collective-permute-start(f32[144,128]{1,0:T(8,128)S(1)} %get-tuple-element.62), channel_id=1, source_target_pairs={{0,1},{1,0},{2,3},{3,2},{4,5},{5,4},{6,7},{7,6},{8,9},{9,8},{10,11... | collective-permute-start | bytes 221192 | tf_op jit(solution)/shard_map/ppermute | solution.py:481
  81.4 0.9 collective-permute-done.12
  82.3 1.5 %collective-permute-start.13 = (f32[72,128]{1,0:T(8,128)S(1)}, f32[72,128]{1,0:T(8,128)S(1)}, u32[]{:S(2)}, u32[]{:S(2)}) collective-permute-start(f32[72,128]{1,0:T(8,128)S(1)} %get-tuple-element.72), channel_id=1, source_target_pairs={{0,17},{1,16},{2,19},{3,18},{4,21},{5,20},{6,23},{7,22},{8,25},{9,... | collective-permute-start | bytes 110600 | tf_op jit(solution)/shard_map/ppermute | solution.py:484
  84.6 1.3 %collective-permute-done.13 = f32[72,128]{1,0:T(8,128)S(1)} collective-permute-done((f32[72,128]{1,0:T(8,128)S(1)}, f32[72,128]{1,0:T(8,128)S(1)}, u32[]{:S(2)}, u32[]{:S(2)}) %collective-permute-start.13) | collective-permute-done | bytes 36896 | tf_op jit(solution)/shard_map/ppermute | solution.py:484
  85.9 1.4 %collective-permute-done.19 = f32[72,128]{1,0:T(8,128)S(1)} collective-permute-done((f32[72,128]{1,0:T(8,128)S(1)}, f32[72,128]{1,0:T(8,128)S(1)}, u32[]{:S(2)}, u32[]{:S(2)}) %collective-permute-start.19) | collective-permute-done | bytes 36896 | tf_op jit(solution)/shard_map/ppermute | solution.py:484
  87.4 1.0 collective-permute-start.20
  88.4 3.6 %collective-permute-done.14 = f32[72,128]{1,0:T(8,128)S(1)} collective-permute-done((f32[72,128]{1,0:T(8,128)S(1)}, f32[72,128]{1,0:T(8,128)S(1)}, u32[]{:S(2)}, u32[]{:S(2)}) %collective-permute-start.14) | collective-permute-done | bytes 36896 | tf_op jit(solution)/shard_map/ppermute | solution.py:484
  92.6 2.7 %collective-permute-done.15 = f32[72,128]{1,0:T(8,128)S(1)} collective-permute-done((f32[72,128]{1,0:T(8,128)S(1)}, f32[72,128]{1,0:T(8,128)S(1)}, u32[]{:S(2)}, u32[]{:S(2)}) %collective-permute-start.15) | collective-permute-done | bytes 36896 | tf_op jit(solution)/shard_map/ppermute | solution.py:484
  96.0 2.4 %collective-permute-start.22 = (f32[72,128]{1,0:T(8,128)S(1)}, f32[72,128]{1,0:T(8,128)S(1)}, u32[]{:S(2)}, u32[]{:S(2)}) collective-permute-start(f32[72,128]{1,0:T(8,128)S(1)} %add.48), channel_id=1, source_target_pairs={{0,19},{1,18},{2,17},{3,16},{4,23},{5,22},{6,21},{7,20},{8,27},{9,... | collective-permute-start | bytes 110600 | tf_op jit(solution)/shard_map/ppermute | solution.py:484
  98.4 1.5 %collective-permute-done.16 = f32[72,128]{1,0:T(8,128)S(1)} collective-permute-done((f32[72,128]{1,0:T(8,128)S(1)}, f32[72,128]{1,0:T(8,128)S(1)}, u32[]{:S(2)}, u32[]{:S(2)}) %collective-permute-start.16) | collective-permute-done | bytes 36896 | tf_op jit(solution)/shard_map/ppermute | solution.py:484
  101.9 1.4 %collective-permute-done.17 = f32[72,128]{1,0:T(8,128)S(1)} collective-permute-done((f32[72,128]{1,0:T(8,128)S(1)}, f32[72,128]{1,0:T(8,128)S(1)}, u32[]{:S(2)}, u32[]{:S(2)}) %collective-permute-start.17) | collective-permute-done | bytes 36896 | tf_op jit(solution)/shard_map/ppermute | solution.py:484
  103.3 0.9 collective-permute-start.18
  104.7 1.7 %collective-permute-start.24 = (f32[72,128]{1,0:T(8,128)S(1)}, f32[72,128]{1,0:T(8,128)S(1)}, u32[]{:S(2)}, u32[]{:S(2)}) collective-permute-start(f32[72,128]{1,0:T(8,128)S(1)} %add.50), channel_id=1, source_target_pairs={{0,13},{1,12},{2,15},{3,14},{4,9},{5,8},{6,11},{7,10},{8,5},{9,4},... | collective-permute-start | bytes 110600 | tf_op jit(solution)/shard_map/ppermute | solution.py:484
  106.5 1.4 %collective-permute-done.18 = f32[72,128]{1,0:T(8,128)S(1)} collective-permute-done((f32[72,128]{1,0:T(8,128)S(1)}, f32[72,128]{1,0:T(8,128)S(1)}, u32[]{:S(2)}, u32[]{:S(2)}) %collective-permute-start.18) | collective-permute-done | bytes 36896 | tf_op jit(solution)/shard_map/ppermute | solution.py:484
  107.9 1.5 %collective-permute-done.24 = f32[72,128]{1,0:T(8,128)S(1)} collective-permute-done((f32[72,128]{1,0:T(8,128)S(1)}, f32[72,128]{1,0:T(8,128)S(1)}, u32[]{:S(2)}, u32[]{:S(2)}) %collective-permute-start.24) | collective-permute-done | bytes 36896 | tf_op jit(solution)/shard_map/ppermute | solution.py:484
  109.9 0.9 collective-permute-done.25.other_ref
  110.8 1.8 %shard_map.181 = (f32[45,3,32]{2,1,0:T(4,128)}, f32[1,32]{1,0:T(1,128)}, f32[27,32,32]{2,1,0:T(8,128)}, f32[1,32]{1,0:T(1,128)}, f32[45,3,32]{2,1,0:T(4,128)}, /*index=5*/f32[1,5]{1,0:T(1,128)}, f32[1,1]{1,0:T(1,128)}) custom-call(s32[2]{0:T(128)S(1)} %pad_add_fusion.place.refs_0_, f32[144,128]{1,0:T(8,128)S(1)} %pad_maximum_fusion.mine_ref, ...), custom_call_target="tpu_custom_call" | custom-call | bytes 1000000 | tf_op jit(solution)/shard_map/pallas_call | solution.py:573
  (61 shorter events, 7.0 us)
Async XLA Ops:
  0.7 1.1 copy-start
  2.6 19.6 %collective-permute-start = (f32[5,4,2048]{2,1,0:T(4,128)S(1)}, f32[5,4,2048]{2,1,0:T(4,128)S(1)}, u32[]{:S(2)}, u32[]{:S(2)}) collective-permute-start(f32[5,4,2048]{2,1,0:T(4,128)S(1)} %get-tuple-element.39), channel_id=1, source_target_pairs={{0,16},{16,0},{32,48},{48,32},{64,80},{80,64},{96,112},{112,96},{1... | collective-permute-start | bytes 491528 | tf_op jit(solution)/shard_map/ppermute | solution.py:135
  5.1 17.1 %collective-permute-start.1 = (f32[5,4,2048]{2,1,0:T(4,128)S(1)}, f32[5,4,2048]{2,1,0:T(4,128)S(1)}, u32[]{:S(2)}, u32[]{:S(2)}) collective-permute-start(f32[5,4,2048]{2,1,0:T(4,128)S(1)} %get-tuple-element.40), channel_id=1, source_target_pairs={{0,112},{16,32},{32,16},{48,64},{64,48},{80,96},{96,80},{112,0},{1... | collective-permute-start | bytes 491528 | tf_op jit(solution)/shard_map/ppermute | solution.py:135
  7.4 14.8 %collective-permute-start.2 = (f32[5,4,2048]{2,1,0:T(4,128)S(1)}, f32[5,4,2048]{2,1,0:T(4,128)S(1)}, u32[]{:S(2)}, u32[]{:S(2)}) collective-permute-start(f32[5,4,2048]{2,1,0:T(4,128)S(1)} %get-tuple-element.41), channel_id=1, source_target_pairs={{0,15},{1,2},{2,1},{3,4},{4,3},{5,6},{6,5},{7,8},{8,7},{9,10},{10,... | collective-permute-start | bytes 491528 | tf_op jit(solution)/shard_map/ppermute | solution.py:136
  11.8 10.4 %collective-permute-start.3 = (f32[5,4,2048]{2,1,0:T(4,128)S(1)}, f32[5,4,2048]{2,1,0:T(4,128)S(1)}, u32[]{:S(2)}, u32[]{:S(2)}) collective-permute-start(f32[5,4,2048]{2,1,0:T(4,128)S(1)} %get-tuple-element.42), channel_id=1, source_target_pairs={{0,1},{1,0},{2,3},{3,2},{4,5},{5,4},{6,7},{7,6},{8,9},{9,8},{10,11... | collective-permute-start | bytes 491528 | tf_op jit(solution)/shard_map/ppermute | solution.py:136
  14.8 41.1 %all-to-all-start.1 = ((f32[16,2,40,128]{3,2,1,0:T(8,128)}), f32[16,2,40,128]{3,2,1,0:T(8,128)S(1)}, u32[]{:S(2)}, u32[]{:S(2)}) async-start(f32[16,2,40,128]{3,2,1,0:T(8,128)} %shard_map.178), calls=%async_computation.1 | async-start | bytes 1310720 | tf_op jit(solution)/shard_map/all_to_all | solution.py:510
  18.3 1.1 copy-start.1
  19.3 1.0 copy-start.9
  20.3 0.9 copy-start.11
  21.2 40.6 %copy-start.2 = (f32[32,32,3,3,3]{1,0,4,3,2:T(8,128)S(1)}, f32[32,32,3,3,3]{1,0,4,3,2:T(8,128)}, u32[]{:S(2)}) copy-start(f32[32,32,3,3,3]{1,0,4,3,2:T(8,128)} %param.18) | copy-start | bytes 331780
  21.2 40.6 %copy-start.3 = (f32[32,5,3,3,3]{0,4,3,2,1:T(4,128)S(1)}, f32[32,5,3,3,3]{0,4,3,2,1:T(4,128)}, u32[]{:S(2)}) copy-start(f32[32,5,3,3,3]{0,4,3,2,1:T(4,128)} %param.16) | copy-start | bytes 51844
  21.3 40.6 %copy-start.4 = (f32[5,32,3,3,3]{1,4,3,2,0:T(4,128)S(1)}, f32[5,32,3,3,3]{1,4,3,2,0:T(4,128)}, u32[]{:S(2)}) copy-start(f32[5,32,3,3,3]{1,4,3,2,0:T(4,128)} %param.20) | copy-start | bytes 51844
  21.3 40.6 %copy-start.6 = (f32[32]{0:T(128)S(1)}, f32[32]{0:T(128)}, u32[]{:S(2)}) copy-start(f32[32]{0:T(128)} %param.17) | copy-start | bytes 388
  21.3 40.6 %copy-start.7 = (f32[32]{0:T(128)S(1)}, f32[32]{0:T(128)}, u32[]{:S(2)}) copy-start(f32[32]{0:T(128)} %param.19) | copy-start | bytes 388
  21.3 40.6 %copy-start.8 = (f32[5]{0:T(128)S(1)}, f32[5]{0:T(128)}, u32[]{:S(2)}) copy-start(f32[5]{0:T(128)} %param.21) | copy-start | bytes 64
  21.3 42.3 %copy-start.5 = (s32[1,1,2]{2,1,0:T(1,128)S(1)}, s32[1,1,2]{2,1,0:T(1,128)}, u32[]{:S(2)}) copy-start(s32[1,1,2]{2,1,0:T(1,128)} %param.14) | copy-start | bytes 28
  22.2 1.0 copy-start.10
  23.2 0.9 copy-start.12
  25.2 12.2 %collective-permute-start.4 = (f32[5,4,2048]{2,1,0:T(4,128)S(1)}, f32[5,4,2048]{2,1,0:T(4,128)S(1)}, u32[]{:S(2)}, u32[]{:S(2)}) collective-permute-start(f32[5,4,2048]{2,1,0:T(4,128)S(1)} %get-tuple-element.44), channel_id=1, source_target_pairs={{0,16},{16,0},{32,48},{48,32},{64,80},{80,64},{96,112},{112,96},{1... | collective-permute-start | bytes 491528 | tf_op jit(solution)/shard_map/ppermute | solution.py:135
  25.3 12.1 %collective-permute-start.5 = (f32[5,4,2048]{2,1,0:T(4,128)S(1)}, f32[5,4,2048]{2,1,0:T(4,128)S(1)}, u32[]{:S(2)}, u32[]{:S(2)}) collective-permute-start(f32[5,4,2048]{2,1,0:T(4,128)S(1)} %get-tuple-element.45), channel_id=1, source_target_pairs={{0,112},{16,32},{32,16},{48,64},{64,48},{80,96},{96,80},{112,0},{1... | collective-permute-start | bytes 491528 | tf_op jit(solution)/shard_map/ppermute | solution.py:135
  27.0 14.3 %collective-permute-start.6 = (f32[5,4,2048]{2,1,0:T(4,128)S(1)}, f32[5,4,2048]{2,1,0:T(4,128)S(1)}, u32[]{:S(2)}, u32[]{:S(2)}) collective-permute-start(f32[5,4,2048]{2,1,0:T(4,128)S(1)} %get-tuple-element.46), channel_id=1, source_target_pairs={{0,15},{1,2},{2,1},{3,4},{4,3},{5,6},{6,5},{7,8},{8,7},{9,10},{10,... | collective-permute-start | bytes 491528 | tf_op jit(solution)/shard_map/ppermute | solution.py:136
  30.6 10.7 %collective-permute-start.7 = (f32[5,4,2048]{2,1,0:T(4,128)S(1)}, f32[5,4,2048]{2,1,0:T(4,128)S(1)}, u32[]{:S(2)}, u32[]{:S(2)}) collective-permute-start(f32[5,4,2048]{2,1,0:T(4,128)S(1)} %get-tuple-element.47), channel_id=1, source_target_pairs={{0,1},{1,0},{2,3},{3,2},{4,5},{5,4},{6,7},{7,6},{8,9},{9,8},{10,11... | collective-permute-start | bytes 491528 | tf_op jit(solution)/shard_map/ppermute | solution.py:136
  42.4 9.5 %collective-permute-start.10 = (f32[5,4,2048]{2,1,0:T(4,128)S(1)}, f32[5,4,2048]{2,1,0:T(4,128)S(1)}, u32[]{:S(2)}, u32[]{:S(2)}) collective-permute-start(f32[5,4,2048]{2,1,0:T(4,128)S(1)} %get-tuple-element.51), channel_id=1, source_target_pairs={{0,16},{16,0},{32,48},{48,32},{64,80},{80,64},{96,112},{112,96},{1... | collective-permute-start | bytes 491528 | tf_op jit(solution)/shard_map/ppermute | solution.py:135
  42.5 9.4 %collective-permute-start.11 = (f32[5,4,2048]{2,1,0:T(4,128)S(1)}, f32[5,4,2048]{2,1,0:T(4,128)S(1)}, u32[]{:S(2)}, u32[]{:S(2)}) collective-permute-start(f32[5,4,2048]{2,1,0:T(4,128)S(1)} %get-tuple-element.52), channel_id=1, source_target_pairs={{0,112},{16,32},{32,16},{48,64},{64,48},{80,96},{96,80},{112,0},{1... | collective-permute-start | bytes 491528 | tf_op jit(solution)/shard_map/ppermute | solution.py:135
  44.4 9.4 %collective-permute-start.8 = (f32[5,4,2048]{2,1,0:T(4,128)S(1)}, f32[5,4,2048]{2,1,0:T(4,128)S(1)}, u32[]{:S(2)}, u32[]{:S(2)}) collective-permute-start(f32[5,4,2048]{2,1,0:T(4,128)S(1)} %get-tuple-element.49), channel_id=1, source_target_pairs={{0,15},{1,2},{2,1},{3,4},{4,3},{5,6},{6,5},{7,8},{8,7},{9,10},{10,... | collective-permute-start | bytes 491528 | tf_op jit(solution)/shard_map/ppermute | solution.py:136
  46.0 7.8 %collective-permute-start.9 = (f32[5,4,2048]{2,1,0:T(4,128)S(1)}, f32[5,4,2048]{2,1,0:T(4,128)S(1)}, u32[]{:S(2)}, u32[]{:S(2)}) collective-permute-start(f32[5,4,2048]{2,1,0:T(4,128)S(1)} %get-tuple-element.50), channel_id=1, source_target_pairs={{0,1},{1,0},{2,3},{3,2},{4,5},{5,4},{6,7},{7,6},{8,9},{9,8},{10,11... | collective-permute-start | bytes 491528 | tf_op jit(solution)/shard_map/ppermute | solution.py:136
  55.9 17.6 %all-to-all-start = ((f32[16,2,40,128]{3,2,1,0:T(8,128)}), f32[16,2,40,128]{3,2,1,0:T(8,128)S(1)}, u32[]{:S(2)}, u32[]{:S(2)}) async-start(f32[16,2,40,128]{3,2,1,0:T(8,128)} %get-tuple-element.54), calls=%async_computation | async-start | bytes 1310720 | tf_op jit(solution)/shard_map/all_to_all | solution.py:554
  79.8 2.5 %collective-permute-start.12 = (f32[144,128]{1,0:T(8,128)S(1)}, f32[144,128]{1,0:T(8,128)S(1)}, u32[]{:S(2)}, u32[]{:S(2)}) collective-permute-start(f32[144,128]{1,0:T(8,128)S(1)} %get-tuple-element.62), channel_id=1, source_target_pairs={{0,1},{1,0},{2,3},{3,2},{4,5},{5,4},{6,7},{7,6},{8,9},{9,8},{10,11... | collective-permute-start | bytes 221192 | tf_op jit(solution)/shard_map/ppermute | solution.py:481
  82.3 3.5 %collective-permute-start.13 = (f32[72,128]{1,0:T(8,128)S(1)}, f32[72,128]{1,0:T(8,128)S(1)}, u32[]{:S(2)}, u32[]{:S(2)}) collective-permute-start(f32[72,128]{1,0:T(8,128)S(1)} %get-tuple-element.72), channel_id=1, source_target_pairs={{0,17},{1,16},{2,19},{3,18},{4,21},{5,20},{6,23},{7,22},{8,25},{9,... | collective-permute-start | bytes 110600 | tf_op jit(solution)/shard_map/ppermute | solution.py:484
  83.9 3.4 %collective-permute-start.19 = (f32[72,128]{1,0:T(8,128)S(1)}, f32[72,128]{1,0:T(8,128)S(1)}, u32[]{:S(2)}, u32[]{:S(2)}) collective-permute-start(f32[72,128]{1,0:T(8,128)S(1)} %get-tuple-element.73), channel_id=1, source_target_pairs={{0,33},{1,32},{2,35},{3,34},{4,37},{5,36},{6,39},{7,38},{8,41},{9,... | collective-permute-start | bytes 110600 | tf_op jit(solution)/shard_map/ppermute | solution.py:484
  87.3 4.7 %collective-permute-start.14 = (f32[72,128]{1,0:T(8,128)S(1)}, f32[72,128]{1,0:T(8,128)S(1)}, u32[]{:S(2)}, u32[]{:S(2)}) collective-permute-start(f32[72,128]{1,0:T(8,128)S(1)} %get-tuple-element.70), channel_id=1, source_target_pairs={{0,19},{1,18},{2,17},{3,16},{4,23},{5,22},{6,21},{7,20},{8,27},{9,... | collective-permute-start | bytes 110600 | tf_op jit(solution)/shard_map/ppermute | solution.py:484
  87.4 4.7 %collective-permute-start.20 = (f32[72,128]{1,0:T(8,128)S(1)}, f32[72,128]{1,0:T(8,128)S(1)}, u32[]{:S(2)}, u32[]{:S(2)}) collective-permute-start(f32[72,128]{1,0:T(8,128)S(1)} %get-tuple-element.71), channel_id=1, source_target_pairs={{0,97},{1,96},{2,99},{3,98},{4,101},{5,100},{6,103},{7,102},{8,105... | collective-permute-start | bytes 110600 | tf_op jit(solution)/shard_map/ppermute | solution.py:484
  91.9 3.4 %collective-permute-start.15 = (f32[72,128]{1,0:T(8,128)S(1)}, f32[72,128]{1,0:T(8,128)S(1)}, u32[]{:S(2)}, u32[]{:S(2)}) collective-permute-start(f32[72,128]{1,0:T(8,128)S(1)} %add.41), channel_id=1, source_target_pairs={{0,5},{1,4},{2,7},{3,6},{4,1},{5,0},{6,3},{7,2},{8,13},{9,12},{10,... | collective-permute-start | bytes 110600 | tf_op jit(solution)/shard_map/ppermute | solution.py:484
  92.0 3.9 %collective-permute-start.21 = (f32[72,128]{1,0:T(8,128)S(1)}, f32[72,128]{1,0:T(8,128)S(1)}, u32[]{:S(2)}, u32[]{:S(2)}) collective-permute-start(f32[72,128]{1,0:T(8,128)S(1)} %add.47), channel_id=1, source_target_pairs={{0,17},{1,16},{2,19},{3,18},{4,21},{5,20},{6,23},{7,22},{8,25},{9,... | collective-permute-start | bytes 110600 | tf_op jit(solution)/shard_map/ppermute | solution.py:484
  95.3 4.6 %collective-permute-start.16 = (f32[72,128]{1,0:T(8,128)S(1)}, f32[72,128]{1,0:T(8,128)S(1)}, u32[]{:S(2)}, u32[]{:S(2)}) collective-permute-start(f32[72,128]{1,0:T(8,128)S(1)} %add.42), channel_id=1, source_target_pairs={{0,13},{1,12},{2,15},{3,14},{4,9},{5,8},{6,11},{7,10},{8,5},{9,4},... | collective-permute-start | bytes 110600 | tf_op jit(solution)/shard_map/ppermute | solution.py:484
  96.0 5.3 %collective-permute-start.22 = (f32[72,128]{1,0:T(8,128)S(1)}, f32[72,128]{1,0:T(8,128)S(1)}, u32[]{:S(2)}, u32[]{:S(2)}) collective-permute-start(f32[72,128]{1,0:T(8,128)S(1)} %add.48), channel_id=1, source_target_pairs={{0,19},{1,18},{2,17},{3,16},{4,23},{5,22},{6,21},{7,20},{8,27},{9,... | collective-permute-start | bytes 110600 | tf_op jit(solution)/shard_map/ppermute | solution.py:484
  99.9 3.4 %collective-permute-start.17 = (f32[72,128]{1,0:T(8,128)S(1)}, f32[72,128]{1,0:T(8,128)S(1)}, u32[]{:S(2)}, u32[]{:S(2)}) collective-permute-start(f32[72,128]{1,0:T(8,128)S(1)} %add.43), channel_id=1, source_target_pairs={{0,33},{1,32},{2,35},{3,34},{4,37},{5,36},{6,39},{7,38},{8,41},{9,... | collective-permute-start | bytes 110600 | tf_op jit(solution)/shard_map/ppermute | solution.py:484
  101.2 3.5 %collective-permute-start.23 = (f32[72,128]{1,0:T(8,128)S(1)}, f32[72,128]{1,0:T(8,128)S(1)}, u32[]{:S(2)}, u32[]{:S(2)}) collective-permute-start(f32[72,128]{1,0:T(8,128)S(1)} %add.49), channel_id=1, source_target_pairs={{0,5},{1,4},{2,7},{3,6},{4,1},{5,0},{6,3},{7,2},{8,13},{9,12},{10,... | collective-permute-start | bytes 110600 | tf_op jit(solution)/shard_map/ppermute | solution.py:484
  103.3 4.6 %collective-permute-start.18 = (f32[72,128]{1,0:T(8,128)S(1)}, f32[72,128]{1,0:T(8,128)S(1)}, u32[]{:S(2)}, u32[]{:S(2)}) collective-permute-start(f32[72,128]{1,0:T(8,128)S(1)} %add.44), channel_id=1, source_target_pairs={{0,97},{1,96},{2,99},{3,98},{4,101},{5,100},{6,103},{7,102},{8,105... | collective-permute-start | bytes 110600 | tf_op jit(solution)/shard_map/ppermute | solution.py:484
  104.7 4.7 %collective-permute-start.24 = (f32[72,128]{1,0:T(8,128)S(1)}, f32[72,128]{1,0:T(8,128)S(1)}, u32[]{:S(2)}, u32[]{:S(2)}) collective-permute-start(f32[72,128]{1,0:T(8,128)S(1)} %add.50), channel_id=1, source_target_pairs={{0,13},{1,12},{2,15},{3,14},{4,9},{5,8},{6,11},{7,10},{8,5},{9,4},... | collective-permute-start | bytes 110600 | tf_op jit(solution)/shard_map/ppermute | solution.py:484
  109.4 1.4 %collective-permute-start.25 = (f32[144,128]{1,0:T(8,128)S(1)}, f32[144,128]{1,0:T(8,128)S(1)}, u32[]{:S(2)}, u32[]{:S(2)}) collective-permute-start(f32[144,128]{1,0:T(8,128)S(1)} %pad_maximum_fusion.mine_ref), channel_id=1, source_target_pairs={{0,1},{1,0},{2,3},{3,2},{4,5},{5,4},{6,7},{7,6},{8,9},{9,8},{10,11... | collective-permute-start | bytes 221192 | tf_op jit(solution)/shard_map/ppermute | solution.py:487
